TPU v7x, 32 devices: a whole 2x2x4 slice. The times are simulated.
32 devices in a mesh: dp: 2 (over y), row: 4 (over z), col: 4 (over x, core).
Axes of the slice: x: 2, y: 2, z: 4, core: 2. Of those that a mesh axis runs over, the one named last changes fastest.
Arguments:
- hidden_in: bfloat16 [4096, 1600], P(('dp', 'col'), 'row'), may hold values from -6 to 6
- upstream: bfloat16 [4096, 1600], P(('dp', 'col'), 'row')
- segment_ids: int32 [4096], P('dp'), may hold values from 1 to 3, as said below
- qkv_weight: float32 [1600, 4800], P(('row', 'dp'), 'col')
- proj_weight: float32 [1600, 1600], P(('col', 'dp'), 'row'), may hold values from -0.625 to 0.625
- up_weight: float32 [1600, 6400], P(('row', 'dp'), 'col'), may hold values from -0.15625 to 0.15625
- down_weight: float32 [6400, 1600], P(('col', 'dp'), 'row'), may hold values from -0.078125 to 0.078125
- vectors: float32 [8, 1600], replicated
- up_bias: float32 [6400], replicated, may hold values from -3 to 3
- qkv_moments: float32 [2, 1600, 4800], P(None, ('row', 'dp'), 'col'), as said below
- proj_moments: float32 [2, 1600, 1600], P(None, ('col', 'dp'), 'row'), as said below
- up_moments: float32 [2, 1600, 6400], P(None, ('row', 'dp'), 'col'), as said below
- down_moments: float32 [2, 6400, 1600], P(None, ('col', 'dp'), 'row'), as said below
- vector_moments: float32 [2, 8, 1600], replicated, as said below
- bias_moments: float32 [2, 6400], replicated, as said below
Outputs:
- block_out: bfloat16 [4096, 1600], P(('dp', 'col'), 'row')
- input_grad: bfloat16 [4096, 1600], P(('dp', 'col'), 'row')
- qkv_grad: float32 [1600, 4800], P(('row', 'dp'), 'col')
- proj_grad: float32 [1600, 1600], P(('col', 'dp'), 'row')
- up_grad: float32 [1600, 6400], P(('row', 'dp'), 'col')
- down_grad: float32 [6400, 1600], P(('col', 'dp'), 'row')
- vector_grad: float32 [8, 1600], replicated
- bias_grad: float32 [6400], replicated
- new_qkv: float32 [1600, 4800], P(('row', 'dp'), 'col')
- new_proj: float32 [1600, 1600], P(('col', 'dp'), 'row')
- new_up: float32 [1600, 6400], P(('row', 'dp'), 'col')
- new_down: float32 [6400, 1600], P(('col', 'dp'), 'row')
- new_vectors: float32 [8, 1600], replicated
- new_bias: float32 [6400], replicated
- qkv_state: float32 [2, 1600, 4800], P(None, ('row', 'dp'), 'col')
- proj_state: float32 [2, 1600, 1600], P(None, ('col', 'dp'), 'row')
- up_state: float32 [2, 1600, 6400], P(None, ('row', 'dp'), 'col')
- down_state: float32 [2, 6400, 1600], P(None, ('col', 'dp'), 'row')
- vector_state: float32 [2, 8, 1600], replicated
- bias_state: float32 [2, 6400], replicated
Inputs may be any that keep to these rules, and one draw needn't show every extreme that they name: `segment_ids`: ids never fall; a sequence is a run of equal ids; no sequence crosses a multiple of 2048 tokens; the first 2048 tokens form one sequence. `qkv_moments`: the second row is positive. `proj_moments`: the second row is positive. `up_moments`: the second row is positive. `down_moments`: the second row is positive. `vector_moments`: the second row is positive. `bias_moments`: the second row is positive.
All inputs are finite; a program needn't handle non-finite values.
Results may differ from a plain program's by a relative error of at most 0.025.
Values may be sent and summed in bfloat16 or wider, within the bound.
No kernel may reach another device: no remote copies, remote signals or barrier semaphores. Data moves between devices by JAX's collectives and lax.ppermute only.
A program may use at most 256 MiB of HBM per device.

v0:
```python
import math

import jax
import jax.numpy as jnp
from jax import lax
from jax.sharding import PartitionSpec as P

D = 1600
HEADS = 25
HEAD_DIM = 64
HEAD_BLOCK = 5
STEP = 3


EPS_NORM = 1e-05
BETA_ONE = 0.9
BETA_TWO = 0.95
EPS_ADAM = 1e-08
LR_MATRIX = 0.08
LR_VECTOR = 0.3
DECAY = 0.1
NEG_FILL = -1e30
GELU_COEF = 0.7978845608028654
GELU_CUBE = 0.044715


def gelu_tanh(pre_act):
    inside = GELU_COEF * (pre_act + GELU_CUBE * pre_act * pre_act * pre_act)
    return 0.5 * pre_act * (1.0 + jnp.tanh(inside))


def gelu_slope(pre_act):
    inside = GELU_COEF * (pre_act + GELU_CUBE * pre_act * pre_act * pre_act)
    tanh_val = jnp.tanh(inside)
    return 0.5 * (1.0 + tanh_val) + 0.5 * pre_act * (1.0 - tanh_val * tanh_val) * GELU_COEF * (
        1.0 + 3.0 * GELU_CUBE * pre_act * pre_act
    )


def row_totals(first_term, second_term):
    return lax.psum(
        (jnp.sum(first_term, axis=1, keepdims=True), jnp.sum(second_term, axis=1, keepdims=True)),
        "row",
    )


def norm_forward(values, gain_vec, shift_vec):
    row_sums, squares = row_totals(values, values * values)
    center = row_sums / D
    spread = squares / D - center * center
    inverse = lax.rsqrt(spread + EPS_NORM)
    normed = (values - center) * inverse
    return (normed, inverse, (normed * gain_vec + shift_vec).astype(jnp.bfloat16))


def norm_backward(grad_normed, normed, inverse, gain_vec):
    scaled = grad_normed * gain_vec
    first_sum, second_sum = row_totals(scaled, scaled * normed)
    return inverse * (scaled - first_sum / D - normed * (second_sum / D))


def widen(local_rows, weight_block, flipped):
    gathered = lax.all_gather(local_rows, "col", axis=0, tiled=True)
    right_side = weight_block.T if flipped else weight_block
    partial_rows = jnp.dot(gathered, right_side, preferred_element_type=jnp.float32)
    return (
        gathered,
        lax.psum_scatter(
            partial_rows.astype(jnp.bfloat16), "row", scatter_dimension=0, tiled=True
        ).astype(jnp.float32),
    )


def narrow(local_rows, weight_block, flipped):
    gathered = lax.all_gather(local_rows, "row", axis=0, tiled=True)
    right_side = weight_block.T if flipped else weight_block
    partial_rows = jnp.dot(gathered, right_side, preferred_element_type=jnp.float32)
    return (
        gathered,
        lax.psum_scatter(
            partial_rows.astype(jnp.bfloat16), "col", scatter_dimension=0, tiled=True
        ).astype(jnp.float32),
    )


def to_heads(feature_rows):
    return lax.all_to_all(feature_rows, "col", split_axis=0, concat_axis=1, tiled=True)


def from_heads(head_rows):
    return lax.all_to_all(head_rows, "col", split_axis=1, concat_axis=0, tiled=True)


def split_heads(matrix):
    return matrix.reshape(matrix.shape[0], HEADS // HEAD_BLOCK, HEAD_BLOCK, HEAD_DIM).transpose(
        1, 2, 0, 3
    )


def merge_heads(blocks):
    return blocks.transpose(2, 0, 1, 3).reshape(blocks.shape[2], D)


def masked_scores(query_blk, key_blk, allowed):
    scores = jnp.einsum("hqe,hke->hqk", query_blk, key_blk, preferred_element_type=jnp.float32) * (
        1.0 / math.sqrt(HEAD_DIM)
    )
    return jnp.where(allowed[None], scores, NEG_FILL)


def attend(query_blk, key_blk, value_blk, allowed):
    scores = masked_scores(query_blk, key_blk, allowed)
    row_max = jnp.max(scores, axis=2, keepdims=True)
    log_total = row_max + jnp.log(jnp.sum(jnp.exp(scores - row_max), axis=2, keepdims=True))
    chances = jnp.exp(scores - log_total)
    mixed_out = jnp.einsum(
        "hqk,hke->hqe", chances.astype(jnp.bfloat16), value_blk, preferred_element_type=jnp.float32
    )
    return (mixed_out.astype(jnp.bfloat16), log_total)


def query_side(query_blk, key_blk, value_blk, log_total, grad_blk, allowed):
    chances = jnp.exp(masked_scores(query_blk, key_blk, allowed) - log_total)
    grad_chances = jnp.einsum(
        "hqe,hke->hqk", grad_blk, value_blk, preferred_element_type=jnp.float32
    )
    row_dot = jnp.sum(chances * grad_chances, axis=2, keepdims=True)
    grad_scores = (chances * (grad_chances - row_dot)).astype(jnp.bfloat16)
    grad_query = jnp.einsum(
        "hqk,hke->hqe", grad_scores, key_blk, preferred_element_type=jnp.float32
    ) * (1.0 / math.sqrt(HEAD_DIM))
    return (chances, grad_scores, grad_query, row_dot)


def adam_step(weight, gradient, moments, rate):
    first_moment = BETA_ONE * moments[0] + (1.0 - BETA_ONE) * gradient
    second = BETA_TWO * moments[1] + (1.0 - BETA_TWO) * gradient * gradient
    first_fix = 1.0 - BETA_ONE**STEP
    second_fix = 1.0 - BETA_TWO**STEP
    stepped = weight - rate * (
        first_moment / first_fix / (jnp.sqrt(second / second_fix) + EPS_ADAM) + DECAY * weight
    )
    return (stepped, jnp.stack([first_moment, second]))


def per_device(
    hidden_in,
    upstream,
    segment_ids,
    qkv_weight,
    proj_weight,
    up_weight,
    down_weight,
    vectors,
    up_bias,
    qkv_moments,
    proj_moments,
    up_moments,
    down_moments,
    vector_moments,
    bias_moments,
):
    factor = 1.0 / math.sqrt(HEAD_DIM)
    row_index = lax.axis_index("row")
    col_index = lax.axis_index("col")
    row_width = D // lax.axis_size("row")
    qkv_cols = qkv_weight.shape[1]
    up_cols = up_weight.shape[1]
    w_qkv, w_proj, w_up, w_down = (
        lax.all_gather(qkv_weight.astype(jnp.bfloat16), "dp", axis=0, tiled=True),
        lax.all_gather(proj_weight.astype(jnp.bfloat16), "dp", axis=0, tiled=True),
        lax.all_gather(up_weight.astype(jnp.bfloat16), "dp", axis=0, tiled=True),
        lax.all_gather(down_weight.astype(jnp.bfloat16), "dp", axis=0, tiled=True),
    )

    def row_slice(vector_row):
        return lax.dynamic_slice_in_dim(vector_row, row_index * row_width, row_width)

    def place_rows(partial_vec):
        return lax.dynamic_update_slice_in_dim(
            jnp.zeros((D,), jnp.float32), partial_vec, row_index * row_width, 0
        )

    gain_one = row_slice(vectors[0])
    shift_one = row_slice(vectors[1])
    shift_proj = row_slice(vectors[4])
    gain_two = row_slice(vectors[5])
    shift_two = row_slice(vectors[6])
    shift_down = row_slice(vectors[7])
    qkv_full_shift = jnp.concatenate([vectors[2], jnp.zeros((D,), jnp.float32), vectors[3]])
    qkv_shift = lax.dynamic_slice_in_dim(qkv_full_shift, col_index * qkv_cols, qkv_cols)
    up_shift = lax.dynamic_slice_in_dim(up_bias, col_index * up_cols, up_cols)
    inputs_f = hidden_in.astype(jnp.float32)
    normed_one, inverse_one, ln_one = norm_forward(inputs_f, gain_one, shift_one)
    gathered_one, qkv_sum = widen(ln_one, w_qkv, False)
    qkv_rows = (qkv_sum + qkv_shift).astype(jnp.bfloat16)
    qkv_heads = to_heads(qkv_rows)
    query_count = qkv_heads.shape[0]
    group_len = segment_ids.shape[0]
    query_start = (row_index * lax.axis_size("col") + col_index) * query_count
    query_ids = lax.dynamic_slice_in_dim(segment_ids, query_start, query_count)
    query_pos = query_start + jnp.arange(query_count, dtype=jnp.int32)
    key_pos = jnp.arange(group_len, dtype=jnp.int32)
    allowed = (query_ids[:, None] == segment_ids[None, :]) & (
        key_pos[None, :] <= query_pos[:, None]
    )
    key_values = lax.all_gather(qkv_heads[:, D:], ("row", "col"), axis=0, tiled=True)
    query_blocks = split_heads(qkv_heads[:, :D])
    key_blocks = split_heads(key_values[:, :D])
    value_blocks = split_heads(key_values[:, D:])
    attn_blocks, log_totals = lax.map(
        lambda block_items: attend(block_items[0], block_items[1], block_items[2], allowed),
        (query_blocks, key_blocks, value_blocks),
    )
    attn_rows = from_heads(merge_heads(attn_blocks))
    gathered_attn, proj_sum = narrow(attn_rows, w_proj, False)
    resid_mid = inputs_f + proj_sum + shift_proj
    normed_two, inverse_two, ln_two = norm_forward(resid_mid, gain_two, shift_two)
    gathered_two, up_sum = widen(ln_two, w_up, False)
    pre_act = up_sum + up_shift
    activated = gelu_tanh(pre_act).astype(jnp.bfloat16)
    gathered_act, down_sum = narrow(activated, w_down, False)
    block_out = (resid_mid + down_sum + shift_down).astype(jnp.bfloat16)
    grad_top = upstream.astype(jnp.float32)
    gathered_top, grad_act = widen(upstream, w_down, True)
    grad_pre = grad_act * gelu_slope(pre_act)
    grad_pre_half = grad_pre.astype(jnp.bfloat16)
    gathered_pre, grad_ln_two = narrow(grad_pre_half, w_up, True)
    down_part = jnp.dot(gathered_act.T, gathered_top, preferred_element_type=jnp.float32)
    up_part = jnp.dot(gathered_two.T, gathered_pre, preferred_element_type=jnp.float32)
    grad_mid = grad_top + norm_backward(grad_ln_two, normed_two, inverse_two, gain_two)
    grad_mid_half = grad_mid.astype(jnp.bfloat16)
    gathered_mid, grad_attn = widen(grad_mid_half, w_proj, True)
    proj_part = jnp.dot(gathered_attn.T, gathered_mid, preferred_element_type=jnp.float32)
    grad_heads = to_heads(grad_attn.astype(jnp.bfloat16))
    grad_blocks = split_heads(grad_heads)

    def full_pass(block_items):
        query_blk, key_blk, value_blk, log_total, grad_blk = block_items
        chances, grad_scores, grad_query, row_dot = query_side(
            query_blk, key_blk, value_blk, log_total, grad_blk, allowed
        )
        grad_key = (
            jnp.einsum("hqk,hqe->hke", grad_scores, query_blk, preferred_element_type=jnp.float32)
            * factor
        )
        grad_value = jnp.einsum(
            "hqk,hqe->hke",
            chances.astype(jnp.bfloat16),
            grad_blk,
            preferred_element_type=jnp.float32,
        )
        return (grad_query, grad_key, grad_value)

    grad_query_blocks, key_grad_blocks, value_grad_blocks = lax.map(
        full_pass, (query_blocks, key_blocks, value_blocks, log_totals, grad_blocks)
    )
    key_value_grads = jnp.concatenate(
        [merge_heads(key_grad_blocks), merge_heads(value_grad_blocks)], axis=1
    )
    own_kv = lax.psum_scatter(
        key_value_grads.astype(jnp.bfloat16), ("row", "col"), scatter_dimension=0, tiled=True
    ).astype(jnp.float32)
    grad_query_rows = merge_heads(grad_query_blocks)
    bias_query = jnp.sum(grad_query_rows, axis=0)
    bias_value = jnp.sum(own_kv[:, D:], axis=0)
    grad_qkv = jnp.concatenate([grad_query_rows, own_kv], axis=1).astype(jnp.bfloat16)
    gathered_qkv, grad_ln_one = narrow(from_heads(grad_qkv), w_qkv, True)
    qkv_part = jnp.dot(gathered_one.T, gathered_qkv, preferred_element_type=jnp.float32)
    grad_input = grad_mid + norm_backward(grad_ln_one, normed_one, inverse_one, gain_one)
    input_grad = grad_input.astype(jnp.bfloat16)
    vector_part = jnp.stack(
        [
            place_rows(jnp.sum(grad_ln_one * normed_one, axis=0)),
            place_rows(jnp.sum(grad_ln_one, axis=0)),
            bias_query,
            bias_value,
            place_rows(jnp.sum(grad_mid, axis=0)),
            place_rows(jnp.sum(grad_ln_two * normed_two, axis=0)),
            place_rows(jnp.sum(grad_ln_two, axis=0)),
            place_rows(jnp.sum(grad_top, axis=0)),
        ]
    )
    bias_part = lax.dynamic_update_slice_in_dim(
        jnp.zeros((up_bias.shape[0],), jnp.float32),
        jnp.sum(grad_pre, axis=0),
        col_index * up_cols,
        0,
    )
    vector_grad, bias_grad = lax.psum((vector_part, bias_part), ("dp", "row", "col"))
    qkv_grad, proj_grad, up_grad, down_grad = (
        lax.psum_scatter(
            qkv_part.astype(jnp.bfloat16), "dp", scatter_dimension=0, tiled=True
        ).astype(jnp.float32),
        lax.psum_scatter(
            proj_part.astype(jnp.bfloat16), "dp", scatter_dimension=0, tiled=True
        ).astype(jnp.float32),
        lax.psum_scatter(
            up_part.astype(jnp.bfloat16), "dp", scatter_dimension=0, tiled=True
        ).astype(jnp.float32),
        lax.psum_scatter(
            down_part.astype(jnp.bfloat16), "dp", scatter_dimension=0, tiled=True
        ).astype(jnp.float32),
    )
    new_qkv, qkv_state = adam_step(qkv_weight, qkv_grad, qkv_moments, LR_MATRIX)
    new_proj, proj_state = adam_step(proj_weight, proj_grad, proj_moments, LR_MATRIX)
    new_up, up_state = adam_step(up_weight, up_grad, up_moments, LR_MATRIX)
    new_down, down_state = adam_step(down_weight, down_grad, down_moments, LR_MATRIX)
    new_vectors, vector_state = adam_step(vectors, vector_grad, vector_moments, LR_VECTOR)
    new_bias, bias_state = adam_step(up_bias, bias_grad, bias_moments, LR_VECTOR)
    return (
        block_out,
        input_grad,
        qkv_grad,
        proj_grad,
        up_grad,
        down_grad,
        vector_grad,
        bias_grad,
        new_qkv,
        new_proj,
        new_up,
        new_down,
        new_vectors,
        new_bias,
        qkv_state,
        proj_state,
        up_state,
        down_state,
        vector_state,
        bias_state,
    )


def solution(mesh):
    placed = (
        P(("dp", "col"), "row"),
        P(("dp", "col"), "row"),
        P("dp"),
        P(("row", "dp"), "col"),
        P(("col", "dp"), "row"),
        P(("row", "dp"), "col"),
        P(("col", "dp"), "row"),
        P(),
        P(),
        P(None, ("row", "dp"), "col"),
        P(None, ("col", "dp"), "row"),
        P(None, ("row", "dp"), "col"),
        P(None, ("col", "dp"), "row"),
        P(),
        P(),
    )
    return jax.shard_map(
        per_device,
        mesh=mesh,
        in_specs=placed,
        out_specs=(
            P(("dp", "col"), "row"),
            P(("dp", "col"), "row"),
            P(("row", "dp"), "col"),
            P(("col", "dp"), "row"),
            P(("row", "dp"), "col"),
            P(("col", "dp"), "row"),
            P(),
            P(),
            P(("row", "dp"), "col"),
            P(("col", "dp"), "row"),
            P(("row", "dp"), "col"),
            P(("col", "dp"), "row"),
            P(),
            P(),
            P(None, ("row", "dp"), "col"),
            P(None, ("col", "dp"), "row"),
            P(None, ("row", "dp"), "col"),
            P(None, ("col", "dp"), "row"),
            P(),
            P(),
        ),
        check_vma=False,
    )
```

profile of v0, /device:TPU:0, one launch (start us, length us, event | category | flops | bytes accessed | tf_op | source)
XLA Modules:
  0.0 1602.7 jit_solution(6416699591523800499)
XLA Ops:
  10.8 13.4 all-reduce.5
  26.3 12.0 all_gather.40
  51.2 88.4 %reduce-scatter.20.cloned.1.call-done = bf16[512,1200]{0,1:T(8,128)(2,1)} async-done(((bf16[2048,1200]{0,1:T(8,128)(2,1)}), bf16[512,1200]{0,1:T(8,128)(2,1)}) %reduce-scatter.20.cloned.1.call-update) | async-done | bytes 1228816 | tf_op jit(solution)/shard_map/reduce_scatter | solution.py:68
  141.2 18.9 %all_to_all.70 = bf16[4,128,1200]{1,2,0:T(8,128)(2,1)S(1)} all-to-all(bf16[4,128,1200]{1,2,0:T(8,128)(2,1)S(1)} %copy_bitcast_fusion.1), channel_id=1, replica_groups=mesh['dp'=2,'row'=4,'col'=4] {'col'}, dimensions={0} | all-to-all | bytes 2457600 | tf_op jit(solution)/shard_map/all_to_all | solution.py:87
  161.3 106.8 %all-gather.15.cloned.1.call-done = bf16[2048,3200]{0,1:T(8,128)(2,1)} async-done(((bf16[128,3200]{0,1:T(8,128)(2,1)}), bf16[2048,3200]{0,1:T(8,128)(2,1)}) %all-gather.15.cloned.1.call-update) | async-done | bytes 13107216 | tf_op jit(solution)/shard_map/all_gather | solution.py:207
  268.1 11.0 fusion.116
  279.1 36.2 %while.28 = (s32[]{:T(128)}, bf16[5,5,128,64]{2,3,1,0:T(8,128)(2,1)S(1)}, f32[5,5,128,1]{2,1,3,0:T(8,128)S(1)}, bf16[5,5,128,64]{2,3,1,0:T(8,128)(2,1)S(1)}, bf1...) while((s32[]{:T(128)}, ...), condition=%wide.region_8.9_spmd.clone, body=%wide.region_5.8_spmd.clone.sunk | while | flops 350788992 | bytes 19602032 | solution.py:211
  315.3 10.3 all_to_all.71
  334.2 28.6 %all-gather.17.cloned.1.call-done = bf16[2048,400]{0,1:T(8,128)(2,1)} async-done(((bf16[512,400]{0,1:T(8,128)(2,1)}), bf16[2048,400]{0,1:T(8,128)(2,1)}) %all-gather.17.cloned.1.call-update) | async-done | bytes 1638416 | tf_op jit(solution)/shard_map/all_gather | solution.py:75
  371.8 22.2 %reduce-scatter.22.cloned.1.call-done = bf16[512,400]{0,1:T(8,128)(2,1)} async-done(((bf16[2048,400]{0,1:T(8,128)(2,1)}), bf16[512,400]{0,1:T(8,128)(2,1)}) %reduce-scatter.22.cloned.1.call-update) | async-done | bytes 409616 | tf_op jit(solution)/shard_map/reduce_scatter | solution.py:80
  395.2 11.7 all-reduce.4
  422.9 18.1 %all-gather.21.cloned.1.call-done = bf16[400,1600]{1,0:T(8,128)(2,1)} async-done(((bf16[200,1600]{1,0:T(8,128)(2,1)}), bf16[400,1600]{1,0:T(8,128)(2,1)}) %all-gather.21.cloned.1.call-update) | async-done | bytes 1280016 | tf_op jit(solution)/shard_map/all_gather | solution.py:172
  441.1 22.1 %all-gather.19.cloned.1.call-done = bf16[2048,400]{0,1:T(8,128)(2,1)} async-done(((bf16[512,400]{0,1:T(8,128)(2,1)}), bf16[2048,400]{0,1:T(8,128)(2,1)}) %all-gather.19.cloned.1.call-update) | async-done | bytes 1638416 | tf_op jit(solution)/shard_map/all_gather | solution.py:63
  472.2 65.9 %reduce-scatter.28.cloned.1.call-done = bf16[512,1600]{0,1:T(8,128)(2,1)} async-done(((bf16[2048,1600]{0,1:T(8,128)(2,1)}), bf16[512,1600]{0,1:T(8,128)(2,1)}) %reduce-scatter.28.cloned.1.call-update) | async-done | bytes 1638416 | tf_op jit(solution)/shard_map/reduce_scatter | solution.py:68
  538.1 117.8 %reduce-scatter.24.cloned.1.call-done = bf16[512,1600]{0,1:T(8,128)(2,1)} async-done(((bf16[2048,1600]{0,1:T(8,128)(2,1)}), bf16[512,1600]{0,1:T(8,128)(2,1)}) %reduce-scatter.24.cloned.1.call-update) | async-done | bytes 1638416 | tf_op jit(solution)/shard_map/reduce_scatter | solution.py:68
  662.5 119.3 %all-gather.27.cloned.1.call-done = bf16[2048,1600]{0,1:T(8,128)(2,1)} async-done(((bf16[512,1600]{0,1:T(8,128)(2,1)}), bf16[2048,1600]{0,1:T(8,128)(2,1)}) %all-gather.27.cloned.1.call-update) | async-done | bytes 6553616 | tf_op jit(solution)/shard_map/all_gather | solution.py:75
  789.4 112.4 %all-gather.23.cloned.1.call-done = bf16[2048,1600]{0,1:T(8,128)(2,1)} async-done(((bf16[512,1600]{0,1:T(8,128)(2,1)}), bf16[2048,1600]{0,1:T(8,128)(2,1)}) %all-gather.23.cloned.1.call-update) | async-done | bytes 6553616 | tf_op jit(solution)/shard_map/all_gather | solution.py:75
  910.7 8.7 all-reduce.3
  919.4 16.4 %reduce-scatter.26.cloned.1.call-done = bf16[512,400]{0,1:T(8,128)(2,1)} async-done(((bf16[2048,400]{0,1:T(8,128)(2,1)}), bf16[512,400]{0,1:T(8,128)(2,1)}) %reduce-scatter.26.cloned.1.call-update) | async-done | bytes 409616 | tf_op jit(solution)/shard_map/reduce_scatter | solution.py:80
  939.8 19.9 %all-gather.29.cloned.1.call-done = bf16[2048,400]{0,1:T(8,128)(2,1)} async-done(((bf16[512,400]{0,1:T(8,128)(2,1)}), bf16[2048,400]{0,1:T(8,128)(2,1)}) %all-gather.29.cloned.1.call-update) | async-done | bytes 1638416 | tf_op jit(solution)/shard_map/all_gather | solution.py:63
  963.4 36.5 %reduce-scatter.32.cloned.1.call-done = bf16[512,400]{0,1:T(8,128)(2,1)} async-done(((bf16[2048,400]{0,1:T(8,128)(2,1)}), bf16[512,400]{0,1:T(8,128)(2,1)}) %reduce-scatter.32.cloned.1.call-update) | async-done | bytes 409616 | tf_op jit(solution)/shard_map/reduce_scatter | solution.py:68
  1012.7 61.5 %while.29 = (s32[]{:T(128)}, f32[5,5,128,64]{2,3,1,0:T(8,128)S(1)}, bf16[5,5,2048,64]{2,3,1,0:T(8,128)(2,1)}, bf16[5,5,2048,64]{2,3,1,0:T(8,128)(2,1)}, bf16[5,5...) while((s32[]{:T(128)}, f32[5,5,128,64]{2,3,1,0:T(8,128)S(1)}, ...), condition=%wide.region_25.26_spmd.clone, body=%wide.region_23.25_spmd.clone.sunk | while | flops 852139392 | bytes 49541256 | solution.py:255
  1074.2 10.3 pad_maximum_fusion
  1084.5 17.3 %copy.50 = bf16[2048,3200]{1,0:T(8,128)(2,1)} copy(bf16[2048,3200]{0,1:T(8,128)(2,1)} %pad_maximum_fusion) | data formatting | bytes 26214400
  1114.1 124.4 %reduce-scatter.40.cloned.1.call-done = bf16[128,3200]{1,0:T(8,128)(2,1)} async-done(((bf16[2048,3200]{1,0:T(8,128)(2,1)}), bf16[128,3200]{1,0:T(8,128)(2,1)}) %reduce-scatter.40.cloned.1.call-update) | async-done | bytes 819216
  1241.3 18.9 %all_to_all.72 = bf16[128,4,1200]{0,2,1:T(8,128)(2,1)S(1)} all-to-all(bf16[128,4,1200]{0,2,1:T(8,128)(2,1)S(1)} %bitcast.304), channel_id=1, replica_groups=mesh['dp'=2,'row'=4,'col'=4] {'col'}, dimensions={1} | all-to-all | bytes 2457600 | tf_op jit(solution)/shard_map/all_to_all | solution.py:91
  1276.3 85.8 %all-gather.31.cloned.1.call-done = bf16[2048,1200]{0,1:T(8,128)(2,1)} async-done(((bf16[512,1200]{0,1:T(8,128)(2,1)}), bf16[2048,1200]{0,1:T(8,128)(2,1)}) %all-gather.31.cloned.1.call-update) | async-done | bytes 4915216 | tf_op jit(solution)/shard_map/all_gather | solution.py:75
  1375.5 11.5 reduce-scatter.44.cloned.1.call-done
  1409.0 16.9 %reduce-scatter.36.cloned.1.call-done = bf16[200,1200]{1,0:T(8,128)(2,1)} async-done(((bf16[400,1200]{1,0:T(8,128)(2,1)}), bf16[200,1200]{1,0:T(8,128)(2,1)}) %reduce-scatter.36.cloned.1.call-update) | async-done | bytes 480016 | tf_op jit(solution)/shard_map/reduce_scatter | solution.py:292
  1430.9 26.0 %reduce-scatter.34.cloned.1.call-done = bf16[512,400]{0,1:T(8,128)(2,1)} async-done(((bf16[2048,400]{0,1:T(8,128)(2,1)}), bf16[512,400]{0,1:T(8,128)(2,1)}) %reduce-scatter.34.cloned.1.call-update) | async-done | bytes 409616 | tf_op jit(solution)/shard_map/reduce_scatter | solution.py:80
  1458.3 11.7 all-reduce.2
  1473.3 114.9 %all-reduce.8.cloned.1.call-done = (f32[8,1600]{1,0:T(8,128)}, f32[6400]{0:T(1024)}) async-done(((f32[8,1600]{1,0:T(8,128)}, f32[6400]{0:T(1024)}), (f32[8,1600]{1,0:T(8,128)}, f32[6400]{0:T(1024)})) %all-reduce.8.cloned.1.call-update) | async-done | bytes 76816 | tf_op jit(solution)/shard_map/psum | solution.py:290
  (310 shorter events, 287.8 us)
Async XLA Ops:
  8.0 36.5 %all-gather.13.cloned.1.call-start = ((), (), s32[]{:S(2)}) async-start(), calls=%async_computation.17 | async-start | bytes 2048000 | tf_op jit(solution)/shard_map/all_gather | solution.py:63
  26.2 113.4 %reduce-scatter.20.cloned.1.call-start = ((), (), s32[]{:S(2)}) async-start(), calls=%async_computation.18 | async-start | bytes 6144000 | tf_op jit(solution)/shard_map/reduce_scatter | solution.py:68
  51.0 217.1 %all-gather.15.cloned.1.call-start = ((), (), s32[]{:S(2)}) async-start(), calls=%async_computation.19 | async-start | bytes 13926400 | tf_op jit(solution)/shard_map/all_gather | solution.py:207
  161.1 201.6 %all-gather.17.cloned.1.call-start = ((), (), s32[]{:S(2)}) async-start(), calls=%async_computation.20 | async-start | bytes 2048000 | tf_op jit(solution)/shard_map/all_gather | solution.py:75
  326.4 67.6 %reduce-scatter.22.cloned.1.call-start = ((), (), s32[]{:S(2)}) async-start(), calls=%async_computation.21 | async-start | bytes 2048000 | tf_op jit(solution)/shard_map/reduce_scatter | solution.py:80
  366.4 43.1 %all-gather.33.cloned.1.call-start = ((), (), s32[]{:S(2)}) async-start(), calls=%async_computation.37 | async-start | bytes 2150400 | tf_op jit(solution)/shard_map/all_gather | solution.py:173
  368.7 46.0 %all-gather.25.cloned.1.call-start = ((), (), s32[]{:S(2)}) async-start(), calls=%async_computation.27 | async-start | bytes 2048000 | tf_op jit(solution)/shard_map/all_gather | solution.py:63
  369.3 71.8 %all-gather.21.cloned.1.call-start = ((), (), s32[]{:S(2)}) async-start(), calls=%async_computation.23 | async-start | bytes 1996800 | tf_op jit(solution)/shard_map/all_gather | solution.py:172
  371.6 91.5 %all-gather.19.cloned.1.call-start = ((), (), s32[]{:S(2)}) async-start(), calls=%async_computation.22 | async-start | bytes 2048000 | tf_op jit(solution)/shard_map/all_gather | solution.py:63
  409.0 129.1 %reduce-scatter.28.cloned.1.call-start = ((), (), s32[]{:S(2)}) async-start(), calls=%async_computation.28 | async-start | bytes 8192000 | tf_op jit(solution)/shard_map/reduce_scatter | solution.py:68
  422.9 233.0 %reduce-scatter.24.cloned.1.call-start = ((), (), s32[]{:S(2)}) async-start(), calls=%async_computation.24 | async-start | bytes 8192000 | tf_op jit(solution)/shard_map/reduce_scatter | solution.py:68
  471.4 310.4 %all-gather.27.cloned.1.call-start = ((), (), s32[]{:S(2)}) async-start(), calls=%async_computation.29 | async-start | bytes 8192000 | tf_op jit(solution)/shard_map/all_gather | solution.py:75
  661.5 240.4 %all-gather.23.cloned.1.call-start = ((), (), s32[]{:S(2)}) async-start(), calls=%async_computation.25 | async-start | bytes 8192000 | tf_op jit(solution)/shard_map/all_gather | solution.py:75
  662.2 239.7 %copy-start.19 = (bf16[1600,400]{0,1:T(8,128)(2,1)S(1)}, bf16[1600,400]{0,1:T(8,128)(2,1)}, u32[]{:S(2)}) copy-start(bf16[1600,400]{0,1:T(8,128)(2,1)} %reshape.176) | copy-start | bytes 3840004
  662.2 246.9 %reduce-scatter.30.cloned.1.call-start = ((), (), s32[]{:S(2)}) async-start(), calls=%async_computation.30 | async-start | bytes 2048000 | tf_op jit(solution)/shard_map/reduce_scatter | solution.py:80
  789.4 119.7 %copy-start.1 = (bf16[512,400]{0,1:T(8,128)(2,1)S(1)}, bf16[512,400]{0,1:T(8,128)(2,1)}, u32[]{:S(2)}) copy-start(bf16[512,400]{0,1:T(8,128)(2,1)} %reduce-scatter.22.cloned.1.call-done) | copy-start | bytes 1228804
  789.4 146.4 %reduce-scatter.26.cloned.1.call-start = ((), (), s32[]{:S(2)}) async-start(), calls=%async_computation.26 | async-start | bytes 2048000 | tf_op jit(solution)/shard_map/reduce_scatter | solution.py:80
  909.0 50.8 %all-gather.29.cloned.1.call-start = ((), (), s32[]{:S(2)}) async-start(), calls=%async_computation.31 | async-start | bytes 2048000 | tf_op jit(solution)/shard_map/all_gather | solution.py:63
  939.8 60.1 %reduce-scatter.32.cloned.1.call-start = ((), (), s32[]{:S(2)}) async-start(), calls=%async_computation.32 | async-start | bytes 2048000 | tf_op jit(solution)/shard_map/reduce_scatter | solution.py:68
  1001.7 11.1 all-to-all-start.2
  1005.1 233.3 %reduce-scatter.40.cloned.1.call-start = ((), (), s32[]{:S(2)}) async-start(), calls=%async_computation.38 | async-start | bytes 13926400
  1101.8 168.3 %reduce-scatter.42.cloned.1.call-start = ((), (), s32[]{:S(2)}) async-start(), calls=%async_computation.39 | async-start | bytes 2457600
  1113.2 248.8 %all-gather.31.cloned.1.call-start = ((), (), s32[]{:S(2)}) async-start(), calls=%async_computation.33 | async-start | bytes 6144000 | tf_op jit(solution)/shard_map/all_gather | solution.py:75
  1261.4 125.7 %reduce-scatter.44.cloned.1.call-start = ((), (), s32[]{:S(2)}) async-start(), calls=%async_computation.40 | async-start | bytes 1996800
  1269.1 134.3 %reduce-scatter.38.cloned.1.call-start = ((), (), s32[]{:S(2)}) async-start(), calls=%async_computation.36 | async-start | bytes 614400 | tf_op jit(solution)/shard_map/reduce_scatter | solution.py:295
  1276.2 149.7 %reduce-scatter.36.cloned.1.call-start = ((), (), s32[]{:S(2)}) async-start(), calls=%async_computation.35 | async-start | bytes 1536000 | tf_op jit(solution)/shard_map/reduce_scatter | solution.py:292
  1368.2 88.7 %reduce-scatter.34.cloned.1.call-start = ((), (), s32[]{:S(2)}) async-start(), calls=%async_computation.34 | async-start | bytes 2048000 | tf_op jit(solution)/shard_map/reduce_scatter | solution.py:80
  1396.4 191.8 %all-reduce.8.cloned.1.call-start = ((), (), s32[]{:S(2)}) async-start(), calls=%async_computation.41 | async-start | bytes 163840 | tf_op jit(solution)/shard_map/psum | solution.py:290
  1430.9 157.2 %copy-start.27 = (f32[6400]{0:T(1024)S(1)}, f32[6400]{0:T(1024)}, u32[]{:S(2)}) copy-start(f32[6400]{0:T(1024)} %get-tuple-element.184) | copy-start | bytes 76804
  1430.9 157.2 %copy-start.30 = (f32[6400]{0:T(1024)S(1)}, f32[6400]{0:T(1024)}, u32[]{:S(2)}) copy-start(f32[6400]{0:T(1024)} %param.27) | copy-start | bytes 76804
  1430.9 159.3 %copy-start.25 = (f32[8,1600]{1,0:T(8,128)S(1)}, f32[8,1600]{1,0:T(8,128)}, u32[]{:S(2)}) copy-start(f32[8,1600]{1,0:T(8,128)} %param.26) | copy-start | bytes 153604
  1430.9 159.3 %copy-start.28 = (f32[2,8,1600]{2,1,0:T(8,128)S(1)}, f32[2,8,1600]{2,1,0:T(8,128)}, u32[]{:S(2)}) copy-start(f32[2,8,1600]{2,1,0:T(8,128)} %param.32) | copy-start | bytes 307204
  (36 other events, 510.7 us)
Sparse Core Ops, SparseCore 0:
  26.3 18.2 all-gather.12
  51.1 88.4 reduce-scatter.19
  161.2 106.8 all-gather.14
  326.5 36.1 all-gather.16
  366.6 27.4 reduce-scatter.21
  423.0 115.0 reduce-scatter.27
  540.4 115.5 reduce-scatter.23
  661.6 120.1 all-gather.26
  784.0 117.8 all-gather.22
  963.5 36.2 reduce-scatter.31
  1102.0 136.4 reduce-scatter.39
  1241.2 25.9 reduce-scatter.41
  1269.3 92.6 all-gather.30
  1364.8 22.1 reduce-scatter.43
  1389.8 13.3 reduce-scatter.37
  1405.8 20.0 reduce-scatter.35
  1428.3 28.5 reduce-scatter.33
Sparse Core Ops, SparseCore 1:
  369.0 24.3 all-gather.32
  394.8 19.8 all-gather.24
  416.7 24.3 all-gather.20
  443.2 19.9 all-gather.18
  789.5 26.7 reduce-scatter.29
  909.1 26.7 reduce-scatter.25
  939.8 19.8 all-gather.28
  1471.3 116.8 all-reduce.7
where the time goes:
time: 1610 us; the launch traced here: 1600 us
  waiting for transfers between devices  1170 us (73%)
  matrix products  160 us (10%)
  blocking collectives  113 us (7%)
  other arithmetic  82 us (5%)
  local copies, waits for them, and re-layouts  55.2 us (3%)
  between operations  16.6 us (1%)
    all_gather x4, waiting for transfers between devices, narrow(): gathered = lax.all_gather(local_rows, 'row', axis=0, tiled=True)  346 us
    reduce_scatter x4, waiting for transfers between devices, widen(): lax.psum_scatter(partial_rows.astype(jnp.bfloat16), 'row', scatter_dimens...  309 us
    unnamed x28, waiting for transfers between devices  137 us
    psum x1, waiting for transfers between devices, per_device(): lax.psum((vector_part, bias_part), ('dp', 'row', 'col'))  115 us
    all_gather x1, waiting for transfers between devices, per_device(): lax.all_gather(qkv_heads[:, D:], ('row', 'col'), axis=0, tiled=True)  107 us
    reduce_scatter x4, waiting for transfers between devices, narrow(): lax.psum_scatter(partial_rows.astype(jnp.bfloat16), 'col', scatter_dimens...  64.5 us
    all_gather x4, waiting for transfers between devices, widen(): gathered = lax.all_gather(local_rows, 'col', axis=0, tiled=True)  49.1 us
    psum x4, blocking collectives, row_totals(): lax.psum((jnp.sum(first_term, axis=1, keepdims=True), jnp.sum(second_term...  45.5 us
  transfers between devices with their start and end apart: 26, of which 22 were waited for; matrix products, arithmetic and copies ran while one was open for 7% of the time, Pallas kernels for 0%

commit v1 on v0

v1 whole, which is shorter than its diff:
```python
import math

import jax
import jax.numpy as jnp
import numpy as np
from jax import lax
from jax.experimental import pallas as pl
from jax.experimental.pallas import tpu as pltpu
from jax.sharding import PartitionSpec as P

D = 1600
HEADS = 25
HEAD_DIM = 64
STEP = 3

EPS_NORM = 1e-05
BETA_ONE = 0.9
BETA_TWO = 0.95
EPS_ADAM = 1e-08
LR_MATRIX = 0.08
LR_VECTOR = 0.3
DECAY = 0.1
NEG_FILL = -1e30
GELU_COEF = 0.7978845608028654
GELU_CUBE = 0.044715
UNIT = 16

F32 = jnp.float32
BF16 = jnp.bfloat16


def mm(spec, left, right):
    return jnp.einsum(spec, left, right, preferred_element_type=F32)


def adam_step(weight, gradient, moments, rate):
    first_moment = BETA_ONE * moments[0] + (1.0 - BETA_ONE) * gradient
    second = BETA_TWO * moments[1] + (1.0 - BETA_TWO) * gradient * gradient
    first_fix = 1.0 - BETA_ONE**STEP
    second_fix = 1.0 - BETA_TWO**STEP
    stepped = weight - rate * (
        first_moment / first_fix / (jnp.sqrt(second / second_fix) + EPS_ADAM) + DECAY * weight
    )
    return (stepped, jnp.stack([first_moment, second]))


def head_tables(rows, cols):
    slots = -(-HEADS // rows)
    per_block = 3 * D // cols // UNIT
    per_head = HEAD_DIM // UNIT
    lists = [[[] for _ in range(rows)] for _ in range(cols)]
    for g in range(3 * D // UNIT):
        head = (g // per_head) % HEADS
        lists[g // per_block][head % rows].append(g)
    longest = max(len(entry) for block in lists for entry in block)
    width = -(-longest // 8) * 8
    source = np.full((cols, rows, width * UNIT), -1, np.int32)
    unpack_block = np.full((rows, 3 * slots * per_head), -1, np.int32)
    unpack_rank = np.zeros((rows, 3 * slots * per_head), np.int32)
    pack_final = np.full((rows, cols, width), -1, np.int32)
    for c in range(cols):
        for z in range(rows):
            for rank, g in enumerate(lists[c][z]):
                local = g - c * per_block
                source[c, z, rank * UNIT : (rank + 1) * UNIT] = local * UNIT + np.arange(UNIT)
                part, head = g // per_head // HEADS, (g // per_head) % HEADS
                final = (part * slots + head // rows) * per_head + g % per_head
                unpack_block[z, final] = c
                unpack_rank[z, final] = rank
                pack_final[z, c, rank] = final
    return slots, width, source, unpack_block, unpack_rank, pack_final


def move_units(table, values, bias, out_rows, out_dtype):
    width = values.shape[1]
    count = out_rows // UNIT

    def body(tab, val, off, out):
        for i in range(count):
            src = tab[i]
            rows = pl.ds(i * UNIT, UNIT)
            safe = pl.multiple_of(jnp.maximum(src, 0) * UNIT, UNIT)
            block = val[pl.ds(safe, UNIT), :].astype(F32)
            block = jnp.where(src >= 0, block, 0.0)
            out[rows, :] = (block + off[rows, :]).astype(out_dtype)

    return pl.pallas_call(
        body,
        out_shape=jax.ShapeDtypeStruct((out_rows, width), out_dtype),
        in_specs=[
            pl.BlockSpec(memory_space=pltpu.SMEM),
            pl.BlockSpec(memory_space=pltpu.VMEM),
            pl.BlockSpec(memory_space=pltpu.VMEM),
        ],
        out_specs=pl.BlockSpec(memory_space=pltpu.VMEM),
        compiler_params=pltpu.CompilerParams(vmem_limit_bytes=32 * 2**20),
        name="move_units",
    )(table, values, bias)


def dot_tn(left, right):
    return lax.dot_general(left, right, (((0,), (0,)), ((), ())), preferred_element_type=F32)


def dot_nt(left, right):
    return lax.dot_general(left, right, (((1,), (1,)), ((), ())), preferred_element_type=F32)


def dot_nn(left, right):
    return lax.dot_general(left, right, (((1,), (0,)), ((), ())), preferred_element_type=F32)


def key_mask(block, me, start, keys, queries, diagonal):
    key_pos = block * keys + lax.broadcasted_iota(jnp.int32, (keys, queries), 0)
    mask = key_pos >= start
    if diagonal:
        query_pos = me * queries + lax.broadcasted_iota(jnp.int32, (keys, queries), 1)
        mask = mask & (key_pos <= query_pos)
    return mask


def attention_forward(me, start, query, key_values, offsets):
    rows, tokens = query.shape
    slots = rows // HEAD_DIM
    factor = 1.0 / math.sqrt(HEAD_DIM)
    n = len(offsets)

    def body(me_ref, start_ref, q_ref, *refs):
        kv, (o_ref, lse_ref), (top, total, acc) = refs[: 2 * n], refs[2 * n : 2 * n + 2], refs[2 * n + 2 :]
        my = me_ref[0]
        start_row = start_ref[...]
        q = q_ref[...] * jnp.asarray(factor, BF16)
        for i, off in enumerate(offsets):
            block = my ^ off
            k_ref, v_ref = kv[2 * i], kv[2 * i + 1]

            def run(first=(i == 0), off=off, block=block, k_ref=k_ref, v_ref=v_ref):
                s = dot_tn(k_ref[...], q)
                mask = key_mask(block, my, start_row, tokens, tokens, off == 0)
                s = jnp.where(mask, s, NEG_FILL)
                high = jnp.max(s, axis=0, keepdims=True)
                if not first:
                    high = jnp.maximum(high, top[...])
                p = jnp.exp(s - high)
                part = jnp.sum(p, axis=0, keepdims=True)
                mixed = dot_nn(v_ref[...], p.astype(BF16))
                if first:
                    total[...] = part
                    acc[...] = mixed
                else:
                    scale = jnp.exp(top[...] - high)
                    total[...] = total[...] * scale + part
                    acc[...] = acc[...] * scale + mixed
                top[...] = high

            if off == 0:
                run()
            else:
                pl.when(block < my)(run)
        o_ref[...] = (acc[...] / total[...]).astype(BF16)
        lse_ref[0] = top[...] + jnp.log(total[...])

    piece = (HEAD_DIM, tokens)
    specs = [
        pl.BlockSpec(memory_space=pltpu.SMEM),
        pl.BlockSpec((1, tokens), lambda j: (0, 0)),
        pl.BlockSpec(piece, lambda j: (j, 0)),
    ]
    args = [me, start, query]
    for array in key_values:
        specs += [pl.BlockSpec(piece, lambda j: (j, 0)), pl.BlockSpec(piece, lambda j: (slots + j, 0))]
        args += [array, array]
    return pl.pallas_call(
        body,
        grid=(slots,),
        in_specs=specs,
        out_specs=[
            pl.BlockSpec(piece, lambda j: (j, 0)),
            pl.BlockSpec((1, 1, tokens), lambda j: (j, 0, 0)),
        ],
        out_shape=[
            jax.ShapeDtypeStruct((rows, tokens), BF16),
            jax.ShapeDtypeStruct((slots, 1, tokens), F32),
        ],
        scratch_shapes=[
            pltpu.VMEM((1, tokens), F32),
            pltpu.VMEM((1, tokens), F32),
            pltpu.VMEM((HEAD_DIM, tokens), F32),
        ],
        compiler_params=pltpu.CompilerParams(vmem_limit_bytes=32 * 2**20),
        name="attention_forward",
    )(*args)


def attention_backward(me, start, query, key_values, offsets, out_rows, lse, grad_rows):
    rows, tokens = query.shape
    slots = rows // HEAD_DIM
    factor = 1.0 / math.sqrt(HEAD_DIM)
    n = len(offsets)

    def body(me_ref, start_ref, q_ref, o_ref, lse_ref, g_ref, *refs):
        kv, outs, (acc,) = refs[: 2 * n], refs[2 * n : -1], refs[-1:]
        dq_ref, dq_sum, dv_sum = outs[:3]
        grads = outs[3:]
        my = me_ref[0]
        start_row = start_ref[...]
        q = q_ref[...] * jnp.asarray(factor, BF16)
        g = g_ref[...]
        log_total = lse_ref[0]
        row_dot = jnp.sum(g.astype(F32) * o_ref[...].astype(F32), axis=0, keepdims=True)
        for i, off in enumerate(offsets):
            block = my ^ off
            k_ref, v_ref = kv[2 * i], kv[2 * i + 1]
            dk_ref, dv_ref = grads[2 * i], grads[2 * i + 1]

            def run(first=(i == 0), off=off, block=block, k_ref=k_ref, v_ref=v_ref, dk_ref=dk_ref, dv_ref=dv_ref):
                k = k_ref[...]
                s = dot_tn(k, q)
                mask = key_mask(block, my, start_row, tokens, tokens, off == 0)
                p = jnp.exp(jnp.where(mask, s, NEG_FILL) - log_total)
                dp = dot_tn(v_ref[...], g)
                ds = (p * (dp - row_dot)).astype(BF16)
                dv = dot_nt(g, p.astype(BF16))
                dv_ref[...] = dv.astype(BF16)
                dk_ref[...] = dot_nt(q, ds).astype(BF16)
                dq = dot_nn(k, ds)
                value_total = jnp.sum(dv, axis=1, keepdims=True)
                if first:
                    acc[...] = dq
                    dv_sum[...] = value_total
                else:
                    acc[...] += dq
                    dv_sum[...] += value_total

            def skip(dk_ref=dk_ref, dv_ref=dv_ref):
                dk_ref[...] = jnp.zeros_like(dk_ref)
                dv_ref[...] = jnp.zeros_like(dv_ref)

            if off == 0:
                run()
            else:
                pl.when(block < my)(run)
                pl.when(block >= my)(skip)
        dq = acc[...] * factor
        dq_ref[...] = dq.astype(BF16)
        dq_sum[...] = jnp.sum(dq, axis=1, keepdims=True)

    piece = (HEAD_DIM, tokens)
    head_spec = pl.BlockSpec(piece, lambda j: (j, 0))
    column = pl.BlockSpec((HEAD_DIM, 1), lambda j: (j, 0))
    specs = [
        pl.BlockSpec(memory_space=pltpu.SMEM),
        pl.BlockSpec((1, tokens), lambda j: (0, 0)),
        head_spec,
        head_spec,
        pl.BlockSpec((1, 1, tokens), lambda j: (j, 0, 0)),
        head_spec,
    ]
    args = [me, start, query, out_rows, lse, grad_rows]
    for array in key_values:
        specs += [head_spec, pl.BlockSpec(piece, lambda j: (slots + j, 0))]
        args += [array, array]
    full = jax.ShapeDtypeStruct((rows, tokens), BF16)
    thin = jax.ShapeDtypeStruct((rows, 1), F32)
    return pl.pallas_call(
        body,
        grid=(slots,),
        in_specs=specs,
        out_specs=[head_spec, column, column] + [head_spec] * (2 * n),
        out_shape=[full, thin, thin] + [full] * (2 * n),
        scratch_shapes=[pltpu.VMEM(piece, F32)],
        compiler_params=pltpu.CompilerParams(vmem_limit_bytes=32 * 2**20),
        name="attention_backward",
    )(*args)


def make_block(mesh):
    rows, dps, cols = mesh.shape["row"], mesh.shape["dp"], mesh.shape["col"]
    slots, width, source, unpack_block, unpack_rank, pack_final = head_tables(rows, cols)
    packed = width * UNIT
    offsets = list(range(0, cols, 2)) + list(range(1, cols, 2))
    even = [(d, b) for d in range(dps) for b in range(0, cols, 2)]
    plane = even + [(d, b + 1) for d, b in even]
    place = {entry: i for i, entry in enumerate(plane)}

    def to_row(values, k):
        return lax.ppermute(values, "row", [(i, (i + k) % rows) for i in range(rows)])

    def row_gather(values):
        return [values] + [to_row(values, rows - k) for k in range(1, rows)]

    def row_exchange(chunks):
        return [chunks[0]] + [to_row(chunks[rows - k], rows - k) for k in range(1, rows)]

    def row_reduce(chunks):
        total = chunks[0].astype(F32)
        for k in range(1, rows):
            total = total + to_row(chunks[k], k).astype(F32)
        return total

    def to_plane(values, d, b):
        return lax.ppermute(
            values,
            ("dp", "col"),
            [(y * cols + c, (y ^ d) * cols + (c ^ b)) for y in range(dps) for c in range(cols)],
        )

    def plane_gather(values):
        first = [values] + [to_plane(values, d, b) for d, b in even[1:]]
        return first + [to_plane(item, 0, 1) for item in first]

    def plane_reduce(pieces):
        half = len(even)
        sums = [
            pieces[i].astype(F32) + to_plane(pieces[half + i], 0, 1).astype(F32) for i in range(half)
        ]
        total = sums[0]
        for (d, b), item in list(zip(even, sums))[1:]:
            total = total + to_plane(item.astype(BF16), d, b).astype(F32)
        return total

    def dp_exchange(chunks):
        return [chunks[0]] + [
            lax.ppermute(chunks[d], "dp", [(y, y ^ d) for y in range(dps)]) for d in range(1, dps)
        ]

    def sum_everywhere(values):
        for axis, size in (("col", cols), ("dp", dps), ("row", rows)):
            step = 1
            while step < size:
                values = values + lax.ppermute(values, axis, [(i, i ^ step) for i in range(size)])
                step *= 2
        return values

    def sum_rows(values):
        step = 1
        while step < rows:
            values = values + lax.ppermute(values, "row", [(i, i ^ step) for i in range(rows)])
            step *= 2
        return values

    def at(array, index, axis=0):
        return lax.dynamic_index_in_dim(array, index, axis, keepdims=False)

    def per_device(
        hidden_in,
        upstream,
        segment_ids,
        qkv_weight,
        proj_weight,
        up_weight,
        down_weight,
        vectors,
        up_bias,
        qkv_moments,
        proj_moments,
        up_moments,
        down_moments,
        vector_moments,
        bias_moments,
    ):
        z, y, c = lax.axis_index("row"), lax.axis_index("dp"), lax.axis_index("col")
        tokens, feats = hidden_in.shape
        few = tokens // rows
        half = feats // dps
        hidden = down_weight.shape[0]
        group = segment_ids.shape[0]

        def swapped(blocks, axis):
            return jnp.stack([at(blocks, y ^ d, axis) for d in range(dps)], axis=axis)

        def rolled(array, axis):
            return jnp.stack([at(array, (z + k) % rows, axis) for k in range(rows)], axis=axis)

        def unrolled(pieces, axis):
            stacked = jnp.stack(pieces)
            return jnp.concatenate([at(stacked, (t - z) % rows) for t in range(rows)], axis=axis)

        def token_chunks(array):
            return [
                lax.dynamic_slice_in_dim(array, ((z + k) % rows) * few, few, array.ndim - 1)
                for k in range(rows)
            ]

        vec_rel = rolled(vectors.reshape(8, rows, feats), 1)
        vec_swap = swapped(vec_rel.reshape(8, rows, dps, half), 2).reshape(8, D)
        vec_rel = vec_rel.reshape(8, D)

        columns = rolled(at(jnp.asarray(source), c), 0).reshape(rows * packed)
        local_cols = qkv_weight.shape[1]
        select = (
            lax.broadcasted_iota(jnp.int32, (local_cols, rows * packed), 0) == columns[None, :]
        ).astype(BF16)
        sorted_cols = mm("fn,nm->fm", qkv_weight.astype(BF16), select).astype(BF16)
        arrived = row_exchange([sorted_cols[:, k * packed : (k + 1) * packed] for k in range(rows)])
        qkv_pieces = plane_gather(jnp.stack(arrived))
        w_qkv = jnp.stack(
            [
                jnp.concatenate([qkv_pieces[place[(d, b)]] for b in offsets], axis=2)
                for d in range(dps)
            ],
            axis=1,
        ).reshape(D, cols * packed)

        x_own = swapped(hidden_in.T.reshape(dps, half, tokens), 0).reshape(feats, tokens)
        x_all = jnp.concatenate(row_gather(x_own), axis=0)
        up_chunks = token_chunks(upstream.T)
        top_few = jnp.concatenate(row_exchange(up_chunks), axis=0)
        top_all = jnp.concatenate(plane_gather(top_few), axis=1)

        w_proj = jnp.concatenate(
            plane_gather(jnp.concatenate(row_gather(proj_weight.astype(BF16)), axis=1)), axis=0
        )
        up_parts = up_weight.astype(BF16).reshape(half, dps, hidden).transpose(1, 0, 2)
        up_arrived = dp_exchange([at(up_parts, y ^ d) for d in range(dps)])
        up_rows = swapped(jnp.stack(up_arrived), 0).reshape(feats, hidden)
        w_up = jnp.concatenate(row_gather(up_rows), axis=0)
        w_down = jnp.concatenate(row_gather(down_weight.astype(BF16)), axis=1)

        x_f = x_all.astype(F32)
        mean_one = jnp.mean(x_f, axis=0, keepdims=True)
        spread_one = jnp.mean(x_f * x_f, axis=0, keepdims=True) - mean_one * mean_one
        inverse_one = lax.rsqrt(spread_one + EPS_NORM)
        normed_one = (x_f - mean_one) * inverse_one
        h1 = (normed_one * vec_swap[0][:, None] + vec_swap[1][:, None]).astype(BF16)
        qkv_packed = mm("fn,ft->nt", w_qkv, h1)

        order = np.argsort(np.asarray(offsets)).astype(np.int32)
        where_block = at(jnp.asarray(unpack_block), z)
        unpack = jnp.where(
            where_block >= 0,
            jnp.asarray(order)[c ^ jnp.maximum(where_block, 0)] * width + at(jnp.asarray(unpack_rank), z),
            -1,
        )

        def own_heads(vector):
            padded = jnp.pad(vector, (0, (rows * slots - HEADS) * HEAD_DIM))
            return at(padded.reshape(slots, rows, HEAD_DIM), z, 1).reshape(slots * HEAD_DIM)

        wide = slots * HEAD_DIM
        shift = jnp.concatenate([own_heads(vectors[2]), jnp.zeros((wide,), F32), own_heads(vectors[3])])
        qkv_rows = move_units(unpack, qkv_packed, shift[:, None], 3 * wide, BF16)
        query = qkv_rows[:wide]
        own_kv = qkv_rows[wide:]

        held = [own_kv]
        for b in offsets[1 : cols // 2]:
            held.append(lax.ppermute(own_kv, "col", [(i, i ^ b) for i in range(cols) if (i ^ b) > i]))
        key_values = held + [
            lax.ppermute(item, "col", [(i, i ^ 1) for i in range(cols)]) for item in held
        ]
        me = c.astype(jnp.int32).reshape(1)
        query_ids = lax.dynamic_slice_in_dim(segment_ids, c * tokens, tokens)
        start = jnp.sum((segment_ids[:, None] < query_ids[None, :]).astype(jnp.int32), axis=0)[None, :]
        attn, lse = attention_forward(me, start, query, key_values, offsets)

        attn_pieces = row_exchange(token_chunks(attn))
        attn_abs = unrolled([item.reshape(slots, 1, HEAD_DIM, few) for item in attn_pieces], 1)
        attn_abs = attn_abs.reshape(rows * wide, few)[:D]
        blocks = attn_abs.reshape(cols, dps, D // cols // dps, few)
        attn_rel = jnp.concatenate([at(at(blocks, c ^ b), y ^ d) for d, b in plane], axis=0)
        x_few = lax.dynamic_slice_in_dim(x_all, z * few, few, 1)
        x_few = swapped(x_few.reshape(rows, dps, half, few), 1).reshape(D, few).astype(F32)
        mid = x_few + mm("rf,rt->ft", w_proj, attn_rel) + vec_rel[4][:, None]
        mean_two = jnp.mean(mid, axis=0, keepdims=True)
        spread_two = jnp.mean(mid * mid, axis=0, keepdims=True) - mean_two * mean_two
        inverse_two = lax.rsqrt(spread_two + EPS_NORM)
        normed_two = (mid - mean_two) * inverse_two
        h2 = (normed_two * vec_rel[5][:, None] + vec_rel[6][:, None]).astype(BF16)
        h2_all = jnp.concatenate(plane_gather(h2), axis=1)

        up_shift = lax.dynamic_slice_in_dim(up_bias, (c * dps + y) * hidden, hidden)
        pre = mm("fh,ft->ht", w_up, h2_all) + up_shift[:, None]
        inside = GELU_COEF * (pre + GELU_CUBE * pre * pre * pre)
        tanh_val = jnp.tanh(inside)
        act = (0.5 * pre * (1.0 + tanh_val)).astype(BF16)
        slope = 0.5 * (1.0 + tanh_val) + 0.5 * pre * (1.0 - tanh_val * tanh_val) * GELU_COEF * (
            1.0 + 3.0 * GELU_CUBE * pre * pre
        )
        grad_pre = mm("hf,ft->ht", w_down, top_all) * slope
        grad_pre_half = grad_pre.astype(BF16)
        bias_part = jnp.sum(grad_pre, axis=1)

        def by_plane(array):
            return [array[:, i * few : (i + 1) * few] for i in range(len(plane))]

        grad_ln_two = plane_reduce(by_plane(mm("fh,ht->ft", w_up, grad_pre_half).astype(BF16)))
        down_sum = plane_reduce(by_plane(mm("hf,ht->ft", w_down, act).astype(BF16)))
        out_few = (mid + down_sum + vec_rel[7][:, None]).astype(BF16)
        block_out = unrolled(
            row_exchange([out_few[k * feats : (k + 1) * feats] for k in range(rows)]), 1
        ).T

        down_part = mm("ht,ft->hf", act, top_all).astype(BF16)
        down_grad = row_reduce([down_part[:, k * feats : (k + 1) * feats] for k in range(rows)])
        up_part = mm("ft,ht->fh", h2_all, grad_pre_half).astype(BF16)
        up_sum = row_reduce([up_part[k * feats : (k + 1) * feats] for k in range(rows)]).astype(BF16)
        up_blocks = up_sum.reshape(dps, half, hidden)
        up_back = dp_exchange([at(up_blocks, y ^ d) for d in range(dps)])
        up_grad = swapped(jnp.stack(up_back), 0).transpose(1, 0, 2).reshape(half, dps * hidden).astype(F32)

        scaled = grad_ln_two * vec_rel[5][:, None]
        first_mean = jnp.mean(scaled, axis=0, keepdims=True)
        second_mean = jnp.mean(scaled * normed_two, axis=0, keepdims=True)
        grad_mid = top_few.astype(F32) + inverse_two * (scaled - first_mean - normed_two * second_mean)
        grad_mid_half = grad_mid.astype(BF16)
        grad_attn = mm("rf,ft->rt", w_proj, grad_mid_half).astype(BF16)
        n_rows = D // cols // dps
        natural = jnp.stack(
            [
                jnp.stack([grad_attn[place[(d, b)] * n_rows : (place[(d, b)] + 1) * n_rows] for d in range(dps)])
                for b in range(cols)
            ]
        )
        natural = swapped(natural, 1)
        grad_abs = jnp.stack([at(natural, c ^ b) for b in range(cols)]).reshape(D, few)
        grad_abs = jnp.pad(grad_abs, ((0, rows * wide - D), (0, 0))).reshape(slots, rows, HEAD_DIM, few)
        grad_heads = unrolled(
            row_exchange([at(grad_abs, (z + k) % rows, 1).reshape(wide, few) for k in range(rows)]), 1
        )
        proj_part = mm("rt,ft->rf", attn_rel, grad_mid_half).astype(BF16)
        proj_sum = plane_reduce([proj_part[i * n_rows : (i + 1) * n_rows] for i in range(len(plane))])
        proj_sum = proj_sum.astype(BF16)
        proj_grad = row_reduce([proj_sum[:, k * feats : (k + 1) * feats] for k in range(rows)])
        grad_mid_own = unrolled(
            row_exchange([grad_mid_half[k * feats : (k + 1) * feats] for k in range(rows)]), 1
        )

        results = attention_backward(me, start, query, key_values, offsets, attn, lse, grad_heads)
        grad_query, query_total, value_total = results[:3]
        kv_grads = [jnp.concatenate(results[3 + 2 * i : 5 + 2 * i], axis=0) for i in range(cols)]
        half_cols = cols // 2
        kv_sums = [
            kv_grads[i].astype(F32)
            + lax.ppermute(kv_grads[half_cols + i], "col", [(j, j ^ 1) for j in range(cols)]).astype(F32)
            for i in range(half_cols)
        ]
        own_sum = kv_sums[0]
        for i in range(1, half_cols):
            b = offsets[i]
            own_sum = own_sum + lax.ppermute(
                kv_sums[i].astype(BF16), "col", [(j, j ^ b) for j in range(cols) if (j ^ b) < j]
            ).astype(F32)
        grad_qkv = jnp.concatenate([grad_query, own_sum.astype(BF16)], axis=0)
        finals = at(jnp.asarray(pack_final), z)
        pack = jnp.concatenate([at(finals, c ^ b) for b in offsets])
        grad_packed = move_units(pack, grad_qkv, jnp.zeros((cols * packed, 1), F32), cols * packed, BF16)

        grad_ln_part = mm("fn,nt->ft", w_qkv, grad_packed)
        gain_one = vec_swap[0][:, None]
        scaled_part = grad_ln_part * gain_one
        stats = sum_rows(
            jnp.stack([jnp.sum(scaled_part, axis=0), jnp.sum(scaled_part * normed_one, axis=0)])
        )
        part_half = grad_ln_part.astype(BF16)
        grad_ln_own = row_reduce([part_half[k * feats : (k + 1) * feats] for k in range(rows)])
        first_row, second_row = stats[0:1] / D, stats[1:2] / D
        inner = inverse_one * (
            grad_ln_own * gain_one[:feats] - first_row - normed_one[:feats] * second_row
        )
        inner = swapped(inner.reshape(dps, half, tokens), 0).reshape(feats, tokens)
        input_grad = (grad_mid_own.astype(F32) + inner).astype(BF16).T

        qkv_part = mm("ft,nt->fn", h1, grad_packed).astype(BF16).reshape(rows, dps, half, cols * packed)
        qkv_sum = plane_reduce(
            [
                qkv_part[:, d, :, offsets.index(b) * packed : (offsets.index(b) + 1) * packed]
                for d, b in plane
            ]
        ).astype(BF16)
        qkv_back = jnp.concatenate(row_exchange([qkv_sum[k] for k in range(rows)]), axis=1)
        qkv_grad = mm("fm,nm->fn", qkv_back, select)

        def back_from_rel(vector):
            blocks = vector.reshape(rows, feats)
            return jnp.concatenate([at(blocks, (t - z) % rows) for t in range(rows)])

        def back_from_swap(vector):
            return back_from_rel(swapped(vector.reshape(rows, dps, half), 1).reshape(D))

        def from_heads(vector):
            blocks = vector.reshape(slots, 1, HEAD_DIM)
            mine = (jnp.arange(rows) == z)[None, :, None]
            return jnp.where(mine, blocks, 0.0).reshape(rows * wide)[:D]

        top_sum = jnp.sum(upstream.astype(F32), axis=0)
        parts = jnp.stack(
            [
                back_from_swap(jnp.sum(grad_ln_part * normed_one, axis=1)),
                back_from_swap(jnp.sum(grad_ln_part, axis=1)),
                from_heads(query_total[:, 0]),
                from_heads(value_total[:, 0]),
                back_from_rel(jnp.sum(grad_mid, axis=1)),
                back_from_rel(jnp.sum(grad_ln_two * normed_two, axis=1)),
                back_from_rel(jnp.sum(grad_ln_two, axis=1)),
                lax.dynamic_update_slice_in_dim(jnp.zeros((D,), F32), top_sum, z * feats, 0),
            ]
        )
        bias_full = lax.dynamic_update_slice_in_dim(
            jnp.zeros((up_bias.shape[0],), F32), bias_part, (c * dps + y) * hidden, 0
        )
        summed = sum_everywhere(jnp.concatenate([parts.reshape(-1), bias_full]))
        vector_grad = summed[: 8 * D].reshape(8, D)
        bias_grad = summed[8 * D :]

        new_qkv, qkv_state = adam_step(qkv_weight, qkv_grad, qkv_moments, LR_MATRIX)
        new_proj, proj_state = adam_step(proj_weight, proj_grad, proj_moments, LR_MATRIX)
        new_up, up_state = adam_step(up_weight, up_grad, up_moments, LR_MATRIX)
        new_down, down_state = adam_step(down_weight, down_grad, down_moments, LR_MATRIX)
        new_vectors, vector_state = adam_step(vectors, vector_grad, vector_moments, LR_VECTOR)
        new_bias, bias_state = adam_step(up_bias, bias_grad, bias_moments, LR_VECTOR)
        return (
            block_out,
            input_grad,
            qkv_grad,
            proj_grad,
            up_grad,
            down_grad,
            vector_grad,
            bias_grad,
            new_qkv,
            new_proj,
            new_up,
            new_down,
            new_vectors,
            new_bias,
            qkv_state,
            proj_state,
            up_state,
            down_state,
            vector_state,
            bias_state,
        )

    return per_device


def solution(mesh):
    acts = P(("dp", "col"), "row")
    wide = P(("row", "dp"), "col")
    tall = P(("col", "dp"), "row")
    wide_pair = P(None, ("row", "dp"), "col")
    tall_pair = P(None, ("col", "dp"), "row")
    return jax.shard_map(
        make_block(mesh),
        mesh=mesh,
        in_specs=(
            acts,
            acts,
            P("dp"),
            wide,
            tall,
            wide,
            tall,
            P(),
            P(),
            wide_pair,
            tall_pair,
            wide_pair,
            tall_pair,
            P(),
            P(),
        ),
        out_specs=(
            acts,
            acts,
            wide,
            tall,
            wide,
            tall,
            P(),
            P(),
            wide,
            tall,
            wide,
            tall,
            P(),
            P(),
            wide_pair,
            tall_pair,
            wide_pair,
            tall_pair,
            P(),
            P(),
        ),
        check_vma=False,
    )
```

time: 1610 us -> 826 us (0.51)
  waiting for transfers between devices: 1170 us -> 375 us
  starting transfers between devices: 5.62 us -> 175 us
  blocking collectives: 113 us -> 0 us
  matrix products: 160 us -> 51.7 us
  local copies, waits for them, and re-layouts: 55.2 us -> 116 us
    all_gather x11 -> x0, waiting for transfers between devices: 520 us -> none  [the longest x4 346 us: narrow(): gathered = lax.all_gather(local_rows, 'row', axis=0, tiled=True)]
    reduce_scatter x10 -> x0, waiting for transfers between devices: 390 us -> none  [the longest x4 309 us: widen(): lax.psum_scatter(partial_rows.astype(jnp.bfloat16), 'row', scatter_dimens...]
    ppermute x0 -> x116, waiting for transfers between devices: none -> 375 us  [the longest x45 222 us: to_row(): lax.ppermute(values, 'row', [(i, (i + k) % rows) for i in range(rows)])]
    ppermute x0 -> x116, starting transfers between devices: none -> 175 us  [the longest x45 103 us: to_row(): lax.ppermute(values, 'row', [(i, (i + k) % rows) for i in range(rows)])]
    unnamed x28 -> x0, waiting for transfers between devices: 137 us -> none
    psum x1 -> x0, waiting for transfers between devices: 115 us -> none  [per_device(): lax.psum((vector_part, bias_part), ('dp', 'row', 'col'))]
    dot_general x47 -> x14, matrix products: 160 us -> 51.7 us  [mm(): return jnp.einsum(spec, left, right, preferred_element_type=F32)]
    all_to_all x3 -> x0, blocking collectives: 48.1 us -> none  [the longest x2 29.2 us: from_heads(): lax.all_to_all(head_rows, 'col', split_axis=1, concat_axis=0, tiled=True)]
  transfers between devices with their start and end apart: 26 -> 116, of which waited for: 22 -> 36; matrix products, arithmetic and copies ran while one was open for 7% -> 24% of each run, Pallas kernels for 0% -> 2%
where the time goes in v1:
time: 826 us; the launch traced here: 816 us
  waiting for transfers between devices  375 us (45%)
  starting transfers between devices  175 us (21%)
  local copies, waits for them, and re-layouts  116 us (14%)
  other arithmetic  81.3 us (10%)
  matrix products  51.7 us (6%)
  Pallas kernels  14.5 us (2%)
    ppermute x45, waiting for transfers between devices, to_row(): lax.ppermute(values, 'row', [(i, (i + k) % rows) for i in range(rows)])  222 us
    ppermute x56, waiting for transfers between devices, to_plane(): lax.ppermute(values, ('dp', 'col'), [(y * cols + c, (y ^ d) * cols + (c ^...  112 us
    ppermute x45, starting transfers between devices, to_row(): lax.ppermute(values, 'row', [(i, (i + k) % rows) for i in range(rows)])  103 us
    dot_general x14, matrix products, mm(): return jnp.einsum(spec, left, right, preferred_element_type=F32)  51.7 us
    ppermute x56, starting transfers between devices, to_plane(): lax.ppermute(values, ('dp', 'col'), [(y * cols + c, (y ^ d) * cols + (c ^...  50.5 us
    unnamed x252, local copies, waits for them, and re-layouts  36.1 us
    another operation x12, other arithmetic, adam_step(): return (stepped, jnp.stack([first_moment, second]))  21.5 us
    ppermute x1, waiting for transfers between devices, per_device(): lax.ppermute(own_kv, 'col', [(i, i ^ b) for i in range(cols) if i ^ b > i])  16.7 us
  transfers between devices with their start and end apart: 116, of which 36 were waited for; matrix products, arithmetic and copies ran while one was open for 24% of the time, Pallas kernels for 2%

profile of v1, /device:TPU:0, one launch (start us, length us, event | category | flops | bytes accessed | tf_op | source)
XLA Modules:
  0.0 816.2 jit_solution(12429247032031187775)
XLA Ops:
  62.6 15.8 %collective-permute-done.14 = bf16[200,384]{1,0:T(8,128)(2,1)S(1)} collective-permute-done((bf16[200,384]{1,0:T(8,128)(2,1)}, bf16[200,384]{1,0:T(8,128)(2,1)S(1)}, u32[]{:S(2)}, u32[]{:S(2)}) %collective-permute-start.14) | collective-permute-done | bytes 153632 | tf_op jit(solution)/shard_map/ppermute | solution.py:287
  95.2 12.9 %collective-permute-done.1 = bf16[400,512]{1,0:T(8,128)(2,1)} collective-permute-done((bf16[400,512]{1,0:T(8,128)(2,1)S(1)}, bf16[400,512]{1,0:T(8,128)(2,1)}, u32[]{:S(2)}, u32[]{:S(2)}) %collective-permute-start.1) | collective-permute-done | bytes 409632 | tf_op jit(solution)/shard_map/ppermute | solution.py:287
  113.8 21.4 %collective-permute-done.19 = bf16[4,200,384]{2,1,0:T(8,128)(2,1)S(1)} collective-permute-done((bf16[4,200,384]{2,1,0:T(8,128)(2,1)S(1)}, bf16[4,200,384]{2,1,0:T(8,128)(2,1)S(1)}, u32[]{:S(2)}, u32[]{:S(2)}) %collective-permute-start.19) | collective-permute-done | bytes 614432 | tf_op jit(solution)/shard_map/ppermute | solution.py:302
  157.6 13.6 %collective-permute-done.7 = bf16[200,1600]{1,0:T(8,128)(2,1)S(1)} collective-permute-done((bf16[200,1600]{1,0:T(8,128)(2,1)S(1)}, bf16[200,1600]{1,0:T(8,128)(2,1)S(1)}, u32[]{:S(2)}, u32[]{:S(2)}) %collective-permute-start.7) | collective-permute-done | bytes 640032 | tf_op jit(solution)/shard_map/ppermute | solution.py:302
  172.0 16.7 %collective-permute-done.23.refs_2_.refs_3_ = bf16[896,512]{1,0:T(8,128)(2,1)S(1)} collective-permute-done((bf16[896,512]{1,0:T(8,128)(2,1)S(1)}, bf16[896,512]{1,0:T(8,128)(2,1)S(1)}, u32[]{:S(2)}, u32[]{:S(2)}) %collective-permute-start.23) | collective-permute-done | bytes 917536 | tf_op jit(solution)/shard_map/ppermute | solution.py:448
  189.5 5.5 collective-permute-start.35
  206.5 22.9 %collective-permute-done.28 = bf16[448,128]{1,0:T(8,128)(2,1)S(1)} collective-permute-done((bf16[448,128]{1,0:T(8,128)(2,1)S(1)}, bf16[448,128]{1,0:T(8,128)(2,1)S(1)}, u32[]{:S(2)}, u32[]{:S(2)}) %collective-permute-start.28) | collective-permute-done | bytes 114720 | tf_op jit(solution)/shard_map/ppermute | solution.py:287
  229.5 18.2 %collective-permute-done.27 = bf16[448,128]{1,0:T(8,128)(2,1)S(1)} collective-permute-done((bf16[448,128]{1,0:T(8,128)(2,1)S(1)}, bf16[448,128]{1,0:T(8,128)(2,1)S(1)}, u32[]{:S(2)}, u32[]{:S(2)}) %collective-permute-start.27) | collective-permute-done | bytes 114720 | tf_op jit(solution)/shard_map/ppermute | solution.py:287
  255.5 7.8 collective-permute-done.36
  266.3 8.7 %collective-permute-done.38 = bf16[1600,128]{1,0:T(8,128)(2,1)S(1)} collective-permute-done((bf16[1600,128]{1,0:T(8,128)(2,1)S(1)}, bf16[1600,128]{1,0:T(8,128)(2,1)S(1)}, u32[]{:S(2)}, u32[]{:S(2)}) %collective-permute-start.38) | collective-permute-done | bytes 409632 | tf_op jit(solution)/shard_map/ppermute | solution.py:302
  277.3 19.1 %collective-permute-start.31 = (bf16[800,400]{0,1:T(8,128)(2,1)S(1)}, bf16[800,400]{0,1:T(8,128)(2,1)S(1)}, u32[]{:S(2)}, u32[]{:S(2)}) collective-permute-start(bf16[800,400]{0,1:T(8,128)(2,1)S(1)} %copy-done.50), channel_id=1, source_target_pairs={{0,4},{4,8},{8,12},{12,0},{1,5},{5,9},{9,13},{13,1},{2,6},{6,10},{... | collective-permute-start | bytes 1920008 | tf_op jit(solution)/shard_map/ppermute | solution.py:287
  308.5 7.7 collective-permute-done.31
  316.2 30.2 %collective-permute-done.30 = bf16[800,400]{0,1:T(8,128)(2,1)S(1)} collective-permute-done((bf16[800,400]{0,1:T(8,128)(2,1)S(1)}, bf16[800,400]{0,1:T(8,128)(2,1)S(1)}, u32[]{:S(2)}, u32[]{:S(2)}) %collective-permute-start.30) | collective-permute-done | bytes 640032 | tf_op jit(solution)/shard_map/ppermute | solution.py:287
  346.4 5.4 fusion.99
  356.9 6.9 convolution_convert_fusion.2
  385.4 15.6 %collective-permute-start.110 = (bf16[800,400]{0,1:T(8,128)(2,1)S(1)}, bf16[800,400]{0,1:T(8,128)(2,1)S(1)}, u32[]{:S(2)}, u32[]{:S(2)}) collective-permute-start(bf16[800,400]{0,1:T(8,128)(2,1)S(1)} %copy-done.51), channel_id=1, source_target_pairs={{0,12},{4,0},{8,4},{12,8},{1,13},{5,1},{9,5},{13,9},{2,14},{6,2},{... | collective-permute-start | bytes 1920008 | tf_op jit(solution)/shard_map/ppermute | solution.py:287
  408.9 8.6 %collective-permute-done.110 = bf16[800,400]{0,1:T(8,128)(2,1)S(1)} collective-permute-done((bf16[800,400]{0,1:T(8,128)(2,1)S(1)}, bf16[800,400]{0,1:T(8,128)(2,1)S(1)}, u32[]{:S(2)}, u32[]{:S(2)}) %collective-permute-start.110) | collective-permute-done | bytes 640032 | tf_op jit(solution)/shard_map/ppermute | solution.py:287
  424.9 56.2 %collective-permute-done.109 = bf16[800,400]{0,1:T(8,128)(2,1)} collective-permute-done((bf16[800,400]{0,1:T(8,128)(2,1)}, bf16[800,400]{0,1:T(8,128)(2,1)}, u32[]{:S(2)}, u32[]{:S(2)}) %collective-permute-start.109) | collective-permute-done | bytes 640032 | tf_op jit(solution)/shard_map/ppermute | solution.py:287
  510.3 16.0 %collective-permute-done.105 = bf16[400,800]{1,0:T(8,128)(2,1)} collective-permute-done((bf16[400,800]{1,0:T(8,128)(2,1)}, bf16[400,800]{1,0:T(8,128)(2,1)}, u32[]{:S(2)}, u32[]{:S(2)}) %collective-permute-start.105) | collective-permute-done | bytes 640032 | tf_op jit(solution)/shard_map/ppermute | solution.py:287
  533.9 6.1 collective-permute-done.49
  539.9 7.0 collective-permute-done.47
  594.8 7.6 attention_backward.1
  616.0 5.8 collective-permute-start.77
  634.9 13.6 %collective-permute-start.100 = (bf16[200,1600]{1,0:T(8,128)(2,1)S(1)}, bf16[200,1600]{1,0:T(8,128)(2,1)S(1)}, u32[]{:S(2)}, u32[]{:S(2)}) collective-permute-start(bf16[200,1600]{1,0:T(8,128)(2,1)S(1)} %get-tuple-element.200), channel_id=1, source_target_pairs={{0,18},{1,19},{2,16},{3,17},{16,2},{17,3},{18,0},{19,1},{4,22},{5,... | collective-permute-start | bytes 1920008 | tf_op jit(solution)/shard_map/ppermute | solution.py:302
  653.7 10.6 %collective-permute-done.100 = bf16[200,1600]{1,0:T(8,128)(2,1)S(1)} collective-permute-done((bf16[200,1600]{1,0:T(8,128)(2,1)S(1)}, bf16[200,1600]{1,0:T(8,128)(2,1)S(1)}, u32[]{:S(2)}, u32[]{:S(2)}) %collective-permute-start.100) | collective-permute-done | bytes 640032 | tf_op jit(solution)/shard_map/ppermute | solution.py:302
  664.3 13.6 %collective-permute-done.98 = bf16[200,1600]{1,0:T(8,128)(2,1)S(1)} collective-permute-done((bf16[200,1600]{1,0:T(8,128)(2,1)S(1)}, bf16[200,1600]{1,0:T(8,128)(2,1)S(1)}, u32[]{:S(2)}, u32[]{:S(2)}) %collective-permute-start.98) | collective-permute-done | bytes 640032 | tf_op jit(solution)/shard_map/ppermute | solution.py:302
  689.2 12.3 %collective-permute-done.102 = bf16[200,400]{1,0:T(8,128)(2,1)S(1)} collective-permute-done((bf16[200,400]{1,0:T(8,128)(2,1)S(1)}, bf16[200,400]{1,0:T(8,128)(2,1)S(1)}, u32[]{:S(2)}, u32[]{:S(2)}) %collective-permute-start.102) | collective-permute-done | bytes 160032 | tf_op jit(solution)/shard_map/ppermute | solution.py:287
  723.8 11.1 %collective-permute-done.82 = f32[2,512]{1,0:T(2,128)S(1)} collective-permute-done((f32[2,512]{1,0:T(2,128)S(1)}, f32[2,512]{1,0:T(2,128)S(1)}, u32[]{:S(2)}, u32[]{:S(2)}) %collective-permute-start.82) | collective-permute-done | bytes 4128 | tf_op jit(solution)/shard_map/ppermute | solution.py:338
  751.2 5.4 collective-permute-done.115
  769.0 6.6 collective-permute-done.79
  782.5 12.0 %collective-permute-done.88 = bf16[4,200,384]{2,1,0:T(8,128)(2,1)S(1)} collective-permute-done((bf16[4,200,384]{2,1,0:T(8,128)(2,1)S(1)}, bf16[4,200,384]{2,1,0:T(8,128)(2,1)S(1)}, u32[]{:S(2)}, u32[]{:S(2)}) %collective-permute-start.88) | collective-permute-done | bytes 614432 | tf_op jit(solution)/shard_map/ppermute | solution.py:302
  804.9 5.7 collective-permute-done.92
  (678 shorter events, 386.5 us)
Async XLA Ops:
  2.4 80.4 %collective-permute-start.3 = (bf16[200,400]{1,0:T(8,128)(2,1)}, bf16[200,400]{1,0:T(8,128)(2,1)}, u32[]{:S(2)}, u32[]{:S(2)}) collective-permute-start(bf16[200,400]{1,0:T(8,128)(2,1)} %convert_element_type.376), channel_id=1, source_target_pairs={{0,12},{4,0},{8,4},{12,8},{1,13},{5,1},{9,5},{13,9},{2,14},{6,2},{... | collective-permute-start | bytes 480008 | tf_op jit(solution)/shard_map/ppermute | solution.py:287
  12.4 47.3 %collective-permute-start.15 = (bf16[200,384]{1,0:T(8,128)(2,1)}, bf16[200,384]{1,0:T(8,128)(2,1)}, u32[]{:S(2)}, u32[]{:S(2)}) collective-permute-start(bf16[200,384]{1,0:T(8,128)(2,1)} %get-tuple-element.265), channel_id=1, source_target_pairs={{0,4},{4,8},{8,12},{12,0},{1,5},{5,9},{9,13},{13,1},{2,6},{6,10},{... | collective-permute-start | bytes 460808 | tf_op jit(solution)/shard_map/ppermute | solution.py:287
  13.2 41.5 %collective-permute-start.55 = (bf16[400,128]{1,0:T(8,128)(2,1)}, bf16[400,128]{1,0:T(8,128)(2,1)}, u32[]{:S(2)}, u32[]{:S(2)}) collective-permute-start(bf16[400,128]{1,0:T(8,128)(2,1)} %get-tuple-element.311), channel_id=1, source_target_pairs={{0,4},{4,8},{8,12},{12,0},{1,5},{5,9},{9,13},{13,1},{2,6},{6,10},{... | collective-permute-start | bytes 307208 | tf_op jit(solution)/shard_map/ppermute | solution.py:287
  13.2 43.1 %collective-permute-start.54 = (bf16[400,128]{1,0:T(8,128)(2,1)}, bf16[400,128]{1,0:T(8,128)(2,1)}, u32[]{:S(2)}, u32[]{:S(2)}) collective-permute-start(bf16[400,128]{1,0:T(8,128)(2,1)} %get-tuple-element.309), channel_id=1, source_target_pairs={{0,8},{4,12},{8,0},{12,4},{1,9},{5,13},{9,1},{13,5},{2,10},{6,14},... | collective-permute-start | bytes 307208 | tf_op jit(solution)/shard_map/ppermute | solution.py:287
  17.6 39.3 %collective-permute-start.53 = (bf16[400,128]{1,0:T(8,128)(2,1)}, bf16[400,128]{1,0:T(8,128)(2,1)}, u32[]{:S(2)}, u32[]{:S(2)}) collective-permute-start(bf16[400,128]{1,0:T(8,128)(2,1)} %get-tuple-element.310), channel_id=1, source_target_pairs={{0,12},{4,0},{8,4},{12,8},{1,13},{5,1},{9,5},{13,9},{2,14},{6,2},{... | collective-permute-start | bytes 307208 | tf_op jit(solution)/shard_map/ppermute | solution.py:287
  90.9 46.1 %collective-permute-start.57 = (bf16[1600,128]{1,0:T(8,128)(2,1)}, bf16[1600,128]{1,0:T(8,128)(2,1)S(1)}, u32[]{:S(2)}, u32[]{:S(2)}) collective-permute-start(bf16[1600,128]{1,0:T(8,128)(2,1)} %get-tuple-element.306), channel_id=1, source_target_pairs={{0,16},{1,17},{2,18},{3,19},{16,0},{17,1},{18,2},{19,3},{4,20},{5,... | collective-permute-start | bytes 1228808 | tf_op jit(solution)/shard_map/ppermute | solution.py:302
  150.3 38.3 %collective-permute-start.23 = (bf16[896,512]{1,0:T(8,128)(2,1)S(1)}, bf16[896,512]{1,0:T(8,128)(2,1)S(1)}, u32[]{:S(2)}, u32[]{:S(2)}) collective-permute-start(bf16[896,512]{1,0:T(8,128)(2,1)S(1)} %slice.443.refs_0_.refs_1_), channel_id=1, source_target_pairs={{0,2},{1,3},{4,6},{5,7},{8,10},{9,11},{12,14},{13,15},{16,18},{17,... | collective-permute-start | bytes 2752520 | tf_op jit(solution)/shard_map/ppermute | solution.py:448
  189.5 110.6 %collective-permute-start.35 = (bf16[400,800]{1,0:T(8,128)(2,1)S(1)}, bf16[400,800]{1,0:T(8,128)(2,1)S(1)}, u32[]{:S(2)}, u32[]{:S(2)}) collective-permute-start(bf16[400,800]{1,0:T(8,128)(2,1)S(1)} %bitcast.384), channel_id=1, source_target_pairs={{0,4},{4,8},{8,12},{12,0},{1,5},{5,9},{9,13},{13,1},{2,6},{6,10},{... | collective-permute-start | bytes 1920008 | tf_op jit(solution)/shard_map/ppermute | solution.py:287
  195.1 105.5 %collective-permute-start.34 = (bf16[400,800]{1,0:T(8,128)(2,1)S(1)}, bf16[400,800]{1,0:T(8,128)(2,1)S(1)}, u32[]{:S(2)}, u32[]{:S(2)}) collective-permute-start(bf16[400,800]{1,0:T(8,128)(2,1)S(1)} %bitcast.385), channel_id=1, source_target_pairs={{0,8},{4,12},{8,0},{12,4},{1,9},{5,13},{9,1},{13,5},{2,10},{6,14},... | collective-permute-start | bytes 1920008 | tf_op jit(solution)/shard_map/ppermute | solution.py:287
  201.8 45.9 %collective-permute-start.27 = (bf16[448,128]{1,0:T(8,128)(2,1)S(1)}, bf16[448,128]{1,0:T(8,128)(2,1)S(1)}, u32[]{:S(2)}, u32[]{:S(2)}) collective-permute-start(bf16[448,128]{1,0:T(8,128)(2,1)S(1)} %get-tuple-element.282), channel_id=1, source_target_pairs={{0,8},{4,12},{8,0},{12,4},{1,9},{5,13},{9,1},{13,5},{2,10},{6,14},... | collective-permute-start | bytes 344072 | tf_op jit(solution)/shard_map/ppermute | solution.py:287
  203.5 44.2 %collective-permute-start.26 = (bf16[448,128]{1,0:T(8,128)(2,1)S(1)}, bf16[448,128]{1,0:T(8,128)(2,1)S(1)}, u32[]{:S(2)}, u32[]{:S(2)}) collective-permute-start(bf16[448,128]{1,0:T(8,128)(2,1)S(1)} %get-tuple-element.283), channel_id=1, source_target_pairs={{0,12},{4,0},{8,4},{12,8},{1,13},{5,1},{9,5},{13,9},{2,14},{6,2},{... | collective-permute-start | bytes 344072 | tf_op jit(solution)/shard_map/ppermute | solution.py:287
  229.3 71.3 %collective-permute-start.33 = (bf16[400,800]{1,0:T(8,128)(2,1)S(1)}, bf16[400,800]{1,0:T(8,128)(2,1)S(1)}, u32[]{:S(2)}, u32[]{:S(2)}) collective-permute-start(bf16[400,800]{1,0:T(8,128)(2,1)S(1)} %bitcast.386), channel_id=1, source_target_pairs={{0,12},{4,0},{8,4},{12,8},{1,13},{5,1},{9,5},{13,9},{2,14},{6,2},{... | collective-permute-start | bytes 1920008 | tf_op jit(solution)/shard_map/ppermute | solution.py:287
  277.3 38.9 %collective-permute-start.31 = (bf16[800,400]{0,1:T(8,128)(2,1)S(1)}, bf16[800,400]{0,1:T(8,128)(2,1)S(1)}, u32[]{:S(2)}, u32[]{:S(2)}) collective-permute-start(bf16[800,400]{0,1:T(8,128)(2,1)S(1)} %copy-done.50), channel_id=1, source_target_pairs={{0,4},{4,8},{8,12},{12,0},{1,5},{5,9},{9,13},{13,1},{2,6},{6,10},{... | collective-permute-start | bytes 1920008 | tf_op jit(solution)/shard_map/ppermute | solution.py:287
  296.5 49.9 %collective-permute-start.30 = (bf16[800,400]{0,1:T(8,128)(2,1)S(1)}, bf16[800,400]{0,1:T(8,128)(2,1)S(1)}, u32[]{:S(2)}, u32[]{:S(2)}) collective-permute-start(bf16[800,400]{0,1:T(8,128)(2,1)S(1)} %copy-done.50), channel_id=1, source_target_pairs={{0,8},{4,12},{8,0},{12,4},{1,9},{5,13},{9,1},{13,5},{2,10},{6,14},... | collective-permute-start | bytes 1920008 | tf_op jit(solution)/shard_map/ppermute | solution.py:287
  300.2 46.3 %collective-permute-start.29 = (bf16[800,400]{0,1:T(8,128)(2,1)S(1)}, bf16[800,400]{0,1:T(8,128)(2,1)S(1)}, u32[]{:S(2)}, u32[]{:S(2)}) collective-permute-start(bf16[800,400]{0,1:T(8,128)(2,1)S(1)} %copy-done.50), channel_id=1, source_target_pairs={{0,12},{4,0},{8,4},{12,8},{1,13},{5,1},{9,5},{13,9},{2,14},{6,2},{... | collective-permute-start | bytes 1920008 | tf_op jit(solution)/shard_map/ppermute | solution.py:287
  401.0 80.2 %collective-permute-start.109 = (bf16[800,400]{0,1:T(8,128)(2,1)}, bf16[800,400]{0,1:T(8,128)(2,1)}, u32[]{:S(2)}, u32[]{:S(2)}) collective-permute-start(bf16[800,400]{0,1:T(8,128)(2,1)} %copy.191), channel_id=1, source_target_pairs={{0,8},{4,12},{8,0},{12,4},{1,9},{5,13},{9,1},{13,5},{2,10},{6,14},... | collective-permute-start | bytes 1920008 | tf_op jit(solution)/shard_map/ppermute | solution.py:287
  402.7 80.8 %collective-permute-start.108 = (bf16[800,400]{0,1:T(8,128)(2,1)}, bf16[800,400]{0,1:T(8,128)(2,1)}, u32[]{:S(2)}, u32[]{:S(2)}) collective-permute-start(bf16[800,400]{0,1:T(8,128)(2,1)} %copy.189), channel_id=1, source_target_pairs={{0,4},{4,8},{8,12},{12,0},{1,5},{5,9},{9,13},{13,1},{2,6},{6,10},{... | collective-permute-start | bytes 1920008 | tf_op jit(solution)/shard_map/ppermute | solution.py:287
  405.6 84.6 %collective-permute-start.63 = (bf16[1600,128]{1,0:T(8,128)(2,1)}, bf16[1600,128]{1,0:T(8,128)(2,1)}, u32[]{:S(2)}, u32[]{:S(2)}) collective-permute-start(bf16[1600,128]{1,0:T(8,128)(2,1)} %get-tuple-element.214), channel_id=1, source_target_pairs={{0,1},{1,0},{2,3},{3,2},{16,17},{17,16},{18,19},{19,18},{4,5},{5,4... | collective-permute-start | bytes 1228808 | tf_op jit(solution)/shard_map/ppermute | solution.py:302
  405.7 102.7 %collective-permute-start.43 = (bf16[1600,128]{1,0:T(8,128)(2,1)}, bf16[1600,128]{1,0:T(8,128)(2,1)}, u32[]{:S(2)}, u32[]{:S(2)}) collective-permute-start(bf16[1600,128]{1,0:T(8,128)(2,1)} %get-tuple-element.221), channel_id=1, source_target_pairs={{0,1},{1,0},{2,3},{3,2},{16,17},{17,16},{18,19},{19,18},{4,5},{5,4... | collective-permute-start | bytes 1228808 | tf_op jit(solution)/shard_map/ppermute | solution.py:302
  418.4 91.3 %collective-permute-start.106 = (bf16[400,800]{1,0:T(8,128)(2,1)}, bf16[400,800]{1,0:T(8,128)(2,1)}, u32[]{:S(2)}, u32[]{:S(2)}) collective-permute-start(bf16[400,800]{1,0:T(8,128)(2,1)} %get-tuple-element.234), channel_id=1, source_target_pairs={{0,12},{4,0},{8,4},{12,8},{1,13},{5,1},{9,5},{13,9},{2,14},{6,2},{... | collective-permute-start | bytes 1920008 | tf_op jit(solution)/shard_map/ppermute | solution.py:287
  481.2 45.2 %collective-permute-start.105 = (bf16[400,800]{1,0:T(8,128)(2,1)}, bf16[400,800]{1,0:T(8,128)(2,1)}, u32[]{:S(2)}, u32[]{:S(2)}) collective-permute-start(bf16[400,800]{1,0:T(8,128)(2,1)} %get-tuple-element.235), channel_id=1, source_target_pairs={{0,8},{4,12},{8,0},{12,4},{1,9},{5,13},{9,1},{13,5},{2,10},{6,14},... | collective-permute-start | bytes 1920008 | tf_op jit(solution)/shard_map/ppermute | solution.py:287
  483.5 44.6 %collective-permute-start.104 = (bf16[400,800]{1,0:T(8,128)(2,1)}, bf16[400,800]{1,0:T(8,128)(2,1)}, u32[]{:S(2)}, u32[]{:S(2)}) collective-permute-start(bf16[400,800]{1,0:T(8,128)(2,1)} %get-tuple-element.233), channel_id=1, source_target_pairs={{0,4},{4,8},{8,12},{12,0},{1,5},{5,9},{9,13},{13,1},{2,6},{6,10},{... | collective-permute-start | bytes 1920008 | tf_op jit(solution)/shard_map/ppermute | solution.py:287
  490.2 39.1 %collective-permute-start.69 = (bf16[1600,128]{1,0:T(8,128)(2,1)}, bf16[1600,128]{1,0:T(8,128)(2,1)}, u32[]{:S(2)}, u32[]{:S(2)}) collective-permute-start(bf16[1600,128]{1,0:T(8,128)(2,1)} %get-tuple-element.219), channel_id=1, source_target_pairs={{0,18},{1,19},{2,16},{3,17},{16,2},{17,3},{18,0},{19,1},{4,22},{5,... | collective-permute-start | bytes 1228808 | tf_op jit(solution)/shard_map/ppermute | solution.py:302
  533.1 83.0 %collective-permute-start.107 = (bf16[200,800]{1,0:T(8,128)(2,1)}, bf16[200,800]{1,0:T(8,128)(2,1)}, u32[]{:S(2)}, u32[]{:S(2)}) collective-permute-start(bf16[200,800]{1,0:T(8,128)(2,1)} %get-tuple-element.251), channel_id=1, source_target_pairs={{0,16},{16,0},{1,17},{17,1},{2,18},{18,2},{3,19},{19,3},{4,20},{20... | collective-permute-start | bytes 960008 | tf_op jit(solution)/shard_map/ppermute | solution.py:324
  590.3 41.9 %collective-permute-start.95 = (bf16[200,1600]{1,0:T(8,128)(2,1)}, bf16[200,1600]{1,0:T(8,128)(2,1)}, u32[]{:S(2)}, u32[]{:S(2)}) collective-permute-start(bf16[200,1600]{1,0:T(8,128)(2,1)} %get-tuple-element.198), channel_id=1, source_target_pairs={{0,1},{1,0},{2,3},{3,2},{16,17},{17,16},{18,19},{19,18},{4,5},{5,4... | collective-permute-start | bytes 1920008 | tf_op jit(solution)/shard_map/ppermute | solution.py:302
  592.9 39.3 %collective-permute-start.99 = (bf16[200,1600]{1,0:T(8,128)(2,1)}, bf16[200,1600]{1,0:T(8,128)(2,1)}, u32[]{:S(2)}, u32[]{:S(2)}) collective-permute-start(bf16[200,1600]{1,0:T(8,128)(2,1)} %get-tuple-element.196), channel_id=1, source_target_pairs={{0,1},{1,0},{2,3},{3,2},{16,17},{17,16},{18,19},{19,18},{4,5},{5,4... | collective-permute-start | bytes 1920008 | tf_op jit(solution)/shard_map/ppermute | solution.py:302
  594.1 38.2 %collective-permute-start.97 = (bf16[200,1600]{1,0:T(8,128)(2,1)}, bf16[200,1600]{1,0:T(8,128)(2,1)}, u32[]{:S(2)}, u32[]{:S(2)}) collective-permute-start(bf16[200,1600]{1,0:T(8,128)(2,1)} %get-tuple-element.197), channel_id=1, source_target_pairs={{0,1},{1,0},{2,3},{3,2},{16,17},{17,16},{18,19},{19,18},{4,5},{5,4... | collective-permute-start | bytes 1920008 | tf_op jit(solution)/shard_map/ppermute | solution.py:302
  594.1 58.4 %collective-permute-start.94 = (bf16[200,1600]{1,0:T(8,128)(2,1)}, bf16[200,1600]{1,0:T(8,128)(2,1)}, u32[]{:S(2)}, u32[]{:S(2)}) collective-permute-start(bf16[200,1600]{1,0:T(8,128)(2,1)} %get-tuple-element.195), channel_id=1, source_target_pairs={{0,1},{1,0},{2,3},{3,2},{16,17},{17,16},{18,19},{19,18},{4,5},{5,4... | collective-permute-start | bytes 1920008 | tf_op jit(solution)/shard_map/ppermute | solution.py:302
  650.7 53.1 %collective-permute-start.76 = (bf16[896,512]{1,0:T(8,128)(2,1)S(1)}, bf16[896,512]{1,0:T(8,128)(2,1)S(1)}, u32[]{:S(2)}, u32[]{:S(2)}) collective-permute-start(bf16[896,512]{1,0:T(8,128)(2,1)S(1)} %copy-done.47), channel_id=1, source_target_pairs={{0,1},{1,0},{2,3},{3,2},{4,5},{5,4},{6,7},{7,6},{8,9},{9,8},{10,11... | collective-permute-start | bytes 2752520 | tf_op jit(solution)/shard_map/ppermute | solution.py:535
  652.4 51.4 %collective-permute-start.78 = (bf16[896,512]{1,0:T(8,128)(2,1)S(1)}, bf16[896,512]{1,0:T(8,128)(2,1)S(1)}, u32[]{:S(2)}, u32[]{:S(2)}) collective-permute-start(bf16[896,512]{1,0:T(8,128)(2,1)S(1)} %add_convert_fusion.2), channel_id=1, source_target_pairs={{2,0},{3,1},{6,4},{7,5},{10,8},{11,9},{14,12},{15,13},{18,16},{19,... | collective-permute-start | bytes 2752520 | tf_op jit(solution)/shard_map/ppermute | solution.py:541
  717.3 48.5 %collective-permute-start.81 = (bf16[400,512]{1,0:T(8,128)(2,1)}, bf16[400,512]{1,0:T(8,128)(2,1)}, u32[]{:S(2)}, u32[]{:S(2)}) collective-permute-start(bf16[400,512]{1,0:T(8,128)(2,1)} %get-tuple-element.242), channel_id=1, source_target_pairs={{0,12},{4,0},{8,4},{12,8},{1,13},{5,1},{9,5},{13,9},{2,14},{6,2},{... | collective-permute-start | bytes 1228808 | tf_op jit(solution)/shard_map/ppermute | solution.py:287
  717.3 49.8 %collective-permute-start.80 = (bf16[400,512]{1,0:T(8,128)(2,1)}, bf16[400,512]{1,0:T(8,128)(2,1)}, u32[]{:S(2)}, u32[]{:S(2)}) collective-permute-start(bf16[400,512]{1,0:T(8,128)(2,1)} %get-tuple-element.243), channel_id=1, source_target_pairs={{0,8},{4,12},{8,0},{12,4},{1,9},{5,13},{9,1},{13,5},{2,10},{6,14},... | collective-permute-start | bytes 1228808 | tf_op jit(solution)/shard_map/ppermute | solution.py:287
  (193 other events, 2698.6 us)

commit v2 on v1

--- a/solution.py
+++ b/solution.py
@@ -71,31 +71,148 @@
     return slots, width, source, unpack_block, unpack_rank, pack_final
 
 
-def move_units(table, values, bias, out_rows, out_dtype):
-    width = values.shape[1]
+def move_units(table, sources, bias, out_rows, out_dtype):
+    width = sources[0].shape[1]
+    units = sources[0].shape[0] // UNIT
     count = out_rows // UNIT
 
-    def body(tab, val, off, out):
+    def body(tab, *refs):
+        vals, out = refs[: len(sources)], refs[-1]
         for i in range(count):
             src = tab[i]
             rows = pl.ds(i * UNIT, UNIT)
-            safe = pl.multiple_of(jnp.maximum(src, 0) * UNIT, UNIT)
-            block = val[pl.ds(safe, UNIT), :].astype(F32)
-            block = jnp.where(src >= 0, block, 0.0)
-            out[rows, :] = (block + off[rows, :]).astype(out_dtype)
-
+            block = jnp.zeros((UNIT, width), F32)
+            for n, val in enumerate(vals):
+                own = src - n * units
+                safe = pl.multiple_of(jnp.clip(own, 0, units - 1) * UNIT, UNIT)
+                inside = jnp.logical_and(own >= 0, own < units)
+                block = jnp.where(inside, val[pl.ds(safe, UNIT), :].astype(F32), block)
+            if bias is not None:
+                block = block + refs[len(sources)][rows, :]
+            out[rows, :] = block.astype(out_dtype)
+
+    extra = [] if bias is None else [bias]
     return pl.pallas_call(
         body,
         out_shape=jax.ShapeDtypeStruct((out_rows, width), out_dtype),
-        in_specs=[
-            pl.BlockSpec(memory_space=pltpu.SMEM),
-            pl.BlockSpec(memory_space=pltpu.VMEM),
-            pl.BlockSpec(memory_space=pltpu.VMEM),
-        ],
+        in_specs=[pl.BlockSpec(memory_space=pltpu.SMEM)]
+        + [pl.BlockSpec(memory_space=pltpu.VMEM)] * (len(sources) + len(extra)),
         out_specs=pl.BlockSpec(memory_space=pltpu.VMEM),
         compiler_params=pltpu.CompilerParams(vmem_limit_bytes=32 * 2**20),
         name="move_units",
-    )(table, values, bias)
+    )(table, *sources, *extra)
+
+
+def qkv_product(weight, rows_in):
+    dps, blocks, rows, packed = weight.shape
+    tokens = rows_in.shape[2]
+
+    def body(w_ref, h_ref, out):
+        total = dot_tn(w_ref[0, 0], h_ref[0])
+        for d in range(1, dps):
+            total = total + dot_tn(w_ref[d, 0], h_ref[d])
+        out[...] = total
+
+    return pl.pallas_call(
+        body,
+        grid=(blocks,),
+        in_specs=[
+            pl.BlockSpec((dps, 1, rows, packed), lambda i: (0, i, 0, 0)),
+            pl.BlockSpec((dps, rows, tokens), lambda i: (0, 0, 0)),
+        ],
+        out_specs=pl.BlockSpec((packed, tokens), lambda i: (i, 0)),
+        out_shape=jax.ShapeDtypeStruct((blocks * packed, tokens), F32),
+        compiler_params=pltpu.CompilerParams(vmem_limit_bytes=40 * 2**20),
+        name="qkv_product",
+    )(weight, rows_in)
+
+
+def qkv_weight_part(rows_in, grads, blocks, packed):
+    dps, rows, tokens = rows_in.shape
+
+    def body(h_ref, g_ref, out):
+        out[0, 0] = dot_nt(h_ref[0], g_ref[...]).astype(BF16)
+
+    return pl.pallas_call(
+        body,
+        grid=(dps, blocks),
+        in_specs=[
+            pl.BlockSpec((1, rows, tokens), lambda d, i: (d, 0, 0)),
+            pl.BlockSpec((packed, tokens), lambda d, i: (i, 0)),
+        ],
+        out_specs=pl.BlockSpec((1, 1, rows, packed), lambda d, i: (d, i, 0, 0)),
+        out_shape=jax.ShapeDtypeStruct((dps, blocks, rows, packed), BF16),
+        compiler_params=pltpu.CompilerParams(vmem_limit_bytes=40 * 2**20),
+        name="qkv_weight_part",
+    )(rows_in, grads)
+
+
+def qkv_back(halves, grads, inputs, mean, inverse, gain, row_devices):
+    dps, blocks, rows, packed = halves[0].shape
+    tokens = inputs.shape[2]
+    few = rows // row_devices
+
+    def body(first, second, g_ref, x_ref, mean_ref, inv_ref, gain_ref, part, with_norm, plain, stats):
+        total = None
+        for n, w_ref in enumerate((first, second)):
+            for i in range(blocks):
+                start = (n * blocks + i) * packed
+                term = dot_nn(w_ref[0, i], g_ref[start : start + packed, :])
+                total = term if total is None else total + term
+        normed = (x_ref[0].astype(F32) - mean_ref[...]) * inv_ref[...]
+        product = total * normed
+        with_norm[0] = jnp.sum(product, axis=1, keepdims=True)
+        plain[0] = jnp.sum(total, axis=1, keepdims=True)
+        weight = gain_ref[0]
+        now = jnp.concatenate(
+            [
+                jnp.sum(total * weight, axis=0, keepdims=True),
+                jnp.sum(product * weight, axis=0, keepdims=True),
+            ],
+            axis=0,
+        )
+
+        @pl.when(pl.program_id(0) == 0)
+        def _():
+            stats[...] = now
+
+        @pl.when(pl.program_id(0) > 0)
+        def _():
+            stats[...] += now
+
+        for k in range(row_devices):
+            part[k, 0] = total[k * few : (k + 1) * few].astype(BF16)
+
+    weight_spec = pl.BlockSpec((1, blocks, rows, packed), lambda d: (d, 0, 0, 0))
+    row_spec = pl.BlockSpec((1, tokens), lambda d: (0, 0))
+    column = pl.BlockSpec((1, rows, 1), lambda d: (d, 0, 0))
+    return pl.pallas_call(
+        body,
+        grid=(dps,),
+        in_specs=[
+            weight_spec,
+            weight_spec,
+            pl.BlockSpec((2 * blocks * packed, tokens), lambda d: (0, 0)),
+            pl.BlockSpec((1, rows, tokens), lambda d: (d, 0, 0)),
+            row_spec,
+            row_spec,
+            column,
+        ],
+        out_specs=[
+            pl.BlockSpec((row_devices, 1, few, tokens), lambda d: (0, d, 0, 0)),
+            column,
+            column,
+            pl.BlockSpec((2, tokens), lambda d: (0, 0)),
+        ],
+        out_shape=[
+            jax.ShapeDtypeStruct((row_devices, dps, few, tokens), BF16),
+            jax.ShapeDtypeStruct((dps, rows, 1), F32),
+            jax.ShapeDtypeStruct((dps, rows, 1), F32),
+            jax.ShapeDtypeStruct((2, tokens), F32),
+        ],
+        compiler_params=pltpu.CompilerParams(vmem_limit_bytes=48 * 2**20),
+        name="qkv_back",
+    )(*halves, grads, inputs, mean, inverse, gain)
 
 
 def dot_tn(left, right):
@@ -281,7 +398,6 @@
     offsets = list(range(0, cols, 2)) + list(range(1, cols, 2))
     even = [(d, b) for d in range(dps) for b in range(0, cols, 2)]
     plane = even + [(d, b + 1) for d, b in even]
-    place = {entry: i for i, entry in enumerate(plane)}
 
     def to_row(values, k):
         return lax.ppermute(values, "row", [(i, (i + k) % rows) for i in range(rows)])
@@ -305,17 +421,19 @@
             [(y * cols + c, (y ^ d) * cols + (c ^ b)) for y in range(dps) for c in range(cols)],
         )
 
-    def plane_gather(values):
-        first = [values] + [to_plane(values, d, b) for d, b in even[1:]]
-        return first + [to_plane(item, 0, 1) for item in first]
-
-    def plane_reduce(pieces):
-        half = len(even)
-        sums = [
-            pieces[i].astype(F32) + to_plane(pieces[half + i], 0, 1).astype(F32) for i in range(half)
-        ]
-        total = sums[0]
-        for (d, b), item in list(zip(even, sums))[1:]:
+    def plane_direct(values, axis):
+        return jnp.concatenate([values] + [to_plane(values, d, b) for d, b in even[1:]], axis=axis)
+
+    def plane_gather(values, axis):
+        first = plane_direct(values, axis)
+        return jnp.concatenate([first, to_plane(first, 0, 1)], axis=axis)
+
+    def plane_reduce(near, far, axis):
+        sums = near.astype(F32) + to_plane(far, 0, 1).astype(F32)
+        size = sums.shape[axis] // len(even)
+        parts = [lax.slice_in_dim(sums, i * size, (i + 1) * size, axis=axis) for i in range(len(even))]
+        total = parts[0]
+        for (d, b), item in list(zip(even, parts))[1:]:
             total = total + to_plane(item.astype(BF16), d, b).astype(F32)
         return total
 
@@ -323,14 +441,6 @@
         return [chunks[0]] + [
             lax.ppermute(chunks[d], "dp", [(y, y ^ d) for y in range(dps)]) for d in range(1, dps)
         ]
-
-    def sum_everywhere(values):
-        for axis, size in (("col", cols), ("dp", dps), ("row", rows)):
-            step = 1
-            while step < size:
-                values = values + lax.ppermute(values, axis, [(i, i ^ step) for i in range(size)])
-                step *= 2
-        return values
 
     def sum_rows(values):
         step = 1
@@ -382,9 +492,8 @@
                 for k in range(rows)
             ]
 
-        vec_rel = rolled(vectors.reshape(8, rows, feats), 1)
-        vec_swap = swapped(vec_rel.reshape(8, rows, dps, half), 2).reshape(8, D)
-        vec_rel = vec_rel.reshape(8, D)
+        vec_swap = swapped(rolled(vectors.reshape(8, rows, feats), 1).reshape(8, rows, dps, half), 2)
+        vec_swap = vec_swap.transpose(0, 2, 1, 3).reshape(8, D)
 
         columns = rolled(at(jnp.asarray(source), c), 0).reshape(rows * packed)
         local_cols = qkv_weight.shape[1]
@@ -393,37 +502,31 @@
         ).astype(BF16)
         sorted_cols = mm("fn,nm->fm", qkv_weight.astype(BF16), select).astype(BF16)
         arrived = row_exchange([sorted_cols[:, k * packed : (k + 1) * packed] for k in range(rows)])
-        qkv_pieces = plane_gather(jnp.stack(arrived))
-        w_qkv = jnp.stack(
-            [
-                jnp.concatenate([qkv_pieces[place[(d, b)]] for b in offsets], axis=2)
-                for d in range(dps)
-            ],
-            axis=1,
-        ).reshape(D, cols * packed)
-
-        x_own = swapped(hidden_in.T.reshape(dps, half, tokens), 0).reshape(feats, tokens)
-        x_all = jnp.concatenate(row_gather(x_own), axis=0)
-        up_chunks = token_chunks(upstream.T)
-        top_few = jnp.concatenate(row_exchange(up_chunks), axis=0)
-        top_all = jnp.concatenate(plane_gather(top_few), axis=1)
-
-        w_proj = jnp.concatenate(
-            plane_gather(jnp.concatenate(row_gather(proj_weight.astype(BF16)), axis=1)), axis=0
-        )
+        qkv_first = plane_direct(jnp.stack(arrived).reshape(1, rows * half, packed), 0)
+
+        x_own = swapped(hidden_in.T.reshape(dps, half, tokens), 0)
+        x_all = jnp.stack(row_gather(x_own), axis=1).reshape(dps, rows * half, tokens)
         up_parts = up_weight.astype(BF16).reshape(half, dps, hidden).transpose(1, 0, 2)
         up_arrived = dp_exchange([at(up_parts, y ^ d) for d in range(dps)])
         up_rows = swapped(jnp.stack(up_arrived), 0).reshape(feats, hidden)
-        w_up = jnp.concatenate(row_gather(up_rows), axis=0)
-        w_down = jnp.concatenate(row_gather(down_weight.astype(BF16)), axis=1)
-
-        x_f = x_all.astype(F32)
+        down_rows = down_weight.astype(BF16).T
+        proj_own = proj_weight.astype(BF16)
+        qkv_first, x_all, up_rows, down_rows, proj_own = lax.optimization_barrier(
+            (qkv_first, x_all, up_rows, down_rows, proj_own)
+        )
+        qkv_second = to_plane(qkv_first, 0, 1)
+        halves = [item.reshape(dps, cols // 2, rows * half, packed) for item in (qkv_first, qkv_second)]
+        w_up = lax.all_gather(up_rows, "row", axis=0, tiled=True)
+        w_down = lax.all_gather(down_rows, "row", axis=0, tiled=True)
+
+        x_f = x_all.astype(F32).reshape(D, tokens)
         mean_one = jnp.mean(x_f, axis=0, keepdims=True)
         spread_one = jnp.mean(x_f * x_f, axis=0, keepdims=True) - mean_one * mean_one
         inverse_one = lax.rsqrt(spread_one + EPS_NORM)
         normed_one = (x_f - mean_one) * inverse_one
         h1 = (normed_one * vec_swap[0][:, None] + vec_swap[1][:, None]).astype(BF16)
-        qkv_packed = mm("fn,ft->nt", w_qkv, h1)
+        h1 = h1.reshape(dps, rows * half, tokens)
+        qkv_packed = [qkv_product(item, h1) for item in halves]
 
         order = np.argsort(np.asarray(offsets)).astype(np.int32)
         where_block = at(jnp.asarray(unpack_block), z)
@@ -449,25 +552,32 @@
         key_values = held + [
             lax.ppermute(item, "col", [(i, i ^ 1) for i in range(cols)]) for item in held
         ]
+        key_values, upstream_late, proj_own = lax.optimization_barrier((key_values, upstream, proj_own))
+        w_proj = plane_gather(unrolled(row_gather(proj_own), 1), 0)
+        top_few = unrolled(row_exchange(token_chunks(upstream_late.T)), 0)
+        top_all = plane_gather(top_few, 1)
         me = c.astype(jnp.int32).reshape(1)
         query_ids = lax.dynamic_slice_in_dim(segment_ids, c * tokens, tokens)
         start = jnp.sum((segment_ids[:, None] < query_ids[None, :]).astype(jnp.int32), axis=0)[None, :]
         attn, lse = attention_forward(me, start, query, key_values, offsets)
 
+
+        n_rows = D // cols // dps
         attn_pieces = row_exchange(token_chunks(attn))
         attn_abs = unrolled([item.reshape(slots, 1, HEAD_DIM, few) for item in attn_pieces], 1)
         attn_abs = attn_abs.reshape(rows * wide, few)[:D]
-        blocks = attn_abs.reshape(cols, dps, D // cols // dps, few)
-        attn_rel = jnp.concatenate([at(at(blocks, c ^ b), y ^ d) for d, b in plane], axis=0)
-        x_few = lax.dynamic_slice_in_dim(x_all, z * few, few, 1)
-        x_few = swapped(x_few.reshape(rows, dps, half, few), 1).reshape(D, few).astype(F32)
-        mid = x_few + mm("rf,rt->ft", w_proj, attn_rel) + vec_rel[4][:, None]
+        blocks = attn_abs.reshape(cols, dps, n_rows, few)
+        attn_few = jnp.concatenate([at(at(blocks, c ^ b), y ^ d) for d, b in plane], axis=0)
+        x_few = lax.dynamic_slice_in_dim(x_all, z * few, few, 2).reshape(dps, rows, half, few)
+        x_few = swapped(x_few, 0).transpose(1, 0, 2, 3).reshape(rows, feats, few)
+        x_few = unrolled([x_few[k] for k in range(rows)], 0).astype(F32)
+        mid = x_few + mm("rf,rt->ft", w_proj, attn_few) + vectors[4][:, None]
         mean_two = jnp.mean(mid, axis=0, keepdims=True)
         spread_two = jnp.mean(mid * mid, axis=0, keepdims=True) - mean_two * mean_two
         inverse_two = lax.rsqrt(spread_two + EPS_NORM)
         normed_two = (mid - mean_two) * inverse_two
-        h2 = (normed_two * vec_rel[5][:, None] + vec_rel[6][:, None]).astype(BF16)
-        h2_all = jnp.concatenate(plane_gather(h2), axis=1)
+        h2 = (normed_two * vectors[5][:, None] + vectors[6][:, None]).astype(BF16)
+        h2_all = plane_gather(h2, 1)
 
         up_shift = lax.dynamic_slice_in_dim(up_bias, (c * dps + y) * hidden, hidden)
         pre = mm("fh,ft->ht", w_up, h2_all) + up_shift[:, None]
@@ -477,54 +587,56 @@
         slope = 0.5 * (1.0 + tanh_val) + 0.5 * pre * (1.0 - tanh_val * tanh_val) * GELU_COEF * (
             1.0 + 3.0 * GELU_CUBE * pre * pre
         )
-        grad_pre = mm("hf,ft->ht", w_down, top_all) * slope
+        grad_pre = mm("fh,ft->ht", w_down, top_all) * slope
         grad_pre_half = grad_pre.astype(BF16)
         bias_part = jnp.sum(grad_pre, axis=1)
 
-        def by_plane(array):
-            return [array[:, i * few : (i + 1) * few] for i in range(len(plane))]
-
-        grad_ln_two = plane_reduce(by_plane(mm("fh,ht->ft", w_up, grad_pre_half).astype(BF16)))
-        down_sum = plane_reduce(by_plane(mm("hf,ht->ft", w_down, act).astype(BF16)))
-        out_few = (mid + down_sum + vec_rel[7][:, None]).astype(BF16)
-        block_out = unrolled(
-            row_exchange([out_few[k * feats : (k + 1) * feats] for k in range(rows)]), 1
-        ).T
-
-        down_part = mm("ht,ft->hf", act, top_all).astype(BF16)
-        down_grad = row_reduce([down_part[:, k * feats : (k + 1) * feats] for k in range(rows)])
-        up_part = mm("ft,ht->fh", h2_all, grad_pre_half).astype(BF16)
-        up_sum = row_reduce([up_part[k * feats : (k + 1) * feats] for k in range(rows)]).astype(BF16)
-        up_blocks = up_sum.reshape(dps, half, hidden)
-        up_back = dp_exchange([at(up_blocks, y ^ d) for d in range(dps)])
-        up_grad = swapped(jnp.stack(up_back), 0).transpose(1, 0, 2).reshape(half, dps * hidden).astype(F32)
-
-        scaled = grad_ln_two * vec_rel[5][:, None]
+        middle = len(even) * few
+
+        def features_back(weight, values):
+            far = mm("fh,ht->ft", weight, values[:, middle:]).astype(BF16)
+            near = mm("fh,ht->ft", weight, values[:, :middle]).astype(BF16)
+            return plane_reduce(near, far, 1), (near, far)
+
+        def row_chunks(array):
+            return [lax.dynamic_slice_in_dim(array, ((z + k) % rows) * feats, feats, 0) for k in range(rows)]
+
+        grad_ln_two, partial = features_back(w_up, grad_pre_half)
+
+        scaled = grad_ln_two * vectors[5][:, None]
         first_mean = jnp.mean(scaled, axis=0, keepdims=True)
         second_mean = jnp.mean(scaled * normed_two, axis=0, keepdims=True)
         grad_mid = top_few.astype(F32) + inverse_two * (scaled - first_mean - normed_two * second_mean)
         grad_mid_half = grad_mid.astype(BF16)
         grad_attn = mm("rf,ft->rt", w_proj, grad_mid_half).astype(BF16)
-        n_rows = D // cols // dps
-        natural = jnp.stack(
-            [
-                jnp.stack([grad_attn[place[(d, b)] * n_rows : (place[(d, b)] + 1) * n_rows] for d in range(dps)])
-                for b in range(cols)
-            ]
-        )
-        natural = swapped(natural, 1)
+        natural = grad_attn.reshape(2, dps, cols // 2, n_rows, few).transpose(2, 0, 1, 3, 4)
+        natural = swapped(natural.reshape(cols, dps, n_rows, few), 1)
         grad_abs = jnp.stack([at(natural, c ^ b) for b in range(cols)]).reshape(D, few)
         grad_abs = jnp.pad(grad_abs, ((0, rows * wide - D), (0, 0))).reshape(slots, rows, HEAD_DIM, few)
         grad_heads = unrolled(
             row_exchange([at(grad_abs, (z + k) % rows, 1).reshape(wide, few) for k in range(rows)]), 1
         )
-        proj_part = mm("rt,ft->rf", attn_rel, grad_mid_half).astype(BF16)
-        proj_sum = plane_reduce([proj_part[i * n_rows : (i + 1) * n_rows] for i in range(len(plane))])
-        proj_sum = proj_sum.astype(BF16)
-        proj_grad = row_reduce([proj_sum[:, k * feats : (k + 1) * feats] for k in range(rows)])
-        grad_mid_own = unrolled(
-            row_exchange([grad_mid_half[k * feats : (k + 1) * feats] for k in range(rows)]), 1
-        )
+
+        act_late, pre_late, _ = lax.optimization_barrier((act, grad_pre_half, partial))
+        down_part = mm("ft,ht->fh", top_all, act_late).astype(BF16)
+        up_part = mm("ft,ht->fh", h2_all, pre_late).astype(BF16)
+        act_late, _ = lax.optimization_barrier((act, grad_ln_two))
+        down_sum, _ = features_back(w_down, act_late)
+        out_few = (mid + down_sum + vectors[7][:, None]).astype(BF16)
+        block_out = unrolled(row_exchange(row_chunks(out_few)), 1).T
+
+        middle_rows = len(even) * n_rows
+        proj_far = mm("rt,ft->rf", attn_few[middle_rows:], grad_mid_half).astype(BF16)
+        proj_near = mm("rt,ft->rf", attn_few[:middle_rows], grad_mid_half).astype(BF16)
+        grad_heads, proj_far, proj_near, down_part, up_part = lax.optimization_barrier(
+            (grad_heads, proj_far, proj_near, down_part, up_part)
+        )
+        down_sum_part = lax.psum_scatter(down_part, "row", scatter_dimension=0, tiled=True)
+        up_sum = lax.psum_scatter(up_part, "row", scatter_dimension=0, tiled=True)
+        proj_sum = plane_reduce(proj_near, proj_far, 0).astype(BF16)
+        proj_cols = proj_sum.reshape(n_rows, rows, feats).transpose(1, 0, 2)
+        proj_grad = row_reduce([at(proj_cols, (z + k) % rows) for k in range(rows)])
+        grad_mid_own = unrolled(row_exchange(row_chunks(grad_mid_half)), 1)
 
         results = attention_backward(me, start, query, key_values, offsets, attn, lse, grad_heads)
         grad_query, query_total, value_total = results[:3]
@@ -543,40 +655,43 @@
             ).astype(F32)
         grad_qkv = jnp.concatenate([grad_query, own_sum.astype(BF16)], axis=0)
         finals = at(jnp.asarray(pack_final), z)
-        pack = jnp.concatenate([at(finals, c ^ b) for b in offsets])
-        grad_packed = move_units(pack, grad_qkv, jnp.zeros((cols * packed, 1), F32), cols * packed, BF16)
-
-        grad_ln_part = mm("fn,nt->ft", w_qkv, grad_packed)
-        gain_one = vec_swap[0][:, None]
-        scaled_part = grad_ln_part * gain_one
-        stats = sum_rows(
-            jnp.stack([jnp.sum(scaled_part, axis=0), jnp.sum(scaled_part * normed_one, axis=0)])
-        )
-        part_half = grad_ln_part.astype(BF16)
-        grad_ln_own = row_reduce([part_half[k * feats : (k + 1) * feats] for k in range(rows)])
+        finals = jnp.concatenate([at(finals, c ^ b) for b in offsets])
+        grad_packed = move_units(finals, [grad_qkv], None, cols * packed, BF16)
+
+        gain_one = vec_swap[0].reshape(dps, rows * half, 1)
+        part_half, sum_norm, sum_plain, stats = qkv_back(
+            halves, grad_packed, x_all, mean_one, inverse_one, gain_one, rows
+        )
+        near_cols = cols // 2 * packed
+        qkv_far = qkv_weight_part(h1, grad_packed[near_cols:], cols // 2, packed)
+        qkv_near = qkv_weight_part(h1, grad_packed[:near_cols], cols // 2, packed)
+        stats = sum_rows(stats)
+        grad_ln_own = row_reduce([part_half[k] for k in range(rows)])
         first_row, second_row = stats[0:1] / D, stats[1:2] / D
-        inner = inverse_one * (
-            grad_ln_own * gain_one[:feats] - first_row - normed_one[:feats] * second_row
-        )
-        inner = swapped(inner.reshape(dps, half, tokens), 0).reshape(feats, tokens)
+        own_normed = normed_one.reshape(dps, rows, half, tokens)[:, 0]
+        own_gain = gain_one.reshape(dps, rows, half, 1)[:, 0]
+        inner = inverse_one * (grad_ln_own * own_gain - first_row - own_normed * second_row)
+        inner = swapped(inner, 0).reshape(feats, tokens)
         input_grad = (grad_mid_own.astype(F32) + inner).astype(BF16).T
 
-        qkv_part = mm("ft,nt->fn", h1, grad_packed).astype(BF16).reshape(rows, dps, half, cols * packed)
-        qkv_sum = plane_reduce(
-            [
-                qkv_part[:, d, :, offsets.index(b) * packed : (offsets.index(b) + 1) * packed]
-                for d, b in plane
-            ]
-        ).astype(BF16)
-        qkv_back = jnp.concatenate(row_exchange([qkv_sum[k] for k in range(rows)]), axis=1)
-        qkv_grad = mm("fm,nm->fn", qkv_back, select)
+        flat = (dps * (cols // 2), rows * half, packed)
+        qkv_sum = plane_reduce(qkv_near.reshape(flat), qkv_far.reshape(flat), 0)[0].astype(BF16)
+        qkv_sum = qkv_sum.reshape(rows, half, packed)
+        qkv_home = jnp.concatenate(row_exchange([qkv_sum[k] for k in range(rows)]), axis=1)
+        qkv_grad = mm("fm,nm->fn", qkv_home, select)
+
+        up_sum, down_sum_part, _ = lax.optimization_barrier((up_sum, down_sum_part, part_half))
+        down_grad = down_sum_part.T.astype(F32)
+        up_blocks = up_sum.reshape(dps, half, hidden)
+        up_back = dp_exchange([at(up_blocks, y ^ d) for d in range(dps)])
+        up_grad = swapped(jnp.stack(up_back), 0).transpose(1, 0, 2).reshape(half, dps * hidden).astype(F32)
 
         def back_from_rel(vector):
             blocks = vector.reshape(rows, feats)
             return jnp.concatenate([at(blocks, (t - z) % rows) for t in range(rows)])
 
         def back_from_swap(vector):
-            return back_from_rel(swapped(vector.reshape(rows, dps, half), 1).reshape(D))
+            return back_from_rel(swapped(vector.reshape(dps, rows, half), 0).transpose(1, 0, 2).reshape(D))
 
         def from_heads(vector):
             blocks = vector.reshape(slots, 1, HEAD_DIM)
@@ -586,20 +701,21 @@
         top_sum = jnp.sum(upstream.astype(F32), axis=0)
         parts = jnp.stack(
             [
-                back_from_swap(jnp.sum(grad_ln_part * normed_one, axis=1)),
-                back_from_swap(jnp.sum(grad_ln_part, axis=1)),
+                back_from_swap(sum_norm),
+                back_from_swap(sum_plain),
                 from_heads(query_total[:, 0]),
                 from_heads(value_total[:, 0]),
-                back_from_rel(jnp.sum(grad_mid, axis=1)),
-                back_from_rel(jnp.sum(grad_ln_two * normed_two, axis=1)),
-                back_from_rel(jnp.sum(grad_ln_two, axis=1)),
+                jnp.sum(grad_mid, axis=1),
+                jnp.sum(grad_ln_two * normed_two, axis=1),
+                jnp.sum(grad_ln_two, axis=1),
                 lax.dynamic_update_slice_in_dim(jnp.zeros((D,), F32), top_sum, z * feats, 0),
             ]
         )
         bias_full = lax.dynamic_update_slice_in_dim(
             jnp.zeros((up_bias.shape[0],), F32), bias_part, (c * dps + y) * hidden, 0
         )
-        summed = sum_everywhere(jnp.concatenate([parts.reshape(-1), bias_full]))
+        summed = lax.psum(jnp.concatenate([parts.reshape(-1), bias_full]), ("dp", "row", "col"))
+        summed, _ = lax.optimization_barrier((summed, qkv_home))
         vector_grad = summed[: 8 * D].reshape(8, D)
         bias_grad = summed[8 * D :]
 

time: 826 us -> 780 us (0.944)
  waiting for transfers between devices: 375 us -> 320 us
  starting transfers between devices: 175 us -> 150 us
  Pallas kernels: 14.5 us -> 37.5 us
  between operations: 3.33 us -> 16.1 us
    ppermute x45 -> x33, waiting for transfers between devices: 222 us -> 163 us  [to_row(): lax.ppermute(values, 'row', [(i, (i + k) % rows) for i in range(rows)])]
    ppermute x56 -> x32, waiting for transfers between devices: 112 us -> 61.2 us  [to_plane(): lax.ppermute(values, ('dp', 'col'), [(y * cols + c, (y ^ d) * cols + (c ^...]
    psum x0 -> x1, waiting for transfers between devices: none -> 50.2 us  [per_device(): lax.psum(jnp.concatenate([parts.reshape(-1), bias_full]), ('dp', 'row', '...]
    ppermute x1, waiting for transfers between devices: 0.01 us -> 21.1 us  [per_device(): lax.ppermute(kv_sums[i].astype(BF16), 'col', [(j, j ^ b) for j in range(c...]
    unnamed x252 -> x272, local copies, waits for them, and re-layouts: 36.1 us -> 55.7 us
    pallas_call x0 -> x5, Pallas kernels: none -> 19.4 us  [the longest x2 6.7 us: qkv_product(): pl.pallas_call(body, grid=(blocks,), in_specs=[pl.BlockSpec((dps, 1, rows...]
    slice x12 -> x10, local copies, waits for them, and re-layouts: 20.1 us -> 2.53 us  [the longest x4 1.64 us: plane_reduce(): lax.slice_in_dim(sums, i * size, (i + 1) * size, axis=axis)]
    convert_element_type x9 -> x6, other arithmetic: 18.9 us -> 6.18 us  [the longest x1 1.94 us: per_device(): out_few = (mid + down_sum + vectors[7][:, None]).astype(BF16)]
  transfers between devices with their start and end apart: 116 -> 80, of which waited for: 36 -> 32; matrix products, arithmetic and copies ran while one was open for 24% -> 23% of each run, Pallas kernels for 2% -> 3%
where the time goes in v2:
time: 780 us; the launch traced here: 769 us
  waiting for transfers between devices  320 us (41%)
  starting transfers between devices  150 us (19%)
  local copies, waits for them, and re-layouts  114 us (15%)
  other arithmetic  75.4 us (10%)
  matrix products  57.5 us (7%)
  Pallas kernels  37.5 us (5%)
  between operations  16.1 us (2%)
    ppermute x33, waiting for transfers between devices, to_row(): lax.ppermute(values, 'row', [(i, (i + k) % rows) for i in range(rows)])  163 us
    ppermute x33, starting transfers between devices, to_row(): lax.ppermute(values, 'row', [(i, (i + k) % rows) for i in range(rows)])  96.1 us
    ppermute x32, waiting for transfers between devices, to_plane(): lax.ppermute(values, ('dp', 'col'), [(y * cols + c, (y ^ d) * cols + (c ^...  61.2 us
    dot_general x14, matrix products, mm(): return jnp.einsum(spec, left, right, preferred_element_type=F32)  57.5 us
    unnamed x272, local copies, waits for them, and re-layouts  55.7 us
    psum x1, waiting for transfers between devices, per_device(): lax.psum(jnp.concatenate([parts.reshape(-1), bias_full]), ('dp', 'row', '...  50.2 us
    ppermute x32, starting transfers between devices, to_plane(): lax.ppermute(values, ('dp', 'col'), [(y * cols + c, (y ^ d) * cols + (c ^...  40.2 us
    ppermute x1, waiting for transfers between devices, per_device(): lax.ppermute(kv_sums[i].astype(BF16), 'col', [(j, j ^ b) for j in range(c...  21.1 us
  transfers between devices with their start and end apart: 80, of which 32 were waited for; matrix products, arithmetic and copies ran while one was open for 23% of the time, Pallas kernels for 3%

profile of v2, /device:TPU:0, one launch (start us, length us, event | category | flops | bytes accessed | tf_op | source)
XLA Modules:
  0.0 769.5 jit_solution(2195426971862344026)
XLA Ops:
  29.8 16.4 %collective-permute-done.1 = bf16[200,384]{1,0:T(8,128)(2,1)S(1)} collective-permute-done((bf16[200,384]{1,0:T(8,128)(2,1)S(1)}, bf16[200,384]{1,0:T(8,128)(2,1)S(1)}, u32[]{:S(2)}, u32[]{:S(2)}) %collective-permute-start.1) | collective-permute-done | bytes 153632 | tf_op jit(solution)/shard_map/ppermute | solution.py:403
  53.0 9.7 %collective-permute-done.7 = bf16[2,200,512]{2,1,0:T(8,128)(2,1)} collective-permute-done((bf16[2,200,512]{2,1,0:T(8,128)(2,1)}, bf16[2,200,512]{2,1,0:T(8,128)(2,1)}, u32[]{:S(2)}, u32[]{:S(2)}) %collective-permute-start.7) | collective-permute-done | bytes 409632 | tf_op jit(solution)/shard_map/ppermute | solution.py:403
  64.2 10.2 %collective-permute-done.4 = bf16[1,800,384]{2,1,0:T(8,128)(2,1)} collective-permute-done((bf16[1,800,384]{2,1,0:T(8,128)(2,1)S(1)}, bf16[1,800,384]{2,1,0:T(8,128)(2,1)}, u32[]{:S(2)}, u32[]{:S(2)}) %collective-permute-start.4) | collective-permute-done | bytes 614432 | tf_op jit(solution)/shard_map/ppermute | solution.py:418
  95.1 19.9 %collective-permute-done.11.refs_2_.refs_3_ = bf16[896,512]{1,0:T(8,128)(2,1)S(1)} collective-permute-done((bf16[896,512]{1,0:T(8,128)(2,1)S(1)}, bf16[896,512]{1,0:T(8,128)(2,1)S(1)}, u32[]{:S(2)}, u32[]{:S(2)}) %collective-permute-start.11) | collective-permute-done | bytes 917536 | tf_op jit(solution)/shard_map/ppermute | solution.py:551
  128.7 7.4 collective-permute-done.14
  136.1 19.6 %collective-permute-done.15 = bf16[200,400]{1,0:T(8,128)(2,1)S(1)} collective-permute-done((bf16[200,400]{1,0:T(8,128)(2,1)S(1)}, bf16[200,400]{1,0:T(8,128)(2,1)S(1)}, u32[]{:S(2)}, u32[]{:S(2)}) %collective-permute-start.15) | collective-permute-done | bytes 160032 | tf_op jit(solution)/shard_map/ppermute | solution.py:403
  167.5 6.8 attention_forward.1
  191.6 8.3 %collective-permute-start.31 = (bf16[1600,128]{1,0:T(8,128)(2,1)S(1)}, bf16[1600,128]{1,0:T(8,128)(2,1)S(1)}, u32[]{:S(2)}, u32[]{:S(2)}) collective-permute-start(bf16[1600,128]{1,0:T(8,128)(2,1)S(1)} %get-tuple-element.342), channel_id=1, source_target_pairs={{0,2},{1,3},{2,0},{3,1},{16,18},{17,19},{18,16},{19,17},{4,6},{5,7... | collective-permute-start | bytes 1228808 | tf_op jit(solution)/shard_map/ppermute | solution.py:418
  210.6 8.0 %collective-permute-done.32 = bf16[1600,128]{1,0:T(8,128)(2,1)S(1)} collective-permute-done((bf16[1600,128]{1,0:T(8,128)(2,1)S(1)}, bf16[1600,128]{1,0:T(8,128)(2,1)S(1)}, u32[]{:S(2)}, u32[]{:S(2)}) %collective-permute-start.32) | collective-permute-done | bytes 409632 | tf_op jit(solution)/shard_map/ppermute | solution.py:418
  239.0 7.7 %collective-permute-done.24 = bf16[1600,128]{1,0:T(8,128)(2,1)} collective-permute-done((bf16[1600,128]{1,0:T(8,128)(2,1)}, bf16[1600,128]{1,0:T(8,128)(2,1)}, u32[]{:S(2)}, u32[]{:S(2)}) %collective-permute-start.24) | collective-permute-done | bytes 409632 | tf_op jit(solution)/shard_map/ppermute | solution.py:418
  247.1 8.4 %collective-permute-done.26 = bf16[1600,128]{1,0:T(8,128)(2,1)} collective-permute-done((bf16[1600,128]{1,0:T(8,128)(2,1)}, bf16[1600,128]{1,0:T(8,128)(2,1)}, u32[]{:S(2)}, u32[]{:S(2)}) %collective-permute-start.26) | collective-permute-done | bytes 409632 | tf_op jit(solution)/shard_map/ppermute | solution.py:418
  269.3 9.0 %multiply_convert_fusion = (bf16[800,1024]{1,0:T(8,128)(2,1)}, f32[800,1024]{1,0:T(8,128)}) fusion(f32[800]{0:T(1024)} %dynamic_slice.420, bf16[1600,800]{1,0:T(8,128)(2,1)} %all-gather.5.cloned.1.call-done, bf16[1600,1024]{1,0:T(8,128)(2,1)} %constant_dynamic-update-slice_fusion.13), kind=kOutput, calls=%fused_computation.23 | convolution fusion | flops 2629632000 | bytes 10755200 | tf_op jit(solution)/shard_map/fh,ft->ht/dot_general | solution.py:33
  278.3 10.0 %fusion.117 = (f32[800]{0:T(1024)}, bf16[800,1024]{1,0:T(8,128)(2,1)S(1)}) fusion(f32[800,1024]{1,0:T(8,128)} %get-tuple-element.408, f32[800]{0:T(1024)} %dynamic_slice.420, bf16[1600,800]{1,0:T(8,128)(2,1)} %all-gather.3.cloned.1.call-done, bf16[1600,1024]{1,0:T(8,128)(2,1)} %constant_dynamic-update-slice_fusion.18), kind=kOutput, calls=%fused_computation.406 | convolution fusion | flops 2638642432 | bytes 10758400 | tf_op jit(solution)/shard_map/fh,ft->ht/dot_general | solution.py:33
  295.8 6.6 convolution_convert_fusion
  315.0 8.7 %collective-permute-done.37 = bf16[1600,128]{1,0:T(8,128)(2,1)S(1)} collective-permute-done((bf16[1600,128]{1,0:T(8,128)(2,1)S(1)}, bf16[1600,128]{1,0:T(8,128)(2,1)S(1)}, u32[]{:S(2)}, u32[]{:S(2)}) %collective-permute-start.37) | collective-permute-done | bytes 409632 | tf_op jit(solution)/shard_map/ppermute | solution.py:418
  342.5 9.0 %attention_backward.1 = (bf16[448,512]{1,0:T(8,128)(2,1)S(1)}, f32[448,1]{1,0:T(8,128)S(1)}, f32[448,1]{1,0:T(8,128)S(1)}, bf16[448,512]{1,0:T(8,128)(2,1)S(1)},...) custom-call(s32[1]{0:T(128)} %bitcast.49.me_ref, ...), custom_call_target="tpu_custom_call" | custom-call | tf_op jit(solution)/shard_map/attention_backward/pallas_call | solution.py:382
  377.9 21.1 %collective-permute-done.54 = bf16[896,512]{1,0:T(8,128)(2,1)} collective-permute-done((bf16[896,512]{1,0:T(8,128)(2,1)}, bf16[896,512]{1,0:T(8,128)(2,1)}, u32[]{:S(2)}, u32[]{:S(2)}) %collective-permute-start.54) | collective-permute-done | bytes 917536 | tf_op jit(solution)/shard_map/ppermute | solution.py:653
  402.1 6.7 qkv_back.1
  446.7 8.1 %collective-permute-done.47 = bf16[400,128]{1,0:T(8,128)(2,1)S(1)} collective-permute-done((bf16[400,128]{1,0:T(8,128)(2,1)S(1)}, bf16[400,128]{1,0:T(8,128)(2,1)S(1)}, u32[]{:S(2)}, u32[]{:S(2)}) %collective-permute-start.47) | collective-permute-done | bytes 102432 | tf_op jit(solution)/shard_map/ppermute | solution.py:403
  455.6 5.4 copy.172
  461.1 6.1 fusion.125
  485.3 50.2 %all-reduce.5.cloned.1.call-done = f32[19200]{0:T(1024)} async-done(((f32[19200]{0:T(1024)}), f32[19200]{0:T(1024)}) %all-reduce.5.cloned.1.call-update) | async-done | bytes 76816 | tf_op jit(solution)/shard_map/psum | solution.py:717
  541.3 5.3 collective-permute-start.43
  552.1 12.6 %collective-permute-start.55 = (bf16[2,200,512]{2,1,0:T(8,128)(2,1)}, bf16[2,200,512]{2,1,0:T(8,128)(2,1)S(1)}, u32[]{:S(2)}, u32[]{:S(2)}) collective-permute-start(bf16[2,200,512]{2,1,0:T(8,128)(2,1)} %get-tuple-element.265), channel_id=1, source_target_pairs={{0,4},{4,8},{8,12},{12,0},{1,5},{5,9},{9,13},{13,1},{2,6},{6,10},{... | collective-permute-start | bytes 1228808 | tf_op jit(solution)/shard_map/ppermute | solution.py:403
  564.6 15.9 %collective-permute-done.44 = bf16[400,128]{1,0:T(8,128)(2,1)S(1)} collective-permute-done((bf16[400,128]{1,0:T(8,128)(2,1)S(1)}, bf16[400,128]{1,0:T(8,128)(2,1)S(1)}, u32[]{:S(2)}, u32[]{:S(2)}) %collective-permute-start.44) | collective-permute-done | bytes 102432 | tf_op jit(solution)/shard_map/ppermute | solution.py:403
  585.8 27.3 %collective-permute-done.56 = bf16[2,200,512]{2,1,0:T(8,128)(2,1)S(1)} collective-permute-done((bf16[2,200,512]{2,1,0:T(8,128)(2,1)}, bf16[2,200,512]{2,1,0:T(8,128)(2,1)S(1)}, u32[]{:S(2)}, u32[]{:S(2)}) %collective-permute-start.56) | collective-permute-done | bytes 409632 | tf_op jit(solution)/shard_map/ppermute | solution.py:403
  618.6 6.0 collective-permute-done.70
  630.9 24.8 %collective-permute-start.71 = (bf16[200,400]{1,0:T(8,128)(2,1)S(1)}, bf16[200,400]{1,0:T(8,128)(2,1)S(1)}, u32[]{:S(2)}, u32[]{:S(2)}) collective-permute-start(bf16[200,400]{1,0:T(8,128)(2,1)S(1)} %bitcast.435), channel_id=1, source_target_pairs={{0,4},{4,8},{8,12},{12,0},{1,5},{5,9},{9,13},{13,1},{2,6},{6,10},{... | collective-permute-start | bytes 480008 | tf_op jit(solution)/shard_map/ppermute | solution.py:403
  673.0 12.0 %collective-permute-done.72 = bf16[200,400]{1,0:T(8,128)(2,1)S(1)} collective-permute-done((bf16[200,400]{1,0:T(8,128)(2,1)S(1)}, bf16[200,400]{1,0:T(8,128)(2,1)S(1)}, u32[]{:S(2)}, u32[]{:S(2)}) %collective-permute-start.72) | collective-permute-done | bytes 160032 | tf_op jit(solution)/shard_map/ppermute | solution.py:403
  685.0 6.5 collective-permute-done.73
  692.1 6.4 collective-permute-start.64
  707.5 16.4 %collective-permute-done.65 = bf16[200,384]{1,0:T(8,128)(2,1)S(1)} collective-permute-done((bf16[200,384]{1,0:T(8,128)(2,1)S(1)}, bf16[200,384]{1,0:T(8,128)(2,1)S(1)}, u32[]{:S(2)}, u32[]{:S(2)}) %collective-permute-start.65) | collective-permute-done | bytes 153632 | tf_op jit(solution)/shard_map/ppermute | solution.py:403
  (624 shorter events, 356.6 us)
Async XLA Ops:
  7.2 262.1 %all-gather.5.cloned.1.call-start = ((), (), s32[]{:S(2)}) async-start(), calls=%async_computation.3 | async-start | bytes 3584000 | tf_op jit(solution)/shard_map/all_gather | solution.py:519
  9.2 38.7 %collective-permute-start.6 = (bf16[2,200,512]{2,1,0:T(8,128)(2,1)}, bf16[2,200,512]{2,1,0:T(8,128)(2,1)}, u32[]{:S(2)}, u32[]{:S(2)}) collective-permute-start(bf16[2,200,512]{2,1,0:T(8,128)(2,1)} %get-tuple-element.363), channel_id=1, source_target_pairs={{0,12},{4,0},{8,4},{12,8},{1,13},{5,1},{9,5},{13,9},{2,14},{6,2},{... | collective-permute-start | bytes 1228808 | tf_op jit(solution)/shard_map/ppermute | solution.py:403
  17.3 30.6 %collective-permute-start.9 = (bf16[200,800]{1,0:T(8,128)(2,1)}, bf16[200,800]{1,0:T(8,128)(2,1)}, u32[]{:S(2)}, u32[]{:S(2)}) collective-permute-start(bf16[200,800]{1,0:T(8,128)(2,1)} %bitcast.387), channel_id=1, source_target_pairs={{0,16},{16,0},{1,17},{17,1},{2,18},{18,2},{3,19},{19,3},{4,20},{20... | collective-permute-start | bytes 960008 | tf_op jit(solution)/shard_map/ppermute | solution.py:442
  29.8 32.9 %collective-permute-start.7 = (bf16[2,200,512]{2,1,0:T(8,128)(2,1)}, bf16[2,200,512]{2,1,0:T(8,128)(2,1)}, u32[]{:S(2)}, u32[]{:S(2)}) collective-permute-start(bf16[2,200,512]{2,1,0:T(8,128)(2,1)} %get-tuple-element.363), channel_id=1, source_target_pairs={{0,8},{4,12},{8,0},{12,4},{1,9},{5,13},{9,1},{13,5},{2,10},{6,14},... | collective-permute-start | bytes 1228808 | tf_op jit(solution)/shard_map/ppermute | solution.py:403
  78.1 200.3 %all-gather.3.cloned.1.call-start = ((), (), s32[]{:S(2)}) async-start(), calls=%async_computation.2 | async-start | bytes 3584000 | tf_op jit(solution)/shard_map/all_gather | solution.py:520
  121.2 34.5 %collective-permute-start.15 = (bf16[200,400]{1,0:T(8,128)(2,1)S(1)}, bf16[200,400]{1,0:T(8,128)(2,1)S(1)}, u32[]{:S(2)}, u32[]{:S(2)}) collective-permute-start(bf16[200,400]{1,0:T(8,128)(2,1)S(1)} %copy-done.70), channel_id=1, source_target_pairs={{0,8},{4,12},{8,0},{12,4},{1,9},{5,13},{9,1},{13,5},{2,10},{6,14},... | collective-permute-start | bytes 480008 | tf_op jit(solution)/shard_map/ppermute | solution.py:403
  122.9 32.7 %collective-permute-start.16 = (bf16[200,400]{1,0:T(8,128)(2,1)S(1)}, bf16[200,400]{1,0:T(8,128)(2,1)S(1)}, u32[]{:S(2)}, u32[]{:S(2)}) collective-permute-start(bf16[200,400]{1,0:T(8,128)(2,1)S(1)} %copy-done.70), channel_id=1, source_target_pairs={{0,4},{4,8},{8,12},{12,0},{1,5},{5,9},{9,13},{13,1},{2,6},{6,10},{... | collective-permute-start | bytes 480008 | tf_op jit(solution)/shard_map/ppermute | solution.py:403
  126.5 47.8 %collective-permute-start.28 = (bf16[400,128]{1,0:T(8,128)(2,1)}, bf16[400,128]{1,0:T(8,128)(2,1)}, u32[]{:S(2)}, u32[]{:S(2)}) collective-permute-start(bf16[400,128]{1,0:T(8,128)(2,1)} %get-tuple-element.351), channel_id=1, source_target_pairs={{0,12},{4,0},{8,4},{12,8},{1,13},{5,1},{9,5},{13,9},{2,14},{6,2},{... | collective-permute-start | bytes 307208 | tf_op jit(solution)/shard_map/ppermute | solution.py:403
  160.5 31.1 %collective-permute-start.18 = (bf16[200,1600]{1,0:T(8,128)(2,1)}, bf16[200,1600]{1,0:T(8,128)(2,1)}, u32[]{:S(2)}, u32[]{:S(2)}) collective-permute-start(bf16[200,1600]{1,0:T(8,128)(2,1)} %concatenate.90), channel_id=1, source_target_pairs={{0,16},{1,17},{2,18},{3,19},{16,0},{17,1},{18,2},{19,3},{4,20},{5,... | collective-permute-start | bytes 1920008 | tf_op jit(solution)/shard_map/ppermute | solution.py:418
  161.8 38.0 %collective-permute-start.19 = (bf16[200,1600]{1,0:T(8,128)(2,1)}, bf16[200,1600]{1,0:T(8,128)(2,1)}, u32[]{:S(2)}, u32[]{:S(2)}) collective-permute-start(bf16[200,1600]{1,0:T(8,128)(2,1)} %concatenate.90), channel_id=1, source_target_pairs={{0,18},{1,19},{2,16},{3,17},{16,2},{17,3},{18,0},{19,1},{4,22},{5,... | collective-permute-start | bytes 1920008 | tf_op jit(solution)/shard_map/ppermute | solution.py:418
  164.2 371.2 %all-reduce.5.cloned.1.call-start = ((), (), s32[]{:S(2)}) async-start(), calls=%async_computation.4 | async-start | bytes 155648 | tf_op jit(solution)/shard_map/psum | solution.py:717
  222.6 37.1 %collective-permute-start.34 = (bf16[1600,512]{1,0:T(8,128)(2,1)}, bf16[1600,512]{1,0:T(8,128)(2,1)}, u32[]{:S(2)}, u32[]{:S(2)}) collective-permute-start(bf16[1600,512]{1,0:T(8,128)(2,1)} %pad_maximum_fusion.7), channel_id=1, source_target_pairs={{0,1},{1,0},{2,3},{3,2},{16,17},{17,16},{18,19},{19,18},{4,5},{5,4... | collective-permute-start | bytes 4915208 | tf_op jit(solution)/shard_map/ppermute | solution.py:418
  366.4 32.6 %collective-permute-start.54 = (bf16[896,512]{1,0:T(8,128)(2,1)}, bf16[896,512]{1,0:T(8,128)(2,1)}, u32[]{:S(2)}, u32[]{:S(2)}) collective-permute-start(bf16[896,512]{1,0:T(8,128)(2,1)} %add_convert_fusion.2), channel_id=1, source_target_pairs={{2,0},{3,1},{6,4},{7,5},{10,8},{11,9},{14,12},{15,13},{18,16},{19,... | collective-permute-start | bytes 2752520 | tf_op jit(solution)/shard_map/ppermute | solution.py:653
  416.2 312.9 %reduce-scatter.7.cloned.1.call-start = ((), (), s32[]{:S(2)}) async-start(), calls=%async_computation.5 | async-start | bytes 3584000
  421.5 309.0 %reduce-scatter.9.cloned.1.call-start = ((), (), s32[]{:S(2)}) async-start(), calls=%async_computation.6 | async-start | bytes 3584000
  426.6 34.5 %collective-permute-start.39 = (bf16[1600,512]{1,0:T(8,128)(2,1)}, bf16[1600,512]{1,0:T(8,128)(2,1)}, u32[]{:S(2)}, u32[]{:S(2)}) collective-permute-start(bf16[1600,512]{1,0:T(8,128)(2,1)} %convolution_convert_fusion.4), channel_id=1, source_target_pairs={{0,1},{1,0},{2,3},{3,2},{16,17},{17,16},{18,19},{19,18},{4,5},{5,4... | collective-permute-start | bytes 4915208 | tf_op jit(solution)/shard_map/ppermute | solution.py:418
  461.0 119.6 %collective-permute-start.67 = (bf16[800,1600]{1,0:T(8,128)(2,1)}, bf16[800,1600]{1,0:T(8,128)(2,1)}, u32[]{:S(2)}, u32[]{:S(2)}) collective-permute-start(bf16[800,1600]{1,0:T(8,128)(2,1)} %convolution_convert_fusion.3), channel_id=1, source_target_pairs={{0,1},{1,0},{2,3},{3,2},{16,17},{17,16},{18,19},{19,18},{4,5},{5,4... | collective-permute-start | bytes 7680008 | tf_op jit(solution)/shard_map/ppermute | solution.py:418
  468.3 71.0 %collective-permute-start.40 = (bf16[1600,128]{1,0:T(8,128)(2,1)}, bf16[1600,128]{1,0:T(8,128)(2,1)}, u32[]{:S(2)}, u32[]{:S(2)}) collective-permute-start(bf16[1600,128]{1,0:T(8,128)(2,1)} %get-tuple-element.268), channel_id=1, source_target_pairs={{0,2},{1,3},{2,0},{3,1},{16,18},{17,19},{18,16},{19,17},{4,6},{5,7... | collective-permute-start | bytes 1228808 | tf_op jit(solution)/shard_map/ppermute | solution.py:418
  468.3 71.0 %collective-permute-start.41 = (bf16[1600,128]{1,0:T(8,128)(2,1)}, bf16[1600,128]{1,0:T(8,128)(2,1)}, u32[]{:S(2)}, u32[]{:S(2)}) collective-permute-start(bf16[1600,128]{1,0:T(8,128)(2,1)} %get-tuple-element.270), channel_id=1, source_target_pairs={{0,16},{1,17},{2,18},{3,19},{16,0},{17,1},{18,2},{19,3},{4,20},{5,... | collective-permute-start | bytes 1228808 | tf_op jit(solution)/shard_map/ppermute | solution.py:418
  469.1 70.2 %collective-permute-start.42 = (bf16[1600,128]{1,0:T(8,128)(2,1)}, bf16[1600,128]{1,0:T(8,128)(2,1)}, u32[]{:S(2)}, u32[]{:S(2)}) collective-permute-start(bf16[1600,128]{1,0:T(8,128)(2,1)} %get-tuple-element.269), channel_id=1, source_target_pairs={{0,18},{1,19},{2,16},{3,17},{16,2},{17,3},{18,0},{19,1},{4,22},{5,... | collective-permute-start | bytes 1228808 | tf_op jit(solution)/shard_map/ppermute | solution.py:418
  485.2 170.5 %collective-permute-start.60 = (bf16[4,800,384]{2,1,0:T(8,128)(2,1)}, bf16[4,800,384]{2,1,0:T(8,128)(2,1)}, u32[]{:S(2)}, u32[]{:S(2)}) collective-permute-start(bf16[4,800,384]{2,1,0:T(8,128)(2,1)} %bitcast.134), channel_id=1, source_target_pairs={{0,1},{1,0},{2,3},{3,2},{16,17},{17,16},{18,19},{19,18},{4,5},{5,4... | collective-permute-start | bytes 7372808 | tf_op jit(solution)/shard_map/ppermute | solution.py:418
  546.7 33.8 %collective-permute-start.44 = (bf16[400,128]{1,0:T(8,128)(2,1)S(1)}, bf16[400,128]{1,0:T(8,128)(2,1)S(1)}, u32[]{:S(2)}, u32[]{:S(2)}) collective-permute-start(bf16[400,128]{1,0:T(8,128)(2,1)S(1)} %get-tuple-element.340), channel_id=1, source_target_pairs={{0,8},{4,12},{8,0},{12,4},{1,9},{5,13},{9,1},{13,5},{2,10},{6,14},... | collective-permute-start | bytes 307208 | tf_op jit(solution)/shard_map/ppermute | solution.py:403
  547.3 33.3 %collective-permute-start.45 = (bf16[400,128]{1,0:T(8,128)(2,1)S(1)}, bf16[400,128]{1,0:T(8,128)(2,1)S(1)}, u32[]{:S(2)}, u32[]{:S(2)}) collective-permute-start(bf16[400,128]{1,0:T(8,128)(2,1)S(1)} %get-tuple-element.339), channel_id=1, source_target_pairs={{0,4},{4,8},{8,12},{12,0},{1,5},{5,9},{9,13},{13,1},{2,6},{6,10},{... | collective-permute-start | bytes 307208 | tf_op jit(solution)/shard_map/ppermute | solution.py:403
  552.1 32.8 %collective-permute-start.55 = (bf16[2,200,512]{2,1,0:T(8,128)(2,1)}, bf16[2,200,512]{2,1,0:T(8,128)(2,1)S(1)}, u32[]{:S(2)}, u32[]{:S(2)}) collective-permute-start(bf16[2,200,512]{2,1,0:T(8,128)(2,1)} %get-tuple-element.265), channel_id=1, source_target_pairs={{0,4},{4,8},{8,12},{12,0},{1,5},{5,9},{9,13},{13,1},{2,6},{6,10},{... | collective-permute-start | bytes 1228808 | tf_op jit(solution)/shard_map/ppermute | solution.py:403
  580.5 32.6 %collective-permute-start.56 = (bf16[2,200,512]{2,1,0:T(8,128)(2,1)}, bf16[2,200,512]{2,1,0:T(8,128)(2,1)S(1)}, u32[]{:S(2)}, u32[]{:S(2)}) collective-permute-start(bf16[2,200,512]{2,1,0:T(8,128)(2,1)} %get-tuple-element.267), channel_id=1, source_target_pairs={{0,8},{4,12},{8,0},{12,4},{1,9},{5,13},{9,1},{13,5},{2,10},{6,14},... | collective-permute-start | bytes 1228808 | tf_op jit(solution)/shard_map/ppermute | solution.py:403
  580.5 35.7 %collective-permute-start.57 = (bf16[2,200,512]{2,1,0:T(8,128)(2,1)}, bf16[2,200,512]{2,1,0:T(8,128)(2,1)S(1)}, u32[]{:S(2)}, u32[]{:S(2)}) collective-permute-start(bf16[2,200,512]{2,1,0:T(8,128)(2,1)} %get-tuple-element.266), channel_id=1, source_target_pairs={{0,12},{4,0},{8,4},{12,8},{1,13},{5,1},{9,5},{13,9},{2,14},{6,2},{... | collective-permute-start | bytes 1228808 | tf_op jit(solution)/shard_map/ppermute | solution.py:403
  583.3 35.4 %collective-permute-start.68 = (bf16[200,1600]{1,0:T(8,128)(2,1)S(1)}, bf16[200,1600]{1,0:T(8,128)(2,1)S(1)}, u32[]{:S(2)}, u32[]{:S(2)}) collective-permute-start(bf16[200,1600]{1,0:T(8,128)(2,1)S(1)} %get-tuple-element.255), channel_id=1, source_target_pairs={{0,2},{1,3},{2,0},{3,1},{16,18},{17,19},{18,16},{19,17},{4,6},{5,7... | collective-permute-start | bytes 1920008 | tf_op jit(solution)/shard_map/ppermute | solution.py:418
  584.9 33.8 %collective-permute-start.69 = (bf16[200,1600]{1,0:T(8,128)(2,1)S(1)}, bf16[200,1600]{1,0:T(8,128)(2,1)S(1)}, u32[]{:S(2)}, u32[]{:S(2)}) collective-permute-start(bf16[200,1600]{1,0:T(8,128)(2,1)S(1)} %get-tuple-element.257), channel_id=1, source_target_pairs={{0,16},{1,17},{2,18},{3,19},{16,0},{17,1},{18,2},{19,3},{4,20},{5,... | collective-permute-start | bytes 1920008 | tf_op jit(solution)/shard_map/ppermute | solution.py:418
  630.9 37.8 %collective-permute-start.71 = (bf16[200,400]{1,0:T(8,128)(2,1)S(1)}, bf16[200,400]{1,0:T(8,128)(2,1)S(1)}, u32[]{:S(2)}, u32[]{:S(2)}) collective-permute-start(bf16[200,400]{1,0:T(8,128)(2,1)S(1)} %bitcast.435), channel_id=1, source_target_pairs={{0,4},{4,8},{8,12},{12,0},{1,5},{5,9},{9,13},{13,1},{2,6},{6,10},{... | collective-permute-start | bytes 480008 | tf_op jit(solution)/shard_map/ppermute | solution.py:403
  658.3 33.3 %collective-permute-start.61 = (bf16[1,800,384]{2,1,0:T(8,128)(2,1)S(1)}, bf16[1,800,384]{2,1,0:T(8,128)(2,1)S(1)}, u32[]{:S(2)}, u32[]{:S(2)}) collective-permute-start(bf16[1,800,384]{2,1,0:T(8,128)(2,1)S(1)} %get-tuple-element.261), channel_id=1, source_target_pairs={{0,2},{1,3},{2,0},{3,1},{16,18},{17,19},{18,16},{19,17},{4,6},{5,7... | collective-permute-start | bytes 1843208 | tf_op jit(solution)/shard_map/ppermute | solution.py:418
  659.8 31.9 %collective-permute-start.62 = (bf16[1,800,384]{2,1,0:T(8,128)(2,1)S(1)}, bf16[1,800,384]{2,1,0:T(8,128)(2,1)S(1)}, u32[]{:S(2)}, u32[]{:S(2)}) collective-permute-start(bf16[1,800,384]{2,1,0:T(8,128)(2,1)S(1)} %get-tuple-element.263), channel_id=1, source_target_pairs={{0,16},{1,17},{2,18},{3,19},{16,0},{17,1},{18,2},{19,3},{4,20},{5,... | collective-permute-start | bytes 1843208 | tf_op jit(solution)/shard_map/ppermute | solution.py:418
  660.0 31.7 %collective-permute-start.63 = (bf16[1,800,384]{2,1,0:T(8,128)(2,1)S(1)}, bf16[1,800,384]{2,1,0:T(8,128)(2,1)S(1)}, u32[]{:S(2)}, u32[]{:S(2)}) collective-permute-start(bf16[1,800,384]{2,1,0:T(8,128)(2,1)S(1)} %get-tuple-element.262), channel_id=1, source_target_pairs={{0,18},{1,19},{2,16},{3,17},{16,2},{17,3},{18,0},{19,1},{4,22},{5,... | collective-permute-start | bytes 1843208 | tf_op jit(solution)/shard_map/ppermute | solution.py:418
  (167 other events, 2306.0 us)
Sparse Core Ops, SparseCore 0:
  78.2 76.3 all-gather.4
  164.3 70.6 all-gather.2
  416.3 119.1 all-reduce.4
  538.2 88.4 reduce-scatter.6
  628.9 83.9 reduce-scatter.8

commit v3 on v2

--- a/solution.py
+++ b/solution.py
@@ -29,19 +29,58 @@
 BF16 = jnp.bfloat16
 
 
+def cost(micros):
+    return pl.CostEstimate(
+        flops=int(micros * 1.15e9), bytes_accessed=int(micros * 3.6e6), transcendentals=0
+    )
+
+
+def after(values, event):
+    return lax.optimization_barrier((values, event))[0]
+
+
 def mm(spec, left, right):
     return jnp.einsum(spec, left, right, preferred_element_type=F32)
 
 
-def adam_step(weight, gradient, moments, rate):
-    first_moment = BETA_ONE * moments[0] + (1.0 - BETA_ONE) * gradient
-    second = BETA_TWO * moments[1] + (1.0 - BETA_TWO) * gradient * gradient
+def adam_terms(weight, gradient, first, second, rate):
+    first_moment = BETA_ONE * first + (1.0 - BETA_ONE) * gradient
+    second = BETA_TWO * second + (1.0 - BETA_TWO) * gradient * gradient
     first_fix = 1.0 - BETA_ONE**STEP
     second_fix = 1.0 - BETA_TWO**STEP
     stepped = weight - rate * (
         first_moment / first_fix / (jnp.sqrt(second / second_fix) + EPS_ADAM) + DECAY * weight
     )
-    return (stepped, jnp.stack([first_moment, second]))
+    return stepped, first_moment, second
+
+
+def adam_step(weight, gradient, moments, rate):
+    stepped, first, second = adam_terms(weight, gradient, moments[0], moments[1], rate)
+    return (stepped, jnp.stack([first, second]))
+
+
+def adam_matrix(weight, gradient, moments):
+    n, m = weight.shape
+    step = next(size for size in (160, 80, 40, n) if n % size == 0 and size * m <= 160 * 512)
+
+    def body(w_ref, g_ref, m_ref, new_ref, state_ref):
+        new, first, second = adam_terms(w_ref[...], g_ref[...], m_ref[0], m_ref[1], LR_MATRIX)
+        new_ref[...] = new
+        state_ref[0] = first
+        state_ref[1] = second
+
+    block = pl.BlockSpec((step, m), lambda i: (i, 0))
+    pair = pl.BlockSpec((2, step, m), lambda i: (0, i, 0))
+    return pl.pallas_call(
+        body,
+        grid=(n // step,),
+        in_specs=[block, block, pair],
+        out_specs=[block, pair],
+        out_shape=[jax.ShapeDtypeStruct((n, m), F32), jax.ShapeDtypeStruct((2, n, m), F32)],
+        compiler_params=pltpu.CompilerParams(vmem_limit_bytes=32 * 2**20),
+        cost_estimate=cost(3),
+        name="adam_matrix",
+    )(weight, gradient, moments)
 
 
 def head_tables(rows, cols):
@@ -99,6 +138,7 @@
         + [pl.BlockSpec(memory_space=pltpu.VMEM)] * (len(sources) + len(extra)),
         out_specs=pl.BlockSpec(memory_space=pltpu.VMEM),
         compiler_params=pltpu.CompilerParams(vmem_limit_bytes=32 * 2**20),
+        cost_estimate=cost(3),
         name="move_units",
     )(table, *sources, *extra)
 
@@ -123,6 +163,7 @@
         out_specs=pl.BlockSpec((packed, tokens), lambda i: (i, 0)),
         out_shape=jax.ShapeDtypeStruct((blocks * packed, tokens), F32),
         compiler_params=pltpu.CompilerParams(vmem_limit_bytes=40 * 2**20),
+        cost_estimate=cost(4),
         name="qkv_product",
     )(weight, rows_in)
 
@@ -143,6 +184,7 @@
         out_specs=pl.BlockSpec((1, 1, rows, packed), lambda d, i: (d, i, 0, 0)),
         out_shape=jax.ShapeDtypeStruct((dps, blocks, rows, packed), BF16),
         compiler_params=pltpu.CompilerParams(vmem_limit_bytes=40 * 2**20),
+        cost_estimate=cost(4),
         name="qkv_weight_part",
     )(rows_in, grads)
 
@@ -211,6 +253,7 @@
             jax.ShapeDtypeStruct((2, tokens), F32),
         ],
         compiler_params=pltpu.CompilerParams(vmem_limit_bytes=48 * 2**20),
+        cost_estimate=cost(7),
         name="qkv_back",
     )(*halves, grads, inputs, mean, inverse, gain)
 
@@ -236,14 +279,21 @@
     return mask
 
 
-def attention_forward(me, start, query, key_values, offsets):
+def attention_forward(me, start, query, key_values, offsets, carried=None):
     rows, tokens = query.shape
     slots = rows // HEAD_DIM
     factor = 1.0 / math.sqrt(HEAD_DIM)
     n = len(offsets)
+    fresh = carried is None
 
     def body(me_ref, start_ref, q_ref, *refs):
-        kv, (o_ref, lse_ref), (top, total, acc) = refs[: 2 * n], refs[2 * n : 2 * n + 2], refs[2 * n + 2 :]
+        kv, refs = refs[: 2 * n], refs[2 * n :]
+        top, total, acc = refs[-3:]
+        if not fresh:
+            top[...] = refs[0][0]
+            total[...] = refs[1][0]
+            acc[...] = refs[2][...]
+            refs = refs[3:]
         my = me_ref[0]
         start_row = start_ref[...]
         q = q_ref[...] * jnp.asarray(factor, BF16)
@@ -251,7 +301,8 @@
             block = my ^ off
             k_ref, v_ref = kv[2 * i], kv[2 * i + 1]
 
-            def run(first=(i == 0), off=off, block=block, k_ref=k_ref, v_ref=v_ref):
+            def run(off=off, block=block, k_ref=k_ref, v_ref=v_ref):
+                first = off == 0
                 s = dot_tn(k_ref[...], q)
                 mask = key_mask(block, my, start_row, tokens, tokens, off == 0)
                 s = jnp.where(mask, s, NEG_FILL)
@@ -274,51 +325,69 @@
                 run()
             else:
                 pl.when(block < my)(run)
-        o_ref[...] = (acc[...] / total[...]).astype(BF16)
-        lse_ref[0] = top[...] + jnp.log(total[...])
+        if fresh:
+            refs[0][0] = top[...]
+            refs[1][0] = total[...]
+            refs[2][...] = acc[...]
+        else:
+            refs[0][...] = (acc[...] / total[...]).astype(BF16)
+            refs[1][0] = top[...] + jnp.log(total[...])
 
     piece = (HEAD_DIM, tokens)
+    head_spec = pl.BlockSpec(piece, lambda j: (j, 0))
+    row_spec = pl.BlockSpec((1, 1, tokens), lambda j: (j, 0, 0))
     specs = [
         pl.BlockSpec(memory_space=pltpu.SMEM),
         pl.BlockSpec((1, tokens), lambda j: (0, 0)),
-        pl.BlockSpec(piece, lambda j: (j, 0)),
+        head_spec,
     ]
     args = [me, start, query]
     for array in key_values:
-        specs += [pl.BlockSpec(piece, lambda j: (j, 0)), pl.BlockSpec(piece, lambda j: (slots + j, 0))]
+        specs += [head_spec, pl.BlockSpec(piece, lambda j: (slots + j, 0))]
         args += [array, array]
+    row_shape = jax.ShapeDtypeStruct((slots, 1, tokens), F32)
+    if fresh:
+        out_specs = [row_spec, row_spec, head_spec]
+        out_shape = [row_shape, row_shape, jax.ShapeDtypeStruct((rows, tokens), F32)]
+    else:
+        specs += [row_spec, row_spec, head_spec]
+        args += list(carried)
+        out_specs = [head_spec, row_spec]
+        out_shape = [jax.ShapeDtypeStruct((rows, tokens), BF16), row_shape]
     return pl.pallas_call(
         body,
         grid=(slots,),
         in_specs=specs,
-        out_specs=[
-            pl.BlockSpec(piece, lambda j: (j, 0)),
-            pl.BlockSpec((1, 1, tokens), lambda j: (j, 0, 0)),
-        ],
-        out_shape=[
-            jax.ShapeDtypeStruct((rows, tokens), BF16),
-            jax.ShapeDtypeStruct((slots, 1, tokens), F32),
-        ],
+        out_specs=out_specs,
+        out_shape=out_shape,
         scratch_shapes=[
             pltpu.VMEM((1, tokens), F32),
             pltpu.VMEM((1, tokens), F32),
             pltpu.VMEM((HEAD_DIM, tokens), F32),
         ],
         compiler_params=pltpu.CompilerParams(vmem_limit_bytes=32 * 2**20),
+        cost_estimate=cost(11),
         name="attention_forward",
     )(*args)
 
 
-def attention_backward(me, start, query, key_values, offsets, out_rows, lse, grad_rows):
+def attention_backward(me, start, query, key_values, offsets, out_rows, lse, grad_rows, carried=None):
     rows, tokens = query.shape
     slots = rows // HEAD_DIM
     factor = 1.0 / math.sqrt(HEAD_DIM)
     n = len(offsets)
+    fresh = carried is None
 
     def body(me_ref, start_ref, q_ref, o_ref, lse_ref, g_ref, *refs):
-        kv, outs, (acc,) = refs[: 2 * n], refs[2 * n : -1], refs[-1:]
-        dq_ref, dq_sum, dv_sum = outs[:3]
-        grads = outs[3:]
+        kv, refs = refs[: 2 * n], refs[2 * n :]
+        acc, value_acc = refs[-2:]
+        if fresh:
+            acc[...] = jnp.zeros_like(acc)
+        else:
+            acc[...] = refs[0][...]
+            refs = refs[1:]
+        grads, (dv_sum, dq_ref), rest = refs[: 2 * n], refs[2 * n : 2 * n + 2], refs[2 * n + 2 : -2]
+        value_acc[...] = jnp.zeros_like(value_acc)
         my = me_ref[0]
         start_row = start_ref[...]
         q = q_ref[...] * jnp.asarray(factor, BF16)
@@ -330,7 +399,7 @@
             k_ref, v_ref = kv[2 * i], kv[2 * i + 1]
             dk_ref, dv_ref = grads[2 * i], grads[2 * i + 1]
 
-            def run(first=(i == 0), off=off, block=block, k_ref=k_ref, v_ref=v_ref, dk_ref=dk_ref, dv_ref=dv_ref):
+            def run(off=off, block=block, k_ref=k_ref, v_ref=v_ref, dk_ref=dk_ref, dv_ref=dv_ref):
                 k = k_ref[...]
                 s = dot_tn(k, q)
                 mask = key_mask(block, my, start_row, tokens, tokens, off == 0)
@@ -340,14 +409,8 @@
                 dv = dot_nt(g, p.astype(BF16))
                 dv_ref[...] = dv.astype(BF16)
                 dk_ref[...] = dot_nt(q, ds).astype(BF16)
-                dq = dot_nn(k, ds)
-                value_total = jnp.sum(dv, axis=1, keepdims=True)
-                if first:
-                    acc[...] = dq
-                    dv_sum[...] = value_total
-                else:
-                    acc[...] += dq
-                    dv_sum[...] += value_total
+                acc[...] += dot_nn(k, ds)
+                value_acc[...] += jnp.sum(dv, axis=1, keepdims=True)
 
             def skip(dk_ref=dk_ref, dv_ref=dv_ref):
                 dk_ref[...] = jnp.zeros_like(dk_ref)
@@ -358,9 +421,13 @@
             else:
                 pl.when(block < my)(run)
                 pl.when(block >= my)(skip)
-        dq = acc[...] * factor
-        dq_ref[...] = dq.astype(BF16)
-        dq_sum[...] = jnp.sum(dq, axis=1, keepdims=True)
+        dv_sum[...] = value_acc[...]
+        if fresh:
+            dq_ref[...] = acc[...]
+        else:
+            dq = acc[...] * factor
+            dq_ref[...] = dq.astype(BF16)
+            rest[0][...] = jnp.sum(dq, axis=1, keepdims=True)
 
     piece = (HEAD_DIM, tokens)
     head_spec = pl.BlockSpec(piece, lambda j: (j, 0))
@@ -379,14 +446,21 @@
         args += [array, array]
     full = jax.ShapeDtypeStruct((rows, tokens), BF16)
     thin = jax.ShapeDtypeStruct((rows, 1), F32)
+    if fresh:
+        out_specs, out_shape = [column, head_spec], [thin, jax.ShapeDtypeStruct((rows, tokens), F32)]
+    else:
+        specs += [head_spec]
+        args += [carried]
+        out_specs, out_shape = [column, head_spec, column], [thin, full, thin]
     return pl.pallas_call(
         body,
         grid=(slots,),
         in_specs=specs,
-        out_specs=[head_spec, column, column] + [head_spec] * (2 * n),
-        out_shape=[full, thin, thin] + [full] * (2 * n),
-        scratch_shapes=[pltpu.VMEM(piece, F32)],
+        out_specs=[head_spec] * (2 * n) + out_specs,
+        out_shape=[full] * (2 * n) + out_shape,
+        scratch_shapes=[pltpu.VMEM(piece, F32), pltpu.VMEM((HEAD_DIM, 1), F32)],
         compiler_params=pltpu.CompilerParams(vmem_limit_bytes=32 * 2**20),
+        cost_estimate=cost(14),
         name="attention_backward",
     )(*args)
 
@@ -421,26 +495,36 @@
             [(y * cols + c, (y ^ d) * cols + (c ^ b)) for y in range(dps) for c in range(cols)],
         )
 
-    def plane_direct(values, axis):
-        return jnp.concatenate([values] + [to_plane(values, d, b) for d, b in even[1:]], axis=axis)
-
-    def plane_gather(values, axis):
-        first = plane_direct(values, axis)
-        return jnp.concatenate([first, to_plane(first, 0, 1)], axis=axis)
-
-    def plane_reduce(near, far, axis):
-        sums = near.astype(F32) + to_plane(far, 0, 1).astype(F32)
+    def plane_send(values):
+        return [values] + [to_plane(values, d, b) for d, b in even[1:]]
+
+    def core_send(far):
+        return to_plane(far, 0, 1)
+
+    def plane_scatter(near, far_received, axis):
+        sums = near.astype(F32) + far_received.astype(F32)
         size = sums.shape[axis] // len(even)
         parts = [lax.slice_in_dim(sums, i * size, (i + 1) * size, axis=axis) for i in range(len(even))]
-        total = parts[0]
-        for (d, b), item in list(zip(even, parts))[1:]:
-            total = total + to_plane(item.astype(BF16), d, b).astype(F32)
+        return [parts[0]] + [to_plane(item.astype(BF16), d, b) for (d, b), item in list(zip(even, parts))[1:]]
+
+    def total_of(terms):
+        total = terms[0].astype(F32)
+        for item in terms[1:]:
+            total = total + item.astype(F32)
         return total
 
     def dp_exchange(chunks):
         return [chunks[0]] + [
             lax.ppermute(chunks[d], "dp", [(y, y ^ d) for y in range(dps)]) for d in range(1, dps)
         ]
+
+    def sum_everywhere(values):
+        for axis, size in (("row", rows), ("dp", dps), ("col", cols)):
+            step = 1
+            while step < size:
+                values = values + lax.ppermute(values, axis, [(i, i ^ step) for i in range(size)])
+                step *= 2
+        return values
 
     def sum_rows(values):
         step = 1
@@ -486,10 +570,10 @@
             stacked = jnp.stack(pieces)
             return jnp.concatenate([at(stacked, (t - z) % rows) for t in range(rows)], axis=axis)
 
-        def token_chunks(array):
+        def chunks_of(array, axis):
+            size = array.shape[axis] // rows
             return [
-                lax.dynamic_slice_in_dim(array, ((z + k) % rows) * few, few, array.ndim - 1)
-                for k in range(rows)
+                lax.dynamic_slice_in_dim(array, ((z + k) % rows) * size, size, axis) for k in range(rows)
             ]
 
         vec_swap = swapped(rolled(vectors.reshape(8, rows, feats), 1).reshape(8, rows, dps, half), 2)
@@ -502,7 +586,6 @@
         ).astype(BF16)
         sorted_cols = mm("fn,nm->fm", qkv_weight.astype(BF16), select).astype(BF16)
         arrived = row_exchange([sorted_cols[:, k * packed : (k + 1) * packed] for k in range(rows)])
-        qkv_first = plane_direct(jnp.stack(arrived).reshape(1, rows * half, packed), 0)
 
         x_own = swapped(hidden_in.T.reshape(dps, half, tokens), 0)
         x_all = jnp.stack(row_gather(x_own), axis=1).reshape(dps, rows * half, tokens)
@@ -510,14 +593,15 @@
         up_arrived = dp_exchange([at(up_parts, y ^ d) for d in range(dps)])
         up_rows = swapped(jnp.stack(up_arrived), 0).reshape(feats, hidden)
         down_rows = down_weight.astype(BF16).T
-        proj_own = proj_weight.astype(BF16)
-        qkv_first, x_all, up_rows, down_rows, proj_own = lax.optimization_barrier(
-            (qkv_first, x_all, up_rows, down_rows, proj_own)
-        )
-        qkv_second = to_plane(qkv_first, 0, 1)
+        up_rows, down_rows, arrived = lax.optimization_barrier((up_rows, down_rows, arrived))
+        qkv_first = jnp.concatenate(plane_send(jnp.stack(arrived).reshape(1, rows * half, packed)), axis=0)
+        qkv_first, x_all = lax.optimization_barrier((qkv_first, x_all))
+        qkv_second = core_send(qkv_first)
         halves = [item.reshape(dps, cols // 2, rows * half, packed) for item in (qkv_first, qkv_second)]
         w_up = lax.all_gather(up_rows, "row", axis=0, tiled=True)
         w_down = lax.all_gather(down_rows, "row", axis=0, tiled=True)
+        proj_pieces = row_gather(after(proj_weight.astype(BF16), x_all))
+        top_pieces = row_exchange(chunks_of(after(upstream, x_all), 0))
 
         x_f = x_all.astype(F32).reshape(D, tokens)
         mean_one = jnp.mean(x_f, axis=0, keepdims=True)
@@ -546,69 +630,83 @@
         query = qkv_rows[:wide]
         own_kv = qkv_rows[wide:]
 
-        held = [own_kv]
-        for b in offsets[1 : cols // 2]:
-            held.append(lax.ppermute(own_kv, "col", [(i, i ^ b) for i in range(cols) if (i ^ b) > i]))
-        key_values = held + [
-            lax.ppermute(item, "col", [(i, i ^ 1) for i in range(cols)]) for item in held
+        swap_cores = [(i, i ^ 1) for i in range(cols)]
+        far_near = [
+            lax.ppermute(own_kv, "col", [(i, i ^ b) for i in range(cols) if (i ^ b) > i])
+            for b in range(2, cols, 2)
         ]
-        key_values, upstream_late, proj_own = lax.optimization_barrier((key_values, upstream, proj_own))
-        w_proj = plane_gather(unrolled(row_gather(proj_own), 1), 0)
-        top_few = unrolled(row_exchange(token_chunks(upstream_late.T)), 0)
-        top_all = plane_gather(top_few, 1)
+        near_kv = [own_kv, lax.ppermute(own_kv, "col", swap_cores)]
+        near_offsets = [0, 1]
+        far_offsets = list(range(2, cols, 2)) + list(range(3, cols, 2))
         me = c.astype(jnp.int32).reshape(1)
         query_ids = lax.dynamic_slice_in_dim(segment_ids, c * tokens, tokens)
         start = jnp.sum((segment_ids[:, None] < query_ids[None, :]).astype(jnp.int32), axis=0)[None, :]
-        attn, lse = attention_forward(me, start, query, key_values, offsets)
-
+        carried = attention_forward(me, start, query, near_kv, near_offsets)
+        carried, far_near, proj_pieces, top_pieces = lax.optimization_barrier(
+            (carried, far_near, proj_pieces, top_pieces)
+        )
+        far_kv = far_near + [lax.ppermute(item, "col", swap_cores) for item in far_near]
+        proj_sent = plane_send(unrolled(proj_pieces, 1))
+        top_few = unrolled(top_pieces, 1)
+        attn, lse = attention_forward(me, start, query, far_kv, far_offsets, carried)
+        attn, proj_sent = lax.optimization_barrier((attn, proj_sent))
+        proj_first = jnp.concatenate(proj_sent, axis=0)
+        w_proj = jnp.concatenate([proj_first, core_send(proj_first)], axis=0)
+        top_sent = plane_send(after(top_few, proj_first))
 
         n_rows = D // cols // dps
-        attn_pieces = row_exchange(token_chunks(attn))
+        attn_pieces = row_exchange(chunks_of(attn, 1))
         attn_abs = unrolled([item.reshape(slots, 1, HEAD_DIM, few) for item in attn_pieces], 1)
         attn_abs = attn_abs.reshape(rows * wide, few)[:D]
         blocks = attn_abs.reshape(cols, dps, n_rows, few)
         attn_few = jnp.concatenate([at(at(blocks, c ^ b), y ^ d) for d, b in plane], axis=0)
         x_few = lax.dynamic_slice_in_dim(x_all, z * few, few, 2).reshape(dps, rows, half, few)
         x_few = swapped(x_few, 0).transpose(1, 0, 2, 3).reshape(rows, feats, few)
-        x_few = unrolled([x_few[k] for k in range(rows)], 0).astype(F32)
-        mid = x_few + mm("rf,rt->ft", w_proj, attn_few) + vectors[4][:, None]
-        mean_two = jnp.mean(mid, axis=0, keepdims=True)
-        spread_two = jnp.mean(mid * mid, axis=0, keepdims=True) - mean_two * mean_two
+        x_few = unrolled([x_few[k] for k in range(rows)], 0).T.astype(F32)
+        mid = x_few + mm("rt,rf->tf", attn_few, w_proj) + vectors[4]
+        mean_two = jnp.mean(mid, axis=1, keepdims=True)
+        spread_two = jnp.mean(mid * mid, axis=1, keepdims=True) - mean_two * mean_two
         inverse_two = lax.rsqrt(spread_two + EPS_NORM)
         normed_two = (mid - mean_two) * inverse_two
-        h2 = (normed_two * vectors[5][:, None] + vectors[6][:, None]).astype(BF16)
-        h2_all = plane_gather(h2, 1)
+        h2 = (normed_two * vectors[5] + vectors[6]).astype(BF16)
+        h2, top_sent = lax.optimization_barrier((h2, top_sent))
+        top_first = jnp.concatenate(top_sent, axis=0)
+        top_second = core_send(top_first)
+        h2_first = jnp.concatenate(plane_send(h2), axis=0)
+        h2_second = core_send(h2_first)
 
         up_shift = lax.dynamic_slice_in_dim(up_bias, (c * dps + y) * hidden, hidden)
-        pre = mm("fh,ft->ht", w_up, h2_all) + up_shift[:, None]
-        inside = GELU_COEF * (pre + GELU_CUBE * pre * pre * pre)
-        tanh_val = jnp.tanh(inside)
-        act = (0.5 * pre * (1.0 + tanh_val)).astype(BF16)
-        slope = 0.5 * (1.0 + tanh_val) + 0.5 * pre * (1.0 - tanh_val * tanh_val) * GELU_COEF * (
-            1.0 + 3.0 * GELU_CUBE * pre * pre
-        )
-        grad_pre = mm("fh,ft->ht", w_down, top_all) * slope
-        grad_pre_half = grad_pre.astype(BF16)
-        bias_part = jnp.sum(grad_pre, axis=1)
-
-        middle = len(even) * few
-
-        def features_back(weight, values):
-            far = mm("fh,ht->ft", weight, values[:, middle:]).astype(BF16)
-            near = mm("fh,ht->ft", weight, values[:, :middle]).astype(BF16)
-            return plane_reduce(near, far, 1), (near, far)
-
-        def row_chunks(array):
-            return [lax.dynamic_slice_in_dim(array, ((z + k) % rows) * feats, feats, 0) for k in range(rows)]
-
-        grad_ln_two, partial = features_back(w_up, grad_pre_half)
-
-        scaled = grad_ln_two * vectors[5][:, None]
-        first_mean = jnp.mean(scaled, axis=0, keepdims=True)
-        second_mean = jnp.mean(scaled * normed_two, axis=0, keepdims=True)
+
+        def hidden_part(h2_rows, top_rows):
+            pre = mm("tf,fh->th", h2_rows, w_up) + up_shift
+            inside = GELU_COEF * (pre + GELU_CUBE * pre * pre * pre)
+            tanh_val = jnp.tanh(inside)
+            act = (0.5 * pre * (1.0 + tanh_val)).astype(BF16)
+            slope = 0.5 * (1.0 + tanh_val) + 0.5 * pre * (1.0 - tanh_val * tanh_val) * GELU_COEF * (
+                1.0 + 3.0 * GELU_CUBE * pre * pre
+            )
+            grad_pre = mm("tf,fh->th", top_rows, w_down) * slope
+            return act, grad_pre.astype(BF16), jnp.sum(grad_pre, axis=0)
+
+        act_near, pre_near, bias_near = hidden_part(h2_first, top_first)
+        act_far, pre_far, bias_far = hidden_part(h2_second, top_second)
+        bias_part = bias_near + bias_far
+        back_far = mm("th,fh->tf", pre_far, w_up).astype(BF16)
+        back_near = mm("th,fh->tf", pre_near, w_up).astype(BF16)
+        grad_ln_two = total_of(plane_scatter(back_near, core_send(back_far), 0))
+
+        act_near, act_far, pre_near, pre_far, _ = lax.optimization_barrier(
+            (act_near, act_far, pre_near, pre_far, back_near)
+        )
+        up_part = (mm("tf,th->fh", h2_first, pre_near) + mm("tf,th->fh", h2_second, pre_far)).astype(BF16)
+        down_part = (mm("tf,th->fh", top_first, act_near) + mm("tf,th->fh", top_second, act_far)).astype(BF16)
+
+        scaled = grad_ln_two * vectors[5]
+        first_mean = jnp.mean(scaled, axis=1, keepdims=True)
+        second_mean = jnp.mean(scaled * normed_two, axis=1, keepdims=True)
         grad_mid = top_few.astype(F32) + inverse_two * (scaled - first_mean - normed_two * second_mean)
         grad_mid_half = grad_mid.astype(BF16)
-        grad_attn = mm("rf,ft->rt", w_proj, grad_mid_half).astype(BF16)
+        grad_attn = mm("rf,tf->rt", w_proj, grad_mid_half).astype(BF16)
         natural = grad_attn.reshape(2, dps, cols // 2, n_rows, few).transpose(2, 0, 1, 3, 4)
         natural = swapped(natural.reshape(cols, dps, n_rows, few), 1)
         grad_abs = jnp.stack([at(natural, c ^ b) for b in range(cols)]).reshape(D, few)
@@ -617,46 +715,57 @@
             row_exchange([at(grad_abs, (z + k) % rows, 1).reshape(wide, few) for k in range(rows)]), 1
         )
 
-        act_late, pre_late, _ = lax.optimization_barrier((act, grad_pre_half, partial))
-        down_part = mm("ft,ht->fh", top_all, act_late).astype(BF16)
-        up_part = mm("ft,ht->fh", h2_all, pre_late).astype(BF16)
-        act_late, _ = lax.optimization_barrier((act, grad_ln_two))
-        down_sum, _ = features_back(w_down, act_late)
-        out_few = (mid + down_sum + vectors[7][:, None]).astype(BF16)
-        block_out = unrolled(row_exchange(row_chunks(out_few)), 1).T
-
+        act_near, act_far = after((act_near, act_far), up_part)
+        down_far = mm("th,fh->tf", act_far, w_down).astype(BF16)
+        down_near = mm("th,fh->tf", act_near, w_down).astype(BF16)
+        down_received = core_send(down_far)
+        down_terms = plane_scatter(after(down_near, grad_ln_two), down_received, 0)
         middle_rows = len(even) * n_rows
-        proj_far = mm("rt,ft->rf", attn_few[middle_rows:], grad_mid_half).astype(BF16)
-        proj_near = mm("rt,ft->rf", attn_few[:middle_rows], grad_mid_half).astype(BF16)
-        grad_heads, proj_far, proj_near, down_part, up_part = lax.optimization_barrier(
-            (grad_heads, proj_far, proj_near, down_part, up_part)
-        )
+        proj_far = mm("rt,tf->rf", attn_few[middle_rows:], grad_mid_half).astype(BF16)
+        proj_near = mm("rt,tf->rf", attn_few[:middle_rows], grad_mid_half).astype(BF16)
+        proj_received = core_send(proj_far)
+        grad_heads, proj_received, proj_near, down_part, up_part, down_terms = lax.optimization_barrier(
+            (grad_heads, proj_received, proj_near, down_part, up_part, down_terms)
+        )
+        up_sum = lax.psum_scatter(up_part, "row", scatter_dimension=0, tiled=True)
         down_sum_part = lax.psum_scatter(down_part, "row", scatter_dimension=0, tiled=True)
-        up_sum = lax.psum_scatter(up_part, "row", scatter_dimension=0, tiled=True)
-        proj_sum = plane_reduce(proj_near, proj_far, 0).astype(BF16)
-        proj_cols = proj_sum.reshape(n_rows, rows, feats).transpose(1, 0, 2)
-        proj_grad = row_reduce([at(proj_cols, (z + k) % rows) for k in range(rows)])
-        grad_mid_own = unrolled(row_exchange(row_chunks(grad_mid_half)), 1)
-
-        results = attention_backward(me, start, query, key_values, offsets, attn, lse, grad_heads)
-        grad_query, query_total, value_total = results[:3]
-        kv_grads = [jnp.concatenate(results[3 + 2 * i : 5 + 2 * i], axis=0) for i in range(cols)]
-        half_cols = cols // 2
-        kv_sums = [
-            kv_grads[i].astype(F32)
-            + lax.ppermute(kv_grads[half_cols + i], "col", [(j, j ^ 1) for j in range(cols)]).astype(F32)
-            for i in range(half_cols)
-        ]
-        own_sum = kv_sums[0]
-        for i in range(1, half_cols):
-            b = offsets[i]
-            own_sum = own_sum + lax.ppermute(
-                kv_sums[i].astype(BF16), "col", [(j, j ^ b) for j in range(cols) if (j ^ b) < j]
-            ).astype(F32)
+        out_few = (mid + total_of(down_terms) + vectors[7]).astype(BF16)
+        proj_terms = plane_scatter(proj_near, proj_received, 0)
+        mid_pieces = row_exchange(chunks_of(grad_mid_half, 1))
+
+        far = attention_backward(me, start, query, far_kv, far_offsets, attn, lse, grad_heads)
+        half_far = len(far_offsets) // 2
+        far_grads = [jnp.concatenate(far[2 * i : 2 * i + 2], axis=0) for i in range(len(far_offsets))]
+        far_value_total, carried_query = far[-2:]
+        far_sent = []
+        for i in range(half_far):
+            b = far_offsets[i]
+            both = far_grads[i].astype(F32) + lax.ppermute(far_grads[half_far + i], "col", swap_cores).astype(F32)
+            far_sent.append(
+                lax.ppermute(both.astype(BF16), "col", [(j, j ^ b) for j in range(cols) if (j ^ b) < j])
+            )
+        carried_query, mid_pieces = lax.optimization_barrier((carried_query, mid_pieces))
+        grad_mid_own = unrolled(mid_pieces, 0)
+        out_pieces = row_exchange(chunks_of(out_few, 1))
+        near = attention_backward(
+            me, start, query, near_kv, near_offsets, attn, lse, grad_heads, carried_query
+        )
+        near, far_sent, proj_terms, out_pieces = lax.optimization_barrier(
+            (near, far_sent, proj_terms, out_pieces)
+        )
+        block_out = unrolled(out_pieces, 0)
+        near_value_total, grad_query, query_total = near[-3:]
+        value_total = near_value_total + far_value_total
+        own_sum = jnp.concatenate(near[0:2], axis=0).astype(F32)
+        own_sum = own_sum + lax.ppermute(jnp.concatenate(near[2:4], axis=0), "col", swap_cores).astype(F32)
+        for item in far_sent:
+            own_sum = own_sum + item.astype(F32)
+        proj_sum = total_of(proj_terms).astype(BF16)
         grad_qkv = jnp.concatenate([grad_query, own_sum.astype(BF16)], axis=0)
         finals = at(jnp.asarray(pack_final), z)
         finals = jnp.concatenate([at(finals, c ^ b) for b in offsets])
         grad_packed = move_units(finals, [grad_qkv], None, cols * packed, BF16)
+        proj_grad = row_reduce(chunks_of(proj_sum, 1))
 
         gain_one = vec_swap[0].reshape(dps, rows * half, 1)
         part_half, sum_norm, sum_plain, stats = qkv_back(
@@ -671,17 +780,17 @@
         own_normed = normed_one.reshape(dps, rows, half, tokens)[:, 0]
         own_gain = gain_one.reshape(dps, rows, half, 1)[:, 0]
         inner = inverse_one * (grad_ln_own * own_gain - first_row - own_normed * second_row)
-        inner = swapped(inner, 0).reshape(feats, tokens)
-        input_grad = (grad_mid_own.astype(F32) + inner).astype(BF16).T
+        inner = swapped(inner, 0).reshape(feats, tokens).T
+        input_grad = (grad_mid_own.astype(F32) + inner).astype(BF16)
 
         flat = (dps * (cols // 2), rows * half, packed)
-        qkv_sum = plane_reduce(qkv_near.reshape(flat), qkv_far.reshape(flat), 0)[0].astype(BF16)
+        qkv_sum = total_of(plane_scatter(qkv_near.reshape(flat), core_send(qkv_far.reshape(flat)), 0))
+        qkv_sum = qkv_sum[0].astype(BF16)
         qkv_sum = qkv_sum.reshape(rows, half, packed)
         qkv_home = jnp.concatenate(row_exchange([qkv_sum[k] for k in range(rows)]), axis=1)
         qkv_grad = mm("fm,nm->fn", qkv_home, select)
 
         up_sum, down_sum_part, _ = lax.optimization_barrier((up_sum, down_sum_part, part_half))
-        down_grad = down_sum_part.T.astype(F32)
         up_blocks = up_sum.reshape(dps, half, hidden)
         up_back = dp_exchange([at(up_blocks, y ^ d) for d in range(dps)])
         up_grad = swapped(jnp.stack(up_back), 0).transpose(1, 0, 2).reshape(half, dps * hidden).astype(F32)
@@ -705,24 +814,26 @@
                 back_from_swap(sum_plain),
                 from_heads(query_total[:, 0]),
                 from_heads(value_total[:, 0]),
-                jnp.sum(grad_mid, axis=1),
-                jnp.sum(grad_ln_two * normed_two, axis=1),
-                jnp.sum(grad_ln_two, axis=1),
+                jnp.sum(grad_mid, axis=0),
+                jnp.sum(grad_ln_two * normed_two, axis=0),
+                jnp.sum(grad_ln_two, axis=0),
                 lax.dynamic_update_slice_in_dim(jnp.zeros((D,), F32), top_sum, z * feats, 0),
             ]
         )
         bias_full = lax.dynamic_update_slice_in_dim(
             jnp.zeros((up_bias.shape[0],), F32), bias_part, (c * dps + y) * hidden, 0
         )
-        summed = lax.psum(jnp.concatenate([parts.reshape(-1), bias_full]), ("dp", "row", "col"))
-        summed, _ = lax.optimization_barrier((summed, qkv_home))
+        summed = sum_everywhere(jnp.concatenate([parts.reshape(-1), bias_full]))
         vector_grad = summed[: 8 * D].reshape(8, D)
         bias_grad = summed[8 * D :]
 
-        new_qkv, qkv_state = adam_step(qkv_weight, qkv_grad, qkv_moments, LR_MATRIX)
-        new_proj, proj_state = adam_step(proj_weight, proj_grad, proj_moments, LR_MATRIX)
-        new_up, up_state = adam_step(up_weight, up_grad, up_moments, LR_MATRIX)
-        new_down, down_state = adam_step(down_weight, down_grad, down_moments, LR_MATRIX)
+        new_up, up_state = adam_matrix(up_weight, up_grad, up_moments)
+        down_turned = down_sum_part.astype(F32)
+        down_grad = down_turned.T
+        new_down, down_state = adam_matrix(down_weight.T, down_turned, down_moments.transpose(0, 2, 1))
+        new_down, down_state = new_down.T, down_state.transpose(0, 2, 1)
+        new_proj, proj_state = adam_matrix(proj_weight, proj_grad, proj_moments)
+        new_qkv, qkv_state = adam_matrix(qkv_weight, qkv_grad, qkv_moments)
         new_vectors, vector_state = adam_step(vectors, vector_grad, vector_moments, LR_VECTOR)
         new_bias, bias_state = adam_step(up_bias, bias_grad, bias_moments, LR_VECTOR)
         return (

time: 780 us -> 646 us (0.83)
  local copies, waits for them, and re-layouts: 114 us -> 63.5 us
  starting transfers between devices: 150 us -> 102 us
  waiting for transfers between devices: 320 us -> 282 us
  other arithmetic: 75.4 us -> 55.6 us
  Pallas kernels: 37.5 us -> 55.6 us
    psum x1 -> x0, waiting for transfers between devices: 50.2 us -> none  [per_device(): lax.psum(jnp.concatenate([parts.reshape(-1), bias_full]), ('dp', 'row', '...]
    ppermute x33, starting transfers between devices: 96.1 us -> 48.9 us  [to_row(): lax.ppermute(values, 'row', [(i, (i + k) % rows) for i in range(rows)])]
    unnamed x272 -> x249, local copies, waits for them, and re-layouts: 55.7 us -> 26.2 us
    ppermute x2, waiting for transfers between devices: 3.5 us -> 24.1 us  [sum_rows(): lax.ppermute(values, 'row', [(i, i ^ step) for i in range(rows)])]
    ppermute x1, waiting for transfers between devices: 19.9 us -> 0.01 us  [per_device(): lax.ppermute(own_kv, 'col', [(i, i ^ b) for i in range(cols) if i ^ b > i])]
    pallas_call x2 -> x8, Pallas kernels: 15.8 us -> 35 us  [the longest x4 12.6 us: adam_matrix(): pl.pallas_call(body, grid=(n // step,), in_specs=[block, block, pair], ou...]
    concatenate x7 -> x4, other arithmetic: 13 us -> 2.49 us  [the longest x1 1.05 us: per_device(): jnp.concatenate(near[2:4], axis=0)]
    ppermute x2, waiting for transfers between devices: 0.01 us -> 9.66 us  [dp_exchange(): lax.ppermute(chunks[d], 'dp', [(y, y ^ d) for y in range(dps)])]
  transfers between devices with their start and end apart: 80 -> 84, of which waited for: 32 -> 33; matrix products, arithmetic and copies ran while one was open for 23% -> 22% of each run, Pallas kernels for 3% -> 8%
where the time goes in v3:
time: 646 us; the launch traced here: 640 us
  waiting for transfers between devices  282 us (44%)
  starting transfers between devices  102 us (16%)
  matrix products  64.9 us (10%)
  local copies, waits for them, and re-layouts  63.5 us (10%)
  other arithmetic  55.6 us (9%)
  Pallas kernels  55.6 us (9%)
  between operations  16.2 us (3%)
    ppermute x33, waiting for transfers between devices, to_row(): lax.ppermute(values, 'row', [(i, (i + k) % rows) for i in range(rows)])  163 us
    ppermute x32, waiting for transfers between devices, to_plane(): lax.ppermute(values, ('dp', 'col'), [(y * cols + c, (y ^ d) * cols + (c ^...  67 us
    dot_general x18, matrix products, mm(): return jnp.einsum(spec, left, right, preferred_element_type=F32)  64.9 us
    ppermute x33, starting transfers between devices, to_row(): lax.ppermute(values, 'row', [(i, (i + k) % rows) for i in range(rows)])  48.9 us
    ppermute x32, starting transfers between devices, to_plane(): lax.ppermute(values, ('dp', 'col'), [(y * cols + c, (y ^ d) * cols + (c ^...  35.3 us
    unnamed x249, local copies, waits for them, and re-layouts  26.2 us
    ppermute x2, waiting for transfers between devices, sum_rows(): lax.ppermute(values, 'row', [(i, i ^ step) for i in range(rows)])  24.1 us
  transfers between devices with their start and end apart: 84, of which 33 were waited for; matrix products, arithmetic and copies ran while one was open for 22% of the time, Pallas kernels for 8%

profile of v3, /device:TPU:0, one launch (start us, length us, event | category | flops | bytes accessed | tf_op | source)
XLA Modules:
  0.0 640.3 jit_solution(9282001105178339489)
XLA Ops:
  27.5 23.6 %collective-permute-done.2 = bf16[200,384]{1,0:T(8,128)(2,1)S(1)} collective-permute-done((bf16[200,384]{1,0:T(8,128)(2,1)S(1)}, bf16[200,384]{1,0:T(8,128)(2,1)S(1)}, u32[]{:S(2)}, u32[]{:S(2)}) %collective-permute-start.2) | collective-permute-done | bytes 153632 | tf_op jit(solution)/shard_map/ppermute | solution.py:477
  55.7 13.3 %collective-permute-done.8 = bf16[2,200,512]{2,1,0:T(8,128)(2,1)S(1)} collective-permute-done((bf16[2,200,512]{2,1,0:T(8,128)(2,1)S(1)}, bf16[2,200,512]{2,1,0:T(8,128)(2,1)S(1)}, u32[]{:S(2)}, u32[]{:S(2)}) %collective-permute-start.8) | collective-permute-done | bytes 409632 | tf_op jit(solution)/shard_map/ppermute | solution.py:477
  69.0 5.6 collective-permute-done.7
  76.0 5.6 collective-permute-done.5
  114.4 5.6 collective-permute-start.18
  121.6 6.4 attention_forward.2
  128.9 11.0 %collective-permute-done.18 = bf16[128,400]{0,1:T(8,128)(2,1)S(1)} collective-permute-done((bf16[128,400]{0,1:T(8,128)(2,1)S(1)}, bf16[128,400]{0,1:T(8,128)(2,1)S(1)}, u32[]{:S(2)}, u32[]{:S(2)}) %collective-permute-start.18) | collective-permute-done | bytes 102432 | tf_op jit(solution)/shard_map/ppermute | solution.py:477
  139.9 19.6 %collective-permute-done.14 = bf16[200,400]{1,0:T(8,128)(2,1)S(1)} collective-permute-done((bf16[200,400]{1,0:T(8,128)(2,1)}, bf16[200,400]{1,0:T(8,128)(2,1)S(1)}, u32[]{:S(2)}, u32[]{:S(2)}) %collective-permute-start.14) | collective-permute-done | bytes 160032 | tf_op jit(solution)/shard_map/ppermute | solution.py:477
  173.8 9.6 %collective-permute-done.20 = bf16[200,1600]{1,0:T(8,128)(2,1)S(1)} collective-permute-done((bf16[200,1600]{1,0:T(8,128)(2,1)}, bf16[200,1600]{1,0:T(8,128)(2,1)S(1)}, u32[]{:S(2)}, u32[]{:S(2)}) %collective-permute-start.20) | collective-permute-done | bytes 640032 | tf_op jit(solution)/shard_map/ppermute | solution.py:492
  183.3 13.3 %collective-permute-done.21 = bf16[200,1600]{1,0:T(8,128)(2,1)S(1)} collective-permute-done((bf16[200,1600]{1,0:T(8,128)(2,1)}, bf16[200,1600]{1,0:T(8,128)(2,1)S(1)}, u32[]{:S(2)}, u32[]{:S(2)}) %collective-permute-start.21) | collective-permute-done | bytes 640032 | tf_op jit(solution)/shard_map/ppermute | solution.py:492
  210.4 6.9 %collective-permute-done.25 = bf16[448,128]{1,0:T(8,128)(2,1)S(1)} collective-permute-done((bf16[448,128]{1,0:T(8,128)(2,1)S(1)}, bf16[448,128]{1,0:T(8,128)(2,1)S(1)}, u32[]{:S(2)}, u32[]{:S(2)}) %collective-permute-start.25) | collective-permute-done | bytes 114720 | tf_op jit(solution)/shard_map/ppermute | solution.py:477
  233.9 7.3 %collective-permute-done.30 = bf16[128,1600]{0,1:T(8,128)(2,1)S(1)} collective-permute-done((bf16[128,1600]{0,1:T(8,128)(2,1)S(1)}, bf16[128,1600]{0,1:T(8,128)(2,1)S(1)}, u32[]{:S(2)}, u32[]{:S(2)}) %collective-permute-start.30) | collective-permute-done | bytes 409632 | tf_op jit(solution)/shard_map/ppermute | solution.py:492
  242.0 7.2 %collective-permute-done.31 = bf16[128,1600]{0,1:T(8,128)(2,1)S(1)} collective-permute-done((bf16[128,1600]{0,1:T(8,128)(2,1)S(1)}, bf16[128,1600]{0,1:T(8,128)(2,1)S(1)}, u32[]{:S(2)}, u32[]{:S(2)}) %collective-permute-start.31) | collective-permute-done | bytes 409632 | tf_op jit(solution)/shard_map/ppermute | solution.py:492
  260.0 5.6 multiply_convert_fusion
  265.6 5.6 fusion.95
  271.3 10.6 %convolution_convert_fusion.4 = bf16[512,1600]{0,1:T(8,128)(2,1)S(1)} fusion(bf16[1600,800]{1,0:T(8,128)(2,1)S(1)} %copy-done.104, bf16[512,800]{0,1:T(8,128)(2,1)S(1)} %get-tuple-element.163), kind=kOutput, calls=%fused_computation.18 | convolution fusion | flops 1311539200 | bytes 5017600 | tf_op jit(solution)/shard_map/th,fh->tf/dot_general | solution.py:43
  322.3 7.0 %collective-permute-start.41 = (bf16[448,128]{1,0:T(8,128)(2,1)S(1)}, bf16[448,128]{1,0:T(8,128)(2,1)S(1)}, u32[]{:S(2)}, u32[]{:S(2)}) collective-permute-start(bf16[448,128]{1,0:T(8,128)(2,1)S(1)} %bitcast.376), channel_id=1, source_target_pairs={{0,4},{4,8},{8,12},{12,0},{1,5},{5,9},{9,13},{13,1},{2,6},{6,10},{... | collective-permute-start | bytes 344072 | tf_op jit(solution)/shard_map/ppermute | solution.py:477
  345.2 10.0 %collective-permute-done.45 = bf16[128,1600]{0,1:T(8,128)(2,1)} collective-permute-done((bf16[128,1600]{0,1:T(8,128)(2,1)S(1)}, bf16[128,1600]{0,1:T(8,128)(2,1)}, u32[]{:S(2)}, u32[]{:S(2)}) %collective-permute-start.45) | collective-permute-done | bytes 409632 | tf_op jit(solution)/shard_map/ppermute | solution.py:492
  355.2 5.2 copy.128
  389.2 7.8 %collective-permute-start.52 = (bf16[200,1600]{1,0:T(8,128)(2,1)}, bf16[200,1600]{1,0:T(8,128)(2,1)}, u32[]{:S(2)}, u32[]{:S(2)}) collective-permute-start(bf16[200,1600]{1,0:T(8,128)(2,1)} %get-tuple-element.273), channel_id=1, source_target_pairs={{0,2},{1,3},{2,0},{3,1},{16,18},{17,19},{18,16},{19,17},{4,6},{5,7... | collective-permute-start | bytes 1920008 | tf_op jit(solution)/shard_map/ppermute | solution.py:492
  405.7 8.3 %attention_backward.3 = (bf16[448,512]{1,0:T(8,128)(2,1)S(1)}, bf16[448,512]{1,0:T(8,128)(2,1)S(1)}, bf16[448,512]{1,0:T(8,128)(2,1)S(1)}, bf16[448,512]{1,0:T(8...) custom-call(s32[1]{0:T(128)} %bitcast.me_ref, s32[1,512]{1,0:T(1,128)S(1)} %bitcast.323, ...), custom_call_target="tpu_custom_call" | custom-call | flops 16099999744 | bytes 50400000 | tf_op jit(solution)/shard_map/attention_backward/pallas_call | solution.py:455
  416.0 12.2 %collective-permute-done.56 = bf16[128,400]{0,1:T(8,128)(2,1)S(1)} collective-permute-done((bf16[128,400]{0,1:T(8,128)(2,1)S(1)}, bf16[128,400]{0,1:T(8,128)(2,1)S(1)}, u32[]{:S(2)}, u32[]{:S(2)}) %collective-permute-start.56) | collective-permute-done | bytes 102432 | tf_op jit(solution)/shard_map/ppermute | solution.py:477
  429.0 6.5 %collective-permute-done.57 = bf16[128,400]{0,1:T(8,128)(2,1)S(1)} collective-permute-done((bf16[128,400]{0,1:T(8,128)(2,1)S(1)}, bf16[128,400]{0,1:T(8,128)(2,1)S(1)}, u32[]{:S(2)}, u32[]{:S(2)}) %collective-permute-start.57) | collective-permute-done | bytes 102432 | tf_op jit(solution)/shard_map/ppermute | solution.py:477
  435.5 11.3 %collective-permute-done.51 = bf16[896,512]{1,0:T(8,128)(2,1)S(1)} collective-permute-done((bf16[896,512]{1,0:T(8,128)(2,1)S(1)}, bf16[896,512]{1,0:T(8,128)(2,1)S(1)}, u32[]{:S(2)}, u32[]{:S(2)}) %collective-permute-start.51) | collective-permute-done | bytes 917536 | tf_op jit(solution)/shard_map/ppermute | solution.py:745
  456.7 9.6 %collective-permute-done.73 = bf16[200,400]{1,0:T(8,128)(2,1)} collective-permute-done((bf16[200,400]{1,0:T(8,128)(2,1)}, bf16[200,400]{1,0:T(8,128)(2,1)}, u32[]{:S(2)}, u32[]{:S(2)}) %collective-permute-start.73) | collective-permute-done | bytes 160032 | tf_op jit(solution)/shard_map/ppermute | solution.py:477
  466.4 26.5 %collective-permute-done.72 = bf16[200,400]{1,0:T(8,128)(2,1)} collective-permute-done((bf16[200,400]{1,0:T(8,128)(2,1)}, bf16[200,400]{1,0:T(8,128)(2,1)}, u32[]{:S(2)}, u32[]{:S(2)}) %collective-permute-start.72) | collective-permute-done | bytes 160032 | tf_op jit(solution)/shard_map/ppermute | solution.py:477
  499.6 6.7 %qkv_back.1 = (bf16[4,2,200,512]{3,2,1,0:T(8,128)(2,1)S(1)}, f32[2,800,1]{2,1,0:T(8,128)S(1)}, f32[2,800,1]{2,1,0:T(8,128)S(1)}, f32[2,512]{1,0:T(2,128)S(1)}) custom-call(bf16[2,2,800,384]{3,2,1,0:T(8,128)(2,1)} %bitcast.316, bf16[2,2,800,384]{3,2,1,0:T(8,128)(2,1)} %bitcast.32.w_ref.second, bf16[1536,512]{1,0:T(8,128)(2,1)S(1)} %move_units.3.g_ref, ...), custom_call_target="tpu_custom_call" | custom-call | flops 8049999872 | bytes 25200000 | tf_op jit(solution)/shard_map/qkv_back/pallas_call | solution.py:231
  531.1 17.6 %collective-permute-done.62 = f32[2,512]{1,0:T(2,128)S(1)} collective-permute-done((f32[2,512]{1,0:T(2,128)S(1)}, f32[2,512]{1,0:T(2,128)S(1)}, u32[]{:S(2)}, u32[]{:S(2)}) %collective-permute-start.62) | collective-permute-done | bytes 4128 | tf_op jit(solution)/shard_map/ppermute | solution.py:532
  553.4 6.5 %collective-permute-done.63 = f32[2,512]{1,0:T(2,128)S(1)} collective-permute-done((f32[2,512]{1,0:T(2,128)S(1)}, f32[2,512]{1,0:T(2,128)S(1)}, u32[]{:S(2)}, u32[]{:S(2)}) %collective-permute-start.63) | collective-permute-done | bytes 4128 | tf_op jit(solution)/shard_map/ppermute | solution.py:532
  590.2 9.7 %collective-permute-done.74 = bf16[200,800]{1,0:T(8,128)(2,1)S(1)} collective-permute-done((bf16[200,800]{1,0:T(8,128)(2,1)S(1)}, bf16[200,800]{1,0:T(8,128)(2,1)S(1)}, u32[]{:S(2)}, u32[]{:S(2)}) %collective-permute-start.74) | collective-permute-done | bytes 320032 | tf_op jit(solution)/shard_map/ppermute | solution.py:518
  601.9 10.5 %collective-permute-done.66 = bf16[1,800,384]{2,1,0:T(8,128)(2,1)} collective-permute-done((bf16[1,800,384]{2,1,0:T(8,128)(2,1)}, bf16[1,800,384]{2,1,0:T(8,128)(2,1)}, u32[]{:S(2)}, u32[]{:S(2)}) %collective-permute-start.66) | collective-permute-done | bytes 614432 | tf_op jit(solution)/shard_map/ppermute | solution.py:492
  623.4 5.1 collective-permute-done.69
  (610 shorter events, 306.7 us)
Async XLA Ops:
  7.2 247.4 %all-gather.5.cloned.1.call-start = ((), (), s32[]{:S(2)}) async-start(), calls=%async_computation.3 | async-start | bytes 3584000 | tf_op jit(solution)/shard_map/all_gather | solution.py:601
  20.7 30.5 %collective-permute-start.2 = (bf16[200,384]{1,0:T(8,128)(2,1)S(1)}, bf16[200,384]{1,0:T(8,128)(2,1)S(1)}, u32[]{:S(2)}, u32[]{:S(2)}) collective-permute-start(bf16[200,384]{1,0:T(8,128)(2,1)S(1)} %get-tuple-element.324), channel_id=1, source_target_pairs={{0,8},{4,12},{8,0},{12,4},{1,9},{5,13},{9,1},{13,5},{2,10},{6,14},... | collective-permute-start | bytes 460808 | tf_op jit(solution)/shard_map/ppermute | solution.py:477
  20.7 30.5 %collective-permute-start.3 = (bf16[200,384]{1,0:T(8,128)(2,1)S(1)}, bf16[200,384]{1,0:T(8,128)(2,1)}, u32[]{:S(2)}, u32[]{:S(2)}) collective-permute-start(bf16[200,384]{1,0:T(8,128)(2,1)S(1)} %get-tuple-element.323), channel_id=1, source_target_pairs={{0,4},{4,8},{8,12},{12,0},{1,5},{5,9},{9,13},{13,1},{2,6},{6,10},{... | collective-permute-start | bytes 460808 | tf_op jit(solution)/shard_map/ppermute | solution.py:477
  21.8 33.9 %collective-permute-start.9 = (bf16[2,200,512]{2,1,0:T(8,128)(2,1)S(1)}, bf16[2,200,512]{2,1,0:T(8,128)(2,1)S(1)}, u32[]{:S(2)}, u32[]{:S(2)}) collective-permute-start(bf16[2,200,512]{2,1,0:T(8,128)(2,1)S(1)} %get-tuple-element.384), channel_id=1, source_target_pairs={{0,4},{4,8},{8,12},{12,0},{1,5},{5,9},{9,13},{13,1},{2,6},{6,10},{... | collective-permute-start | bytes 1228808 | tf_op jit(solution)/shard_map/ppermute | solution.py:477
  53.7 28.0 %collective-permute-start.5 = (bf16[1,800,384]{2,1,0:T(8,128)(2,1)S(1)}, bf16[1,800,384]{2,1,0:T(8,128)(2,1)S(1)}, u32[]{:S(2)}, u32[]{:S(2)}) collective-permute-start(bf16[1,800,384]{2,1,0:T(8,128)(2,1)S(1)} %bitcast.332), channel_id=1, source_target_pairs={{0,16},{1,17},{2,18},{3,19},{16,0},{17,1},{18,2},{19,3},{4,20},{5,... | collective-permute-start | bytes 1843208 | tf_op jit(solution)/shard_map/ppermute | solution.py:492
  55.2 26.4 %collective-permute-start.4 = (bf16[1,800,384]{2,1,0:T(8,128)(2,1)S(1)}, bf16[1,800,384]{2,1,0:T(8,128)(2,1)S(1)}, u32[]{:S(2)}, u32[]{:S(2)}) collective-permute-start(bf16[1,800,384]{2,1,0:T(8,128)(2,1)S(1)} %bitcast.333), channel_id=1, source_target_pairs={{0,2},{1,3},{2,0},{3,1},{16,18},{17,19},{18,16},{19,17},{4,6},{5,7... | collective-permute-start | bytes 1843208 | tf_op jit(solution)/shard_map/ppermute | solution.py:492
  85.1 180.4 %all-gather.3.cloned.1.call-start = ((), (), s32[]{:S(2)}) async-start(), calls=%async_computation.2 | async-start | bytes 3584000 | tf_op jit(solution)/shard_map/all_gather | solution.py:602
  98.8 41.1 %collective-permute-start.13 = (bf16[200,400]{1,0:T(8,128)(2,1)}, bf16[200,400]{1,0:T(8,128)(2,1)S(1)}, u32[]{:S(2)}, u32[]{:S(2)}) collective-permute-start(bf16[200,400]{1,0:T(8,128)(2,1)} %convert_element_type.248), channel_id=1, source_target_pairs={{0,12},{4,0},{8,4},{12,8},{1,13},{5,1},{9,5},{13,9},{2,14},{6,2},{... | collective-permute-start | bytes 480008 | tf_op jit(solution)/shard_map/ppermute | solution.py:477
  103.2 56.3 %collective-permute-start.14 = (bf16[200,400]{1,0:T(8,128)(2,1)}, bf16[200,400]{1,0:T(8,128)(2,1)S(1)}, u32[]{:S(2)}, u32[]{:S(2)}) collective-permute-start(bf16[200,400]{1,0:T(8,128)(2,1)} %convert_element_type.248), channel_id=1, source_target_pairs={{0,8},{4,12},{8,0},{12,4},{1,9},{5,13},{9,1},{13,5},{2,10},{6,14},... | collective-permute-start | bytes 480008 | tf_op jit(solution)/shard_map/ppermute | solution.py:477
  107.7 51.8 %collective-permute-start.15 = (bf16[200,400]{1,0:T(8,128)(2,1)}, bf16[200,400]{1,0:T(8,128)(2,1)S(1)}, u32[]{:S(2)}, u32[]{:S(2)}) collective-permute-start(bf16[200,400]{1,0:T(8,128)(2,1)} %convert_element_type.248), channel_id=1, source_target_pairs={{0,4},{4,8},{8,12},{12,0},{1,5},{5,9},{9,13},{13,1},{2,6},{6,10},{... | collective-permute-start | bytes 480008 | tf_op jit(solution)/shard_map/ppermute | solution.py:477
  114.4 25.5 %collective-permute-start.18 = (bf16[128,400]{0,1:T(8,128)(2,1)S(1)}, bf16[128,400]{0,1:T(8,128)(2,1)S(1)}, u32[]{:S(2)}, u32[]{:S(2)}) collective-permute-start(bf16[128,400]{0,1:T(8,128)(2,1)S(1)} %get-tuple-element.379), channel_id=1, source_target_pairs={{0,4},{4,8},{8,12},{12,0},{1,5},{5,9},{9,13},{13,1},{2,6},{6,10},{... | collective-permute-start | bytes 307208 | tf_op jit(solution)/shard_map/ppermute | solution.py:477
  119.9 39.6 %collective-permute-start.12 = (bf16[896,512]{1,0:T(8,128)(2,1)S(1)}, bf16[896,512]{1,0:T(8,128)(2,1)S(1)}, u32[]{:S(2)}, u32[]{:S(2)}) collective-permute-start(bf16[896,512]{1,0:T(8,128)(2,1)S(1)} %slice.307.refs_0_.refs_1_), channel_id=1, source_target_pairs={{0,2},{1,3},{4,6},{5,7},{8,10},{9,11},{12,14},{13,15},{16,18},{17,... | collective-permute-start | bytes 2752520 | tf_op jit(solution)/shard_map/ppermute | solution.py:635
  160.2 412.0 %reduce-scatter.7.cloned.1.call-start = ((), (), s32[]{:S(2)}) async-start(), calls=%async_computation.5 | async-start | bytes 3584000
  165.3 31.3 %collective-permute-start.21 = (bf16[200,1600]{1,0:T(8,128)(2,1)}, bf16[200,1600]{1,0:T(8,128)(2,1)S(1)}, u32[]{:S(2)}, u32[]{:S(2)}) collective-permute-start(bf16[200,1600]{1,0:T(8,128)(2,1)} %concatenate.81), channel_id=1, source_target_pairs={{0,16},{1,17},{2,18},{3,19},{16,0},{17,1},{18,2},{19,3},{4,20},{5,... | collective-permute-start | bytes 1920008 | tf_op jit(solution)/shard_map/ppermute | solution.py:492
  165.7 31.0 %collective-permute-start.22 = (bf16[200,1600]{1,0:T(8,128)(2,1)}, bf16[200,1600]{1,0:T(8,128)(2,1)S(1)}, u32[]{:S(2)}, u32[]{:S(2)}) collective-permute-start(bf16[200,1600]{1,0:T(8,128)(2,1)} %concatenate.81), channel_id=1, source_target_pairs={{0,18},{1,19},{2,16},{3,17},{16,2},{17,3},{18,0},{19,1},{4,22},{5,... | collective-permute-start | bytes 1920008 | tf_op jit(solution)/shard_map/ppermute | solution.py:492
  197.3 25.4 %collective-permute-start.23 = (bf16[800,1600]{1,0:T(8,128)(2,1)S(1)}, bf16[800,1600]{1,0:T(8,128)(2,1)S(1)}, u32[]{:S(2)}, u32[]{:S(2)}) collective-permute-start(bf16[800,1600]{1,0:T(8,128)(2,1)S(1)} %get-tuple-element.311), channel_id=1, source_target_pairs={{0,1},{1,0},{2,3},{3,2},{16,17},{17,16},{18,19},{19,18},{4,5},{5,4... | collective-permute-start | bytes 7680008 | tf_op jit(solution)/shard_map/ppermute | solution.py:492
  319.8 35.4 %collective-permute-start.42 = (bf16[800,1600]{1,0:T(8,128)(2,1)S(1)}, bf16[800,1600]{1,0:T(8,128)(2,1)}, u32[]{:S(2)}, u32[]{:S(2)}) collective-permute-start(bf16[800,1600]{1,0:T(8,128)(2,1)S(1)} %convolution_convert_fusion.1), channel_id=1, source_target_pairs={{0,1},{1,0},{2,3},{3,2},{16,17},{17,16},{18,19},{19,18},{4,5},{5,4... | collective-permute-start | bytes 7680008 | tf_op jit(solution)/shard_map/ppermute | solution.py:492
  360.5 213.2 %reduce-scatter.5.cloned.1.call-start = ((), (), s32[]{:S(2)}) async-start(), calls=%async_computation.4 | async-start | bytes 3584000 | tf_op jit(solution)/shard_map/reduce_scatter | solution.py:731
  378.6 24.2 %collective-permute-start.50 = (bf16[896,512]{1,0:T(8,128)(2,1)}, bf16[896,512]{1,0:T(8,128)(2,1)}, u32[]{:S(2)}, u32[]{:S(2)}) collective-permute-start(bf16[896,512]{1,0:T(8,128)(2,1)} %pad_maximum_fusion.3), channel_id=1, source_target_pairs={{0,1},{1,0},{2,3},{3,2},{4,5},{5,4},{6,7},{7,6},{8,9},{9,8},{10,11... | collective-permute-start | bytes 2752520 | tf_op jit(solution)/shard_map/ppermute | solution.py:743
  389.2 46.3 %collective-permute-start.52 = (bf16[200,1600]{1,0:T(8,128)(2,1)}, bf16[200,1600]{1,0:T(8,128)(2,1)}, u32[]{:S(2)}, u32[]{:S(2)}) collective-permute-start(bf16[200,1600]{1,0:T(8,128)(2,1)} %get-tuple-element.273), channel_id=1, source_target_pairs={{0,2},{1,3},{2,0},{3,1},{16,18},{17,19},{18,16},{19,17},{4,6},{5,7... | collective-permute-start | bytes 1920008 | tf_op jit(solution)/shard_map/ppermute | solution.py:492
  397.1 38.5 %collective-permute-start.53 = (bf16[200,1600]{1,0:T(8,128)(2,1)}, bf16[200,1600]{1,0:T(8,128)(2,1)}, u32[]{:S(2)}, u32[]{:S(2)}) collective-permute-start(bf16[200,1600]{1,0:T(8,128)(2,1)} %get-tuple-element.272), channel_id=1, source_target_pairs={{0,16},{1,17},{2,18},{3,19},{16,0},{17,1},{18,2},{19,3},{4,20},{5,... | collective-permute-start | bytes 1920008 | tf_op jit(solution)/shard_map/ppermute | solution.py:492
  398.2 37.3 %collective-permute-start.54 = (bf16[200,1600]{1,0:T(8,128)(2,1)}, bf16[200,1600]{1,0:T(8,128)(2,1)}, u32[]{:S(2)}, u32[]{:S(2)}) collective-permute-start(bf16[200,1600]{1,0:T(8,128)(2,1)} %get-tuple-element.271), channel_id=1, source_target_pairs={{0,18},{1,19},{2,16},{3,17},{16,2},{17,3},{18,0},{19,1},{4,22},{5,... | collective-permute-start | bytes 1920008 | tf_op jit(solution)/shard_map/ppermute | solution.py:492
  404.4 42.5 %collective-permute-start.51 = (bf16[896,512]{1,0:T(8,128)(2,1)S(1)}, bf16[896,512]{1,0:T(8,128)(2,1)S(1)}, u32[]{:S(2)}, u32[]{:S(2)}) collective-permute-start(bf16[896,512]{1,0:T(8,128)(2,1)S(1)} %add_convert_fusion.4), channel_id=1, source_target_pairs={{2,0},{3,1},{6,4},{7,5},{10,8},{11,9},{14,12},{15,13},{18,16},{19,... | collective-permute-start | bytes 2752520 | tf_op jit(solution)/shard_map/ppermute | solution.py:745
  447.9 48.8 %collective-permute-start.58 = (bf16[896,512]{1,0:T(8,128)(2,1)}, bf16[896,512]{1,0:T(8,128)(2,1)}, u32[]{:S(2)}, u32[]{:S(2)}) collective-permute-start(bf16[896,512]{1,0:T(8,128)(2,1)} %pad_maximum_fusion.4), channel_id=1, source_target_pairs={{0,1},{1,0},{2,3},{3,2},{4,5},{5,4},{6,7},{7,6},{8,9},{9,8},{10,11... | collective-permute-start | bytes 2752520 | tf_op jit(solution)/shard_map/ppermute | solution.py:760
  453.5 39.3 %collective-permute-start.72 = (bf16[200,400]{1,0:T(8,128)(2,1)}, bf16[200,400]{1,0:T(8,128)(2,1)}, u32[]{:S(2)}, u32[]{:S(2)}) collective-permute-start(bf16[200,400]{1,0:T(8,128)(2,1)} %get-tuple-element.310), channel_id=1, source_target_pairs={{0,8},{4,12},{8,0},{12,4},{1,9},{5,13},{9,1},{13,5},{2,10},{6,14},... | collective-permute-start | bytes 480008 | tf_op jit(solution)/shard_map/ppermute | solution.py:477
  453.5 39.3 %collective-permute-start.71 = (bf16[200,400]{1,0:T(8,128)(2,1)S(1)}, bf16[200,400]{1,0:T(8,128)(2,1)}, u32[]{:S(2)}, u32[]{:S(2)}) collective-permute-start(bf16[200,400]{1,0:T(8,128)(2,1)S(1)} %get-tuple-element.308), channel_id=1, source_target_pairs={{0,4},{4,8},{8,12},{12,0},{1,5},{5,9},{9,13},{13,1},{2,6},{6,10},{... | collective-permute-start | bytes 480008 | tf_op jit(solution)/shard_map/ppermute | solution.py:477
  522.6 45.1 %collective-permute-start.61 = (bf16[2,200,512]{2,1,0:T(8,128)(2,1)}, bf16[2,200,512]{2,1,0:T(8,128)(2,1)S(1)}, u32[]{:S(2)}, u32[]{:S(2)}) collective-permute-start(bf16[2,200,512]{2,1,0:T(8,128)(2,1)} %get-tuple-element.282), channel_id=1, source_target_pairs={{0,12},{4,0},{8,4},{12,8},{1,13},{5,1},{9,5},{13,9},{2,14},{6,2},{... | collective-permute-start | bytes 1228808 | tf_op jit(solution)/shard_map/ppermute | solution.py:477
  522.6 45.1 %collective-permute-start.60 = (bf16[2,200,512]{2,1,0:T(8,128)(2,1)}, bf16[2,200,512]{2,1,0:T(8,128)(2,1)}, u32[]{:S(2)}, u32[]{:S(2)}) collective-permute-start(bf16[2,200,512]{2,1,0:T(8,128)(2,1)} %get-tuple-element.283), channel_id=1, source_target_pairs={{0,8},{4,12},{8,0},{12,4},{1,9},{5,13},{9,1},{13,5},{2,10},{6,14},... | collective-permute-start | bytes 1228808 | tf_op jit(solution)/shard_map/ppermute | solution.py:477
  523.8 43.8 %collective-permute-start.59 = (bf16[2,200,512]{2,1,0:T(8,128)(2,1)}, bf16[2,200,512]{2,1,0:T(8,128)(2,1)}, u32[]{:S(2)}, u32[]{:S(2)}) collective-permute-start(bf16[2,200,512]{2,1,0:T(8,128)(2,1)} %get-tuple-element.281), channel_id=1, source_target_pairs={{0,4},{4,8},{8,12},{12,0},{1,5},{5,9},{9,13},{13,1},{2,6},{6,10},{... | collective-permute-start | bytes 1228808 | tf_op jit(solution)/shard_map/ppermute | solution.py:477
  526.2 24.6 %collective-permute-start.77 = (f32[19200]{0:T(1024)S(1)}, f32[19200]{0:T(1024)S(1)}, u32[]{:S(2)}, u32[]{:S(2)}) collective-permute-start(f32[19200]{0:T(1024)S(1)} %add.775), channel_id=1, source_target_pairs={{0,16},{16,0},{1,17},{17,1},{2,18},{18,2},{3,19},{19,3},{4,20},{20... | collective-permute-start | bytes 230408 | tf_op jit(solution)/shard_map/ppermute | solution.py:525
  583.5 28.9 %collective-permute-start.66 = (bf16[1,800,384]{2,1,0:T(8,128)(2,1)}, bf16[1,800,384]{2,1,0:T(8,128)(2,1)}, u32[]{:S(2)}, u32[]{:S(2)}) collective-permute-start(bf16[1,800,384]{2,1,0:T(8,128)(2,1)} %get-tuple-element.276), channel_id=1, source_target_pairs={{0,16},{1,17},{2,18},{3,19},{16,0},{17,1},{18,2},{19,3},{4,20},{5,... | collective-permute-start | bytes 1843208 | tf_op jit(solution)/shard_map/ppermute | solution.py:492
  583.8 28.6 %collective-permute-start.65 = (bf16[1,800,384]{2,1,0:T(8,128)(2,1)}, bf16[1,800,384]{2,1,0:T(8,128)(2,1)}, u32[]{:S(2)}, u32[]{:S(2)}) collective-permute-start(bf16[1,800,384]{2,1,0:T(8,128)(2,1)} %get-tuple-element.274), channel_id=1, source_target_pairs={{0,2},{1,3},{2,0},{3,1},{16,18},{17,19},{18,16},{19,17},{4,6},{5,7... | collective-permute-start | bytes 1843208 | tf_op jit(solution)/shard_map/ppermute | solution.py:492
  (165 other events, 1608.8 us)
Sparse Core Ops, SparseCore 0:
  85.3 82.1 all-gather.4
  169.6 67.0 all-gather.2
  360.6 63.4 reduce-scatter.6
  426.3 74.0 reduce-scatter.4

commit v4 on v3

--- a/solution.py
+++ b/solution.py
@@ -24,6 +24,7 @@
 GELU_COEF = 0.7978845608028654
 GELU_CUBE = 0.044715
 UNIT = 16
+WIDE = -(-D // 128) * 128
 
 F32 = jnp.float32
 BF16 = jnp.bfloat16
@@ -31,7 +32,7 @@
 
 def cost(micros):
     return pl.CostEstimate(
-        flops=int(micros * 1.15e9), bytes_accessed=int(micros * 3.6e6), transcendentals=0
+        flops=int(micros * 0.35e9), bytes_accessed=int(micros * 1.1e6), transcendentals=0
     )
 
 
@@ -110,6 +111,27 @@
     return slots, width, source, unpack_block, unpack_rank, pack_final
 
 
+def row_tables(rows, dps, cols, slots, plane, n_rows, unit):
+    per_head, per_block = HEAD_DIM // unit, n_rows // unit
+    place = {entry: i for i, entry in enumerate(plane)}
+    to_weight = np.zeros((rows, dps, cols, D // unit), np.int32)
+    to_heads = np.full((rows, dps, cols, rows * slots * per_head), -1, np.int32)
+    to_plain = np.zeros((rows, D // unit), np.int32)
+    for z in range(rows):
+        for y in range(dps):
+            for c in range(cols):
+                for a in range(D // unit):
+                    head, q = a // per_head, a % per_head
+                    k, j = (head - z) % rows, head // rows
+                    n, i = a // per_block, a % per_block
+                    in_heads = (k * slots + j) * per_head + q
+                    in_weight = place[(y ^ (n % dps), c ^ (n // dps))] * per_block + i
+                    to_weight[z, y, c, in_weight] = in_heads
+                    to_heads[z, y, c, in_heads] = in_weight
+                    to_plain[z, ((n % dps) * cols + n // dps) * per_block + i] = in_heads
+    return to_weight, to_heads, to_plain
+
+
 def move_units(table, sources, bias, out_rows, out_dtype):
     width = sources[0].shape[1]
     units = sources[0].shape[0] // UNIT
@@ -131,13 +153,14 @@
             out[rows, :] = block.astype(out_dtype)
 
     extra = [] if bias is None else [bias]
-    return pl.pallas_call(
-        body,
-        out_shape=jax.ShapeDtypeStruct((out_rows, width), out_dtype),
-        in_specs=[pl.BlockSpec(memory_space=pltpu.SMEM)]
-        + [pl.BlockSpec(memory_space=pltpu.VMEM)] * (len(sources) + len(extra)),
-        out_specs=pl.BlockSpec(memory_space=pltpu.VMEM),
-        compiler_params=pltpu.CompilerParams(vmem_limit_bytes=32 * 2**20),
+    shape = jax.ShapeDtypeStruct((out_rows, width), out_dtype)
+    return pl.pallas_call(
+        body,
+        grid=(1,),
+        out_shape=shape,
+        in_specs=[pl.BlockSpec(memory_space=pltpu.SMEM)] + [whole(item) for item in [*sources, *extra]],
+        out_specs=whole(shape),
+        compiler_params=pltpu.CompilerParams(vmem_limit_bytes=40 * 2**20),
         cost_estimate=cost(3),
         name="move_units",
     )(table, *sources, *extra)
@@ -194,7 +217,7 @@
     tokens = inputs.shape[2]
     few = rows // row_devices
 
-    def body(first, second, g_ref, x_ref, mean_ref, inv_ref, gain_ref, part, with_norm, plain, stats):
+    def body(first, second, g_ref, x_ref, mean_ref, inv_ref, gain_ref, part, with_norm, plain):
         total = None
         for n, w_ref in enumerate((first, second)):
             for i in range(blocks):
@@ -206,24 +229,15 @@
         with_norm[0] = jnp.sum(product, axis=1, keepdims=True)
         plain[0] = jnp.sum(total, axis=1, keepdims=True)
         weight = gain_ref[0]
-        now = jnp.concatenate(
-            [
-                jnp.sum(total * weight, axis=0, keepdims=True),
-                jnp.sum(product * weight, axis=0, keepdims=True),
-            ],
-            axis=0,
-        )
-
-        @pl.when(pl.program_id(0) == 0)
-        def _():
-            stats[...] = now
-
-        @pl.when(pl.program_id(0) > 0)
-        def _():
-            stats[...] += now
-
+        sums = []
+        for item in (total, product):
+            exact = jnp.sum(item * weight, axis=0, keepdims=True)
+            rounded = exact.astype(BF16).astype(F32)
+            sums += [rounded, exact - rounded]
+        tail = jnp.concatenate(sums + [jnp.zeros((4, tokens), F32)], axis=0)
         for k in range(row_devices):
-            part[k, 0] = total[k * few : (k + 1) * few].astype(BF16)
+            block = jnp.concatenate([total[k * few : (k + 1) * few], tail], axis=0)
+            part[k, 0] = block.astype(BF16)
 
     weight_spec = pl.BlockSpec((1, blocks, rows, packed), lambda d: (d, 0, 0, 0))
     row_spec = pl.BlockSpec((1, tokens), lambda d: (0, 0))
@@ -241,16 +255,14 @@
             column,
         ],
         out_specs=[
-            pl.BlockSpec((row_devices, 1, few, tokens), lambda d: (0, d, 0, 0)),
+            pl.BlockSpec((row_devices, 1, few + 8, tokens), lambda d: (0, d, 0, 0)),
             column,
             column,
-            pl.BlockSpec((2, tokens), lambda d: (0, 0)),
         ],
         out_shape=[
-            jax.ShapeDtypeStruct((row_devices, dps, few, tokens), BF16),
+            jax.ShapeDtypeStruct((row_devices, dps, few + 8, tokens), BF16),
             jax.ShapeDtypeStruct((dps, rows, 1), F32),
             jax.ShapeDtypeStruct((dps, rows, 1), F32),
-            jax.ShapeDtypeStruct((2, tokens), F32),
         ],
         compiler_params=pltpu.CompilerParams(vmem_limit_bytes=48 * 2**20),
         cost_estimate=cost(7),
@@ -258,6 +270,11 @@
     )(*halves, grads, inputs, mean, inverse, gain)
 
 
+def whole(array):
+    rank = len(array.shape)
+    return pl.BlockSpec(tuple(array.shape), lambda i: (0,) * rank)
+
+
 def dot_tn(left, right):
     return lax.dot_general(left, right, (((0,), (0,)), ((), ())), preferred_element_type=F32)
 
@@ -268,6 +285,254 @@
 
 def dot_nn(left, right):
     return lax.dot_general(left, right, (((1,), (0,)), ((), ())), preferred_element_type=F32)
+
+
+def rows_by_table(table, source, target, unit):
+    def move(i, carry):
+        src = table[i]
+        block = source[pl.ds(pl.multiple_of(jnp.maximum(src, 0) * unit, unit), unit), :]
+        target[pl.ds(pl.multiple_of(i * unit, unit), unit), :] = jnp.where(src >= 0, block, 0.0)
+        return carry
+
+    lax.fori_loop(0, target.shape[0] // unit, move, 0, unroll=8)
+
+
+def project(table, plain_table, pieces, halves, x_rows, vecs, unit):
+    few = pieces[0].shape[1]
+    wide = pieces[0].shape[0]
+    n, m = len(pieces), len(halves)
+
+    def body(tab, plain_tab, *refs):
+        parts, weights, refs = refs[:n], refs[n : n + m], refs[n + m :]
+        (x_ref, vec), outs = refs[:2], refs[2:]
+        rows_ref, mid_ref, h2_ref, mean_ref, inv_ref, source, target = outs
+        for k in range(n):
+            source[k * wide : (k + 1) * wide, :] = parts[k][...].astype(F32)
+        rows_by_table(tab, source, target, unit)
+        mid = x_ref[...].astype(F32) + vec[0:1, :]
+        size = weights[0].shape[0]
+        for i, weight in enumerate(weights):
+            mid = mid + dot_tn(target[i * size : (i + 1) * size, :].astype(BF16), weight[...])
+        mean = jnp.sum(mid, axis=1, keepdims=True) / D
+        spread = jnp.sum(mid * mid, axis=1, keepdims=True) / D - mean * mean
+        inverse = lax.rsqrt(spread + EPS_NORM)
+        mid_ref[...] = mid
+        h2_ref[...] = jnp.zeros_like(h2_ref)
+        h2_ref[:, :D] = ((mid - mean) * inverse * vec[1:2, :] + vec[2:3, :]).astype(BF16)
+        mean_ref[...] = mean
+        inv_ref[...] = inverse
+        rows_by_table(plain_tab, source, target, unit)
+        rows_ref[...] = target[...].astype(BF16)
+
+    args = [*pieces, *halves, x_rows, vecs]
+    shapes = [
+        jax.ShapeDtypeStruct((D, few), BF16),
+        jax.ShapeDtypeStruct((few, D), F32),
+        jax.ShapeDtypeStruct((few, WIDE), BF16),
+        jax.ShapeDtypeStruct((few, 1), F32),
+        jax.ShapeDtypeStruct((few, 1), F32),
+    ]
+    return pl.pallas_call(
+        body,
+        grid=(1,),
+        in_specs=[pl.BlockSpec(memory_space=pltpu.SMEM)] * 2 + [whole(item) for item in args],
+        out_specs=[whole(item) for item in shapes],
+        out_shape=shapes,
+        scratch_shapes=[pltpu.VMEM((n * wide, few), F32), pltpu.VMEM((D, few), F32)],
+        compiler_params=pltpu.CompilerParams(vmem_limit_bytes=48 * 2**20),
+        cost_estimate=cost(5),
+        name="project",
+    )(table, plain_table, *args)
+
+
+def project_back(table, terms, top, mid, mean, inverse, gain, halves, out_rows, unit):
+    few = top.shape[0]
+    n, m = len(terms), len(halves)
+
+    def body(tab, *refs):
+        parts, (top_ref, mid_ref, mean_ref, inv_ref, gain_ref) = refs[:n], refs[n : n + 5]
+        weights = refs[n + 5 : n + 5 + m]
+        half_ref, heads_ref, sums_ref, source, target = refs[n + 5 + m :]
+        grad = parts[0][:, :D].astype(F32)
+        for part in parts[1:]:
+            grad = grad + part[:, :D].astype(F32)
+        inv = inv_ref[...]
+        normed = (mid_ref[...] - mean_ref[...]) * inv
+        scaled = grad * gain_ref[...]
+        first_mean = jnp.sum(scaled, axis=1, keepdims=True) / D
+        second_mean = jnp.sum(scaled * normed, axis=1, keepdims=True) / D
+        out = top_ref[:, :D].astype(F32) + inv * (scaled - first_mean - normed * second_mean)
+        half = out.astype(BF16)
+        half_ref[...] = half
+        sums_ref[0:1, :] = jnp.sum(out, axis=0, keepdims=True)
+        sums_ref[1:2, :] = jnp.sum(grad * normed, axis=0, keepdims=True)
+        sums_ref[2:3, :] = jnp.sum(grad, axis=0, keepdims=True)
+        size = weights[0].shape[0]
+        for i, weight in enumerate(weights):
+            source[i * size : (i + 1) * size, :] = dot_nt(weight[...], half)
+        rows_by_table(tab, source, target, unit)
+        heads_ref[...] = target[...].astype(BF16)
+
+    args = [*terms, top, mid, mean, inverse, gain, *halves]
+    shapes = [
+        jax.ShapeDtypeStruct((few, D), BF16),
+        jax.ShapeDtypeStruct((out_rows, few), BF16),
+        jax.ShapeDtypeStruct((3, D), F32),
+    ]
+    return pl.pallas_call(
+        body,
+        grid=(1,),
+        in_specs=[pl.BlockSpec(memory_space=pltpu.SMEM)] + [whole(item) for item in args],
+        out_specs=[whole(item) for item in shapes],
+        out_shape=shapes,
+        scratch_shapes=[pltpu.VMEM((D, few), F32), pltpu.VMEM((out_rows, few), F32)],
+        compiler_params=pltpu.CompilerParams(vmem_limit_bytes=48 * 2**20),
+        cost_estimate=cost(5),
+        name="project_back",
+    )(table, *args)
+
+
+def hidden_units(h2_rows, top_rows, w_up, w_down, shift):
+    tokens = h2_rows.shape[0]
+    hidden = w_up.shape[1]
+    step = min(tokens, 256)
+
+    def body(h_ref, t_ref, up, down, shift_ref, act_ref, grad_ref, sum_ref):
+        pre = dot_nn(h_ref[:, :D], up[...]) + shift_ref[...]
+        square = pre * pre
+        tanh_val = jnp.tanh(GELU_COEF * (pre + GELU_CUBE * pre * square))
+        act_ref[...] = (0.5 * pre * (1.0 + tanh_val)).astype(BF16)
+        slope = 0.5 * (1.0 + tanh_val) + 0.5 * pre * (1.0 - tanh_val * tanh_val) * GELU_COEF * (
+            1.0 + 3.0 * GELU_CUBE * square
+        )
+        grad = dot_nn(t_ref[:, :D], down[...]) * slope
+        grad_ref[...] = grad.astype(BF16)
+        now = jnp.sum(grad, axis=0, keepdims=True)
+
+        @pl.when(pl.program_id(0) == 0)
+        def _():
+            sum_ref[...] = now
+
+        @pl.when(pl.program_id(0) > 0)
+        def _():
+            sum_ref[...] += now
+
+    rows_in = pl.BlockSpec((step, WIDE), lambda i: (i, 0))
+    weight = pl.BlockSpec((D, hidden), lambda i: (0, 0))
+    rows_out = pl.BlockSpec((step, hidden), lambda i: (i, 0))
+    line = pl.BlockSpec((1, hidden), lambda i: (0, 0))
+    flat = jax.ShapeDtypeStruct((tokens, hidden), BF16)
+    return pl.pallas_call(
+        body,
+        grid=(tokens // step,),
+        in_specs=[rows_in, rows_in, weight, weight, line],
+        out_specs=[rows_out, rows_out, line],
+        out_shape=[flat, flat, jax.ShapeDtypeStruct((1, hidden), F32)],
+        compiler_params=pltpu.CompilerParams(vmem_limit_bytes=44 * 2**20),
+        cost_estimate=cost(6),
+        name="hidden_units",
+    )(h2_rows, top_rows, w_up, w_down, shift)
+
+
+def features_back(grads, weight):
+    tokens, hidden = grads.shape
+
+    def body(g_ref, w_ref, out):
+        out[...] = jnp.zeros_like(out)
+        out[:, :D] = dot_nt(g_ref[...], w_ref[...]).astype(BF16)
+
+    step = min(tokens, 256)
+    return pl.pallas_call(
+        body,
+        grid=(tokens // step,),
+        in_specs=[
+            pl.BlockSpec((step, hidden), lambda i: (i, 0)),
+            pl.BlockSpec((D, hidden), lambda i: (0, 0)),
+        ],
+        out_specs=pl.BlockSpec((step, WIDE), lambda i: (i, 0)),
+        out_shape=jax.ShapeDtypeStruct((tokens, WIDE), BF16),
+        compiler_params=pltpu.CompilerParams(vmem_limit_bytes=32 * 2**20),
+        cost_estimate=cost(2),
+        name="features_back",
+    )(grads, weight)
+
+
+def weight_part(rows_in, grads):
+    n = len(rows_in)
+    hidden = grads[0].shape[1]
+
+    def body(*refs):
+        parts, values, out = refs[:n], refs[n : 2 * n], refs[2 * n]
+        for low in range(0, D, 256):
+            lanes = slice(low, min(low + 256, D))
+            total = dot_tn(parts[0][:, lanes], values[0][...])
+            for part, value in zip(parts[1:], values[1:]):
+                total = total + dot_tn(part[:, lanes], value[...])
+            out[lanes, :] = total.astype(BF16)
+
+    shape = jax.ShapeDtypeStruct((D, hidden), BF16)
+    return pl.pallas_call(
+        body,
+        in_specs=[pl.BlockSpec(memory_space=pltpu.VMEM)] * (2 * n),
+        out_specs=pl.BlockSpec(memory_space=pltpu.VMEM),
+        out_shape=shape,
+        compiler_params=pltpu.CompilerParams(vmem_limit_bytes=48 * 2**20),
+        cost_estimate=cost(4),
+        name="weight_part",
+    )(*rows_in, *grads)
+
+
+def finish(where, terms, x_own, mean, inverse, gain, sides):
+    dps, half, tokens = x_own.shape
+    feats = dps * half
+    few = sides[0].shape[1]
+    n = len(terms)
+
+    def body(tab, *refs):
+        parts, (x_ref, mean_ref, inv_ref, gain_ref) = refs[:n], refs[n : n + 4]
+        side = refs[n + 4 : n + 4 + len(sides)]
+        grad_ref, out_ref, held = refs[n + 4 + len(sides) :]
+        for k, ref in enumerate(side):
+            lanes = pl.ds(pl.multiple_of(tab[k], 128), few)
+            held[:, lanes] = ref[:feats, :].astype(F32)
+            out_ref[:, lanes] = ref[feats:, :]
+        grads, stats = [], None
+        for d in range(dps):
+            total = parts[0][d].astype(F32)
+            for part in parts[1:]:
+                total = total + part[d].astype(F32)
+            tail = total[half : half + 8]
+            stats = tail if stats is None else stats + tail
+            grads.append(total[:half])
+        first_row = (stats[0:1] + stats[1:2]) / D
+        second_row = (stats[2:3] + stats[3:4]) / D
+        inv = inv_ref[...]
+        inner = []
+        for d in range(dps):
+            normed = (x_ref[d].astype(F32) - mean_ref[...]) * inv
+            inner.append(inv * (grads[d] * gain_ref[d] - first_row - normed * second_row))
+        blocks = []
+        for i in range(dps):
+            block = inner[0]
+            for d in range(1, dps):
+                block = jnp.where((tab[len(sides)] ^ d) == i, inner[d], block)
+            blocks.append(block)
+        whole = jnp.concatenate(blocks, axis=0) if dps > 1 else blocks[0]
+        grad_ref[...] = (held[...] + whole).astype(BF16)
+
+    args = [*terms, x_own, mean, inverse, gain, *sides]
+    flat = jax.ShapeDtypeStruct((feats, tokens), BF16)
+    return pl.pallas_call(
+        body,
+        grid=(1,),
+        in_specs=[pl.BlockSpec(memory_space=pltpu.SMEM)] + [whole(item) for item in args],
+        out_specs=[whole(flat)] * 2,
+        out_shape=[flat, flat],
+        scratch_shapes=[pltpu.VMEM((feats, tokens), F32)],
+        compiler_params=pltpu.CompilerParams(vmem_limit_bytes=40 * 2**20),
+        cost_estimate=cost(4),
+        name="finish",
+    )(where, *args)
 
 
 def key_mask(block, me, start, keys, queries, diagonal):
@@ -473,6 +738,11 @@
     even = [(d, b) for d in range(dps) for b in range(0, cols, 2)]
     plane = even + [(d, b + 1) for d, b in even]
 
+    n_rows = D // cols // dps
+    wide = slots * HEAD_DIM
+    unit = math.gcd(n_rows, 8)
+    to_weight, to_heads, to_plain = row_tables(rows, dps, cols, slots, plane, n_rows, unit)
+
     def to_row(values, k):
         return lax.ppermute(values, "row", [(i, (i + k) % rows) for i in range(rows)])
 
@@ -481,12 +751,6 @@
 
     def row_exchange(chunks):
         return [chunks[0]] + [to_row(chunks[rows - k], rows - k) for k in range(1, rows)]
-
-    def row_reduce(chunks):
-        total = chunks[0].astype(F32)
-        for k in range(1, rows):
-            total = total + to_row(chunks[k], k).astype(F32)
-        return total
 
     def to_plane(values, d, b):
         return lax.ppermute(
@@ -519,18 +783,11 @@
         ]
 
     def sum_everywhere(values):
-        for axis, size in (("row", rows), ("dp", dps), ("col", cols)):
-            step = 1
+        for axis, size in (("dp", dps), ("col", cols), ("row", rows)):
+            step = 2 if axis == "col" else 1
             while step < size:
                 values = values + lax.ppermute(values, axis, [(i, i ^ step) for i in range(size)])
                 step *= 2
-        return values
-
-    def sum_rows(values):
-        step = 1
-        while step < rows:
-            values = values + lax.ppermute(values, "row", [(i, i ^ step) for i in range(rows)])
-            step *= 2
         return values
 
     def at(array, index, axis=0):
@@ -576,8 +833,14 @@
                 lax.dynamic_slice_in_dim(array, ((z + k) % rows) * size, size, axis) for k in range(rows)
             ]
 
+        me = c.astype(jnp.int32).reshape(1)
+        weight_table = at(at(at(jnp.asarray(to_weight), z), y), c)
+        heads_table = at(at(at(jnp.asarray(to_heads), z), y), c)
+
         vec_swap = swapped(rolled(vectors.reshape(8, rows, feats), 1).reshape(8, rows, dps, half), 2)
         vec_swap = vec_swap.transpose(0, 2, 1, 3).reshape(8, D)
+        query_ids = lax.dynamic_slice_in_dim(segment_ids, c * tokens, tokens)
+        start = jnp.sum((segment_ids[:, None] < query_ids[None, :]).astype(jnp.int32), axis=0)[None, :]
 
         columns = rolled(at(jnp.asarray(source), c), 0).reshape(rows * packed)
         local_cols = qkv_weight.shape[1]
@@ -586,29 +849,30 @@
         ).astype(BF16)
         sorted_cols = mm("fn,nm->fm", qkv_weight.astype(BF16), select).astype(BF16)
         arrived = row_exchange([sorted_cols[:, k * packed : (k + 1) * packed] for k in range(rows)])
-
-        x_own = swapped(hidden_in.T.reshape(dps, half, tokens), 0)
-        x_all = jnp.stack(row_gather(x_own), axis=1).reshape(dps, rows * half, tokens)
         up_parts = up_weight.astype(BF16).reshape(half, dps, hidden).transpose(1, 0, 2)
         up_arrived = dp_exchange([at(up_parts, y ^ d) for d in range(dps)])
         up_rows = swapped(jnp.stack(up_arrived), 0).reshape(feats, hidden)
-        down_rows = down_weight.astype(BF16).T
-        up_rows, down_rows, arrived = lax.optimization_barrier((up_rows, down_rows, arrived))
-        qkv_first = jnp.concatenate(plane_send(jnp.stack(arrived).reshape(1, rows * half, packed)), axis=0)
-        qkv_first, x_all = lax.optimization_barrier((qkv_first, x_all))
+        arrived, up_rows, down_rows = lax.optimization_barrier((arrived, up_rows, down_weight.astype(BF16).T))
+
+        x_own = swapped(hidden_in.T.reshape(dps, half, tokens), 0)
+        qkv_sent = plane_send(jnp.stack(arrived).reshape(1, rows * half, packed))
+        x_pieces = row_gather(x_own)
+        qkv_sent, x_pieces, proj_own, upstream_late, up_rows, down_rows = lax.optimization_barrier(
+            (qkv_sent, x_pieces, proj_weight.astype(BF16), upstream, up_rows, down_rows)
+        )
+        w_up = lax.all_gather(up_rows, "row", axis=0, tiled=True)
+        w_down = lax.all_gather(down_rows, "row", axis=0, tiled=True)
+
+        proj_pieces = row_gather(proj_own)
+        qkv_first = jnp.concatenate(qkv_sent, axis=0)
         qkv_second = core_send(qkv_first)
         halves = [item.reshape(dps, cols // 2, rows * half, packed) for item in (qkv_first, qkv_second)]
-        w_up = lax.all_gather(up_rows, "row", axis=0, tiled=True)
-        w_down = lax.all_gather(down_rows, "row", axis=0, tiled=True)
-        proj_pieces = row_gather(after(proj_weight.astype(BF16), x_all))
-        top_pieces = row_exchange(chunks_of(after(upstream, x_all), 0))
-
+        x_all = jnp.stack(x_pieces, axis=1).reshape(dps, rows * half, tokens)
         x_f = x_all.astype(F32).reshape(D, tokens)
         mean_one = jnp.mean(x_f, axis=0, keepdims=True)
         spread_one = jnp.mean(x_f * x_f, axis=0, keepdims=True) - mean_one * mean_one
         inverse_one = lax.rsqrt(spread_one + EPS_NORM)
-        normed_one = (x_f - mean_one) * inverse_one
-        h1 = (normed_one * vec_swap[0][:, None] + vec_swap[1][:, None]).astype(BF16)
+        h1 = ((x_f - mean_one) * inverse_one * vec_swap[0][:, None] + vec_swap[1][:, None]).astype(BF16)
         h1 = h1.reshape(dps, rows * half, tokens)
         qkv_packed = [qkv_product(item, h1) for item in halves]
 
@@ -622,178 +886,152 @@
 
         def own_heads(vector):
             padded = jnp.pad(vector, (0, (rows * slots - HEADS) * HEAD_DIM))
-            return at(padded.reshape(slots, rows, HEAD_DIM), z, 1).reshape(slots * HEAD_DIM)
-
-        wide = slots * HEAD_DIM
+            return at(padded.reshape(slots, rows, HEAD_DIM), z, 1).reshape(wide)
+
         shift = jnp.concatenate([own_heads(vectors[2]), jnp.zeros((wide,), F32), own_heads(vectors[3])])
         qkv_rows = move_units(unpack, qkv_packed, shift[:, None], 3 * wide, BF16)
-        query = qkv_rows[:wide]
-        own_kv = qkv_rows[wide:]
-
+        qkv_rows, proj_pieces = lax.optimization_barrier((qkv_rows, proj_pieces))
+
+        query, own_kv = qkv_rows[:wide], qkv_rows[wide:]
         swap_cores = [(i, i ^ 1) for i in range(cols)]
+        near_offsets = [0, 1]
+        far_offsets = list(range(2, cols, 2)) + list(range(3, cols, 2))
         far_near = [
             lax.ppermute(own_kv, "col", [(i, i ^ b) for i in range(cols) if (i ^ b) > i])
             for b in range(2, cols, 2)
         ]
         near_kv = [own_kv, lax.ppermute(own_kv, "col", swap_cores)]
-        near_offsets = [0, 1]
-        far_offsets = list(range(2, cols, 2)) + list(range(3, cols, 2))
-        me = c.astype(jnp.int32).reshape(1)
-        query_ids = lax.dynamic_slice_in_dim(segment_ids, c * tokens, tokens)
-        start = jnp.sum((segment_ids[:, None] < query_ids[None, :]).astype(jnp.int32), axis=0)[None, :]
+        top_pieces = row_exchange(chunks_of(upstream_late.T, 1))
         carried = attention_forward(me, start, query, near_kv, near_offsets)
-        carried, far_near, proj_pieces, top_pieces = lax.optimization_barrier(
-            (carried, far_near, proj_pieces, top_pieces)
-        )
+        proj_rows = unrolled(proj_pieces, 1)
+        carried, far_near, top_pieces, proj_rows = lax.optimization_barrier(
+            (carried, far_near, top_pieces, proj_rows)
+        )
+
         far_kv = far_near + [lax.ppermute(item, "col", swap_cores) for item in far_near]
-        proj_sent = plane_send(unrolled(proj_pieces, 1))
-        top_few = unrolled(top_pieces, 1)
+        proj_sent = plane_send(proj_rows)
         attn, lse = attention_forward(me, start, query, far_kv, far_offsets, carried)
-        attn, proj_sent = lax.optimization_barrier((attn, proj_sent))
-        proj_first = jnp.concatenate(proj_sent, axis=0)
-        w_proj = jnp.concatenate([proj_first, core_send(proj_first)], axis=0)
-        top_sent = plane_send(after(top_few, proj_first))
-
-        n_rows = D // cols // dps
+        attn, w_up, top_pieces, x_late = lax.optimization_barrier((attn, w_up, top_pieces, x_all))
+
         attn_pieces = row_exchange(chunks_of(attn, 1))
-        attn_abs = unrolled([item.reshape(slots, 1, HEAD_DIM, few) for item in attn_pieces], 1)
-        attn_abs = attn_abs.reshape(rows * wide, few)[:D]
-        blocks = attn_abs.reshape(cols, dps, n_rows, few)
-        attn_few = jnp.concatenate([at(at(blocks, c ^ b), y ^ d) for d, b in plane], axis=0)
-        x_few = lax.dynamic_slice_in_dim(x_all, z * few, few, 2).reshape(dps, rows, half, few)
+        x_few = lax.dynamic_slice_in_dim(x_late, z * few, few, 2).reshape(dps, rows, half, few)
         x_few = swapped(x_few, 0).transpose(1, 0, 2, 3).reshape(rows, feats, few)
-        x_few = unrolled([x_few[k] for k in range(rows)], 0).T.astype(F32)
-        mid = x_few + mm("rt,rf->tf", attn_few, w_proj) + vectors[4]
-        mean_two = jnp.mean(mid, axis=1, keepdims=True)
-        spread_two = jnp.mean(mid * mid, axis=1, keepdims=True) - mean_two * mean_two
-        inverse_two = lax.rsqrt(spread_two + EPS_NORM)
-        normed_two = (mid - mean_two) * inverse_two
-        h2 = (normed_two * vectors[5] + vectors[6]).astype(BF16)
-        h2, top_sent = lax.optimization_barrier((h2, top_sent))
+        x_few = unrolled([x_few[k] for k in range(rows)], 0).T
+        top_turned = lax.optimization_barrier(unrolled(top_pieces, 0))
+        top_few = jnp.pad(top_turned.T, ((0, 0), (0, WIDE - D)))
+        attn_pieces, proj_sent, x_few, top_few = lax.optimization_barrier((attn_pieces, proj_sent, x_few, top_few))
+        if n_rows % 8:
+            proj_sent = [jnp.concatenate(proj_sent, axis=0)]
+        proj_halves = proj_sent + [core_send(item) for item in proj_sent]
+        top_sent = plane_send(top_few)
+
+        attn_few, mid, h2, mean_two, inverse_two = project(
+            weight_table, at(jnp.asarray(to_plain), z), attn_pieces, proj_halves, x_few, jnp.stack([vectors[4], vectors[5], vectors[6]]), unit
+        )
+        h2, top_sent, w_down = lax.optimization_barrier((h2, top_sent, w_down))
+
         top_first = jnp.concatenate(top_sent, axis=0)
         top_second = core_send(top_first)
-        h2_first = jnp.concatenate(plane_send(h2), axis=0)
+        h2_sent, top_second = lax.optimization_barrier((plane_send(h2), top_second))
+
+        h2_first = jnp.concatenate(h2_sent, axis=0)
         h2_second = core_send(h2_first)
-
-        up_shift = lax.dynamic_slice_in_dim(up_bias, (c * dps + y) * hidden, hidden)
-
-        def hidden_part(h2_rows, top_rows):
-            pre = mm("tf,fh->th", h2_rows, w_up) + up_shift
-            inside = GELU_COEF * (pre + GELU_CUBE * pre * pre * pre)
-            tanh_val = jnp.tanh(inside)
-            act = (0.5 * pre * (1.0 + tanh_val)).astype(BF16)
-            slope = 0.5 * (1.0 + tanh_val) + 0.5 * pre * (1.0 - tanh_val * tanh_val) * GELU_COEF * (
-                1.0 + 3.0 * GELU_CUBE * pre * pre
-            )
-            grad_pre = mm("tf,fh->th", top_rows, w_down) * slope
-            return act, grad_pre.astype(BF16), jnp.sum(grad_pre, axis=0)
-
-        act_near, pre_near, bias_near = hidden_part(h2_first, top_first)
-        act_far, pre_far, bias_far = hidden_part(h2_second, top_second)
-        bias_part = bias_near + bias_far
-        back_far = mm("th,fh->tf", pre_far, w_up).astype(BF16)
-        back_near = mm("th,fh->tf", pre_near, w_up).astype(BF16)
-        grad_ln_two = total_of(plane_scatter(back_near, core_send(back_far), 0))
-
-        act_near, act_far, pre_near, pre_far, _ = lax.optimization_barrier(
-            (act_near, act_far, pre_near, pre_far, back_near)
-        )
-        up_part = (mm("tf,th->fh", h2_first, pre_near) + mm("tf,th->fh", h2_second, pre_far)).astype(BF16)
-        down_part = (mm("tf,th->fh", top_first, act_near) + mm("tf,th->fh", top_second, act_far)).astype(BF16)
-
-        scaled = grad_ln_two * vectors[5]
-        first_mean = jnp.mean(scaled, axis=1, keepdims=True)
-        second_mean = jnp.mean(scaled * normed_two, axis=1, keepdims=True)
-        grad_mid = top_few.astype(F32) + inverse_two * (scaled - first_mean - normed_two * second_mean)
-        grad_mid_half = grad_mid.astype(BF16)
-        grad_attn = mm("rf,tf->rt", w_proj, grad_mid_half).astype(BF16)
-        natural = grad_attn.reshape(2, dps, cols // 2, n_rows, few).transpose(2, 0, 1, 3, 4)
-        natural = swapped(natural.reshape(cols, dps, n_rows, few), 1)
-        grad_abs = jnp.stack([at(natural, c ^ b) for b in range(cols)]).reshape(D, few)
-        grad_abs = jnp.pad(grad_abs, ((0, rows * wide - D), (0, 0))).reshape(slots, rows, HEAD_DIM, few)
-        grad_heads = unrolled(
-            row_exchange([at(grad_abs, (z + k) % rows, 1).reshape(wide, few) for k in range(rows)]), 1
-        )
-
-        act_near, act_far = after((act_near, act_far), up_part)
-        down_far = mm("th,fh->tf", act_far, w_down).astype(BF16)
-        down_near = mm("th,fh->tf", act_near, w_down).astype(BF16)
+        up_shift = lax.dynamic_slice_in_dim(up_bias, (c * dps + y) * hidden, hidden)[None, :]
+        act_near, pre_near, bias_near = hidden_units(h2_first, top_first, w_up, w_down, up_shift)
+        act_far, pre_far, bias_far = hidden_units(h2_second, top_second, w_up, w_down, up_shift)
+        bias_part = (bias_near + bias_far)[0]
+        back_far = features_back(pre_far, w_up)
+        back_received = core_send(back_far)
+        back_near = features_back(after(pre_near, back_far), w_up)
+        act_near, act_far, pre_near, pre_far, back_near, back_received = lax.optimization_barrier(
+            (act_near, act_far, pre_near, pre_far, back_near, back_received)
+        )
+
+        back_terms = plane_scatter(back_near, back_received, 0)
+        down_far = features_back(act_far, w_down)
         down_received = core_send(down_far)
-        down_terms = plane_scatter(after(down_near, grad_ln_two), down_received, 0)
-        middle_rows = len(even) * n_rows
-        proj_far = mm("rt,tf->rf", attn_few[middle_rows:], grad_mid_half).astype(BF16)
-        proj_near = mm("rt,tf->rf", attn_few[:middle_rows], grad_mid_half).astype(BF16)
-        proj_received = core_send(proj_far)
-        grad_heads, proj_received, proj_near, down_part, up_part, down_terms = lax.optimization_barrier(
-            (grad_heads, proj_received, proj_near, down_part, up_part, down_terms)
+        down_near = features_back(act_near, w_down)
+        up_part = weight_part([h2_first, h2_second], [pre_near, pre_far])
+        down_part = weight_part([top_first, top_second], [act_near, act_far])
+        back_terms, down_received, down_near, up_part, down_part = lax.optimization_barrier(
+            (back_terms, down_received, down_near, up_part, down_part)
         )
         up_sum = lax.psum_scatter(up_part, "row", scatter_dimension=0, tiled=True)
+
+        grad_mid_half, heads_out, mid_sums = project_back(
+            heads_table,
+            back_terms,
+            top_few,
+            mid,
+            mean_two,
+            inverse_two,
+            vectors[5][None, :],
+            proj_halves,
+            rows * wide,
+            unit,
+        )
+        down_terms = plane_scatter(after(down_near, grad_mid_half), down_received, 0)
+        head_pieces = row_exchange([heads_out[k * wide : (k + 1) * wide] for k in range(rows)])
+        proj_part = mm("rt,tf->rf", attn_few, grad_mid_half).astype(BF16)
+        head_pieces, proj_part, down_part = lax.optimization_barrier((head_pieces, proj_part, down_part))
+        proj_sum = lax.psum_scatter(proj_part, ("dp", "col"), scatter_dimension=0, tiled=True)
         down_sum_part = lax.psum_scatter(down_part, "row", scatter_dimension=0, tiled=True)
-        out_few = (mid + total_of(down_terms) + vectors[7]).astype(BF16)
-        proj_terms = plane_scatter(proj_near, proj_received, 0)
-        mid_pieces = row_exchange(chunks_of(grad_mid_half, 1))
+        grad_heads = unrolled(head_pieces, 1)
 
         far = attention_backward(me, start, query, far_kv, far_offsets, attn, lse, grad_heads)
+        far, down_terms = lax.optimization_barrier((far, down_terms))
         half_far = len(far_offsets) // 2
         far_grads = [jnp.concatenate(far[2 * i : 2 * i + 2], axis=0) for i in range(len(far_offsets))]
         far_value_total, carried_query = far[-2:]
+        far_received = [lax.ppermute(item, "col", swap_cores) for item in far_grads[half_far:]]
         far_sent = []
         for i in range(half_far):
             b = far_offsets[i]
-            both = far_grads[i].astype(F32) + lax.ppermute(far_grads[half_far + i], "col", swap_cores).astype(F32)
-            far_sent.append(
-                lax.ppermute(both.astype(BF16), "col", [(j, j ^ b) for j in range(cols) if (j ^ b) < j])
-            )
-        carried_query, mid_pieces = lax.optimization_barrier((carried_query, mid_pieces))
-        grad_mid_own = unrolled(mid_pieces, 0)
-        out_pieces = row_exchange(chunks_of(out_few, 1))
+            both = (far_grads[i].astype(F32) + far_received[i].astype(F32)).astype(BF16)
+            far_sent.append(lax.ppermute(both, "col", [(j, j ^ b) for j in range(cols) if (j ^ b) < j]))
+        out_few = (mid + total_of([item[:, :D] for item in down_terms]) + vectors[7]).astype(BF16)
+        side_rows = jnp.concatenate(
+            [grad_mid_half.T.reshape(rows, feats, few), out_few.T.reshape(rows, feats, few)], axis=1
+        )
+        sides = row_exchange([at(side_rows, (z + k) % rows) for k in range(rows)])
+
+        carried_query, _ = lax.optimization_barrier((carried_query, far_received))
         near = attention_backward(
             me, start, query, near_kv, near_offsets, attn, lse, grad_heads, carried_query
         )
-        near, far_sent, proj_terms, out_pieces = lax.optimization_barrier(
-            (near, far_sent, proj_terms, out_pieces)
-        )
-        block_out = unrolled(out_pieces, 0)
+        near, far_sent, sides, up_sum = lax.optimization_barrier((near, far_sent, sides, up_sum))
+        up_blocks = up_sum.reshape(dps, half, hidden)
+        up_back = dp_exchange([at(up_blocks, y ^ d) for d in range(dps)])
         near_value_total, grad_query, query_total = near[-3:]
         value_total = near_value_total + far_value_total
-        own_sum = jnp.concatenate(near[0:2], axis=0).astype(F32)
-        own_sum = own_sum + lax.ppermute(jnp.concatenate(near[2:4], axis=0), "col", swap_cores).astype(F32)
+        near_received = lax.ppermute(jnp.concatenate(near[2:4], axis=0), "col", swap_cores)
+        own_sum = jnp.concatenate(near[0:2], axis=0).astype(F32) + near_received.astype(F32)
         for item in far_sent:
             own_sum = own_sum + item.astype(F32)
-        proj_sum = total_of(proj_terms).astype(BF16)
         grad_qkv = jnp.concatenate([grad_query, own_sum.astype(BF16)], axis=0)
         finals = at(jnp.asarray(pack_final), z)
         finals = jnp.concatenate([at(finals, c ^ b) for b in offsets])
         grad_packed = move_units(finals, [grad_qkv], None, cols * packed, BF16)
-        proj_grad = row_reduce(chunks_of(proj_sum, 1))
+        grad_packed = lax.optimization_barrier(grad_packed)
 
         gain_one = vec_swap[0].reshape(dps, rows * half, 1)
-        part_half, sum_norm, sum_plain, stats = qkv_back(
+        near_cols = cols // 2 * packed
+        flat = (dps * (cols // 2), rows * half, packed)
+        part_half, sum_norm, sum_plain = qkv_back(
             halves, grad_packed, x_all, mean_one, inverse_one, gain_one, rows
         )
-        near_cols = cols // 2 * packed
+        ln_terms = [part_half[0]] + [to_row(part_half[k], k) for k in range(1, rows)]
+        grad_packed = after(grad_packed, part_half)
         qkv_far = qkv_weight_part(h1, grad_packed[near_cols:], cols // 2, packed)
+        qkv_received = core_send(qkv_far.reshape(flat))
+        grad_packed = after(grad_packed, qkv_far)
         qkv_near = qkv_weight_part(h1, grad_packed[:near_cols], cols // 2, packed)
-        stats = sum_rows(stats)
-        grad_ln_own = row_reduce([part_half[k] for k in range(rows)])
-        first_row, second_row = stats[0:1] / D, stats[1:2] / D
-        own_normed = normed_one.reshape(dps, rows, half, tokens)[:, 0]
-        own_gain = gain_one.reshape(dps, rows, half, 1)[:, 0]
-        inner = inverse_one * (grad_ln_own * own_gain - first_row - own_normed * second_row)
-        inner = swapped(inner, 0).reshape(feats, tokens).T
-        input_grad = (grad_mid_own.astype(F32) + inner).astype(BF16)
-
-        flat = (dps * (cols // 2), rows * half, packed)
-        qkv_sum = total_of(plane_scatter(qkv_near.reshape(flat), core_send(qkv_far.reshape(flat)), 0))
-        qkv_sum = qkv_sum[0].astype(BF16)
-        qkv_sum = qkv_sum.reshape(rows, half, packed)
-        qkv_home = jnp.concatenate(row_exchange([qkv_sum[k] for k in range(rows)]), axis=1)
-        qkv_grad = mm("fm,nm->fn", qkv_home, select)
-
-        up_sum, down_sum_part, _ = lax.optimization_barrier((up_sum, down_sum_part, part_half))
-        up_blocks = up_sum.reshape(dps, half, hidden)
-        up_back = dp_exchange([at(up_blocks, y ^ d) for d in range(dps)])
-        up_grad = swapped(jnp.stack(up_back), 0).transpose(1, 0, 2).reshape(half, dps * hidden).astype(F32)
+        qkv_terms = plane_scatter(qkv_near.reshape(flat), qkv_received, 0)
+        sum_norm, sum_plain, query_total, value_total, mid_sums, bias_part, top_own, up_back, _ = (
+            lax.optimization_barrier(
+                (sum_norm, sum_plain, query_total, value_total, mid_sums, bias_part, upstream, up_back, qkv_near)
+            )
+        )
 
         def back_from_rel(vector):
             blocks = vector.reshape(rows, feats)
@@ -807,23 +1045,44 @@
             mine = (jnp.arange(rows) == z)[None, :, None]
             return jnp.where(mine, blocks, 0.0).reshape(rows * wide)[:D]
 
-        top_sum = jnp.sum(upstream.astype(F32), axis=0)
-        parts = jnp.stack(
-            [
-                back_from_swap(sum_norm),
-                back_from_swap(sum_plain),
-                from_heads(query_total[:, 0]),
-                from_heads(value_total[:, 0]),
-                jnp.sum(grad_mid, axis=0),
-                jnp.sum(grad_ln_two * normed_two, axis=0),
-                jnp.sum(grad_ln_two, axis=0),
-                lax.dynamic_update_slice_in_dim(jnp.zeros((D,), F32), top_sum, z * feats, 0),
-            ]
-        )
-        bias_full = lax.dynamic_update_slice_in_dim(
-            jnp.zeros((up_bias.shape[0],), F32), bias_part, (c * dps + y) * hidden, 0
-        )
-        summed = sum_everywhere(jnp.concatenate([parts.reshape(-1), bias_full]))
+        def token_sums(sum_norm, sum_plain):
+            top_sum = jnp.sum(top_own.astype(F32), axis=0)
+            parts = jnp.stack(
+                [
+                    back_from_swap(sum_norm),
+                    back_from_swap(sum_plain),
+                    from_heads(query_total[:, 0]),
+                    from_heads(value_total[:, 0]),
+                    mid_sums[0],
+                    mid_sums[1],
+                    mid_sums[2],
+                    lax.dynamic_update_slice_in_dim(jnp.zeros((D,), F32), top_sum, z * feats, 0),
+                ]
+            )
+            bias_full = lax.dynamic_update_slice_in_dim(
+                jnp.zeros((up_bias.shape[0],), F32), bias_part, (c * dps + y) * hidden, 0
+            )
+            return jnp.concatenate([parts.reshape(-1), bias_full])
+
+        up_grad = swapped(jnp.stack(up_back), 0).transpose(1, 0, 2).reshape(half, dps * hidden).astype(F32)
+        vector_sums = token_sums(sum_norm, sum_plain)
+        qkv_terms, ln_terms, vector_sums, proj_sum = lax.optimization_barrier(
+            (qkv_terms, ln_terms, vector_sums, proj_sum)
+        )
+        qkv_sum = total_of(qkv_terms)[0].astype(BF16).reshape(rows, half, packed)
+
+        qkv_home = jnp.concatenate(row_exchange([qkv_sum[k] for k in range(rows)]), axis=1)
+        qkv_home, down_sum_part = lax.optimization_barrier((qkv_home, down_sum_part))
+        qkv_grad = mm("fm,nm->fn", qkv_home, select)
+        proj_cols = proj_sum.reshape(n_rows, rows, feats).transpose(1, 0, 2)
+        proj_grad = total_of(row_exchange([at(proj_cols, (z + k) % rows) for k in range(rows)]))
+        own_gain = gain_one.reshape(dps, rows, half, 1)[:, 0]
+        where = jnp.stack([((z + k) % rows) * few for k in range(rows)] + [y]).astype(jnp.int32)
+        input_grad, block_out = finish(where, ln_terms, x_own, mean_one, inverse_one, own_gain, sides)
+        input_grad, block_out = input_grad.T, block_out.T
+
+        vector_sums = vector_sums + lax.ppermute(vector_sums, "col", swap_cores)
+        summed = sum_everywhere(vector_sums)
         vector_grad = summed[: 8 * D].reshape(8, D)
         bias_grad = summed[8 * D :]
 

time: 646 us -> 601 us (0.930)
  waiting for transfers between devices: 282 us -> 200 us
  Pallas kernels: 55.6 us -> 117 us
  matrix products: 64.9 us -> 8.24 us
  local copies, waits for them, and re-layouts: 63.5 us -> 86.3 us
  starting transfers between devices: 102 us -> 124 us
  other arithmetic: 55.6 us -> 38.5 us
    pallas_call x2 -> x13, Pallas kernels: 2.23 us -> 60.6 us  [the longest x4 18.9 us: features_back(): pl.pallas_call(body, grid=(tokens // step,), in_specs=[pl.BlockSpec((step...]
    dot_general x18 -> x3, matrix products: 64.9 us -> 8.24 us  [mm(): return jnp.einsum(spec, left, right, preferred_element_type=F32)]
    ppermute x33 -> x30, waiting for transfers between devices: 163 us -> 126 us  [to_row(): lax.ppermute(values, 'row', [(i, (i + k) % rows) for i in range(rows)])]
    ppermute x4 -> x2, waiting for transfers between devices: 35.4 us -> 0.01 us  [the longest x1 0.01 us: per_device(): lax.ppermute(both, 'col', [(j, j ^ b) for j in range(cols) if j ^ b < j])]
    ppermute x32 -> x31, waiting for transfers between devices: 67 us -> 43 us  [to_plane(): lax.ppermute(values, ('dp', 'col'), [(y * cols + c, (y ^ d) * cols + (c ^...]
    ppermute x33 -> x30, starting transfers between devices: 48.9 us -> 71.6 us  [to_row(): lax.ppermute(values, 'row', [(i, (i + k) % rows) for i in range(rows)])]
    all_gather x1, waiting for transfers between devices: 0.01 us -> 10.4 us  [per_device(): w_down = lax.all_gather(down_rows, 'row', axis=0, tiled=True)]
    unnamed x249 -> x262, local copies, waits for them, and re-layouts: 26.2 us -> 36 us
  transfers between devices with their start and end apart: 84 -> 79, of which waited for: 33 -> 24; matrix products, arithmetic and copies ran while one was open for 22% -> 16% of each run, Pallas kernels for 8% -> 18%
where the time goes in v4:
time: 601 us; the launch traced here: 590 us
  waiting for transfers between devices  200 us (33%)
  starting transfers between devices  124 us (21%)
  Pallas kernels  117 us (19%)
  local copies, waits for them, and re-layouts  86.3 us (14%)
  other arithmetic  38.5 us (6%)
  between operations  16.2 us (3%)
  matrix products  8.24 us (1%)
    ppermute x30, waiting for transfers between devices, to_row(): lax.ppermute(values, 'row', [(i, (i + k) % rows) for i in range(rows)])  126 us
    ppermute x30, starting transfers between devices, to_row(): lax.ppermute(values, 'row', [(i, (i + k) % rows) for i in range(rows)])  71.6 us
    ppermute x31, waiting for transfers between devices, to_plane(): lax.ppermute(values, ('dp', 'col'), [(y * cols + c, (y ^ d) * cols + (c ^...  43 us
    ppermute x31, starting transfers between devices, to_plane(): lax.ppermute(values, ('dp', 'col'), [(y * cols + c, (y ^ d) * cols + (c ^...  37.1 us
    unnamed x262, local copies, waits for them, and re-layouts  36 us
    pallas_call x4, Pallas kernels, features_back(): pl.pallas_call(body, grid=(tokens // step,), in_specs=[pl.BlockSpec((step...  18.9 us
    pallas_call x2, Pallas kernels, attention_backward(): pl.pallas_call(body, grid=(slots,), in_specs=specs, out_specs=[head_spec]...  12.9 us
    pallas_call x2, Pallas kernels, hidden_units(): pl.pallas_call(body, grid=(tokens // step,), in_specs=[rows_in, rows_in,...  12.7 us
  transfers between devices with their start and end apart: 79, of which 24 were waited for; matrix products, arithmetic and copies ran while one was open for 16% of the time, Pallas kernels for 18%

profile of v4, /device:TPU:0, one launch (start us, length us, event | category | flops | bytes accessed | tf_op | source)
XLA Modules:
  0.0 590.1 jit_solution(1609846616696913739)
XLA Ops:
  11.1 5.1 collective-permute-start
  33.8 10.6 %collective-permute-start.8 = (bf16[2,200,512]{2,1,0:T(8,128)(2,1)S(1)}, bf16[2,200,512]{2,1,0:T(8,128)(2,1)S(1)}, u32[]{:S(2)}, u32[]{:S(2)}) collective-permute-start(bf16[2,200,512]{2,1,0:T(8,128)(2,1)S(1)} %pad_maximum_fusion.10.refs_4_), channel_id=1, source_target_pairs={{0,8},{4,12},{8,0},{12,4},{1,9},{5,13},{9,1},{13,5},{2,10},{6,14},... | collective-permute-start | bytes 1228808 | tf_op jit(solution)/shard_map/ppermute | solution.py:747
  45.2 24.9 %collective-permute-done.8 = bf16[2,200,512]{2,1,0:T(8,128)(2,1)S(1)} collective-permute-done((bf16[2,200,512]{2,1,0:T(8,128)(2,1)S(1)}, bf16[2,200,512]{2,1,0:T(8,128)(2,1)S(1)}, u32[]{:S(2)}, u32[]{:S(2)}) %collective-permute-start.8) | collective-permute-done | bytes 409632 | tf_op jit(solution)/shard_map/ppermute | solution.py:747
  93.4 21.8 %collective-permute-done.12 = bf16[200,400]{1,0:T(8,128)(2,1)} collective-permute-done((bf16[200,400]{1,0:T(8,128)(2,1)}, bf16[200,400]{1,0:T(8,128)(2,1)}, u32[]{:S(2)}, u32[]{:S(2)}) %collective-permute-start.12) | collective-permute-done | bytes 160032 | tf_op jit(solution)/shard_map/ppermute | solution.py:747
  122.0 6.2 %collective-permute-start.17 = (bf16[400,128]{1,0:T(8,128)(2,1)}, bf16[400,128]{1,0:T(8,128)(2,1)}, u32[]{:S(2)}, u32[]{:S(2)}) collective-permute-start(bf16[400,128]{1,0:T(8,128)(2,1)} %get-tuple-element.456), channel_id=1, source_target_pairs={{0,8},{4,12},{8,0},{12,4},{1,9},{5,13},{9,1},{13,5},{2,10},{6,14},... | collective-permute-start | bytes 307208 | tf_op jit(solution)/shard_map/ppermute | solution.py:747
  134.5 6.9 %attention_forward.2 = (f32[7,1,512]{2,1,0:T(1,128)S(1)}, f32[7,1,512]{2,1,0:T(1,128)S(1)}, f32[448,512]{1,0:T(8,128)S(1)}) custom-call(s32[1]{0:T(128)} %bitcast.31.me_ref, s32[1,512]{1,0:T(1,128)S(1)} %bitcast.241, bf16[448,512]{1,0:T(8,128)(2,1)S(1)} %slice.233.q_ref, bf16[896,512]{1,0:T(8,128)(2,1)} %slice.234.refs_0_.refs_1_, ...), custom_call_target="tpu_custom_call" | custom-call | flops 3849999872 | bytes 12100000 | tf_op jit(solution)/shard_map/attention_forward/pallas_call | solution.py:622
  142.3 5.0 collective-permute-done.17
  171.2 8.9 %collective-permute-done.25.refs_7_.refs_12_ = bf16[200,1600]{1,0:T(8,128)(2,1)} collective-permute-done((bf16[200,1600]{1,0:T(8,128)(2,1)S(1)}, bf16[200,1600]{1,0:T(8,128)(2,1)}, u32[]{:S(2)}, u32[]{:S(2)}) %collective-permute-start.25) | collective-permute-done | bytes 640032 | tf_op jit(solution)/shard_map/ppermute | solution.py:756
  180.1 8.1 %collective-permute-done.21.refs_2_ = bf16[448,128]{1,0:T(8,128)(2,1)S(1)} collective-permute-done((bf16[448,128]{1,0:T(8,128)(2,1)}, bf16[448,128]{1,0:T(8,128)(2,1)S(1)}, u32[]{:S(2)}, u32[]{:S(2)}) %collective-permute-start.21) | collective-permute-done | bytes 114720 | tf_op jit(solution)/shard_map/ppermute | solution.py:747
  189.9 7.0 %collective-permute-start.30 = (bf16[128,1664]{1,0:T(8,128)(2,1)S(1)}, bf16[128,1664]{1,0:T(8,128)(2,1)}, u32[]{:S(2)}, u32[]{:S(2)}) collective-permute-start(bf16[128,1664]{1,0:T(8,128)(2,1)S(1)} %pad.13.refs_4_), channel_id=1, source_target_pairs={{0,2},{1,3},{2,0},{3,1},{16,18},{17,19},{18,16},{19,17},{4,6},{5,7... | collective-permute-start | bytes 1277960 | tf_op jit(solution)/shard_map/ppermute | solution.py:756
  205.0 5.4 project.1
  212.0 10.4 %all-gather.5.cloned.1.call-done.down.w_ref = bf16[1600,800]{1,0:T(8,128)(2,1)} async-done(((bf16[400,800]{1,0:T(8,128)(2,1)}), bf16[1600,800]{1,0:T(8,128)(2,1)}) %all-gather.5.cloned.1.call-update) | async-done | bytes 2560016 | tf_op jit(solution)/shard_map/all_gather | solution.py:864
  230.9 9.2 %collective-permute-done.33 = bf16[128,1664]{1,0:T(8,128)(2,1)S(1)} collective-permute-done((bf16[128,1664]{1,0:T(8,128)(2,1)S(1)}, bf16[128,1664]{1,0:T(8,128)(2,1)S(1)}, u32[]{:S(2)}, u32[]{:S(2)}) %collective-permute-start.33) | collective-permute-done | bytes 426016 | tf_op jit(solution)/shard_map/ppermute | solution.py:756
  240.1 10.4 %collective-permute-done.34 = bf16[128,1664]{1,0:T(8,128)(2,1)S(1)} collective-permute-done((bf16[128,1664]{1,0:T(8,128)(2,1)S(1)}, bf16[128,1664]{1,0:T(8,128)(2,1)S(1)}, u32[]{:S(2)}, u32[]{:S(2)}) %collective-permute-start.34) | collective-permute-done | bytes 426016 | tf_op jit(solution)/shard_map/ppermute | solution.py:756
  260.2 6.3 %hidden_units.3 = (bf16[512,800]{1,0:T(8,128)(2,1)S(1)}, bf16[512,800]{1,0:T(8,128)(2,1)S(1)}, f32[1,800]{1,0:T(1,128)S(1)}) custom-call(bf16[512,1664]{1,0:T(8,128)(2,1)} %collective-permute-done.37.h_ref.refs_1_, bf16[512,1664]{1,0:T(8,128)(2,1)S(1)} %copy-done.9, bf16[1600,800]{1,0:T(8,128)(2,1)S(1)} %copy-done, ...), custom_call_target="tpu_custom_call" | custom-call | flops 2100000000 | bytes 6600000 | tf_op jit(solution)/shard_map/hidden_units/pallas_call | solution.py:425
  269.1 6.3 %hidden_units.2 = (bf16[512,800]{1,0:T(8,128)(2,1)S(1)}, bf16[512,800]{1,0:T(8,128)(2,1)S(1)}, f32[1,800]{1,0:T(1,128)S(1)}) custom-call(bf16[512,1664]{1,0:T(8,128)(2,1)} %constant_dynamic-update-slice_fusion.8.h_ref.refs_0_, bf16[512,1664]{1,0:T(8,128)(2,1)S(1)} %copy-done.5, bf16[1600,800]{1,0:T(8,128)(2,1)S(1)} %copy-done, ...), custom_call_target="tpu_custom_call" | custom-call | flops 2100000000 | bytes 6600000 | tf_op jit(solution)/shard_map/hidden_units/pallas_call | solution.py:425
  287.4 11.0 %features_back.7 = bf16[512,1664]{1,0:T(8,128)(2,1)S(1)} custom-call(bf16[512,800]{1,0:T(8,128)(2,1)S(1)} %get-tuple-element.268.g_ref.refs_2_, bf16[1600,800]{1,0:T(8,128)(2,1)S(1)} %copy-done.1), custom_call_target="tpu_custom_call" | custom-call | flops 700000000 | bytes 2200000 | tf_op jit(solution)/shard_map/features_back/pallas_call | solution.py:445
  298.5 5.3 weight_part.3
  304.9 7.2 %weight_part.2 = bf16[1600,800]{1,0:T(8,128)(2,1)} custom-call(bf16[512,1664]{1,0:T(8,128)(2,1)} %constant_dynamic-update-slice_fusion.8.h_ref.refs_0_, bf16[512,1664]{1,0:T(8,128)(2,1)} %collective-permute-done.37.h_ref.refs_1_, bf16[512,800]{1,0:T(8,128)(2,1)S(1)} %copy-done.19, bf16[512,800]{1,0:T(8,128)(2,1)S(1)} %copy-done.17), custom_call_target="tpu_custom_call" | custom-call | flops 1400000000 | bytes 4400000 | tf_op jit(solution)/shard_map/weight_part/pallas_call | solution.py:474
  315.4 6.3 %project_back.1 = (bf16[128,1600]{1,0:T(8,128)(2,1)S(1)}, bf16[1792,128]{1,0:T(8,128)(2,1)S(1)}, f32[3,1600]{1,0:T(4,128)S(1)}) custom-call(s32[224]{0:T(256)S(1)} %bitcast.240, f32[128,1664]{1,0:T(8,128)} %slice.305.refs_0_, bf16[128,1664]{1,0:T(8,128)(2,1)} %collective-permute-done.39.refs_1_, bf16[128,1664]{1,0:T(8,128)(2,1)} %collective-permute-done.40.refs_2_, ...), custom_call_target="tpu_custom_call" | custom-call | flops 1750000000 | bytes 5500000 | tf_op jit(solution)/shard_map/project_back/pallas_call | solution.py:382
  332.0 10.9 %collective-permute-done.44 = bf16[448,128]{1,0:T(8,128)(2,1)S(1)} collective-permute-done((bf16[448,128]{1,0:T(8,128)(2,1)S(1)}, bf16[448,128]{1,0:T(8,128)(2,1)S(1)}, u32[]{:S(2)}, u32[]{:S(2)}) %collective-permute-start.44) | collective-permute-done | bytes 114720 | tf_op jit(solution)/shard_map/ppermute | solution.py:747
  358.4 8.7 %collective-permute-done.47 = bf16[128,1664]{1,0:T(8,128)(2,1)S(1)} collective-permute-done((bf16[128,1664]{1,0:T(8,128)(2,1)S(1)}, bf16[128,1664]{1,0:T(8,128)(2,1)S(1)}, u32[]{:S(2)}, u32[]{:S(2)}) %collective-permute-start.47) | collective-permute-done | bytes 426016 | tf_op jit(solution)/shard_map/ppermute | solution.py:756
  377.0 5.3 collective-permute-start.52
  385.5 8.5 %attention_backward.3 = (bf16[448,512]{1,0:T(8,128)(2,1)S(1)}, bf16[448,512]{1,0:T(8,128)(2,1)S(1)}, bf16[448,512]{1,0:T(8,128)(2,1)S(1)}, bf16[448,512]{1,0:T(8...) custom-call(s32[1]{0:T(128)} %bitcast.31.me_ref, ...), custom_call_target="tpu_custom_call" | custom-call | flops 4899999744 | bytes 15400000 | tf_op jit(solution)/shard_map/attention_backward/pallas_call | solution.py:720
  396.2 4.7 collective-permute-done.52.refs_10_
  409.2 7.2 %qkv_back.1 = (bf16[4,2,208,512]{3,2,1,0:T(8,128)(2,1)}, f32[2,800,1]{2,1,0:T(8,128)S(1)}, f32[2,800,1]{2,1,0:T(8,128)S(1)}) custom-call(bf16[2,2,800,384]{3,2,1,0:T(8,128)(2,1)} %bitcast.37.w_ref.first, bf16[2,2,800,384]{3,2,1,0:T(8,128)(2,1)} %bitcast.38.w_ref.second, bf16[1536,512]{1,0:T(8,128)(2,1)S(1)} %move_units.3.g_ref, ...), custom_call_target="tpu_custom_call" | custom-call | flops 2449999872 | bytes 7700000 | tf_op jit(solution)/shard_map/qkv_back/pallas_call | solution.py:245
  430.5 7.8 %collective-permute-done.62 = bf16[200,800]{1,0:T(8,128)(2,1)} collective-permute-done((bf16[200,800]{1,0:T(8,128)(2,1)S(1)}, bf16[200,800]{1,0:T(8,128)(2,1)}, u32[]{:S(2)}, u32[]{:S(2)}) %collective-permute-start.62) | collective-permute-done | bytes 320032 | tf_op jit(solution)/shard_map/ppermute | solution.py:782
  472.7 19.7 %collective-permute-done.60.refs_2_ = bf16[2,208,512]{2,1,0:T(8,128)(2,1)} collective-permute-done((bf16[2,208,512]{2,1,0:T(8,128)(2,1)}, bf16[2,208,512]{2,1,0:T(8,128)(2,1)}, u32[]{:S(2)}, u32[]{:S(2)}) %collective-permute-start.60) | collective-permute-done | bytes 426016 | tf_op jit(solution)/shard_map/ppermute | solution.py:747
  492.4 14.3 %collective-permute-done.61.refs_3_ = bf16[2,208,512]{2,1,0:T(8,128)(2,1)S(1)} collective-permute-done((bf16[2,208,512]{2,1,0:T(8,128)(2,1)}, bf16[2,208,512]{2,1,0:T(8,128)(2,1)S(1)}, u32[]{:S(2)}, u32[]{:S(2)}) %collective-permute-start.61) | collective-permute-done | bytes 426016 | tf_op jit(solution)/shard_map/ppermute | solution.py:747
  510.1 6.2 %collective-permute-start.63 = (bf16[200,384]{1,0:T(8,128)(2,1)}, bf16[200,384]{1,0:T(8,128)(2,1)}, u32[]{:S(2)}, u32[]{:S(2)}) collective-permute-start(bf16[200,384]{1,0:T(8,128)(2,1)} %get-tuple-element.424), channel_id=1, source_target_pairs={{0,12},{4,0},{8,4},{12,8},{1,13},{5,1},{9,5},{13,9},{2,14},{6,2},{... | collective-permute-start | bytes 460808 | tf_op jit(solution)/shard_map/ppermute | solution.py:747
  516.3 12.2 %collective-permute-start.64 = (bf16[200,384]{1,0:T(8,128)(2,1)}, bf16[200,384]{1,0:T(8,128)(2,1)}, u32[]{:S(2)}, u32[]{:S(2)}) collective-permute-start(bf16[200,384]{1,0:T(8,128)(2,1)} %get-tuple-element.423), channel_id=1, source_target_pairs={{0,8},{4,12},{8,0},{12,4},{1,9},{5,13},{9,1},{13,5},{2,10},{6,14},... | collective-permute-start | bytes 460808 | tf_op jit(solution)/shard_map/ppermute | solution.py:747
  541.0 11.2 %collective-permute-done.64 = bf16[200,384]{1,0:T(8,128)(2,1)} collective-permute-done((bf16[200,384]{1,0:T(8,128)(2,1)}, bf16[200,384]{1,0:T(8,128)(2,1)}, u32[]{:S(2)}, u32[]{:S(2)}) %collective-permute-start.64) | collective-permute-done | bytes 153632 | tf_op jit(solution)/shard_map/ppermute | solution.py:747
  (596 shorter events, 275.0 us)
Async XLA Ops:
  7.2 149.8 %all-gather.3.cloned.1.call-start = ((), (), s32[]{:S(2)}) async-start(), calls=%async_computation.3 | async-start | bytes 3584000 | tf_op jit(solution)/shard_map/all_gather | solution.py:863
  30.3 39.7 %collective-permute-start.4 = (bf16[1,800,384]{2,1,0:T(8,128)(2,1)S(1)}, bf16[1,800,384]{2,1,0:T(8,128)(2,1)S(1)}, u32[]{:S(2)}, u32[]{:S(2)}) collective-permute-start(bf16[1,800,384]{2,1,0:T(8,128)(2,1)S(1)} %bitcast.248), channel_id=1, source_target_pairs={{0,2},{1,3},{2,0},{3,1},{16,18},{17,19},{18,16},{19,17},{4,6},{5,7... | collective-permute-start | bytes 1843208 | tf_op jit(solution)/shard_map/ppermute | solution.py:756
  31.8 38.2 %collective-permute-start.5 = (bf16[1,800,384]{2,1,0:T(8,128)(2,1)S(1)}, bf16[1,800,384]{2,1,0:T(8,128)(2,1)S(1)}, u32[]{:S(2)}, u32[]{:S(2)}) collective-permute-start(bf16[1,800,384]{2,1,0:T(8,128)(2,1)S(1)} %bitcast.249), channel_id=1, source_target_pairs={{0,16},{1,17},{2,18},{3,19},{16,0},{17,1},{18,2},{19,3},{4,20},{5,... | collective-permute-start | bytes 1843208 | tf_op jit(solution)/shard_map/ppermute | solution.py:756
  33.4 37.5 %collective-permute-start.6 = (bf16[1,800,384]{2,1,0:T(8,128)(2,1)S(1)}, bf16[1,800,384]{2,1,0:T(8,128)(2,1)S(1)}, u32[]{:S(2)}, u32[]{:S(2)}) collective-permute-start(bf16[1,800,384]{2,1,0:T(8,128)(2,1)S(1)} %bitcast.250), channel_id=1, source_target_pairs={{0,18},{1,19},{2,16},{3,17},{16,2},{17,3},{18,0},{19,1},{4,22},{5,... | collective-permute-start | bytes 1843208 | tf_op jit(solution)/shard_map/ppermute | solution.py:756
  33.8 36.2 %collective-permute-start.8 = (bf16[2,200,512]{2,1,0:T(8,128)(2,1)S(1)}, bf16[2,200,512]{2,1,0:T(8,128)(2,1)S(1)}, u32[]{:S(2)}, u32[]{:S(2)}) collective-permute-start(bf16[2,200,512]{2,1,0:T(8,128)(2,1)S(1)} %pad_maximum_fusion.10.refs_4_), channel_id=1, source_target_pairs={{0,8},{4,12},{8,0},{12,4},{1,9},{5,13},{9,1},{13,5},{2,10},{6,14},... | collective-permute-start | bytes 1228808 | tf_op jit(solution)/shard_map/ppermute | solution.py:747
  70.9 151.4 %all-gather.5.cloned.1.call-start = ((), (), s32[]{:S(2)}) async-start(), calls=%async_computation.4 | async-start | bytes 3584000 | tf_op jit(solution)/shard_map/all_gather | solution.py:864
  78.0 37.1 %collective-permute-start.12 = (bf16[200,400]{1,0:T(8,128)(2,1)}, bf16[200,400]{1,0:T(8,128)(2,1)}, u32[]{:S(2)}, u32[]{:S(2)}) collective-permute-start(bf16[200,400]{1,0:T(8,128)(2,1)} %convert_element_type.152), channel_id=1, source_target_pairs={{0,8},{4,12},{8,0},{12,4},{1,9},{5,13},{9,1},{13,5},{2,10},{6,14},... | collective-permute-start | bytes 480008 | tf_op jit(solution)/shard_map/ppermute | solution.py:747
  78.1 37.1 %collective-permute-start.13 = (bf16[200,400]{1,0:T(8,128)(2,1)}, bf16[200,400]{1,0:T(8,128)(2,1)}, u32[]{:S(2)}, u32[]{:S(2)}) collective-permute-start(bf16[200,400]{1,0:T(8,128)(2,1)} %convert_element_type.152), channel_id=1, source_target_pairs={{0,4},{4,8},{8,12},{12,0},{1,5},{5,9},{9,13},{13,1},{2,6},{6,10},{... | collective-permute-start | bytes 480008 | tf_op jit(solution)/shard_map/ppermute | solution.py:747
  116.1 31.2 %collective-permute-start.15 = (bf16[896,512]{1,0:T(8,128)(2,1)}, bf16[896,512]{1,0:T(8,128)(2,1)}, u32[]{:S(2)}, u32[]{:S(2)}) collective-permute-start(bf16[896,512]{1,0:T(8,128)(2,1)} %slice.234.refs_0_.refs_1_), channel_id=1, source_target_pairs={{0,2},{1,3},{4,6},{5,7},{8,10},{9,11},{12,14},{13,15},{16,18},{17,... | collective-permute-start | bytes 2752520 | tf_op jit(solution)/shard_map/ppermute | solution.py:900
  130.2 272.0 %reduce-scatter.6.cloned.1.call-start = ((), (), s32[]{:S(2)}) async-start(), calls=%async_computation.5 | async-start | bytes 3584000 | tf_op jit(solution)/shard_map/reduce_scatter | solution.py:959
  149.0 31.0 %collective-permute-start.25 = (bf16[200,1600]{1,0:T(8,128)(2,1)S(1)}, bf16[200,1600]{1,0:T(8,128)(2,1)}, u32[]{:S(2)}, u32[]{:S(2)}) collective-permute-start(bf16[200,1600]{1,0:T(8,128)(2,1)S(1)} %concatenate.60.refs_4_.refs_9_), channel_id=1, source_target_pairs={{0,18},{1,19},{2,16},{3,17},{16,2},{17,3},{18,0},{19,1},{4,22},{5,... | collective-permute-start | bytes 1920008 | tf_op jit(solution)/shard_map/ppermute | solution.py:756
  189.9 32.5 %collective-permute-start.30 = (bf16[128,1664]{1,0:T(8,128)(2,1)S(1)}, bf16[128,1664]{1,0:T(8,128)(2,1)}, u32[]{:S(2)}, u32[]{:S(2)}) collective-permute-start(bf16[128,1664]{1,0:T(8,128)(2,1)S(1)} %pad.13.refs_4_), channel_id=1, source_target_pairs={{0,2},{1,3},{2,0},{3,1},{16,18},{17,19},{18,16},{19,17},{4,6},{5,7... | collective-permute-start | bytes 1277960 | tf_op jit(solution)/shard_map/ppermute | solution.py:756
  281.1 31.1 %collective-permute-start.42 = (bf16[512,1664]{1,0:T(8,128)(2,1)}, bf16[512,1664]{1,0:T(8,128)(2,1)}, u32[]{:S(2)}, u32[]{:S(2)}) collective-permute-start(bf16[512,1664]{1,0:T(8,128)(2,1)} %features_back.6), channel_id=1, source_target_pairs={{0,1},{1,0},{2,3},{3,2},{16,17},{17,16},{18,19},{19,18},{4,5},{5,4... | collective-permute-start | bytes 5111816 | tf_op jit(solution)/shard_map/ppermute | solution.py:756
  283.0 29.2 %collective-permute-start.39 = (bf16[128,1664]{1,0:T(8,128)(2,1)}, bf16[128,1664]{1,0:T(8,128)(2,1)}, u32[]{:S(2)}, u32[]{:S(2)}) collective-permute-start(bf16[128,1664]{1,0:T(8,128)(2,1)} %get-tuple-element.398), channel_id=1, source_target_pairs={{0,2},{1,3},{2,0},{3,1},{16,18},{17,19},{18,16},{19,17},{4,6},{5,7... | collective-permute-start | bytes 1277960 | tf_op jit(solution)/shard_map/ppermute | solution.py:756
  284.2 28.0 %collective-permute-start.40 = (bf16[128,1664]{1,0:T(8,128)(2,1)}, bf16[128,1664]{1,0:T(8,128)(2,1)}, u32[]{:S(2)}, u32[]{:S(2)}) collective-permute-start(bf16[128,1664]{1,0:T(8,128)(2,1)} %get-tuple-element.397), channel_id=1, source_target_pairs={{0,16},{1,17},{2,18},{3,19},{16,0},{17,1},{18,2},{19,3},{4,20},{5,... | collective-permute-start | bytes 1277960 | tf_op jit(solution)/shard_map/ppermute | solution.py:756
  284.7 27.4 %collective-permute-start.41 = (bf16[128,1664]{1,0:T(8,128)(2,1)}, bf16[128,1664]{1,0:T(8,128)(2,1)}, u32[]{:S(2)}, u32[]{:S(2)}) collective-permute-start(bf16[128,1664]{1,0:T(8,128)(2,1)} %get-tuple-element.396), channel_id=1, source_target_pairs={{0,18},{1,19},{2,16},{3,17},{16,2},{17,3},{18,0},{19,1},{4,22},{5,... | collective-permute-start | bytes 1277960 | tf_op jit(solution)/shard_map/ppermute | solution.py:756
  312.2 195.2 %reduce-scatter.10.cloned.1.call-start = ((), (), s32[]{:S(2)}) async-start(), calls=%async_computation.7 | async-start | bytes 5990400
  343.6 212.1 %reduce-scatter.8.cloned.1.call-start = ((), (), s32[]{:S(2)}) async-start(), calls=%async_computation.6 | async-start | bytes 3584000 | tf_op jit(solution)/shard_map/reduce_scatter | solution.py:978
  373.3 29.0 %collective-permute-start.50 = (bf16[896,512]{1,0:T(8,128)(2,1)}, bf16[896,512]{1,0:T(8,128)(2,1)}, u32[]{:S(2)}, u32[]{:S(2)}) collective-permute-start(bf16[896,512]{1,0:T(8,128)(2,1)} %add_convert_fusion.2), channel_id=1, source_target_pairs={{2,0},{3,1},{6,4},{7,5},{10,8},{11,9},{14,12},{15,13},{18,16},{19,... | collective-permute-start | bytes 2752520 | tf_op jit(solution)/shard_map/ppermute | solution.py:991
  420.1 25.8 %collective-permute-start.55 = (bf16[4,800,384]{2,1,0:T(8,128)(2,1)}, bf16[4,800,384]{2,1,0:T(8,128)(2,1)}, u32[]{:S(2)}, u32[]{:S(2)}) collective-permute-start(bf16[4,800,384]{2,1,0:T(8,128)(2,1)} %bitcast.93), channel_id=1, source_target_pairs={{0,1},{1,0},{2,3},{3,2},{16,17},{17,16},{18,19},{19,18},{4,5},{5,4... | collective-permute-start | bytes 7372808 | tf_op jit(solution)/shard_map/ppermute | solution.py:756
  443.7 48.7 %collective-permute-start.60 = (bf16[2,208,512]{2,1,0:T(8,128)(2,1)}, bf16[2,208,512]{2,1,0:T(8,128)(2,1)}, u32[]{:S(2)}, u32[]{:S(2)}) collective-permute-start(bf16[2,208,512]{2,1,0:T(8,128)(2,1)} %get-tuple-element.390), channel_id=1, source_target_pairs={{0,8},{4,12},{8,0},{12,4},{1,9},{5,13},{9,1},{13,5},{2,10},{6,14},... | collective-permute-start | bytes 1277960 | tf_op jit(solution)/shard_map/ppermute | solution.py:747
  451.7 55.8 %collective-permute-start.56 = (bf16[1,800,384]{2,1,0:T(8,128)(2,1)}, bf16[1,800,384]{2,1,0:T(8,128)(2,1)}, u32[]{:S(2)}, u32[]{:S(2)}) collective-permute-start(bf16[1,800,384]{2,1,0:T(8,128)(2,1)} %get-tuple-element.388), channel_id=1, source_target_pairs={{0,2},{1,3},{2,0},{3,1},{16,18},{17,19},{18,16},{19,17},{4,6},{5,7... | collective-permute-start | bytes 1843208 | tf_op jit(solution)/shard_map/ppermute | solution.py:756
  456.3 51.2 %collective-permute-start.57 = (bf16[1,800,384]{2,1,0:T(8,128)(2,1)}, bf16[1,800,384]{2,1,0:T(8,128)(2,1)}, u32[]{:S(2)}, u32[]{:S(2)}) collective-permute-start(bf16[1,800,384]{2,1,0:T(8,128)(2,1)} %get-tuple-element.387), channel_id=1, source_target_pairs={{0,16},{1,17},{2,18},{3,19},{16,0},{17,1},{18,2},{19,3},{4,20},{5,... | collective-permute-start | bytes 1843208 | tf_op jit(solution)/shard_map/ppermute | solution.py:756
  457.3 50.2 %collective-permute-start.58 = (bf16[1,800,384]{2,1,0:T(8,128)(2,1)}, bf16[1,800,384]{2,1,0:T(8,128)(2,1)}, u32[]{:S(2)}, u32[]{:S(2)}) collective-permute-start(bf16[1,800,384]{2,1,0:T(8,128)(2,1)} %get-tuple-element.386), channel_id=1, source_target_pairs={{0,18},{1,19},{2,16},{3,17},{16,2},{17,3},{18,0},{19,1},{4,22},{5,... | collective-permute-start | bytes 1843208 | tf_op jit(solution)/shard_map/ppermute | solution.py:756
  463.7 43.0 %collective-permute-start.61 = (bf16[2,208,512]{2,1,0:T(8,128)(2,1)}, bf16[2,208,512]{2,1,0:T(8,128)(2,1)S(1)}, u32[]{:S(2)}, u32[]{:S(2)}) collective-permute-start(bf16[2,208,512]{2,1,0:T(8,128)(2,1)} %get-tuple-element.389), channel_id=1, source_target_pairs={{0,12},{4,0},{8,4},{12,8},{1,13},{5,1},{9,5},{13,9},{2,14},{6,2},{... | collective-permute-start | bytes 1277960 | tf_op jit(solution)/shard_map/ppermute | solution.py:747
  507.5 31.4 %collective-permute-start.69 = (f32[19200]{0:T(1024)S(1)}, f32[19200]{0:T(1024)S(1)}, u32[]{:S(2)}, u32[]{:S(2)}) collective-permute-start(f32[19200]{0:T(1024)S(1)} %pad_maximum_fusion.14), channel_id=1, source_target_pairs={{0,1},{1,0},{2,3},{3,2},{4,5},{5,4},{6,7},{7,6},{8,9},{9,8},{10,11... | collective-permute-start | bytes 230408 | tf_op jit(solution)/shard_map/ppermute | solution.py:1084
  510.1 28.8 %collective-permute-start.63 = (bf16[200,384]{1,0:T(8,128)(2,1)}, bf16[200,384]{1,0:T(8,128)(2,1)}, u32[]{:S(2)}, u32[]{:S(2)}) collective-permute-start(bf16[200,384]{1,0:T(8,128)(2,1)} %get-tuple-element.424), channel_id=1, source_target_pairs={{0,12},{4,0},{8,4},{12,8},{1,13},{5,1},{9,5},{13,9},{2,14},{6,2},{... | collective-permute-start | bytes 460808 | tf_op jit(solution)/shard_map/ppermute | solution.py:747
  516.3 36.0 %collective-permute-start.64 = (bf16[200,384]{1,0:T(8,128)(2,1)}, bf16[200,384]{1,0:T(8,128)(2,1)}, u32[]{:S(2)}, u32[]{:S(2)}) collective-permute-start(bf16[200,384]{1,0:T(8,128)(2,1)} %get-tuple-element.423), channel_id=1, source_target_pairs={{0,8},{4,12},{8,0},{12,4},{1,9},{5,13},{9,1},{13,5},{2,10},{6,14},... | collective-permute-start | bytes 460808 | tf_op jit(solution)/shard_map/ppermute | solution.py:747
  528.5 25.9 %collective-permute-start.65 = (bf16[200,384]{1,0:T(8,128)(2,1)}, bf16[200,384]{1,0:T(8,128)(2,1)}, u32[]{:S(2)}, u32[]{:S(2)}) collective-permute-start(bf16[200,384]{1,0:T(8,128)(2,1)} %get-tuple-element.422), channel_id=1, source_target_pairs={{0,4},{4,8},{8,12},{12,0},{1,5},{5,9},{9,13},{13,1},{2,6},{6,10},{... | collective-permute-start | bytes 460808 | tf_op jit(solution)/shard_map/ppermute | solution.py:747
  532.3 37.9 %collective-permute-start.66 = (bf16[200,400]{1,0:T(8,128)(2,1)}, bf16[200,400]{1,0:T(8,128)(2,1)}, u32[]{:S(2)}, u32[]{:S(2)}) collective-permute-start(bf16[200,400]{1,0:T(8,128)(2,1)} %bitcast.227), channel_id=1, source_target_pairs={{0,12},{4,0},{8,4},{12,8},{1,13},{5,1},{9,5},{13,9},{2,14},{6,2},{... | collective-permute-start | bytes 480008 | tf_op jit(solution)/shard_map/ppermute | solution.py:747
  538.9 31.3 %collective-permute-start.67 = (bf16[200,400]{1,0:T(8,128)(2,1)S(1)}, bf16[200,400]{1,0:T(8,128)(2,1)S(1)}, u32[]{:S(2)}, u32[]{:S(2)}) collective-permute-start(bf16[200,400]{1,0:T(8,128)(2,1)S(1)} %bitcast.280), channel_id=1, source_target_pairs={{0,8},{4,12},{8,0},{12,4},{1,9},{5,13},{9,1},{13,5},{2,10},{6,14},... | collective-permute-start | bytes 480008 | tf_op jit(solution)/shard_map/ppermute | solution.py:747
  538.9 31.2 %collective-permute-start.68 = (bf16[200,400]{1,0:T(8,128)(2,1)S(1)}, bf16[200,400]{1,0:T(8,128)(2,1)S(1)}, u32[]{:S(2)}, u32[]{:S(2)}) collective-permute-start(bf16[200,400]{1,0:T(8,128)(2,1)S(1)} %bitcast.279), channel_id=1, source_target_pairs={{0,4},{4,8},{8,12},{12,0},{1,5},{5,9},{9,13},{13,1},{2,6},{6,10},{... | collective-permute-start | bytes 480008 | tf_op jit(solution)/shard_map/ppermute | solution.py:747
  (171 other events, 1657.1 us)
Sparse Core Ops, SparseCore 0:
  71.0 81.0 all-gather.2
  154.3 67.9 all-gather.4
  312.3 60.9 reduce-scatter.5
  376.6 67.9 reduce-scatter.9
  446.9 76.4 reduce-scatter.7

commit v5 on v4

--- a/solution.py
+++ b/solution.py
@@ -34,10 +34,6 @@
     return pl.CostEstimate(
         flops=int(micros * 0.35e9), bytes_accessed=int(micros * 1.1e6), transcendentals=0
     )
-
-
-def after(values, event):
-    return lax.optimization_barrier((values, event))[0]
 
 
 def mm(spec, left, right):
@@ -392,20 +388,20 @@
     )(table, *args)
 
 
-def hidden_units(h2_rows, top_rows, w_up, w_down, shift):
+def hidden_units(h2_rows, top_rows, weights, shift):
     tokens = h2_rows.shape[0]
-    hidden = w_up.shape[1]
+    row_devices, _, feats, hidden = weights.shape
     step = min(tokens, 256)
 
     def body(h_ref, t_ref, up, down, shift_ref, act_ref, grad_ref, sum_ref):
-        pre = dot_nn(h_ref[:, :D], up[...]) + shift_ref[...]
+        pre = dot_nn(h_ref[:, :D], up[:, 0].reshape(D, hidden)) + shift_ref[...]
         square = pre * pre
         tanh_val = jnp.tanh(GELU_COEF * (pre + GELU_CUBE * pre * square))
         act_ref[...] = (0.5 * pre * (1.0 + tanh_val)).astype(BF16)
         slope = 0.5 * (1.0 + tanh_val) + 0.5 * pre * (1.0 - tanh_val * tanh_val) * GELU_COEF * (
             1.0 + 3.0 * GELU_CUBE * square
         )
-        grad = dot_nn(t_ref[:, :D], down[...]) * slope
+        grad = dot_nn(t_ref[:, :D], down[:, 0].reshape(D, hidden)) * slope
         grad_ref[...] = grad.astype(BF16)
         now = jnp.sum(grad, axis=0, keepdims=True)
 
@@ -418,28 +414,30 @@
             sum_ref[...] += now
 
     rows_in = pl.BlockSpec((step, WIDE), lambda i: (i, 0))
-    weight = pl.BlockSpec((D, hidden), lambda i: (0, 0))
+    up_weight = pl.BlockSpec((row_devices, 1, feats, hidden), lambda i: (0, 0, 0, 0))
+    down_weight = pl.BlockSpec((row_devices, 1, feats, hidden), lambda i: (0, 1, 0, 0))
     rows_out = pl.BlockSpec((step, hidden), lambda i: (i, 0))
     line = pl.BlockSpec((1, hidden), lambda i: (0, 0))
     flat = jax.ShapeDtypeStruct((tokens, hidden), BF16)
     return pl.pallas_call(
         body,
         grid=(tokens // step,),
-        in_specs=[rows_in, rows_in, weight, weight, line],
+        in_specs=[rows_in, rows_in, up_weight, down_weight, line],
         out_specs=[rows_out, rows_out, line],
         out_shape=[flat, flat, jax.ShapeDtypeStruct((1, hidden), F32)],
         compiler_params=pltpu.CompilerParams(vmem_limit_bytes=44 * 2**20),
         cost_estimate=cost(6),
         name="hidden_units",
-    )(h2_rows, top_rows, w_up, w_down, shift)
-
-
-def features_back(grads, weight):
+    )(h2_rows, top_rows, weights, weights, shift)
+
+
+def features_back(grads, weights, which):
     tokens, hidden = grads.shape
+    row_devices, _, feats, _ = weights.shape
 
     def body(g_ref, w_ref, out):
         out[...] = jnp.zeros_like(out)
-        out[:, :D] = dot_nt(g_ref[...], w_ref[...]).astype(BF16)
+        out[:, :D] = dot_nt(g_ref[...], w_ref[:, 0].reshape(D, hidden)).astype(BF16)
 
     step = min(tokens, 256)
     return pl.pallas_call(
@@ -447,39 +445,48 @@
         grid=(tokens // step,),
         in_specs=[
             pl.BlockSpec((step, hidden), lambda i: (i, 0)),
-            pl.BlockSpec((D, hidden), lambda i: (0, 0)),
+            pl.BlockSpec((row_devices, 1, feats, hidden), lambda i: (0, which, 0, 0)),
         ],
         out_specs=pl.BlockSpec((step, WIDE), lambda i: (i, 0)),
         out_shape=jax.ShapeDtypeStruct((tokens, WIDE), BF16),
         compiler_params=pltpu.CompilerParams(vmem_limit_bytes=32 * 2**20),
         cost_estimate=cost(2),
         name="features_back",
-    )(grads, weight)
-
-
-def weight_part(rows_in, grads):
-    n = len(rows_in)
-    hidden = grads[0].shape[1]
+    )(grads, weights)
+
+
+def weight_parts(pairs, row_devices):
+    n = len(pairs[0][0])
+    hidden = pairs[0][1][0].shape[1]
+    feats = D // row_devices
 
     def body(*refs):
-        parts, values, out = refs[:n], refs[n : 2 * n], refs[2 * n]
-        for low in range(0, D, 256):
-            lanes = slice(low, min(low + 256, D))
-            total = dot_tn(parts[0][:, lanes], values[0][...])
-            for part, value in zip(parts[1:], values[1:]):
-                total = total + dot_tn(part[:, lanes], value[...])
-            out[lanes, :] = total.astype(BF16)
-
-    shape = jax.ShapeDtypeStruct((D, hidden), BF16)
-    return pl.pallas_call(
-        body,
-        in_specs=[pl.BlockSpec(memory_space=pltpu.VMEM)] * (2 * n),
-        out_specs=pl.BlockSpec(memory_space=pltpu.VMEM),
-        out_shape=shape,
+        out = refs[-1]
+        for which in range(2):
+            parts = refs[2 * n * which : 2 * n * which + n]
+            values = refs[2 * n * which + n : 2 * n * which + 2 * n]
+            for low in range(0, D, 256):
+                high = min(low + 256, D)
+                total = dot_tn(parts[0][:, low:high], values[0][...])
+                for part, value in zip(parts[1:], values[1:]):
+                    total = total + dot_tn(part[:, low:high], value[...])
+                place = low
+                while place < high:
+                    k = place // feats
+                    end = min(high, (k + 1) * feats)
+                    out[k, which, place - k * feats : end - k * feats, :] = total[place - low : end - low].astype(BF16)
+                    place = end
+
+    vmem = pl.BlockSpec(memory_space=pltpu.VMEM)
+    return pl.pallas_call(
+        body,
+        in_specs=[vmem] * (4 * n),
+        out_specs=vmem,
+        out_shape=jax.ShapeDtypeStruct((row_devices, 2, feats, hidden), BF16),
         compiler_params=pltpu.CompilerParams(vmem_limit_bytes=48 * 2**20),
-        cost_estimate=cost(4),
-        name="weight_part",
-    )(*rows_in, *grads)
+        cost_estimate=cost(9),
+        name="weight_parts",
+    )(*pairs[0][0], *pairs[0][1], *pairs[1][0], *pairs[1][1])
 
 
 def finish(where, terms, x_own, mean, inverse, gain, sides):
@@ -849,19 +856,22 @@
         ).astype(BF16)
         sorted_cols = mm("fn,nm->fm", qkv_weight.astype(BF16), select).astype(BF16)
         arrived = row_exchange([sorted_cols[:, k * packed : (k + 1) * packed] for k in range(rows)])
+        top_pieces = row_exchange(chunks_of(upstream.T, 1))
         up_parts = up_weight.astype(BF16).reshape(half, dps, hidden).transpose(1, 0, 2)
         up_arrived = dp_exchange([at(up_parts, y ^ d) for d in range(dps)])
         up_rows = swapped(jnp.stack(up_arrived), 0).reshape(feats, hidden)
-        arrived, up_rows, down_rows = lax.optimization_barrier((arrived, up_rows, down_weight.astype(BF16).T))
+        arrived, up_rows, down_rows, top_pieces = lax.optimization_barrier(
+            (arrived, up_rows, down_weight.astype(BF16).T, top_pieces)
+        )
 
         x_own = swapped(hidden_in.T.reshape(dps, half, tokens), 0)
         qkv_sent = plane_send(jnp.stack(arrived).reshape(1, rows * half, packed))
         x_pieces = row_gather(x_own)
-        qkv_sent, x_pieces, proj_own, upstream_late, up_rows, down_rows = lax.optimization_barrier(
-            (qkv_sent, x_pieces, proj_weight.astype(BF16), upstream, up_rows, down_rows)
-        )
-        w_up = lax.all_gather(up_rows, "row", axis=0, tiled=True)
-        w_down = lax.all_gather(down_rows, "row", axis=0, tiled=True)
+        both_rows = jnp.concatenate([up_rows, down_rows], axis=0)
+        qkv_sent, x_pieces, proj_own, both_rows = lax.optimization_barrier(
+            (qkv_sent, x_pieces, proj_weight.astype(BF16), both_rows)
+        )
+        w_both = lax.all_gather(both_rows, "row", axis=0, tiled=True).reshape(rows, 2, feats, hidden)
 
         proj_pieces = row_gather(proj_own)
         qkv_first = jnp.concatenate(qkv_sent, axis=0)
@@ -901,7 +911,6 @@
             for b in range(2, cols, 2)
         ]
         near_kv = [own_kv, lax.ppermute(own_kv, "col", swap_cores)]
-        top_pieces = row_exchange(chunks_of(upstream_late.T, 1))
         carried = attention_forward(me, start, query, near_kv, near_offsets)
         proj_rows = unrolled(proj_pieces, 1)
         carried, far_near, top_pieces, proj_rows = lax.optimization_barrier(
@@ -911,7 +920,7 @@
         far_kv = far_near + [lax.ppermute(item, "col", swap_cores) for item in far_near]
         proj_sent = plane_send(proj_rows)
         attn, lse = attention_forward(me, start, query, far_kv, far_offsets, carried)
-        attn, w_up, top_pieces, x_late = lax.optimization_barrier((attn, w_up, top_pieces, x_all))
+        attn, top_pieces, x_late = lax.optimization_barrier((attn, top_pieces, x_all))
 
         attn_pieces = row_exchange(chunks_of(attn, 1))
         x_few = lax.dynamic_slice_in_dim(x_late, z * few, few, 2).reshape(dps, rows, half, few)
@@ -928,35 +937,38 @@
         attn_few, mid, h2, mean_two, inverse_two = project(
             weight_table, at(jnp.asarray(to_plain), z), attn_pieces, proj_halves, x_few, jnp.stack([vectors[4], vectors[5], vectors[6]]), unit
         )
-        h2, top_sent, w_down = lax.optimization_barrier((h2, top_sent, w_down))
+        h2, top_sent = lax.optimization_barrier((h2, top_sent))
 
         top_first = jnp.concatenate(top_sent, axis=0)
         top_second = core_send(top_first)
-        h2_sent, top_second = lax.optimization_barrier((plane_send(h2), top_second))
+        h2_sent, top_second, w_both = lax.optimization_barrier((plane_send(h2), top_second, w_both))
 
         h2_first = jnp.concatenate(h2_sent, axis=0)
         h2_second = core_send(h2_first)
         up_shift = lax.dynamic_slice_in_dim(up_bias, (c * dps + y) * hidden, hidden)[None, :]
-        act_near, pre_near, bias_near = hidden_units(h2_first, top_first, w_up, w_down, up_shift)
-        act_far, pre_far, bias_far = hidden_units(h2_second, top_second, w_up, w_down, up_shift)
+        act_near, pre_near, bias_near = hidden_units(h2_first, top_first, w_both, up_shift)
+        act_far, pre_far, bias_far = hidden_units(h2_second, top_second, w_both, up_shift)
         bias_part = (bias_near + bias_far)[0]
-        back_far = features_back(pre_far, w_up)
+        back_far = features_back(pre_far, w_both, 0)
         back_received = core_send(back_far)
-        back_near = features_back(after(pre_near, back_far), w_up)
+        back_near = features_back(pre_near, w_both, 0)
         act_near, act_far, pre_near, pre_far, back_near, back_received = lax.optimization_barrier(
             (act_near, act_far, pre_near, pre_far, back_near, back_received)
         )
 
         back_terms = plane_scatter(back_near, back_received, 0)
-        down_far = features_back(act_far, w_down)
+        down_far = features_back(act_far, w_both, 1)
         down_received = core_send(down_far)
-        down_near = features_back(act_near, w_down)
-        up_part = weight_part([h2_first, h2_second], [pre_near, pre_far])
-        down_part = weight_part([top_first, top_second], [act_near, act_far])
-        back_terms, down_received, down_near, up_part, down_part = lax.optimization_barrier(
-            (back_terms, down_received, down_near, up_part, down_part)
-        )
-        up_sum = lax.psum_scatter(up_part, "row", scatter_dimension=0, tiled=True)
+        down_near = features_back(act_near, w_both, 1)
+        both_part = weight_parts(
+            [([h2_first, h2_second], [pre_near, pre_far]), ([top_first, top_second], [act_near, act_far])], rows
+        )
+        back_terms, down_received, down_near, both_part = lax.optimization_barrier(
+            (back_terms, down_received, down_near, both_part)
+        )
+        both_sum = lax.psum_scatter(
+            both_part.reshape(rows * 2 * feats, hidden), "row", scatter_dimension=0, tiled=True
+        )
 
         grad_mid_half, heads_out, mid_sums = project_back(
             heads_table,
@@ -970,12 +982,11 @@
             rows * wide,
             unit,
         )
-        down_terms = plane_scatter(after(down_near, grad_mid_half), down_received, 0)
+        down_terms = plane_scatter(down_near, down_received, 0)
         head_pieces = row_exchange([heads_out[k * wide : (k + 1) * wide] for k in range(rows)])
         proj_part = mm("rt,tf->rf", attn_few, grad_mid_half).astype(BF16)
-        head_pieces, proj_part, down_part = lax.optimization_barrier((head_pieces, proj_part, down_part))
+        head_pieces, proj_part = lax.optimization_barrier((head_pieces, proj_part))
         proj_sum = lax.psum_scatter(proj_part, ("dp", "col"), scatter_dimension=0, tiled=True)
-        down_sum_part = lax.psum_scatter(down_part, "row", scatter_dimension=0, tiled=True)
         grad_heads = unrolled(head_pieces, 1)
 
         far = attention_backward(me, start, query, far_kv, far_offsets, attn, lse, grad_heads)
@@ -999,9 +1010,7 @@
         near = attention_backward(
             me, start, query, near_kv, near_offsets, attn, lse, grad_heads, carried_query
         )
-        near, far_sent, sides, up_sum = lax.optimization_barrier((near, far_sent, sides, up_sum))
-        up_blocks = up_sum.reshape(dps, half, hidden)
-        up_back = dp_exchange([at(up_blocks, y ^ d) for d in range(dps)])
+        near, far_sent, sides = lax.optimization_barrier((near, far_sent, sides))
         near_value_total, grad_query, query_total = near[-3:]
         value_total = near_value_total + far_value_total
         near_received = lax.ppermute(jnp.concatenate(near[2:4], axis=0), "col", swap_cores)
@@ -1020,18 +1029,18 @@
         part_half, sum_norm, sum_plain = qkv_back(
             halves, grad_packed, x_all, mean_one, inverse_one, gain_one, rows
         )
+        part_half, grad_packed = lax.optimization_barrier((part_half, grad_packed))
         ln_terms = [part_half[0]] + [to_row(part_half[k], k) for k in range(1, rows)]
-        grad_packed = after(grad_packed, part_half)
         qkv_far = qkv_weight_part(h1, grad_packed[near_cols:], cols // 2, packed)
         qkv_received = core_send(qkv_far.reshape(flat))
-        grad_packed = after(grad_packed, qkv_far)
         qkv_near = qkv_weight_part(h1, grad_packed[:near_cols], cols // 2, packed)
+        sum_norm, sum_plain, query_total, value_total, mid_sums, bias_part, top_own, qkv_near = (
+            lax.optimization_barrier(
+                (sum_norm, sum_plain, query_total, value_total, mid_sums, bias_part, upstream, qkv_near)
+            )
+        )
         qkv_terms = plane_scatter(qkv_near.reshape(flat), qkv_received, 0)
-        sum_norm, sum_plain, query_total, value_total, mid_sums, bias_part, top_own, up_back, _ = (
-            lax.optimization_barrier(
-                (sum_norm, sum_plain, query_total, value_total, mid_sums, bias_part, upstream, up_back, qkv_near)
-            )
-        )
+        up_home, down_sum_part = both_sum[:feats], both_sum[feats:]
 
         def back_from_rel(vector):
             blocks = vector.reshape(rows, feats)
@@ -1064,16 +1073,19 @@
             )
             return jnp.concatenate([parts.reshape(-1), bias_full])
 
+        vector_sums = token_sums(sum_norm, sum_plain)
+        qkv_terms, ln_terms, vector_sums, up_home = lax.optimization_barrier(
+            (qkv_terms, ln_terms, vector_sums, up_home)
+        )
+        up_blocks = up_home.reshape(dps, half, hidden)
+        up_back = dp_exchange([at(up_blocks, y ^ d) for d in range(dps)])
         up_grad = swapped(jnp.stack(up_back), 0).transpose(1, 0, 2).reshape(half, dps * hidden).astype(F32)
-        vector_sums = token_sums(sum_norm, sum_plain)
-        qkv_terms, ln_terms, vector_sums, proj_sum = lax.optimization_barrier(
-            (qkv_terms, ln_terms, vector_sums, proj_sum)
-        )
         qkv_sum = total_of(qkv_terms)[0].astype(BF16).reshape(rows, half, packed)
 
         qkv_home = jnp.concatenate(row_exchange([qkv_sum[k] for k in range(rows)]), axis=1)
-        qkv_home, down_sum_part = lax.optimization_barrier((qkv_home, down_sum_part))
         qkv_grad = mm("fm,nm->fn", qkv_home, select)
+        new_up, up_state = adam_matrix(up_weight, up_grad, up_moments)
+        new_up, up_state, proj_sum = lax.optimization_barrier((new_up, up_state, proj_sum))
         proj_cols = proj_sum.reshape(n_rows, rows, feats).transpose(1, 0, 2)
         proj_grad = total_of(row_exchange([at(proj_cols, (z + k) % rows) for k in range(rows)]))
         own_gain = gain_one.reshape(dps, rows, half, 1)[:, 0]
@@ -1086,7 +1098,6 @@
         vector_grad = summed[: 8 * D].reshape(8, D)
         bias_grad = summed[8 * D :]
 
-        new_up, up_state = adam_matrix(up_weight, up_grad, up_moments)
         down_turned = down_sum_part.astype(F32)
         down_grad = down_turned.T
         new_down, down_state = adam_matrix(down_weight.T, down_turned, down_moments.transpose(0, 2, 1))

time: 601 us -> 571 us (0.950)
  the two profiles are of different devices: /device:TPU:0 before, /device:TPU:9 now
where the time goes in v5:
time: 571 us; the launch traced here: 560 us
  waiting for transfers between devices  163 us (29%)
  Pallas kernels  121 us (21%)
  starting transfers between devices  119 us (21%)
  local copies, waits for them, and re-layouts  92.8 us (16%)
  other arithmetic  39.9 us (7%)
  between operations  16.3 us (3%)
  matrix products  8.29 us (1%)
    ppermute x30, waiting for transfers between devices, to_row(): lax.ppermute(values, 'row', [(i, (i + k) % rows) for i in range(rows)])  106 us
    ppermute x31, starting transfers between devices, to_plane(): lax.ppermute(values, ('dp', 'col'), [(y * cols + c, (y ^ d) * cols + (c ^...  51.3 us
    ppermute x30, starting transfers between devices, to_row(): lax.ppermute(values, 'row', [(i, (i + k) % rows) for i in range(rows)])  47.2 us
    unnamed x272, local copies, waits for them, and re-layouts  36.2 us
    ppermute x31, waiting for transfers between devices, to_plane(): lax.ppermute(values, ('dp', 'col'), [(y * cols + c, (y ^ d) * cols + (c ^...  34.2 us
    pallas_call x2, Pallas kernels, attention_backward(): pl.pallas_call(body, grid=(slots,), in_specs=specs, out_specs=[head_spec]...  18.6 us
    pallas_call x2, Pallas kernels, attention_forward(): pl.pallas_call(body, grid=(slots,), in_specs=specs, out_specs=out_specs,...  14.7 us
    pallas_call x2, Pallas kernels, hidden_units(): pl.pallas_call(body, grid=(tokens // step,), in_specs=[rows_in, rows_in,...  14.5 us
  transfers between devices with their start and end apart: 77, of which 29 were waited for; matrix products, arithmetic and copies ran while one was open for 18% of the time, Pallas kernels for 19%

profile of v5, /device:TPU:9, one launch (start us, length us, event | category | flops | bytes accessed | tf_op | source)
XLA Modules:
  0.0 559.5 jit_solution(6009015445289521745)
XLA Ops:
  22.3 5.9 %collective-permute-done.3 = bf16[200,800]{1,0:T(8,128)(2,1)} collective-permute-done((bf16[200,800]{1,0:T(8,128)(2,1)}, bf16[200,800]{1,0:T(8,128)(2,1)}, u32[]{:S(2)}, u32[]{:S(2)}) %collective-permute-start.3) | collective-permute-done | bytes 320032 | tf_op jit(solution)/shard_map/ppermute | solution.py:789
  46.2 17.1 %collective-permute-done.11 = bf16[2,200,512]{2,1,0:T(8,128)(2,1)S(1)} collective-permute-done((bf16[2,200,512]{2,1,0:T(8,128)(2,1)S(1)}, bf16[2,200,512]{2,1,0:T(8,128)(2,1)S(1)}, u32[]{:S(2)}, u32[]{:S(2)}) %collective-permute-start.11) | collective-permute-done | bytes 409632 | tf_op jit(solution)/shard_map/ppermute | solution.py:754
  63.3 4.4 collective-permute-done.12
  73.5 8.2 %collective-permute-start.13 = (bf16[4,800,384]{2,1,0:T(8,128)(2,1)}, bf16[4,800,384]{2,1,0:T(8,128)(2,1)}, u32[]{:S(2)}, u32[]{:S(2)}) collective-permute-start(bf16[4,800,384]{2,1,0:T(8,128)(2,1)} %constant_dynamic-update-slice_fusion), channel_id=1, source_target_pairs={{0,1},{1,0},{2,3},{3,2},{16,17},{17,16},{18,19},{19,18},{4,5},{5,4... | collective-permute-start | bytes 7372808 | tf_op jit(solution)/shard_map/ppermute | solution.py:763
  101.5 7.6 %collective-permute-done.16 = bf16[200,400]{1,0:T(8,128)(2,1)} collective-permute-done((bf16[200,400]{1,0:T(8,128)(2,1)S(1)}, bf16[200,400]{1,0:T(8,128)(2,1)}, u32[]{:S(2)}, u32[]{:S(2)}) %collective-permute-start.16) | collective-permute-done | bytes 160032 | tf_op jit(solution)/shard_map/ppermute | solution.py:754
  110.2 4.5 collective-permute-start.17
  125.1 10.7 %attention_forward.2 = (f32[7,1,512]{2,1,0:T(1,128)S(1)}, f32[7,1,512]{2,1,0:T(1,128)S(1)}, f32[448,512]{1,0:T(8,128)S(1)}) custom-call(s32[1]{0:T(128)} %bitcast.31.me_ref, s32[1,512]{1,0:T(1,128)S(1)} %bitcast.251, bf16[448,512]{1,0:T(8,128)(2,1)S(1)} %copy-done.35, bf16[896,512]{1,0:T(8,128)(2,1)} %slice.240.refs_0_.refs_1_, ...), custom_call_target="tpu_custom_call" | custom-call | flops 3849999872 | bytes 12100000 | tf_op jit(solution)/shard_map/attention_forward/pallas_call | solution.py:629
  142.4 4.0 attention_forward.3
  147.4 5.9 %collective-permute-start.20 = (bf16[448,128]{1,0:T(8,128)(2,1)}, bf16[448,128]{1,0:T(8,128)(2,1)S(1)}, u32[]{:S(2)}, u32[]{:S(2)}) collective-permute-start(bf16[448,128]{1,0:T(8,128)(2,1)} %get-tuple-element.434), channel_id=1, source_target_pairs={{0,12},{4,0},{8,4},{12,8},{1,13},{5,1},{9,5},{13,9},{2,14},{6,2},{... | collective-permute-start | bytes 344072 | tf_op jit(solution)/shard_map/ppermute | solution.py:754
  165.9 3.9 collective-permute-done.24.refs_6_.refs_11_
  170.5 5.7 %collective-permute-done.22.refs_3_ = bf16[448,128]{1,0:T(8,128)(2,1)S(1)} collective-permute-done((bf16[448,128]{1,0:T(8,128)(2,1)}, bf16[448,128]{1,0:T(8,128)(2,1)S(1)}, u32[]{:S(2)}, u32[]{:S(2)}) %collective-permute-start.22) | collective-permute-done | bytes 114720 | tf_op jit(solution)/shard_map/ppermute | solution.py:754
  178.3 8.0 %collective-permute-start.30 = (bf16[128,1664]{1,0:T(8,128)(2,1)S(1)}, bf16[128,1664]{1,0:T(8,128)(2,1)}, u32[]{:S(2)}, u32[]{:S(2)}) collective-permute-start(bf16[128,1664]{1,0:T(8,128)(2,1)S(1)} %pad.13.refs_4_), channel_id=1, source_target_pairs={{0,2},{1,3},{2,0},{3,1},{16,18},{17,19},{18,16},{19,17},{4,6},{5,7... | collective-permute-start | bytes 1277960 | tf_op jit(solution)/shard_map/ppermute | solution.py:763
  197.5 5.6 %project.1 = (bf16[1600,128]{1,0:T(8,128)(2,1)S(1)}, f32[128,1600]{1,0:T(8,128)}, bf16[128,1664]{1,0:T(8,128)(2,1)S(1)}, f32[128,1]{1,0:T(8,128)S(1)}, f32[128,1]{1,0:T(8,128)S(1)}) custom-call(s32[200]{0:T(256)S(1)} %bitcast.255, s32[200]{0:T(256)S(1)} %bitcast.256, bf16[448,128]{1,0:T(8,128)(2,1)S(1)} %get-tuple-element.234.refs_0_, ...), custom_call_target="tpu_custom_call" | custom-call | flops 1750000000 | bytes 5500000 | tf_op jit(solution)/shard_map/project/pallas_call | solution.py:331
  215.8 8.8 %collective-permute-done.33 = bf16[128,1664]{1,0:T(8,128)(2,1)S(1)} collective-permute-done((bf16[128,1664]{1,0:T(8,128)(2,1)S(1)}, bf16[128,1664]{1,0:T(8,128)(2,1)S(1)}, u32[]{:S(2)}, u32[]{:S(2)}) %collective-permute-start.33) | collective-permute-done | bytes 426016 | tf_op jit(solution)/shard_map/ppermute | solution.py:763
  224.7 9.1 %collective-permute-done.34 = bf16[128,1664]{1,0:T(8,128)(2,1)S(1)} collective-permute-done((bf16[128,1664]{1,0:T(8,128)(2,1)S(1)}, bf16[128,1664]{1,0:T(8,128)(2,1)S(1)}, u32[]{:S(2)}, u32[]{:S(2)}) %collective-permute-start.34) | collective-permute-done | bytes 426016 | tf_op jit(solution)/shard_map/ppermute | solution.py:763
  247.4 7.2 %hidden_units.3 = (bf16[512,800]{1,0:T(8,128)(2,1)S(1)}, bf16[512,800]{1,0:T(8,128)(2,1)S(1)}, f32[1,800]{1,0:T(1,128)S(1)}) custom-call(bf16[512,1664]{1,0:T(8,128)(2,1)} %collective-permute-done.37.h_ref.refs_1_, bf16[512,1664]{1,0:T(8,128)(2,1)S(1)} %copy-done.5, bf16[4,2,400,800]{3,2,1,0:T(8,128)(2,1)} %bitcast.228, bf16[4,2,400,800]{3,2,1,0:T(8,128)(2,1)} %bitcast.229, ...), custom_call_target="tpu_custom_call" | custom-call | flops 2100000000 | bytes 6600000 | tf_op jit(solution)/shard_map/hidden_units/pallas_call | solution.py:422
  258.5 7.3 %hidden_units.2 = (bf16[512,800]{1,0:T(8,128)(2,1)S(1)}, bf16[512,800]{1,0:T(8,128)(2,1)S(1)}, f32[1,800]{1,0:T(1,128)S(1)}) custom-call(bf16[512,1664]{1,0:T(8,128)(2,1)} %constant_dynamic-update-slice_fusion.8.h_ref.refs_0_, bf16[512,1664]{1,0:T(8,128)(2,1)S(1)} %copy-done.1, bf16[4,2,400,800]{3,2,1,0:T(8,128)(2,1)} %bitcast.230, ...), custom_call_target="tpu_custom_call" | custom-call | flops 2100000000 | bytes 6600000 | tf_op jit(solution)/shard_map/hidden_units/pallas_call | solution.py:422
  279.0 12.8 %weight_parts.1 = bf16[4,2,400,800]{3,2,1,0:T(8,128)(2,1)} custom-call(bf16[512,1664]{1,0:T(8,128)(2,1)} %constant_dynamic-update-slice_fusion.8.h_ref.refs_0_, bf16[512,1664]{1,0:T(8,128)(2,1)} %collective-permute-done.37.h_ref.refs_1_, bf16[512,800]{1,0:T(8,128)(2,1)S(1)} %get-tuple-element.265.g_ref.refs_2_, ...), custom_call_target="tpu_custom_call" | custom-call | flops 3150000128 | bytes 9900000 | tf_op jit(solution)/shard_map/weight_parts/pallas_call | solution.py:481
  298.3 6.1 %project_back.1 = (bf16[128,1600]{1,0:T(8,128)(2,1)S(1)}, bf16[1792,128]{1,0:T(8,128)(2,1)S(1)}, f32[3,1600]{1,0:T(4,128)S(1)}) custom-call(s32[224]{0:T(256)S(1)} %bitcast.250, f32[128,1664]{1,0:T(8,128)} %slice.313.refs_0_, bf16[128,1664]{1,0:T(8,128)(2,1)} %collective-permute-done.39.refs_1_, bf16[128,1664]{1,0:T(8,128)(2,1)} %collective-permute-done.40.refs_2_, ...), custom_call_target="tpu_custom_call" | custom-call | flops 1750000000 | bytes 5500000 | tf_op jit(solution)/shard_map/project_back/pallas_call | solution.py:378
  319.4 8.2 %collective-permute-done.45 = bf16[448,128]{1,0:T(8,128)(2,1)} collective-permute-done((bf16[448,128]{1,0:T(8,128)(2,1)}, bf16[448,128]{1,0:T(8,128)(2,1)}, u32[]{:S(2)}, u32[]{:S(2)}) %collective-permute-start.45) | collective-permute-done | bytes 114720 | tf_op jit(solution)/shard_map/ppermute | solution.py:754
  328.8 4.4 attention_backward.2
  344.1 5.9 %collective-permute-start.51 = (bf16[800,128]{1,0:T(8,128)(2,1)S(1)}, bf16[800,128]{1,0:T(8,128)(2,1)S(1)}, u32[]{:S(2)}, u32[]{:S(2)}) collective-permute-start(bf16[800,128]{1,0:T(8,128)(2,1)S(1)} %get-tuple-element.402), channel_id=1, source_target_pairs={{0,12},{4,0},{8,4},{12,8},{1,13},{5,1},{9,5},{13,9},{2,14},{6,2},{... | collective-permute-start | bytes 614408 | tf_op jit(solution)/shard_map/ppermute | solution.py:754
  354.3 14.2 %attention_backward.3 = (bf16[448,512]{1,0:T(8,128)(2,1)S(1)}, bf16[448,512]{1,0:T(8,128)(2,1)S(1)}, bf16[448,512]{1,0:T(8,128)(2,1)S(1)}, bf16[448,512]{1,0:T(8...) custom-call(s32[1]{0:T(128)} %bitcast.31.me_ref, ...), custom_call_target="tpu_custom_call" | custom-call | flops 4899999744 | bytes 15400000 | tf_op jit(solution)/shard_map/attention_backward/pallas_call | solution.py:727
  368.7 6.6 %collective-permute-done.52.refs_10_ = bf16[800,128]{1,0:T(8,128)(2,1)S(1)} collective-permute-done((bf16[800,128]{1,0:T(8,128)(2,1)S(1)}, bf16[800,128]{1,0:T(8,128)(2,1)S(1)}, u32[]{:S(2)}, u32[]{:S(2)}) %collective-permute-start.52) | collective-permute-done | bytes 204832 | tf_op jit(solution)/shard_map/ppermute | solution.py:754
  375.2 16.5 %collective-permute-done.53.refs_11_ = bf16[800,128]{1,0:T(8,128)(2,1)S(1)} collective-permute-done((bf16[800,128]{1,0:T(8,128)(2,1)S(1)}, bf16[800,128]{1,0:T(8,128)(2,1)S(1)}, u32[]{:S(2)}, u32[]{:S(2)}) %collective-permute-start.53) | collective-permute-done | bytes 204832 | tf_op jit(solution)/shard_map/ppermute | solution.py:754
  399.8 7.1 %qkv_back.1 = (bf16[4,2,208,512]{3,2,1,0:T(8,128)(2,1)}, f32[2,800,1]{2,1,0:T(8,128)S(1)}, f32[2,800,1]{2,1,0:T(8,128)S(1)}) custom-call(bf16[2,2,800,384]{3,2,1,0:T(8,128)(2,1)} %bitcast.25.w_ref.first, bf16[2,2,800,384]{3,2,1,0:T(8,128)(2,1)} %bitcast.26.w_ref.second, bf16[1536,512]{1,0:T(8,128)(2,1)S(1)} %move_units.3.g_ref, ...), custom_call_target="tpu_custom_call" | custom-call | flops 2449999872 | bytes 7700000 | tf_op jit(solution)/shard_map/qkv_back/pallas_call | solution.py:241
  432.3 9.7 %collective-permute-start.56 = (bf16[1,800,384]{2,1,0:T(8,128)(2,1)}, bf16[1,800,384]{2,1,0:T(8,128)(2,1)S(1)}, u32[]{:S(2)}, u32[]{:S(2)}) collective-permute-start(bf16[1,800,384]{2,1,0:T(8,128)(2,1)} %get-tuple-element.380), channel_id=1, source_target_pairs={{0,2},{1,3},{2,0},{3,1},{16,18},{17,19},{18,16},{19,17},{4,6},{5,7... | collective-permute-start | bytes 1843208 | tf_op jit(solution)/shard_map/ppermute | solution.py:763
  446.8 13.3 %collective-permute-done.60.refs_2_ = bf16[2,208,512]{2,1,0:T(8,128)(2,1)} collective-permute-done((bf16[2,208,512]{2,1,0:T(8,128)(2,1)}, bf16[2,208,512]{2,1,0:T(8,128)(2,1)}, u32[]{:S(2)}, u32[]{:S(2)}) %collective-permute-start.60) | collective-permute-done | bytes 426016 | tf_op jit(solution)/shard_map/ppermute | solution.py:754
  466.4 11.6 %collective-permute-start.64 = (bf16[200,384]{1,0:T(8,128)(2,1)S(1)}, bf16[200,384]{1,0:T(8,128)(2,1)S(1)}, u32[]{:S(2)}, u32[]{:S(2)}) collective-permute-start(bf16[200,384]{1,0:T(8,128)(2,1)S(1)} %get-tuple-element.417), channel_id=1, source_target_pairs={{0,4},{4,8},{8,12},{12,0},{1,5},{5,9},{9,13},{13,1},{2,6},{6,10},{... | collective-permute-start | bytes 460808 | tf_op jit(solution)/shard_map/ppermute | solution.py:754
  490.7 8.9 %collective-permute-done.70 = f32[19200]{0:T(1024)S(1)} collective-permute-done((f32[19200]{0:T(1024)S(1)}, f32[19200]{0:T(1024)S(1)}, u32[]{:S(2)}, u32[]{:S(2)}) %collective-permute-start.70) | collective-permute-done | bytes 76832 | tf_op jit(solution)/shard_map/ppermute | solution.py:796
  518.0 4.3 reduce-scatter.7.cloned.1.call-done
  534.0 11.5 %collective-permute-done.67 = bf16[200,400]{1,0:T(8,128)(2,1)S(1)} collective-permute-done((bf16[200,400]{1,0:T(8,128)(2,1)S(1)}, bf16[200,400]{1,0:T(8,128)(2,1)S(1)}, u32[]{:S(2)}, u32[]{:S(2)}) %collective-permute-start.67) | collective-permute-done | bytes 160032 | tf_op jit(solution)/shard_map/ppermute | solution.py:754
  (600 shorter events, 278.3 us)
Async XLA Ops:
  7.2 228.9 %all-gather.2.cloned.1.call-start = ((), (), s32[]{:S(2)}) async-start(), calls=%async_computation.2 | async-start | bytes 7168000 | tf_op jit(solution)/shard_map/all_gather | solution.py:874
  11.8 24.1 %collective-permute-start = (bf16[200,384]{1,0:T(8,128)(2,1)}, bf16[200,384]{1,0:T(8,128)(2,1)S(1)}, u32[]{:S(2)}, u32[]{:S(2)}) collective-permute-start(bf16[200,384]{1,0:T(8,128)(2,1)} %get-tuple-element.422), channel_id=1, source_target_pairs={{0,12},{4,0},{8,4},{12,8},{1,13},{5,1},{9,5},{13,9},{2,14},{6,2},{... | collective-permute-start | bytes 460808 | tf_op jit(solution)/shard_map/ppermute | solution.py:754
  11.8 24.1 %collective-permute-start.1 = (bf16[200,384]{1,0:T(8,128)(2,1)}, bf16[200,384]{1,0:T(8,128)(2,1)}, u32[]{:S(2)}, u32[]{:S(2)}) collective-permute-start(bf16[200,384]{1,0:T(8,128)(2,1)} %get-tuple-element.421), channel_id=1, source_target_pairs={{0,8},{4,12},{8,0},{12,4},{1,9},{5,13},{9,1},{13,5},{2,10},{6,14},... | collective-permute-start | bytes 460808 | tf_op jit(solution)/shard_map/ppermute | solution.py:754
  14.3 21.6 %collective-permute-start.2 = (bf16[200,384]{1,0:T(8,128)(2,1)}, bf16[200,384]{1,0:T(8,128)(2,1)}, u32[]{:S(2)}, u32[]{:S(2)}) collective-permute-start(bf16[200,384]{1,0:T(8,128)(2,1)} %get-tuple-element.420), channel_id=1, source_target_pairs={{0,4},{4,8},{8,12},{12,0},{1,5},{5,9},{9,13},{13,1},{2,6},{6,10},{... | collective-permute-start | bytes 460808 | tf_op jit(solution)/shard_map/ppermute | solution.py:754
  37.0 30.7 %collective-permute-start.7 = (bf16[1,800,384]{2,1,0:T(8,128)(2,1)S(1)}, bf16[1,800,384]{2,1,0:T(8,128)(2,1)S(1)}, u32[]{:S(2)}, u32[]{:S(2)}) collective-permute-start(bf16[1,800,384]{2,1,0:T(8,128)(2,1)S(1)} %bitcast.260), channel_id=1, source_target_pairs={{0,2},{1,3},{2,0},{3,1},{16,18},{17,19},{18,16},{19,17},{4,6},{5,7... | collective-permute-start | bytes 1843208 | tf_op jit(solution)/shard_map/ppermute | solution.py:763
  38.3 29.4 %collective-permute-start.8 = (bf16[1,800,384]{2,1,0:T(8,128)(2,1)S(1)}, bf16[1,800,384]{2,1,0:T(8,128)(2,1)}, u32[]{:S(2)}, u32[]{:S(2)}) collective-permute-start(bf16[1,800,384]{2,1,0:T(8,128)(2,1)S(1)} %bitcast.261), channel_id=1, source_target_pairs={{0,16},{1,17},{2,18},{3,19},{16,0},{17,1},{18,2},{19,3},{4,20},{5,... | collective-permute-start | bytes 1843208 | tf_op jit(solution)/shard_map/ppermute | solution.py:763
  39.6 28.1 %collective-permute-start.9 = (bf16[1,800,384]{2,1,0:T(8,128)(2,1)S(1)}, bf16[1,800,384]{2,1,0:T(8,128)(2,1)}, u32[]{:S(2)}, u32[]{:S(2)}) collective-permute-start(bf16[1,800,384]{2,1,0:T(8,128)(2,1)S(1)} %bitcast.262), channel_id=1, source_target_pairs={{0,18},{1,19},{2,16},{3,17},{16,2},{17,3},{18,0},{19,1},{4,22},{5,... | collective-permute-start | bytes 1843208 | tf_op jit(solution)/shard_map/ppermute | solution.py:763
  39.8 23.5 %collective-permute-start.11 = (bf16[2,200,512]{2,1,0:T(8,128)(2,1)S(1)}, bf16[2,200,512]{2,1,0:T(8,128)(2,1)S(1)}, u32[]{:S(2)}, u32[]{:S(2)}) collective-permute-start(bf16[2,200,512]{2,1,0:T(8,128)(2,1)S(1)} %pad_maximum_fusion.10.refs_4_), channel_id=1, source_target_pairs={{0,8},{4,12},{8,0},{12,4},{1,9},{5,13},{9,1},{13,5},{2,10},{6,14},... | collective-permute-start | bytes 1228808 | tf_op jit(solution)/shard_map/ppermute | solution.py:754
  44.9 22.8 %collective-permute-start.12 = (bf16[2,200,512]{2,1,0:T(8,128)(2,1)S(1)}, bf16[2,200,512]{2,1,0:T(8,128)(2,1)}, u32[]{:S(2)}, u32[]{:S(2)}) collective-permute-start(bf16[2,200,512]{2,1,0:T(8,128)(2,1)S(1)} %pad_maximum_fusion.10.refs_4_), channel_id=1, source_target_pairs={{0,4},{4,8},{8,12},{12,0},{1,5},{5,9},{9,13},{13,1},{2,6},{6,10},{... | collective-permute-start | bytes 1228808 | tf_op jit(solution)/shard_map/ppermute | solution.py:754
  86.8 22.3 %collective-permute-start.16 = (bf16[200,400]{1,0:T(8,128)(2,1)S(1)}, bf16[200,400]{1,0:T(8,128)(2,1)}, u32[]{:S(2)}, u32[]{:S(2)}) collective-permute-start(bf16[200,400]{1,0:T(8,128)(2,1)S(1)} %convert_element_type.152), channel_id=1, source_target_pairs={{0,4},{4,8},{8,12},{12,0},{1,5},{5,9},{9,13},{13,1},{2,6},{6,10},{... | collective-permute-start | bytes 480008 | tf_op jit(solution)/shard_map/ppermute | solution.py:754
  89.2 354.9 %reduce-scatter.5.cloned.1.call-start = ((), (), s32[]{:S(2)}) async-start(), calls=%async_computation.3 | async-start | bytes 7168000 | tf_op jit(solution)/shard_map/reduce_scatter | solution.py:969
  114.7 22.0 %collective-permute-start.18 = (bf16[896,512]{1,0:T(8,128)(2,1)}, bf16[896,512]{1,0:T(8,128)(2,1)}, u32[]{:S(2)}, u32[]{:S(2)}) collective-permute-start(bf16[896,512]{1,0:T(8,128)(2,1)} %slice.240.refs_0_.refs_1_), channel_id=1, source_target_pairs={{0,2},{1,3},{4,6},{5,7},{8,10},{9,11},{12,14},{13,15},{16,18},{17,... | collective-permute-start | bytes 2752520 | tf_op jit(solution)/shard_map/ppermute | solution.py:910
  139.0 30.8 %collective-permute-start.24 = (bf16[200,1600]{1,0:T(8,128)(2,1)}, bf16[200,1600]{1,0:T(8,128)(2,1)}, u32[]{:S(2)}, u32[]{:S(2)}) collective-permute-start(bf16[200,1600]{1,0:T(8,128)(2,1)} %concatenate.64.refs_4_.refs_9_), channel_id=1, source_target_pairs={{0,16},{1,17},{2,18},{3,19},{16,0},{17,1},{18,2},{19,3},{4,20},{5,... | collective-permute-start | bytes 1920008 | tf_op jit(solution)/shard_map/ppermute | solution.py:763
  139.0 30.8 %collective-permute-start.25 = (bf16[200,1600]{1,0:T(8,128)(2,1)}, bf16[200,1600]{1,0:T(8,128)(2,1)}, u32[]{:S(2)}, u32[]{:S(2)}) collective-permute-start(bf16[200,1600]{1,0:T(8,128)(2,1)} %concatenate.64.refs_4_.refs_9_), channel_id=1, source_target_pairs={{0,18},{1,19},{2,16},{3,17},{16,2},{17,3},{18,0},{19,1},{4,22},{5,... | collective-permute-start | bytes 1920008 | tf_op jit(solution)/shard_map/ppermute | solution.py:763
  147.4 22.5 %collective-permute-start.20 = (bf16[448,128]{1,0:T(8,128)(2,1)}, bf16[448,128]{1,0:T(8,128)(2,1)S(1)}, u32[]{:S(2)}, u32[]{:S(2)}) collective-permute-start(bf16[448,128]{1,0:T(8,128)(2,1)} %get-tuple-element.434), channel_id=1, source_target_pairs={{0,12},{4,0},{8,4},{12,8},{1,13},{5,1},{9,5},{13,9},{2,14},{6,2},{... | collective-permute-start | bytes 344072 | tf_op jit(solution)/shard_map/ppermute | solution.py:754
  178.3 24.9 %collective-permute-start.30 = (bf16[128,1664]{1,0:T(8,128)(2,1)S(1)}, bf16[128,1664]{1,0:T(8,128)(2,1)}, u32[]{:S(2)}, u32[]{:S(2)}) collective-permute-start(bf16[128,1664]{1,0:T(8,128)(2,1)S(1)} %pad.13.refs_4_), channel_id=1, source_target_pairs={{0,2},{1,3},{2,0},{3,1},{16,18},{17,19},{18,16},{19,17},{4,6},{5,7... | collective-permute-start | bytes 1277960 | tf_op jit(solution)/shard_map/ppermute | solution.py:763
  209.6 25.3 %collective-permute-start.36 = (bf16[512,1664]{1,0:T(8,128)(2,1)S(1)}, bf16[512,1664]{1,0:T(8,128)(2,1)S(1)}, u32[]{:S(2)}, u32[]{:S(2)}) collective-permute-start(bf16[512,1664]{1,0:T(8,128)(2,1)S(1)} %constant_dynamic-update-slice_fusion.4.t_ref.refs_4_), channel_id=1, source_target_pairs={{0,1},{1,0},{2,3},{3,2},{16,17},{17,16},{18,19},{19,18},{4,5},{5,4... | collective-permute-start | bytes 5111816 | tf_op jit(solution)/shard_map/ppermute | solution.py:763
  271.0 23.3 %collective-permute-start.42 = (bf16[512,1664]{1,0:T(8,128)(2,1)S(1)}, bf16[512,1664]{1,0:T(8,128)(2,1)}, u32[]{:S(2)}, u32[]{:S(2)}) collective-permute-start(bf16[512,1664]{1,0:T(8,128)(2,1)S(1)} %features_back.6), channel_id=1, source_target_pairs={{0,1},{1,0},{2,3},{3,2},{16,17},{17,16},{18,19},{19,18},{4,5},{5,4... | collective-permute-start | bytes 5111816 | tf_op jit(solution)/shard_map/ppermute | solution.py:763
  294.2 228.1 %reduce-scatter.7.cloned.1.call-start = ((), (), s32[]{:S(2)}) async-start(), calls=%async_computation.4 | async-start | bytes 5990400
  340.2 51.4 %collective-permute-start.50 = (bf16[896,512]{1,0:T(8,128)(2,1)}, bf16[896,512]{1,0:T(8,128)(2,1)}, u32[]{:S(2)}, u32[]{:S(2)}) collective-permute-start(bf16[896,512]{1,0:T(8,128)(2,1)} %add_convert_fusion.2), channel_id=1, source_target_pairs={{2,0},{3,1},{6,4},{7,5},{10,8},{11,9},{14,12},{15,13},{18,16},{19,... | collective-permute-start | bytes 2752520 | tf_op jit(solution)/shard_map/ppermute | solution.py:1002
  344.1 24.6 %collective-permute-start.51 = (bf16[800,128]{1,0:T(8,128)(2,1)S(1)}, bf16[800,128]{1,0:T(8,128)(2,1)S(1)}, u32[]{:S(2)}, u32[]{:S(2)}) collective-permute-start(bf16[800,128]{1,0:T(8,128)(2,1)S(1)} %get-tuple-element.402), channel_id=1, source_target_pairs={{0,12},{4,0},{8,4},{12,8},{1,13},{5,1},{9,5},{13,9},{2,14},{6,2},{... | collective-permute-start | bytes 614408 | tf_op jit(solution)/shard_map/ppermute | solution.py:754
  349.9 25.3 %collective-permute-start.52 = (bf16[800,128]{1,0:T(8,128)(2,1)S(1)}, bf16[800,128]{1,0:T(8,128)(2,1)S(1)}, u32[]{:S(2)}, u32[]{:S(2)}) collective-permute-start(bf16[800,128]{1,0:T(8,128)(2,1)S(1)} %get-tuple-element.403), channel_id=1, source_target_pairs={{0,8},{4,12},{8,0},{12,4},{1,9},{5,13},{9,1},{13,5},{2,10},{6,14},... | collective-permute-start | bytes 614408 | tf_op jit(solution)/shard_map/ppermute | solution.py:754
  349.9 41.7 %collective-permute-start.53 = (bf16[800,128]{1,0:T(8,128)(2,1)S(1)}, bf16[800,128]{1,0:T(8,128)(2,1)S(1)}, u32[]{:S(2)}, u32[]{:S(2)}) collective-permute-start(bf16[800,128]{1,0:T(8,128)(2,1)S(1)} %get-tuple-element.400), channel_id=1, source_target_pairs={{0,4},{4,8},{8,12},{12,0},{1,5},{5,9},{9,13},{13,1},{2,6},{6,10},{... | collective-permute-start | bytes 614408 | tf_op jit(solution)/shard_map/ppermute | solution.py:754
  421.3 21.9 %collective-permute-start.59 = (bf16[2,208,512]{2,1,0:T(8,128)(2,1)S(1)}, bf16[2,208,512]{2,1,0:T(8,128)(2,1)S(1)}, u32[]{:S(2)}, u32[]{:S(2)}) collective-permute-start(bf16[2,208,512]{2,1,0:T(8,128)(2,1)S(1)} %get-tuple-element.383), channel_id=1, source_target_pairs={{0,4},{4,8},{8,12},{12,0},{1,5},{5,9},{9,13},{13,1},{2,6},{6,10},{... | collective-permute-start | bytes 1277960 | tf_op jit(solution)/shard_map/ppermute | solution.py:754
  423.5 36.5 %collective-permute-start.60 = (bf16[2,208,512]{2,1,0:T(8,128)(2,1)}, bf16[2,208,512]{2,1,0:T(8,128)(2,1)}, u32[]{:S(2)}, u32[]{:S(2)}) collective-permute-start(bf16[2,208,512]{2,1,0:T(8,128)(2,1)} %get-tuple-element.382), channel_id=1, source_target_pairs={{0,8},{4,12},{8,0},{12,4},{1,9},{5,13},{9,1},{13,5},{2,10},{6,14},... | collective-permute-start | bytes 1277960 | tf_op jit(solution)/shard_map/ppermute | solution.py:754
  423.5 37.8 %collective-permute-start.61 = (bf16[2,208,512]{2,1,0:T(8,128)(2,1)}, bf16[2,208,512]{2,1,0:T(8,128)(2,1)}, u32[]{:S(2)}, u32[]{:S(2)}) collective-permute-start(bf16[2,208,512]{2,1,0:T(8,128)(2,1)} %get-tuple-element.381), channel_id=1, source_target_pairs={{0,12},{4,0},{8,4},{12,8},{1,13},{5,1},{9,5},{13,9},{2,14},{6,2},{... | collective-permute-start | bytes 1277960 | tf_op jit(solution)/shard_map/ppermute | solution.py:754
  432.3 29.0 %collective-permute-start.56 = (bf16[1,800,384]{2,1,0:T(8,128)(2,1)}, bf16[1,800,384]{2,1,0:T(8,128)(2,1)S(1)}, u32[]{:S(2)}, u32[]{:S(2)}) collective-permute-start(bf16[1,800,384]{2,1,0:T(8,128)(2,1)} %get-tuple-element.380), channel_id=1, source_target_pairs={{0,2},{1,3},{2,0},{3,1},{16,18},{17,19},{18,16},{19,17},{4,6},{5,7... | collective-permute-start | bytes 1843208 | tf_op jit(solution)/shard_map/ppermute | solution.py:763
  466.4 34.6 %collective-permute-start.64 = (bf16[200,384]{1,0:T(8,128)(2,1)S(1)}, bf16[200,384]{1,0:T(8,128)(2,1)S(1)}, u32[]{:S(2)}, u32[]{:S(2)}) collective-permute-start(bf16[200,384]{1,0:T(8,128)(2,1)S(1)} %get-tuple-element.417), channel_id=1, source_target_pairs={{0,4},{4,8},{8,12},{12,0},{1,5},{5,9},{9,13},{13,1},{2,6},{6,10},{... | collective-permute-start | bytes 460808 | tf_op jit(solution)/shard_map/ppermute | solution.py:754
  478.0 22.9 %collective-permute-start.63 = (bf16[200,384]{1,0:T(8,128)(2,1)S(1)}, bf16[200,384]{1,0:T(8,128)(2,1)S(1)}, u32[]{:S(2)}, u32[]{:S(2)}) collective-permute-start(bf16[200,384]{1,0:T(8,128)(2,1)S(1)} %get-tuple-element.418), channel_id=1, source_target_pairs={{0,8},{4,12},{8,0},{12,4},{1,9},{5,13},{9,1},{13,5},{2,10},{6,14},... | collective-permute-start | bytes 460808 | tf_op jit(solution)/shard_map/ppermute | solution.py:754
  478.0 22.9 %collective-permute-start.62 = (bf16[200,384]{1,0:T(8,128)(2,1)S(1)}, bf16[200,384]{1,0:T(8,128)(2,1)S(1)}, u32[]{:S(2)}, u32[]{:S(2)}) collective-permute-start(bf16[200,384]{1,0:T(8,128)(2,1)S(1)} %get-tuple-element.419), channel_id=1, source_target_pairs={{0,12},{4,0},{8,4},{12,8},{1,13},{5,1},{9,5},{13,9},{2,14},{6,2},{... | collective-permute-start | bytes 460808 | tf_op jit(solution)/shard_map/ppermute | solution.py:754
  479.3 28.6 %collective-permute-start.65 = (bf16[200,800]{1,0:T(8,128)(2,1)S(1)}, bf16[200,800]{1,0:T(8,128)(2,1)S(1)}, u32[]{:S(2)}, u32[]{:S(2)}) collective-permute-start(bf16[200,800]{1,0:T(8,128)(2,1)S(1)} %get-tuple-element.410), channel_id=1, source_target_pairs={{0,16},{16,0},{1,17},{17,1},{2,18},{18,2},{3,19},{19,3},{4,20},{20... | collective-permute-start | bytes 960008 | tf_op jit(solution)/shard_map/ppermute | solution.py:789
  507.4 23.7 %collective-permute-start.73 = (f32[19200]{0:T(1024)S(1)}, f32[19200]{0:T(1024)S(1)}, u32[]{:S(2)}, u32[]{:S(2)}) collective-permute-start(f32[19200]{0:T(1024)S(1)} %add.532), channel_id=1, source_target_pairs={{0,8},{4,12},{8,0},{12,4},{1,9},{5,13},{9,1},{13,5},{2,10},{6,14},... | collective-permute-start | bytes 230408 | tf_op jit(solution)/shard_map/ppermute | solution.py:796
  (174 other events, 1684.5 us)
Sparse Core Ops, SparseCore 0:
  89.3 116.6 all-gather.1
  294.4 129.9 reduce-scatter.4
  428.1 94.1 reduce-scatter.6

commit v6 on v5

--- a/solution.py
+++ b/solution.py
@@ -32,7 +32,7 @@
 
 def cost(micros):
     return pl.CostEstimate(
-        flops=int(micros * 0.35e9), bytes_accessed=int(micros * 1.1e6), transcendentals=0
+        flops=int(micros * 1.1e9), bytes_accessed=int(micros * 3.4e6), transcendentals=0
     )
 
 
@@ -935,7 +935,7 @@
         top_sent = plane_send(top_few)
 
         attn_few, mid, h2, mean_two, inverse_two = project(
-            weight_table, at(jnp.asarray(to_plain), z), attn_pieces, proj_halves, x_few, jnp.stack([vectors[4], vectors[5], vectors[6]]), unit
+            weight_table, weight_table, attn_pieces, proj_halves, x_few, jnp.stack([vectors[4], vectors[5], vectors[6]]), unit
         )
         h2, top_sent = lax.optimization_barrier((h2, top_sent))
 
@@ -984,13 +984,18 @@
         )
         down_terms = plane_scatter(down_near, down_received, 0)
         head_pieces = row_exchange([heads_out[k * wide : (k + 1) * wide] for k in range(rows)])
-        proj_part = mm("rt,tf->rf", attn_few, grad_mid_half).astype(BF16)
-        head_pieces, proj_part = lax.optimization_barrier((head_pieces, proj_part))
-        proj_sum = lax.psum_scatter(proj_part, ("dp", "col"), scatter_dimension=0, tiled=True)
+        middle_rows = len(even) * n_rows
+        proj_far = mm("rt,tf->rf", attn_few[middle_rows:], grad_mid_half).astype(BF16)
+        proj_received = core_send(proj_far)
+        proj_near = mm("rt,tf->rf", attn_few[:middle_rows], grad_mid_half).astype(BF16)
+        head_pieces, proj_near, proj_received = lax.optimization_barrier((head_pieces, proj_near, proj_received))
         grad_heads = unrolled(head_pieces, 1)
 
         far = attention_backward(me, start, query, far_kv, far_offsets, attn, lse, grad_heads)
-        far, down_terms = lax.optimization_barrier((far, down_terms))
+        far, down_terms, proj_near, proj_received = lax.optimization_barrier(
+            (far, down_terms, proj_near, proj_received)
+        )
+        proj_terms = plane_scatter(proj_near, proj_received, 0)
         half_far = len(far_offsets) // 2
         far_grads = [jnp.concatenate(far[2 * i : 2 * i + 2], axis=0) for i in range(len(far_offsets))]
         far_value_total, carried_query = far[-2:]
@@ -1011,6 +1016,7 @@
             me, start, query, near_kv, near_offsets, attn, lse, grad_heads, carried_query
         )
         near, far_sent, sides = lax.optimization_barrier((near, far_sent, sides))
+        proj_sum = total_of(proj_terms).astype(BF16)
         near_value_total, grad_query, query_total = near[-3:]
         value_total = near_value_total + far_value_total
         near_received = lax.ppermute(jnp.concatenate(near[2:4], axis=0), "col", swap_cores)
@@ -1074,8 +1080,8 @@
             return jnp.concatenate([parts.reshape(-1), bias_full])
 
         vector_sums = token_sums(sum_norm, sum_plain)
-        qkv_terms, ln_terms, vector_sums, up_home = lax.optimization_barrier(
-            (qkv_terms, ln_terms, vector_sums, up_home)
+        qkv_terms, ln_terms, vector_sums, up_home, proj_sum = lax.optimization_barrier(
+            (qkv_terms, ln_terms, vector_sums, up_home, proj_sum)
         )
         up_blocks = up_home.reshape(dps, half, hidden)
         up_back = dp_exchange([at(up_blocks, y ^ d) for d in range(dps)])
@@ -1085,7 +1091,6 @@
         qkv_home = jnp.concatenate(row_exchange([qkv_sum[k] for k in range(rows)]), axis=1)
         qkv_grad = mm("fm,nm->fn", qkv_home, select)
         new_up, up_state = adam_matrix(up_weight, up_grad, up_moments)
-        new_up, up_state, proj_sum = lax.optimization_barrier((new_up, up_state, proj_sum))
         proj_cols = proj_sum.reshape(n_rows, rows, feats).transpose(1, 0, 2)
         proj_grad = total_of(row_exchange([at(proj_cols, (z + k) % rows) for k in range(rows)]))
         own_gain = gain_one.reshape(dps, rows, half, 1)[:, 0]

time: 571 us -> 548 us (0.960)
  the two profiles are of different devices: /device:TPU:9 before, /device:TPU:0 now
where the time goes in v6:
time: 548 us; the launch traced here: 537 us
  waiting for transfers between devices  181 us (33%)
  Pallas kernels  112 us (20%)
  starting transfers between devices  94 us (17%)
  local copies, waits for them, and re-layouts  73.7 us (13%)
  other arithmetic  49.8 us (9%)
  between operations  16.3 us (3%)
  matrix products  10.3 us (2%)
    ppermute x35, waiting for transfers between devices, to_plane(): lax.ppermute(values, ('dp', 'col'), [(y * cols + c, (y ^ d) * cols + (c ^...  86.5 us
    ppermute x30, waiting for transfers between devices, to_row(): lax.ppermute(values, 'row', [(i, (i + k) % rows) for i in range(rows)])  72.7 us
    ppermute x30, starting transfers between devices, to_row(): lax.ppermute(values, 'row', [(i, (i + k) % rows) for i in range(rows)])  43.8 us
    ppermute x35, starting transfers between devices, to_plane(): lax.ppermute(values, ('dp', 'col'), [(y * cols + c, (y ^ d) * cols + (c ^...  38.5 us
    unnamed x232, local copies, waits for them, and re-layouts  20.2 us
    pallas_call x2, Pallas kernels, hidden_units(): pl.pallas_call(body, grid=(tokens // step,), in_specs=[rows_in, rows_in,...  14.3 us
    pallas_call x2, Pallas kernels, attention_backward(): pl.pallas_call(body, grid=(slots,), in_specs=specs, out_specs=[head_spec]...  13.1 us
    pallas_call x4, Pallas kernels, adam_matrix(): pl.pallas_call(body, grid=(n // step,), in_specs=[block, block, pair], ou...  12.5 us
  transfers between devices with their start and end apart: 80, of which 28 were waited for; matrix products, arithmetic and copies ran while one was open for 19% of the time, Pallas kernels for 17%

profile of v6, /device:TPU:0, one launch (start us, length us, event | category | flops | bytes accessed | tf_op | source)
XLA Modules:
  0.0 537.2 jit_solution(7273011147886328768)
XLA Ops:
  11.8 5.1 collective-permute-start
  25.6 4.0 collective-permute-done.3
  33.6 5.4 %collective-permute-done.5 = bf16[400,128]{1,0:T(8,128)(2,1)S(1)} collective-permute-done((bf16[400,128]{1,0:T(8,128)(2,1)S(1)}, bf16[400,128]{1,0:T(8,128)(2,1)S(1)}, u32[]{:S(2)}, u32[]{:S(2)}) %collective-permute-start.5) | collective-permute-done | bytes 102432 | tf_op jit(solution)/shard_map/ppermute | solution.py:754
  46.9 4.3 collective-permute-done.10
  53.2 21.0 %collective-permute-done.11 = bf16[2,200,512]{2,1,0:T(8,128)(2,1)} collective-permute-done((bf16[2,200,512]{2,1,0:T(8,128)(2,1)S(1)}, bf16[2,200,512]{2,1,0:T(8,128)(2,1)}, u32[]{:S(2)}, u32[]{:S(2)}) %collective-permute-start.11) | collective-permute-done | bytes 409632 | tf_op jit(solution)/shard_map/ppermute | solution.py:754
  81.2 4.2 collective-permute-start.15
  90.6 3.9 qkv_product.2.refs_0_
  99.3 5.4 %collective-permute-done.15 = bf16[200,400]{1,0:T(8,128)(2,1)} collective-permute-done((bf16[200,400]{1,0:T(8,128)(2,1)}, bf16[200,400]{1,0:T(8,128)(2,1)}, u32[]{:S(2)}, u32[]{:S(2)}) %collective-permute-start.15) | collective-permute-done | bytes 160032 | tf_op jit(solution)/shard_map/ppermute | solution.py:754
  106.4 4.8 collective-permute-start.18
  115.1 6.9 %attention_forward.2 = (f32[7,1,512]{2,1,0:T(1,128)S(1)}, f32[7,1,512]{2,1,0:T(1,128)S(1)}, f32[448,512]{1,0:T(8,128)S(1)}) custom-call(s32[1]{0:T(128)} %bitcast.31.me_ref, s32[1,512]{1,0:T(1,128)S(1)} %bitcast.247, bf16[448,512]{1,0:T(8,128)(2,1)S(1)} %slice.260.q_ref, bf16[896,512]{1,0:T(8,128)(2,1)} %slice.261.refs_0_.refs_1_, ...), custom_call_target="tpu_custom_call" | custom-call | flops 12099999744 | bytes 37400000 | tf_op jit(solution)/shard_map/attention_forward/pallas_call | solution.py:629
  122.9 7.5 %collective-permute-done.18.refs_0_.refs_1_ = bf16[896,512]{1,0:T(8,128)(2,1)} collective-permute-done((bf16[896,512]{1,0:T(8,128)(2,1)}, bf16[896,512]{1,0:T(8,128)(2,1)}, u32[]{:S(2)}, u32[]{:S(2)}) %collective-permute-start.18) | collective-permute-done | bytes 917536 | tf_op jit(solution)/shard_map/ppermute | solution.py:910
  135.6 4.0 attention_forward.3
  153.4 10.9 %collective-permute-done.24.refs_6_.refs_11_ = bf16[200,1600]{1,0:T(8,128)(2,1)} collective-permute-done((bf16[200,1600]{1,0:T(8,128)(2,1)S(1)}, bf16[200,1600]{1,0:T(8,128)(2,1)}, u32[]{:S(2)}, u32[]{:S(2)}) %collective-permute-start.24) | collective-permute-done | bytes 640032 | tf_op jit(solution)/shard_map/ppermute | solution.py:763
  166.1 8.1 %collective-permute-start.30 = (bf16[128,1664]{1,0:T(8,128)(2,1)S(1)}, bf16[128,1664]{1,0:T(8,128)(2,1)S(1)}, u32[]{:S(2)}, u32[]{:S(2)}) collective-permute-start(bf16[128,1664]{1,0:T(8,128)(2,1)S(1)} %pad.13.refs_4_), channel_id=1, source_target_pairs={{0,2},{1,3},{2,0},{3,1},{16,18},{17,19},{18,16},{19,17},{4,6},{5,7... | collective-permute-start | bytes 1277960 | tf_op jit(solution)/shard_map/ppermute | solution.py:763
  177.2 6.1 %project.1 = (bf16[1600,128]{1,0:T(8,128)(2,1)S(1)}, f32[128,1600]{1,0:T(8,128)}, bf16[128,1664]{1,0:T(8,128)(2,1)S(1)}, f32[128,1]{1,0:T(8,128)S(1)}, f32[128,1]{1,0:T(8,128)S(1)}) custom-call(s32[200]{0:T(256)S(1)} %bitcast.252, s32[200]{0:T(256)S(1)} %bitcast.253, bf16[448,128]{1,0:T(8,128)(2,1)S(1)} %get-tuple-element.235.refs_0_, ...), custom_call_target="tpu_custom_call" | custom-call | flops 5500000256 | bytes 17000000 | tf_op jit(solution)/shard_map/project/pallas_call | solution.py:331
  184.9 10.0 %collective-permute-done.31 = bf16[128,1664]{1,0:T(8,128)(2,1)S(1)} collective-permute-done((bf16[128,1664]{1,0:T(8,128)(2,1)S(1)}, bf16[128,1664]{1,0:T(8,128)(2,1)S(1)}, u32[]{:S(2)}, u32[]{:S(2)}) %collective-permute-start.31) | collective-permute-done | bytes 426016 | tf_op jit(solution)/shard_map/ppermute | solution.py:763
  199.8 9.1 %collective-permute-done.33 = bf16[128,1664]{1,0:T(8,128)(2,1)S(1)} collective-permute-done((bf16[128,1664]{1,0:T(8,128)(2,1)S(1)}, bf16[128,1664]{1,0:T(8,128)(2,1)S(1)}, u32[]{:S(2)}, u32[]{:S(2)}) %collective-permute-start.33) | collective-permute-done | bytes 426016 | tf_op jit(solution)/shard_map/ppermute | solution.py:763
  208.9 10.3 %collective-permute-done.34 = bf16[128,1664]{1,0:T(8,128)(2,1)S(1)} collective-permute-done((bf16[128,1664]{1,0:T(8,128)(2,1)S(1)}, bf16[128,1664]{1,0:T(8,128)(2,1)S(1)}, u32[]{:S(2)}, u32[]{:S(2)}) %collective-permute-start.34) | collective-permute-done | bytes 426016 | tf_op jit(solution)/shard_map/ppermute | solution.py:763
  229.5 7.2 %hidden_units.3 = (bf16[512,800]{1,0:T(8,128)(2,1)S(1)}, bf16[512,800]{1,0:T(8,128)(2,1)S(1)}, f32[1,800]{1,0:T(1,128)S(1)}) custom-call(bf16[512,1664]{1,0:T(8,128)(2,1)} %collective-permute-done.37.h_ref.refs_1_, bf16[512,1664]{1,0:T(8,128)(2,1)S(1)} %copy-done.53, bf16[4,2,400,800]{3,2,1,0:T(8,128)(2,1)} %bitcast.226, bf16[4,2,400,800]{3,2,1,0:T(8,128)(2,1)} %bitcast.227, ...), custom_call_target="tpu_custom_call" | custom-call | flops 6600000000 | bytes 20400000 | tf_op jit(solution)/shard_map/hidden_units/pallas_call | solution.py:422
  240.2 7.1 %hidden_units.2 = (bf16[512,800]{1,0:T(8,128)(2,1)S(1)}, bf16[512,800]{1,0:T(8,128)(2,1)S(1)}, f32[1,800]{1,0:T(1,128)S(1)}) custom-call(bf16[512,1664]{1,0:T(8,128)(2,1)S(1)} %constant_dynamic-update-slice_fusion.8.h_ref.refs_0_, bf16[512,1664]{1,0:T(8,128)(2,1)S(1)} %copy-done.48, bf16[4,2,400,800]{3,2,1,0:T(8,128)(2,1)} %bitcast.228, ...), custom_call_target="tpu_custom_call" | custom-call | flops 6600000000 | bytes 20400000 | tf_op jit(solution)/shard_map/hidden_units/pallas_call | solution.py:422
  260.5 12.3 %weight_parts.1 = bf16[4,2,400,800]{3,2,1,0:T(8,128)(2,1)} custom-call(bf16[512,1664]{1,0:T(8,128)(2,1)S(1)} %constant_dynamic-update-slice_fusion.8.h_ref.refs_0_, bf16[512,1664]{1,0:T(8,128)(2,1)} %collective-permute-done.37.h_ref.refs_1_, bf16[512,800]{1,0:T(8,128)(2,1)S(1)} %get-tuple-element.266.g_ref.refs_2_, ...), custom_call_target="tpu_custom_call" | custom-call | flops 9900000256 | bytes 30600000 | tf_op jit(solution)/shard_map/weight_parts/pallas_call | solution.py:481
  279.2 5.9 %project_back.1 = (bf16[128,1600]{1,0:T(8,128)(2,1)S(1)}, bf16[1792,128]{1,0:T(8,128)(2,1)S(1)}, f32[3,1600]{1,0:T(4,128)S(1)}) custom-call(s32[224]{0:T(256)S(1)} %bitcast.251, f32[128,1664]{1,0:T(8,128)} %slice.340.refs_0_, bf16[128,1664]{1,0:T(8,128)(2,1)S(1)} %collective-permute-done.39.refs_1_, bf16[128,1664]{1,0:T(8,128)(2,1)S(1)} %collective-permute-done.40.refs_2_, ...), custom_call_target="tpu_custom_call" | custom-call | flops 5500000256 | bytes 17000000 | tf_op jit(solution)/shard_map/project_back/pallas_call | solution.py:378
  306.3 4.5 attention_backward.2
  313.5 8.7 %collective-permute-done.48 = bf16[128,1664]{1,0:T(8,128)(2,1)S(1)} collective-permute-done((bf16[128,1664]{1,0:T(8,128)(2,1)}, bf16[128,1664]{1,0:T(8,128)(2,1)S(1)}, u32[]{:S(2)}, u32[]{:S(2)}) %collective-permute-start.48) | collective-permute-done | bytes 426016 | tf_op jit(solution)/shard_map/ppermute | solution.py:763
  337.5 8.6 %attention_backward.3 = (bf16[448,512]{1,0:T(8,128)(2,1)S(1)}, bf16[448,512]{1,0:T(8,128)(2,1)S(1)}, bf16[448,512]{1,0:T(8,128)(2,1)S(1)}, bf16[448,512]{1,0:T(8...) custom-call(s32[1]{0:T(128)} %bitcast.31.me_ref, ...), custom_call_target="tpu_custom_call" | custom-call | flops 15399999488 | bytes 47600000 | tf_op jit(solution)/shard_map/attention_backward/pallas_call | solution.py:727
  346.1 29.6 %collective-permute-done.53.refs_10_ = bf16[800,128]{1,0:T(8,128)(2,1)S(1)} collective-permute-done((bf16[800,128]{1,0:T(8,128)(2,1)S(1)}, bf16[800,128]{1,0:T(8,128)(2,1)S(1)}, u32[]{:S(2)}, u32[]{:S(2)}) %collective-permute-start.53) | collective-permute-done | bytes 204832 | tf_op jit(solution)/shard_map/ppermute | solution.py:754
  375.9 4.9 fusion.58
  387.1 7.1 %qkv_back.1 = (bf16[4,2,208,512]{3,2,1,0:T(8,128)(2,1)}, f32[2,800,1]{2,1,0:T(8,128)S(1)}, f32[2,800,1]{2,1,0:T(8,128)S(1)}) custom-call(bf16[2,2,800,384]{3,2,1,0:T(8,128)(2,1)} %bitcast.25.w_ref.first, bf16[2,2,800,384]{3,2,1,0:T(8,128)(2,1)} %bitcast.26.w_ref.second, bf16[1536,512]{1,0:T(8,128)(2,1)S(1)} %move_units.3.g_ref, ...), custom_call_target="tpu_custom_call" | custom-call | flops 7699999744 | bytes 23800000 | tf_op jit(solution)/shard_map/qkv_back/pallas_call | solution.py:241
  402.6 12.5 %collective-permute-done.64 = bf16[200,1600]{1,0:T(8,128)(2,1)} collective-permute-done((bf16[200,1600]{1,0:T(8,128)(2,1)}, bf16[200,1600]{1,0:T(8,128)(2,1)}, u32[]{:S(2)}, u32[]{:S(2)}) %collective-permute-start.64) | collective-permute-done | bytes 640032 | tf_op jit(solution)/shard_map/ppermute | solution.py:763
  448.4 6.7 %collective-permute-done.61.refs_2_ = bf16[2,208,512]{2,1,0:T(8,128)(2,1)} collective-permute-done((bf16[2,208,512]{2,1,0:T(8,128)(2,1)}, bf16[2,208,512]{2,1,0:T(8,128)(2,1)}, u32[]{:S(2)}, u32[]{:S(2)}) %collective-permute-start.61) | collective-permute-done | bytes 426016 | tf_op jit(solution)/shard_map/ppermute | solution.py:754
  455.1 4.1 collective-permute-done.57
  460.1 11.2 %collective-permute-done.59 = bf16[1,800,384]{2,1,0:T(8,128)(2,1)} collective-permute-done((bf16[1,800,384]{2,1,0:T(8,128)(2,1)}, bf16[1,800,384]{2,1,0:T(8,128)(2,1)}, u32[]{:S(2)}, u32[]{:S(2)}) %collective-permute-start.59) | collective-permute-done | bytes 614432 | tf_op jit(solution)/shard_map/ppermute | solution.py:763
  (568 shorter events, 259.6 us)
Async XLA Ops:
  7.2 214.8 %all-gather.2.cloned.1.call-start = ((), (), s32[]{:S(2)}) async-start(), calls=%async_computation.1 | async-start | bytes 7168000 | tf_op jit(solution)/shard_map/all_gather | solution.py:874
  11.8 29.6 %collective-permute-start = (bf16[200,384]{1,0:T(8,128)(2,1)}, bf16[200,384]{1,0:T(8,128)(2,1)S(1)}, u32[]{:S(2)}, u32[]{:S(2)}) collective-permute-start(bf16[200,384]{1,0:T(8,128)(2,1)} %get-tuple-element.429), channel_id=1, source_target_pairs={{0,12},{4,0},{8,4},{12,8},{1,13},{5,1},{9,5},{13,9},{2,14},{6,2},{... | collective-permute-start | bytes 460808 | tf_op jit(solution)/shard_map/ppermute | solution.py:754
  16.9 24.5 %collective-permute-start.1 = (bf16[200,384]{1,0:T(8,128)(2,1)}, bf16[200,384]{1,0:T(8,128)(2,1)}, u32[]{:S(2)}, u32[]{:S(2)}) collective-permute-start(bf16[200,384]{1,0:T(8,128)(2,1)} %get-tuple-element.428), channel_id=1, source_target_pairs={{0,8},{4,12},{8,0},{12,4},{1,9},{5,13},{9,1},{13,5},{2,10},{6,14},... | collective-permute-start | bytes 460808 | tf_op jit(solution)/shard_map/ppermute | solution.py:754
  16.9 24.5 %collective-permute-start.2 = (bf16[200,384]{1,0:T(8,128)(2,1)}, bf16[200,384]{1,0:T(8,128)(2,1)}, u32[]{:S(2)}, u32[]{:S(2)}) collective-permute-start(bf16[200,384]{1,0:T(8,128)(2,1)} %get-tuple-element.427), channel_id=1, source_target_pairs={{0,4},{4,8},{8,12},{12,0},{1,5},{5,9},{9,13},{13,1},{2,6},{6,10},{... | collective-permute-start | bytes 460808 | tf_op jit(solution)/shard_map/ppermute | solution.py:754
  43.1 31.1 %collective-permute-start.7 = (bf16[1,800,384]{2,1,0:T(8,128)(2,1)S(1)}, bf16[1,800,384]{2,1,0:T(8,128)(2,1)S(1)}, u32[]{:S(2)}, u32[]{:S(2)}) collective-permute-start(bf16[1,800,384]{2,1,0:T(8,128)(2,1)S(1)} %bitcast.258), channel_id=1, source_target_pairs={{0,2},{1,3},{2,0},{3,1},{16,18},{17,19},{18,16},{19,17},{4,6},{5,7... | collective-permute-start | bytes 1843208 | tf_op jit(solution)/shard_map/ppermute | solution.py:763
  44.6 29.5 %collective-permute-start.8 = (bf16[1,800,384]{2,1,0:T(8,128)(2,1)S(1)}, bf16[1,800,384]{2,1,0:T(8,128)(2,1)S(1)}, u32[]{:S(2)}, u32[]{:S(2)}) collective-permute-start(bf16[1,800,384]{2,1,0:T(8,128)(2,1)S(1)} %bitcast.259), channel_id=1, source_target_pairs={{0,16},{1,17},{2,18},{3,19},{16,0},{17,1},{18,2},{19,3},{4,20},{5,... | collective-permute-start | bytes 1843208 | tf_op jit(solution)/shard_map/ppermute | solution.py:763
  46.2 28.0 %collective-permute-start.9 = (bf16[1,800,384]{2,1,0:T(8,128)(2,1)S(1)}, bf16[1,800,384]{2,1,0:T(8,128)(2,1)S(1)}, u32[]{:S(2)}, u32[]{:S(2)}) collective-permute-start(bf16[1,800,384]{2,1,0:T(8,128)(2,1)S(1)} %bitcast.260), channel_id=1, source_target_pairs={{0,18},{1,19},{2,16},{3,17},{16,2},{17,3},{18,0},{19,1},{4,22},{5,... | collective-permute-start | bytes 1843208 | tf_op jit(solution)/shard_map/ppermute | solution.py:763
  46.6 27.5 %collective-permute-start.11 = (bf16[2,200,512]{2,1,0:T(8,128)(2,1)S(1)}, bf16[2,200,512]{2,1,0:T(8,128)(2,1)}, u32[]{:S(2)}, u32[]{:S(2)}) collective-permute-start(bf16[2,200,512]{2,1,0:T(8,128)(2,1)S(1)} %pad_maximum_fusion.10.refs_4_), channel_id=1, source_target_pairs={{0,8},{4,12},{8,0},{12,4},{1,9},{5,13},{9,1},{13,5},{2,10},{6,14},... | collective-permute-start | bytes 1228808 | tf_op jit(solution)/shard_map/ppermute | solution.py:754
  51.2 23.0 %collective-permute-start.12 = (bf16[2,200,512]{2,1,0:T(8,128)(2,1)S(1)}, bf16[2,200,512]{2,1,0:T(8,128)(2,1)}, u32[]{:S(2)}, u32[]{:S(2)}) collective-permute-start(bf16[2,200,512]{2,1,0:T(8,128)(2,1)S(1)} %pad_maximum_fusion.10.refs_4_), channel_id=1, source_target_pairs={{0,4},{4,8},{8,12},{12,0},{1,5},{5,9},{9,13},{13,1},{2,6},{6,10},{... | collective-permute-start | bytes 1228808 | tf_op jit(solution)/shard_map/ppermute | solution.py:754
  81.2 23.4 %collective-permute-start.15 = (bf16[200,400]{1,0:T(8,128)(2,1)}, bf16[200,400]{1,0:T(8,128)(2,1)}, u32[]{:S(2)}, u32[]{:S(2)}) collective-permute-start(bf16[200,400]{1,0:T(8,128)(2,1)} %convert_element_type.176), channel_id=1, source_target_pairs={{0,8},{4,12},{8,0},{12,4},{1,9},{5,13},{9,1},{13,5},{2,10},{6,14},... | collective-permute-start | bytes 480008 | tf_op jit(solution)/shard_map/ppermute | solution.py:754
  106.3 339.4 %reduce-scatter.2.cloned.1.call-start = ((), (), s32[]{:S(2)}) async-start(), calls=%async_computation.2 | async-start | bytes 7168000 | tf_op jit(solution)/shard_map/reduce_scatter | solution.py:969
  106.4 24.0 %collective-permute-start.18 = (bf16[896,512]{1,0:T(8,128)(2,1)}, bf16[896,512]{1,0:T(8,128)(2,1)}, u32[]{:S(2)}, u32[]{:S(2)}) collective-permute-start(bf16[896,512]{1,0:T(8,128)(2,1)} %slice.261.refs_0_.refs_1_), channel_id=1, source_target_pairs={{0,2},{1,3},{4,6},{5,7},{8,10},{9,11},{12,14},{13,15},{16,18},{17,... | collective-permute-start | bytes 2752520 | tf_op jit(solution)/shard_map/ppermute | solution.py:910
  132.9 31.5 %collective-permute-start.24 = (bf16[200,1600]{1,0:T(8,128)(2,1)S(1)}, bf16[200,1600]{1,0:T(8,128)(2,1)}, u32[]{:S(2)}, u32[]{:S(2)}) collective-permute-start(bf16[200,1600]{1,0:T(8,128)(2,1)S(1)} %concatenate.64.refs_4_.refs_9_), channel_id=1, source_target_pairs={{0,16},{1,17},{2,18},{3,19},{16,0},{17,1},{18,2},{19,3},{4,20},{5,... | collective-permute-start | bytes 1920008 | tf_op jit(solution)/shard_map/ppermute | solution.py:763
  134.4 29.9 %collective-permute-start.25 = (bf16[200,1600]{1,0:T(8,128)(2,1)S(1)}, bf16[200,1600]{1,0:T(8,128)(2,1)}, u32[]{:S(2)}, u32[]{:S(2)}) collective-permute-start(bf16[200,1600]{1,0:T(8,128)(2,1)S(1)} %concatenate.64.refs_4_.refs_9_), channel_id=1, source_target_pairs={{0,18},{1,19},{2,16},{3,17},{16,2},{17,3},{18,0},{19,1},{4,22},{5,... | collective-permute-start | bytes 1920008 | tf_op jit(solution)/shard_map/ppermute | solution.py:763
  140.5 23.8 %collective-permute-start.20 = (bf16[448,128]{1,0:T(8,128)(2,1)}, bf16[448,128]{1,0:T(8,128)(2,1)S(1)}, u32[]{:S(2)}, u32[]{:S(2)}) collective-permute-start(bf16[448,128]{1,0:T(8,128)(2,1)} %get-tuple-element.441), channel_id=1, source_target_pairs={{0,12},{4,0},{8,4},{12,8},{1,13},{5,1},{9,5},{13,9},{2,14},{6,2},{... | collective-permute-start | bytes 344072 | tf_op jit(solution)/shard_map/ppermute | solution.py:754
  140.5 23.8 %collective-permute-start.21 = (bf16[448,128]{1,0:T(8,128)(2,1)}, bf16[448,128]{1,0:T(8,128)(2,1)}, u32[]{:S(2)}, u32[]{:S(2)}) collective-permute-start(bf16[448,128]{1,0:T(8,128)(2,1)} %get-tuple-element.440), channel_id=1, source_target_pairs={{0,8},{4,12},{8,0},{12,4},{1,9},{5,13},{9,1},{13,5},{2,10},{6,14},... | collective-permute-start | bytes 344072 | tf_op jit(solution)/shard_map/ppermute | solution.py:754
  195.0 25.7 %collective-permute-start.36 = (bf16[512,1664]{1,0:T(8,128)(2,1)S(1)}, bf16[512,1664]{1,0:T(8,128)(2,1)S(1)}, u32[]{:S(2)}, u32[]{:S(2)}) collective-permute-start(bf16[512,1664]{1,0:T(8,128)(2,1)S(1)} %constant_dynamic-update-slice_fusion.4.t_ref.refs_4_), channel_id=1, source_target_pairs={{0,1},{1,0},{2,3},{3,2},{16,17},{17,16},{18,19},{19,18},{4,5},{5,4... | collective-permute-start | bytes 5111816 | tf_op jit(solution)/shard_map/ppermute | solution.py:763
  253.5 25.6 %collective-permute-start.42 = (bf16[512,1664]{1,0:T(8,128)(2,1)}, bf16[512,1664]{1,0:T(8,128)(2,1)}, u32[]{:S(2)}, u32[]{:S(2)}) collective-permute-start(bf16[512,1664]{1,0:T(8,128)(2,1)} %features_back.6), channel_id=1, source_target_pairs={{0,1},{1,0},{2,3},{3,2},{16,17},{17,16},{18,19},{19,18},{4,5},{5,4... | collective-permute-start | bytes 5111816 | tf_op jit(solution)/shard_map/ppermute | solution.py:763
  332.3 43.4 %collective-permute-start.53 = (bf16[800,128]{1,0:T(8,128)(2,1)S(1)}, bf16[800,128]{1,0:T(8,128)(2,1)S(1)}, u32[]{:S(2)}, u32[]{:S(2)}) collective-permute-start(bf16[800,128]{1,0:T(8,128)(2,1)S(1)} %get-tuple-element.410), channel_id=1, source_target_pairs={{0,8},{4,12},{8,0},{12,4},{1,9},{5,13},{9,1},{13,5},{2,10},{6,14},... | collective-permute-start | bytes 614408 | tf_op jit(solution)/shard_map/ppermute | solution.py:754
  332.9 42.9 %collective-permute-start.54 = (bf16[800,128]{1,0:T(8,128)(2,1)S(1)}, bf16[800,128]{1,0:T(8,128)(2,1)S(1)}, u32[]{:S(2)}, u32[]{:S(2)}) collective-permute-start(bf16[800,128]{1,0:T(8,128)(2,1)S(1)} %get-tuple-element.407), channel_id=1, source_target_pairs={{0,4},{4,8},{8,12},{12,0},{1,5},{5,9},{9,13},{13,1},{2,6},{6,10},{... | collective-permute-start | bytes 614408 | tf_op jit(solution)/shard_map/ppermute | solution.py:754
  336.1 39.6 %collective-permute-start.51 = (bf16[896,512]{1,0:T(8,128)(2,1)S(1)}, bf16[896,512]{1,0:T(8,128)(2,1)S(1)}, u32[]{:S(2)}, u32[]{:S(2)}) collective-permute-start(bf16[896,512]{1,0:T(8,128)(2,1)S(1)} %add_convert_fusion.2), channel_id=1, source_target_pairs={{2,0},{3,1},{6,4},{7,5},{10,8},{11,9},{14,12},{15,13},{18,16},{19,... | collective-permute-start | bytes 2752520 | tf_op jit(solution)/shard_map/ppermute | solution.py:1007
  383.8 31.2 %collective-permute-start.64 = (bf16[200,1600]{1,0:T(8,128)(2,1)}, bf16[200,1600]{1,0:T(8,128)(2,1)}, u32[]{:S(2)}, u32[]{:S(2)}) collective-permute-start(bf16[200,1600]{1,0:T(8,128)(2,1)} %get-tuple-element.384), channel_id=1, source_target_pairs={{0,16},{1,17},{2,18},{3,19},{16,0},{17,1},{18,2},{19,3},{4,20},{5,... | collective-permute-start | bytes 1920008 | tf_op jit(solution)/shard_map/ppermute | solution.py:763
  384.9 30.2 %collective-permute-start.63 = (bf16[200,1600]{1,0:T(8,128)(2,1)}, bf16[200,1600]{1,0:T(8,128)(2,1)}, u32[]{:S(2)}, u32[]{:S(2)}) collective-permute-start(bf16[200,1600]{1,0:T(8,128)(2,1)} %get-tuple-element.382), channel_id=1, source_target_pairs={{0,2},{1,3},{2,0},{3,1},{16,18},{17,19},{18,16},{19,17},{4,6},{5,7... | collective-permute-start | bytes 1920008 | tf_op jit(solution)/shard_map/ppermute | solution.py:763
  399.8 38.8 %collective-permute-start.56 = (bf16[4,800,384]{2,1,0:T(8,128)(2,1)}, bf16[4,800,384]{2,1,0:T(8,128)(2,1)}, u32[]{:S(2)}, u32[]{:S(2)}) collective-permute-start(bf16[4,800,384]{2,1,0:T(8,128)(2,1)} %bitcast.93), channel_id=1, source_target_pairs={{0,1},{1,0},{2,3},{3,2},{16,17},{17,16},{18,19},{19,18},{4,5},{5,4... | collective-permute-start | bytes 7372808 | tf_op jit(solution)/shard_map/ppermute | solution.py:763
  422.8 21.1 %collective-permute-start.60 = (bf16[2,208,512]{2,1,0:T(8,128)(2,1)}, bf16[2,208,512]{2,1,0:T(8,128)(2,1)}, u32[]{:S(2)}, u32[]{:S(2)}) collective-permute-start(bf16[2,208,512]{2,1,0:T(8,128)(2,1)} %get-tuple-element.390), channel_id=1, source_target_pairs={{0,4},{4,8},{8,12},{12,0},{1,5},{5,9},{9,13},{13,1},{2,6},{6,10},{... | collective-permute-start | bytes 1277960 | tf_op jit(solution)/shard_map/ppermute | solution.py:754
  423.4 31.7 %collective-permute-start.61 = (bf16[2,208,512]{2,1,0:T(8,128)(2,1)}, bf16[2,208,512]{2,1,0:T(8,128)(2,1)}, u32[]{:S(2)}, u32[]{:S(2)}) collective-permute-start(bf16[2,208,512]{2,1,0:T(8,128)(2,1)} %get-tuple-element.389), channel_id=1, source_target_pairs={{0,8},{4,12},{8,0},{12,4},{1,9},{5,13},{9,1},{13,5},{2,10},{6,14},... | collective-permute-start | bytes 1277960 | tf_op jit(solution)/shard_map/ppermute | solution.py:754
  425.5 29.6 %collective-permute-start.62 = (bf16[2,208,512]{2,1,0:T(8,128)(2,1)}, bf16[2,208,512]{2,1,0:T(8,128)(2,1)}, u32[]{:S(2)}, u32[]{:S(2)}) collective-permute-start(bf16[2,208,512]{2,1,0:T(8,128)(2,1)} %get-tuple-element.388), channel_id=1, source_target_pairs={{0,12},{4,0},{8,4},{12,8},{1,13},{5,1},{9,5},{13,9},{2,14},{6,2},{... | collective-permute-start | bytes 1277960 | tf_op jit(solution)/shard_map/ppermute | solution.py:754
  443.9 27.5 %collective-permute-start.59 = (bf16[1,800,384]{2,1,0:T(8,128)(2,1)}, bf16[1,800,384]{2,1,0:T(8,128)(2,1)}, u32[]{:S(2)}, u32[]{:S(2)}) collective-permute-start(bf16[1,800,384]{2,1,0:T(8,128)(2,1)} %get-tuple-element.385), channel_id=1, source_target_pairs={{0,18},{1,19},{2,16},{3,17},{16,2},{17,3},{18,0},{19,1},{4,22},{5,... | collective-permute-start | bytes 1843208 | tf_op jit(solution)/shard_map/ppermute | solution.py:763
  474.0 21.9 %collective-permute-start.67 = (bf16[200,384]{1,0:T(8,128)(2,1)}, bf16[200,384]{1,0:T(8,128)(2,1)}, u32[]{:S(2)}, u32[]{:S(2)}) collective-permute-start(bf16[200,384]{1,0:T(8,128)(2,1)} %get-tuple-element.425), channel_id=1, source_target_pairs={{0,8},{4,12},{8,0},{12,4},{1,9},{5,13},{9,1},{13,5},{2,10},{6,14},... | collective-permute-start | bytes 460808 | tf_op jit(solution)/shard_map/ppermute | solution.py:754
  475.0 21.4 %collective-permute-start.66 = (bf16[200,384]{1,0:T(8,128)(2,1)}, bf16[200,384]{1,0:T(8,128)(2,1)}, u32[]{:S(2)}, u32[]{:S(2)}) collective-permute-start(bf16[200,384]{1,0:T(8,128)(2,1)} %get-tuple-element.426), channel_id=1, source_target_pairs={{0,12},{4,0},{8,4},{12,8},{1,13},{5,1},{9,5},{13,9},{2,14},{6,2},{... | collective-permute-start | bytes 460808 | tf_op jit(solution)/shard_map/ppermute | solution.py:754
  482.8 25.3 %collective-permute-start.71 = (bf16[200,400]{1,0:T(8,128)(2,1)S(1)}, bf16[200,400]{1,0:T(8,128)(2,1)S(1)}, u32[]{:S(2)}, u32[]{:S(2)}) collective-permute-start(bf16[200,400]{1,0:T(8,128)(2,1)S(1)} %bitcast.287), channel_id=1, source_target_pairs={{0,4},{4,8},{8,12},{12,0},{1,5},{5,9},{9,13},{13,1},{2,6},{6,10},{... | collective-permute-start | bytes 480008 | tf_op jit(solution)/shard_map/ppermute | solution.py:754
  495.9 21.6 %collective-permute-start.72 = (bf16[200,800]{1,0:T(8,128)(2,1)S(1)}, bf16[200,800]{1,0:T(8,128)(2,1)S(1)}, u32[]{:S(2)}, u32[]{:S(2)}) collective-permute-start(bf16[200,800]{1,0:T(8,128)(2,1)S(1)} %get-tuple-element.417), channel_id=1, source_target_pairs={{0,16},{16,0},{1,17},{17,1},{2,18},{18,2},{3,19},{19,3},{4,20},{20... | collective-permute-start | bytes 960008 | tf_op jit(solution)/shard_map/ppermute | solution.py:789
  (157 other events, 1690.9 us)
Sparse Core Ops, SparseCore 0:
  106.4 114.2 all-gather.1
  301.5 114.4 reduce-scatter.1
